TPU v7x, 512 devices: a whole 4x8x8 slice. The times are simulated.
512 devices in a mesh: dom: 128 (over y, z, core), phase: 4 (over x).
Axes of the slice: x: 4, y: 8, z: 8, core: 2. Of those that a mesh axis runs over, the one named last changes fastest.
Arguments:
- grid_in: bfloat16 [4, 131072, 474], P('phase', 'dom'), may hold values from -6 to 6
- mesh_static: bfloat16 [32768, 512], P('dom'), may hold values from -6 to 6
- embed_w: bfloat16 [474, 512], P(None, 'phase'), may hold values from -0.25 to 0.25
- grid_w: bfloat16 [512, 512], P(None, 'phase'), may hold values from -0.25 to 0.25
- enc_w: bfloat16 [512, 512], P(None, 'phase'), may hold values from -0.25 to 0.25
- src_w: bfloat16 [2, 512, 512], P(None, None, 'phase'), may hold values from -0.25 to 0.25
- node_w: bfloat16 [2, 512, 512], P(None, None, 'phase'), may hold values from -0.25 to 0.25
- dec_w: bfloat16 [512, 512], P(None, 'phase'), may hold values from -0.25 to 0.25
- out_w: bfloat16 [512, 227], P('phase'), may hold values from -0.25 to 0.25
- cotangent: bfloat16 [4, 131072, 227], P('phase', 'dom'), may hold values from -6 to 6
- grid_send: int32 [128, 6, 12], P('dom'), may hold values from 0 to 1023
- g2m_src: int32 [128, 2048], P('dom'), may hold values from 0 to 1095, as said below
- g2m_dst: int32 [128, 2048], P('dom'), may hold values from 0 to 255, never falling along the last dimension, each value on 1 to 24 neighbouring positions
- mesh_send: int32 [128, 6, 8], P('dom'), may hold values from 0 to 255
- mesh_src: int32 [128, 2048], P('dom'), may hold values from 0 to 303, as said below
- mesh_dst: int32 [128, 2048], P('dom'), may hold values from 0 to 255, never falling along the last dimension, each value on 1 to 24 neighbouring positions
- dec_send: int32 [128, 6, 8], P('dom'), may hold values from 0 to 255
- m2g_src: int32 [128, 3072], P('dom'), may hold values from 0 to 303, as said below
- m2g_dst: int32 [128, 3072], P('dom'), may hold values from 0 to 1023, never falling along the last dimension, each value on 1 to 8 neighbouring positions
Outputs:
- pred: bfloat16 [4, 131072, 227], P('phase', 'dom')
- input_grad: bfloat16 [4, 131072, 474], P('phase', 'dom')
Inputs may be any that keep to these rules, and one draw needn't show every extreme that they name: `g2m_src`: on partition d, entries below 1024 name own grid rows; every slot entry 1024 + k * 12 + s is named by exactly one edge of d. `mesh_src`: on partition d, entries below 256 name own mesh rows; every slot entry is named by exactly one edge of d. `m2g_src`: on partition d, entries below 256 name own mesh rows; every slot entry is named by exactly one edge of d.
All inputs are finite; a program needn't handle non-finite values.
Results may differ from a plain program's by a relative error of at most 0.02.
Values may be sent and summed in bfloat16 or wider, within the bound.
No kernel may reach another device: no remote copies, remote signals or barrier semaphores. Data moves between devices by JAX's collectives and lax.ppermute only.
A program may use at most 128 MiB of HBM per device.

v0:
```python
import jax
import jax.numpy as jnp
from jax import lax
from jax.sharding import PartitionSpec as P

LAYERS = 2


EPSILON = 1e-06


def from_behind(block, axis, distance):
    devices = range(lax.axis_size(axis))
    route = [((i - distance) % len(devices), i) for i in devices]
    return lax.ppermute(block, axis, route)


def bfloat(values):
    return values.astype(jnp.bfloat16)


def single(values):
    return values.astype(jnp.float32)


def silu_slope(values):
    sigmoid_value = jax.nn.sigmoid(values)
    return sigmoid_value * (1.0 + values * (1.0 - sigmoid_value))


def inverse_rms(values):
    return lax.rsqrt(jnp.mean(values * values, axis=-1, keepdims=True) + EPSILON)


def forward_product(left, right):
    return jnp.dot(left, right, preferred_element_type=jnp.float32)


def backward_product(left, right):
    return lax.dot_general(
        left, right, (((1,), (1,)), ((), ())), preferred_element_type=jnp.float32
    )


def neighbour_list(count):
    return [(position // 2 + 1) * (1 - 2 * (position % 2)) for position in range(count)]


def halo_forward(groups):
    offsets = neighbour_list(groups.shape[0])
    pieces = []
    for position in range(groups.shape[0]):
        pieces.append(from_behind(groups[position], "dom", offsets[position]))
    return jnp.stack(pieces)


def halo_backward(groups):
    offsets = neighbour_list(groups.shape[0])
    pieces = []
    for position in range(groups.shape[0]):
        pieces.append(from_behind(groups[position], "dom", -offsets[position]))
    return jnp.stack(pieces)


def cols_forward(row_block, weight):
    return forward_product(row_block, weight)


def cols_backward(gradient, weight):
    return backward_product(gradient, weight)


def out_forward(row_block, weight):
    return forward_product(row_block, weight)


def out_backward(gradient, weight):
    return backward_product(gradient, weight)


def return_rows(edge_grad, sources, send_table, local_count):
    neighbours, slot_count = send_table.shape
    features = edge_grad.shape[-1]
    span = local_count + neighbours * slot_count
    sums_block = bfloat(jax.ops.segment_sum(single(edge_grad), sources, num_segments=span))
    outgoing = sums_block[local_count:].reshape(neighbours, slot_count, features)
    returned = halo_backward(outgoing)
    own_rows = single(sums_block[:local_count])
    back_rows = single(returned.reshape(-1, features))
    added = jax.ops.segment_sum(back_rows, send_table.reshape(-1), num_segments=local_count)
    return bfloat(own_rows + added)


def per_device(
    grid_in,
    mesh_static,
    embed_w,
    grid_w,
    enc_w,
    src_w,
    node_w,
    dec_w,
    out_w,
    cotangent,
    grid_send,
    g2m_src,
    g2m_dst,
    mesh_send,
    mesh_src,
    mesh_dst,
    dec_send,
    m2g_src,
    m2g_dst,
):
    weights = (
        lax.all_gather(embed_w, "phase", axis=1, tiled=True),
        lax.all_gather(grid_w, "phase", axis=1, tiled=True),
        lax.all_gather(enc_w, "phase", axis=1, tiled=True),
        lax.all_gather(src_w, "phase", axis=2, tiled=True),
        lax.all_gather(node_w, "phase", axis=2, tiled=True),
        lax.all_gather(dec_w, "phase", axis=1, tiled=True),
        lax.all_gather(out_w, "phase", axis=0, tiled=True),
    )
    embed_m, grid_m, enc_m, src_m, node_m, dec_m, out_m = weights
    grid_rows = grid_in[0]
    cotangent_rows = cotangent[0]
    grid_count = grid_rows.shape[0]
    mesh_count = mesh_static.shape[0]
    features = mesh_static.shape[1]
    grid_table = grid_send[0]
    mesh_table = mesh_send[0]
    dec_table = dec_send[0]
    grid_source = g2m_src[0]
    grid_receiver = g2m_dst[0]
    mesh_source = mesh_src[0]
    mesh_receiver = mesh_dst[0]
    dec_source = m2g_src[0]
    dec_receiver = m2g_dst[0]
    pre_hidden = cols_forward(grid_rows, embed_m)
    hidden = bfloat(jax.nn.silu(pre_hidden))
    projected = bfloat(cols_forward(hidden, grid_m))
    incoming = halo_forward(projected[grid_table])
    grid_extended = jnp.concatenate([projected, incoming.reshape(-1, features)], axis=0)
    enc_pre = single(grid_extended[grid_source]) + single(mesh_static[grid_receiver])
    enc_msg = bfloat(jax.nn.silu(enc_pre))
    enc_sum = bfloat(
        jax.ops.segment_sum(
            single(enc_msg), grid_receiver, num_segments=mesh_count, indices_are_sorted=True
        )
    )
    encoded = cols_forward(enc_sum, enc_m)
    enc_scale = inverse_rms(encoded)
    latent = bfloat(single(mesh_static) + encoded * enc_scale)
    stored = []
    for layer_index in range(LAYERS):
        src_proj = bfloat(cols_forward(latent, src_m[layer_index]))
        received = halo_forward(src_proj[mesh_table])
        mesh_extended = jnp.concatenate([src_proj, received.reshape(-1, features)], axis=0)
        edge_pre = single(mesh_extended[mesh_source]) + single(latent[mesh_receiver])
        edge_msg = bfloat(jax.nn.silu(edge_pre))
        edge_sum = bfloat(
            jax.ops.segment_sum(
                single(edge_msg), mesh_receiver, num_segments=mesh_count, indices_are_sorted=True
            )
        )
        update = cols_forward(edge_sum, node_m[layer_index])
        layer_scale = inverse_rms(update)
        stored.append((edge_pre, update, layer_scale))
        latent = bfloat(single(latent) + update * layer_scale)
    decoded = bfloat(cols_forward(latent, dec_m))
    dec_received = halo_forward(decoded[dec_table])
    dec_extended = jnp.concatenate([decoded, dec_received.reshape(-1, features)], axis=0)
    dec_pre = single(dec_extended[dec_source]) + single(hidden[dec_receiver])
    dec_msg = bfloat(jax.nn.silu(dec_pre))
    dec_sum = bfloat(
        jax.ops.segment_sum(
            single(dec_msg), dec_receiver, num_segments=grid_count, indices_are_sorted=True
        )
    )
    prediction = bfloat(out_forward(dec_sum, out_m))
    dec_sum_grad = bfloat(out_backward(cotangent_rows, out_m))
    dec_edge_grad = bfloat(single(dec_sum_grad[dec_receiver]) * silu_slope(dec_pre))
    decoded_grad = return_rows(dec_edge_grad, dec_source, dec_table, mesh_count)
    latent_grad = cols_backward(decoded_grad, dec_m)
    for layer_index in reversed(range(LAYERS)):
        edge_pre, update, layer_scale = stored[layer_index]
        mixed = jnp.mean(latent_grad * update, axis=-1, keepdims=True)
        update_grad = bfloat(layer_scale * latent_grad - update * layer_scale**3 * mixed)
        sum_grad = bfloat(cols_backward(update_grad, node_m[layer_index]))
        edge_grad = bfloat(single(sum_grad[mesh_receiver]) * silu_slope(edge_pre))
        src_grad = return_rows(edge_grad, mesh_source, mesh_table, mesh_count)
        into_rows = jax.ops.segment_sum(
            single(edge_grad), mesh_receiver, num_segments=mesh_count, indices_are_sorted=True
        )
        latent_grad = latent_grad + into_rows + cols_backward(src_grad, src_m[layer_index])
    mixed = jnp.mean(latent_grad * encoded, axis=-1, keepdims=True)
    encoded_grad = bfloat(enc_scale * latent_grad - encoded * enc_scale**3 * mixed)
    summed_grad = bfloat(cols_backward(encoded_grad, enc_m))
    msg_grad = bfloat(single(summed_grad[grid_receiver]) * silu_slope(enc_pre))
    projected_grad = return_rows(msg_grad, grid_source, grid_table, grid_count)
    skip_grad = jax.ops.segment_sum(
        single(dec_edge_grad), dec_receiver, num_segments=grid_count, indices_are_sorted=True
    )
    hidden_grad = cols_backward(projected_grad, grid_m) + skip_grad
    pre_grad = bfloat(hidden_grad * silu_slope(pre_hidden))
    input_gradient = bfloat(cols_backward(pre_grad, embed_m))
    return (prediction[None], input_gradient[None])


def solution(mesh):
    placed = (
        P("phase", "dom", None),
        P("dom", None),
        P(None, "phase"),
        P(None, "phase"),
        P(None, "phase"),
        P(None, None, "phase"),
        P(None, None, "phase"),
        P(None, "phase"),
        P("phase", None),
        P("phase", "dom", None),
        P("dom", None, None),
        P("dom", None),
        P("dom", None),
        P("dom", None, None),
        P("dom", None),
        P("dom", None),
        P("dom", None, None),
        P("dom", None),
        P("dom", None),
    )
    return jax.shard_map(
        per_device,
        mesh=mesh,
        in_specs=placed,
        out_specs=(P("phase", "dom", None), P("phase", "dom", None)),
        check_vma=False,
    )
```

profile of v0, /device:TPU:1, one launch (start us, length us, event | category | flops | bytes accessed | tf_op | source)
XLA Modules:
  0.0 705.7 jit_solution(3717855079830453042)
XLA Ops:
  8.8 12.5 %all_gather.21 = bf16[474,512]{1,0:T(8,128)(2,1)S(1)} all-gather(bf16[474,128]{1,0:T(8,128)(2,1)} %param.21), channel_id=1, replica_groups=mesh['dom'=128,'phase'=4] {'phase'}, dimensions={1}, use_global_device_ids=true | all-gather | bytes 606720 | tf_op jit(solution)/shard_map/all_gather | solution.py:116
  21.2 11.3 %all_gather.22 = bf16[512,512]{1,0:T(8,128)(2,1)S(1)} all-gather(bf16[512,128]{1,0:T(8,128)(2,1)} %param.22), channel_id=1, replica_groups=mesh['dom'=128,'phase'=4] {'phase'}, dimensions={1}, use_global_device_ids=true | all-gather | bytes 655360 | tf_op jit(solution)/shard_map/all_gather | solution.py:117
  36.4 10.6 %collective-permute-start = (bf16[12,512]{1,0:T(8,128)(2,1)S(1)}, bf16[12,512]{1,0:T(8,128)(2,1)S(1)}, u32[]{:S(2)}, u32[]{:S(2)}) collective-permute-start(bf16[12,512]{1,0:T(8,128)(2,1)S(1)} %get-tuple-element.31), channel_id=1, source_target_pairs={{508,0},{0,4},{4,8},{8,12},{12,16},{16,20},{20,24},{24,28},{28,32}... | collective-permute-start | bytes 36872 | tf_op jit(solution)/shard_map/ppermute | solution.py:15
  47.0 5.4 collective-permute-start.1
  54.3 10.4 %collective-permute-start.3 = (bf16[12,512]{1,0:T(8,128)(2,1)S(1)}, bf16[12,512]{1,0:T(8,128)(2,1)S(1)}, u32[]{:S(2)}, u32[]{:S(2)}) collective-permute-start(bf16[12,512]{1,0:T(8,128)(2,1)S(1)} %get-tuple-element.28), channel_id=1, source_target_pairs={{8,0},{12,4},{16,8},{20,12},{24,16},{28,20},{32,24},{36,28},{40,32... | collective-permute-start | bytes 36872 | tf_op jit(solution)/shard_map/ppermute | solution.py:15
  66.6 8.9 %all_gather.27 = bf16[512,227]{0,1:T(8,128)(2,1)S(1)} all-gather(bf16[128,227]{0,1:T(8,128)(2,1)S(1)} %copy-done.24), channel_id=1, replica_groups=mesh['dom'=128,'phase'=4] {'phase'}, dimensions={0}, use_global_device_ids=true | all-gather | bytes 290560 | tf_op jit(solution)/shard_map/all_gather | solution.py:122
  75.6 14.5 %all_gather.26 = bf16[512,512]{1,0:T(8,128)(2,1)} all-gather(bf16[512,128]{1,0:T(8,128)(2,1)S(1)} %copy-done.22), channel_id=1, replica_groups=mesh['dom'=128,'phase'=4] {'phase'}, dimensions={1}, use_global_device_ids=true | all-gather | bytes 655360 | tf_op jit(solution)/shard_map/all_gather | solution.py:121
  90.2 14.7 %all_gather.23 = bf16[512,512]{1,0:T(8,128)(2,1)S(1)} all-gather(bf16[512,128]{1,0:T(8,128)(2,1)S(1)} %copy-done.23), channel_id=1, replica_groups=mesh['dom'=128,'phase'=4] {'phase'}, dimensions={1}, use_global_device_ids=true | all-gather | bytes 655360 | tf_op jit(solution)/shard_map/all_gather | solution.py:118
  109.4 9.2 %gather_fusion.2 = bf16[2048,512]{1,0:T(8,128)(2,1)} fusion(bf16[256,512]{1,0:T(8,128)(2,1)S(1)} %copy-done.2, s32[2048]{0:T(1024)S(1)} %get-tuple-element.70), kind=kCustom, calls=%fused_computation.2 | custom fusion | bytes 4202496 | tf_op jit(solution)/shard_map/gather | solution.py:144
  118.6 13.3 %collective-permute-start.5 = (bf16[12,512]{1,0:T(8,128)(2,1)S(1)}, bf16[12,512]{1,0:T(8,128)(2,1)S(1)}, u32[]{:S(2)}, u32[]{:S(2)}) collective-permute-start(bf16[12,512]{1,0:T(8,128)(2,1)S(1)} %get-tuple-element.26), channel_id=1, source_target_pairs={{12,0},{16,4},{20,8},{24,12},{28,16},{32,20},{36,24},{40,28},{44,3... | collective-permute-start | bytes 36872 | tf_op jit(solution)/shard_map/ppermute | solution.py:15
  135.1 10.6 %gather_fusion.1 = bf16[2048,512]{1,0:T(8,128)(2,1)} fusion(bf16[1096,512]{1,0:T(8,128)(2,1)} %pad_maximum_fusion, s32[2048]{0:T(1024)S(1)} %get-tuple-element.71), kind=kCustom, calls=%fused_computation.1 | custom fusion | bytes 4202496 | tf_op jit(solution)/shard_map/gather | solution.py:144
  145.8 16.3 %scatter_custom_fusion = f32[256,512]{1,0:T(8,128)} fusion(s32[2048]{0:T(1024)} %bitcast.204, bf16[2048,512]{1,0:T(8,128)(2,1)} %gather_fusion.2, bf16[2048,512]{1,0:T(8,128)(2,1)} %gather_fusion.1, f32[]{:T(128)} %constant.12.clone.1, f32[]{:T(128)} %constant.11.clone.1), kind=kCustom, calls=%fused_computation.64 | custom fusion | flops 10485760 | bytes 4719616 | tf_op jit(solution)/shard_map/scatter-add | solution.py:147
  168.5 9.2 %gather_fusion.5 = bf16[2048,512]{1,0:T(8,128)(2,1)} fusion(bf16[256,512]{1,0:T(8,128)(2,1)S(1)} %add_convert_fusion.2, s32[2048]{0:T(1024)S(1)} %get-tuple-element.69), kind=kCustom, calls=%fused_computation.5 | custom fusion | bytes 4202496 | tf_op jit(solution)/shard_map/gather | solution.py:159
  182.1 7.2 %collective-permute-start.9 = (bf16[8,512]{1,0:T(8,128)(2,1)S(1)}, bf16[8,512]{1,0:T(8,128)(2,1)S(1)}, u32[]{:S(2)}, u32[]{:S(2)}) collective-permute-start(bf16[8,512]{1,0:T(8,128)(2,1)S(1)} %get-tuple-element.46), channel_id=1, source_target_pairs={{8,0},{12,4},{16,8},{20,12},{24,16},{28,20},{32,24},{36,28},{40,32... | collective-permute-start | bytes 24584 | tf_op jit(solution)/shard_map/ppermute | solution.py:15
  191.2 7.2 %collective-permute-start.11 = (bf16[8,512]{1,0:T(8,128)(2,1)S(1)}, bf16[8,512]{1,0:T(8,128)(2,1)S(1)}, u32[]{:S(2)}, u32[]{:S(2)}) collective-permute-start(bf16[8,512]{1,0:T(8,128)(2,1)S(1)} %get-tuple-element.44), channel_id=1, source_target_pairs={{12,0},{16,4},{20,8},{24,12},{28,16},{32,20},{36,24},{40,28},{44,3... | collective-permute-start | bytes 24584 | tf_op jit(solution)/shard_map/ppermute | solution.py:15
  198.9 9.2 %gather_fusion.4 = bf16[2048,512]{1,0:T(8,128)(2,1)} fusion(bf16[304,512]{1,0:T(8,128)(2,1)S(1)} %pad_maximum_fusion.1, s32[2048]{0:T(1024)S(1)} %get-tuple-element.68), kind=kCustom, calls=%fused_computation.4 | custom fusion | bytes 4202496 | tf_op jit(solution)/shard_map/gather | solution.py:159
  208.1 16.3 %scatter_custom_fusion.1 = f32[256,512]{1,0:T(8,128)} fusion(s32[2048]{0:T(1024)} %bitcast.207, bf16[2048,512]{1,0:T(8,128)(2,1)} %gather_fusion.5, bf16[2048,512]{1,0:T(8,128)(2,1)} %gather_fusion.4, f32[]{:T(128)} %constant.12.clone.1, f32[]{:T(128)} %constant.11.clone.1), kind=kCustom, calls=%fused_computation.59 | custom fusion | flops 10485760 | bytes 4719616 | tf_op jit(solution)/shard_map/scatter-add | solution.py:162
  228.8 3.6 collective-permute-start.12
  232.5 9.2 %gather_fusion.8 = bf16[2048,512]{1,0:T(8,128)(2,1)} fusion(bf16[256,512]{1,0:T(8,128)(2,1)S(1)} %add_convert_fusion.1, s32[2048]{0:T(1024)S(1)} %get-tuple-element.69), kind=kCustom, calls=%fused_computation.8 | custom fusion | bytes 4202496 | tf_op jit(solution)/shard_map/gather | solution.py:159
  241.7 5.6 collective-permute-start.13
  249.3 6.7 collective-permute-start.15
  257.9 7.1 %collective-permute-start.17 = (bf16[8,512]{1,0:T(8,128)(2,1)S(1)}, bf16[8,512]{1,0:T(8,128)(2,1)S(1)}, u32[]{:S(2)}, u32[]{:S(2)}) collective-permute-start(bf16[8,512]{1,0:T(8,128)(2,1)S(1)} %get-tuple-element.38), channel_id=1, source_target_pairs={{12,0},{16,4},{20,8},{24,12},{28,16},{32,20},{36,24},{40,28},{44,3... | collective-permute-start | bytes 24584 | tf_op jit(solution)/shard_map/ppermute | solution.py:15
  265.8 9.2 %gather_fusion.7 = bf16[2048,512]{1,0:T(8,128)(2,1)} fusion(bf16[304,512]{1,0:T(8,128)(2,1)S(1)} %pad_maximum_fusion.2, s32[2048]{0:T(1024)S(1)} %get-tuple-element.68), kind=kCustom, calls=%fused_computation.7 | custom fusion | bytes 4202496 | tf_op jit(solution)/shard_map/gather | solution.py:159
  275.0 16.3 %scatter_custom_fusion.2 = f32[256,512]{1,0:T(8,128)} fusion(s32[2048]{0:T(1024)} %bitcast.208, bf16[2048,512]{1,0:T(8,128)(2,1)} %gather_fusion.8, bf16[2048,512]{1,0:T(8,128)(2,1)} %gather_fusion.7, f32[]{:T(128)} %constant.12.clone.1, f32[]{:T(128)} %constant.11.clone.1), kind=kCustom, calls=%fused_computation.54 | custom fusion | flops 10485760 | bytes 4719616 | tf_op jit(solution)/shard_map/scatter-add | solution.py:162
  295.0 5.1 collective-permute-start.18
  300.2 13.3 %gather_fusion.11 = bf16[3072,512]{1,0:T(8,128)(2,1)} fusion(bf16[1024,512]{1,0:T(8,128)(2,1)S(1)} %get-tuple-element.56, s32[3072]{0:T(1024)S(1)} %get-tuple-element.66), kind=kCustom, calls=%fused_computation.11 | custom fusion | bytes 6303744 | tf_op jit(solution)/shard_map/gather | solution.py:173
  313.5 13.2 %gather_fusion.12 = bf16[3072,512]{1,0:T(8,128)(2,1)} fusion(bf16[1024,512]{1,0:T(8,128)(2,1)S(1)} %convolution_convert_fusion, s32[3072]{0:T(1024)S(1)} %get-tuple-element.66), kind=kCustom, calls=%fused_computation.12 | custom fusion | bytes 6303744 | tf_op jit(solution)/shard_map/gather | solution.py:182
  327.0 5.6 collective-permute-start.19
  334.5 6.7 collective-permute-start.21
  343.2 7.5 %collective-permute-start.23 = (bf16[8,512]{1,0:T(8,128)(2,1)S(1)}, bf16[8,512]{1,0:T(8,128)(2,1)S(1)}, u32[]{:S(2)}, u32[]{:S(2)}) collective-permute-start(bf16[8,512]{1,0:T(8,128)(2,1)S(1)} %get-tuple-element.32), channel_id=1, source_target_pairs={{12,0},{16,4},{20,8},{24,12},{28,16},{32,20},{36,24},{40,28},{44,3... | collective-permute-start | bytes 24584 | tf_op jit(solution)/shard_map/ppermute | solution.py:15
  351.1 13.3 %gather_fusion.10 = bf16[3072,512]{1,0:T(8,128)(2,1)} fusion(bf16[304,512]{1,0:T(8,128)(2,1)S(1)} %pad_maximum_fusion.3, s32[3072]{0:T(1024)S(1)} %get-tuple-element.67), kind=kCustom, calls=%fused_computation.10 | custom fusion | bytes 6303744 | tf_op jit(solution)/shard_map/gather | solution.py:173
  364.4 6.4 multiply_convert_fusion
  370.8 19.6 %scatter_custom_fusion.4 = f32[304,512]{1,0:T(8,128)S(1)} fusion(s32[3072]{0:T(1024)} %bitcast.201, bf16[3072,512]{1,0:T(8,128)(2,1)} %multiply_convert_fusion, f32[]{:T(128)} %constant.11.clone.1), kind=kCustom, calls=%fused_computation.33 | custom fusion | flops 3145728 | bytes 3768832 | tf_op jit(solution)/shard_map/scatter-add | solution.py:85
  391.3 21.6 %scatter_custom_fusion.3 = f32[1024,512]{1,0:T(8,128)S(1)} fusion(s32[3072]{0:T(1024)} %bitcast.202, bf16[3072,512]{1,0:T(8,128)(2,1)} %gather_fusion.11, bf16[3072,512]{1,0:T(8,128)(2,1)} %gather_fusion.10, f32[]{:T(128)} %constant.12.clone.1, f32[]{:T(128)} %constant.11.clone.1), kind=kCustom, calls=%fused_computation.36 | custom fusion | flops 15728640 | bytes 8389632 | tf_op jit(solution)/shard_map/scatter-add | solution.py:176
  412.9 8.8 %collective-permute-start.24 = (bf16[8,512]{1,0:T(8,128)(2,1)S(1)}, bf16[8,512]{1,0:T(8,128)(2,1)S(1)}, u32[]{:S(2)}, u32[]{:S(2)}) collective-permute-start(bf16[8,512]{1,0:T(8,128)(2,1)S(1)} %get-tuple-element.25), channel_id=1, source_target_pairs={{4,0},{8,4},{12,8},{16,12},{20,16},{24,20},{28,24},{32,28},{36,32}... | collective-permute-start | bytes 24584 | tf_op jit(solution)/shard_map/ppermute | solution.py:15
  424.9 7.7 %collective-permute-start.26 = (bf16[8,512]{1,0:T(8,128)(2,1)S(1)}, bf16[8,512]{1,0:T(8,128)(2,1)S(1)}, u32[]{:S(2)}, u32[]{:S(2)}) collective-permute-start(bf16[8,512]{1,0:T(8,128)(2,1)S(1)} %get-tuple-element.23), channel_id=1, source_target_pairs={{8,0},{12,4},{16,8},{20,12},{24,16},{28,20},{32,24},{36,28},{40,32... | collective-permute-start | bytes 24584 | tf_op jit(solution)/shard_map/ppermute | solution.py:15
  434.5 7.5 %collective-permute-start.28 = (bf16[8,512]{1,0:T(8,128)(2,1)S(1)}, bf16[8,512]{1,0:T(8,128)(2,1)S(1)}, u32[]{:S(2)}, u32[]{:S(2)}) collective-permute-start(bf16[8,512]{1,0:T(8,128)(2,1)S(1)} %get-tuple-element.21), channel_id=1, source_target_pairs={{12,0},{16,4},{20,8},{24,12},{28,16},{32,20},{36,24},{40,28},{44,3... | collective-permute-start | bytes 24584 | tf_op jit(solution)/shard_map/ppermute | solution.py:15
  444.1 6.3 collective-permute-done.29
  457.0 9.2 %gather_fusion.13 = bf16[2048,512]{1,0:T(8,128)(2,1)} fusion(bf16[256,512]{1,0:T(8,128)(2,1)S(1)} %convolution_convert_fusion.6, s32[2048]{0:T(1024)S(1)} %get-tuple-element.69), kind=kCustom, calls=%fused_computation.13 | custom fusion | bytes 4202496 | tf_op jit(solution)/shard_map/gather | solution.py:190
  466.2 5.4 multiply_convert_fusion.4
  471.6 13.6 %scatter_custom_fusion.6 = f32[304,512]{1,0:T(8,128)S(1)} fusion(s32[2048]{0:T(1024)} %bitcast.205, bf16[2048,512]{1,0:T(8,128)(2,1)} %multiply_convert_fusion.4, f32[]{:T(128)} %constant.11.clone.1), kind=kCustom, calls=%fused_computation.47 | custom fusion | flops 2097152 | bytes 2720256 | tf_op jit(solution)/shard_map/scatter-add | solution.py:85
  488.2 3.6 collective-permute-start.31
  491.8 4.8 collective-permute-start.32
  498.5 3.2 collective-permute-start.34
  501.7 3.3 collective-permute-start.35
  505.1 4.9 collective-permute-done.35
  515.2 16.0 %scatter_custom_fusion.8 = f32[256,512]{1,0:T(8,128)} fusion(f32[256,512]{1,0:T(8,128)} %convolution_add_fusion.1, s32[2048]{0:T(1024)} %bitcast.209, bf16[2048,512]{1,0:T(8,128)(2,1)S(1)} %copy-done.6), kind=kCustom, calls=%fused_computation.45 | custom fusion | flops 2097152 | bytes 2621440 | tf_op jit(solution)/shard_map/scatter-add | solution.py:192
  533.9 9.2 %gather_fusion.14 = bf16[2048,512]{1,0:T(8,128)(2,1)} fusion(bf16[256,512]{1,0:T(8,128)(2,1)S(1)} %convolution_convert_fusion.5, s32[2048]{0:T(1024)S(1)} %get-tuple-element.69), kind=kCustom, calls=%fused_computation.14 | custom fusion | bytes 4202496 | tf_op jit(solution)/shard_map/gather | solution.py:190
  543.1 5.4 multiply_convert_fusion.3
  548.5 13.6 %scatter_custom_fusion.9 = f32[304,512]{1,0:T(8,128)S(1)} fusion(s32[2048]{0:T(1024)} %bitcast.206, bf16[2048,512]{1,0:T(8,128)(2,1)} %multiply_convert_fusion.3, f32[]{:T(128)} %constant.11.clone.1), kind=kCustom, calls=%fused_computation.43 | custom fusion | flops 2097152 | bytes 2720256 | tf_op jit(solution)/shard_map/scatter-add | solution.py:85
  562.2 3.2 collective-permute-start.36
  565.5 6.6 collective-permute-start.37
  572.1 5.0 collective-permute-start.38
  581.6 3.9 collective-permute-start.41
  585.6 4.3 collective-permute-done.41
  592.1 16.5 %scatter_custom_fusion.11 = f32[256,512]{1,0:T(8,128)} fusion(f32[256,512]{1,0:T(8,128)} %convolution_add_fusion, s32[2048]{0:T(1024)} %bitcast.210, bf16[2048,512]{1,0:T(8,128)(2,1)} %multiply_convert_fusion.3), kind=kCustom, calls=%fused_computation.41 | custom fusion | flops 2097152 | bytes 2621440 | tf_op jit(solution)/shard_map/scatter-add | solution.py:192
  611.5 25.9 %scatter_custom_fusion.12 = f32[1096,512]{1,0:T(8,128)} fusion(s32[2048]{0:T(1024)} %bitcast.211, bf16[2048,512]{1,0:T(8,128)(2,1)S(1)} %copy-done.3, bf16[2048,512]{1,0:T(8,128)(2,1)} %gather_fusion.1, f32[]{:T(128)} %constant.12.clone.1, f32[]{:T(128)} %constant.11.clone.1, bf16[256,512]{1,0:T(8,128)(2,1)S(1)} %convolution_convert_fusion.4, ...), kind=kCustom, calls=%fused_computation.49 | custom fusion | flops 15728640 | bytes 6710272 | tf_op jit(solution)/shard_map/scatter-add | solution.py:85
  639.2 3.9 collective-permute-start.42
  643.3 6.6 collective-permute-start.43
  649.9 5.0 collective-permute-start.44
  659.4 3.9 collective-permute-start.47
  663.4 4.4 collective-permute-done.47
  671.7 22.4 %scatter_custom_fusion.14 = f32[1024,512]{1,0:T(8,128)} fusion(f32[1024,512]{1,0:T(8,128)} %fusion.25, s32[3072]{0:T(1024)} %bitcast.203, bf16[3072,512]{1,0:T(8,128)(2,1)} %multiply_convert_fusion), kind=kCustom, calls=%fused_computation.31 | custom fusion | flops 3145728 | bytes 5242880 | tf_op jit(solution)/shard_map/scatter-add | solution.py:201
  694.0 4.4 fusion.22
  (258 shorter events, 94.5 us)
Async XLA Ops:
  7.2 157.3 %all-gather.3.cloned.1.call-start = ((), (), s32[]{:S(2)}) async-start(), calls=%async_computation | async-start | bytes 1310720 | tf_op jit(solution)/shard_map/all_gather | solution.py:119
  7.9 216.5 %all-gather.5.cloned.1.call-start = ((), (), s32[]{:S(2)}) async-start(), calls=%async_computation.1 | async-start | bytes 1310720 | tf_op jit(solution)/shard_map/all_gather | solution.py:120
  34.8 40.7 %copy-start.26 = (s32[1,3072]{1,0:T(1,128)S(1)}, s32[1,3072]{1,0:T(1,128)}, u32[]{:S(2)}) copy-start(s32[1,3072]{1,0:T(1,128)} %param.37) | copy-start | bytes 36868
  34.8 40.8 %copy-start.25 = (s32[1,3072]{1,0:T(1,128)S(1)}, s32[1,3072]{1,0:T(1,128)}, u32[]{:S(2)}) copy-start(s32[1,3072]{1,0:T(1,128)} %param.36) | copy-start | bytes 36868
  34.8 40.8 %copy-start.22 = (bf16[512,128]{1,0:T(8,128)(2,1)S(1)}, bf16[512,128]{1,0:T(8,128)(2,1)}, u32[]{:S(2)}) copy-start(bf16[512,128]{1,0:T(8,128)(2,1)} %param.26) | copy-start | bytes 393220
  34.9 55.3 %copy-start.23 = (bf16[512,128]{1,0:T(8,128)(2,1)S(1)}, bf16[512,128]{1,0:T(8,128)(2,1)}, u32[]{:S(2)}) copy-start(bf16[512,128]{1,0:T(8,128)(2,1)} %param.23) | copy-start | bytes 393220
  34.9 72.8 %copy-start.28 = (s32[1,6,8]{2,0,1:T(1,128)S(1)}, s32[1,6,8]{2,0,1:T(1,128)}, u32[]{:S(2)}) copy-start(s32[1,6,8]{2,0,1:T(1,128)} %param.32) | copy-start | bytes 580
  35.6 72.2 %copy-start.14 = (bf16[1024,512]{1,0:T(8,128)(2,1)}, bf16[1024,512]{1,0:T(8,128)(2,1)S(1)}, u32[]{:S(2)}) copy-start(bf16[1024,512]{1,0:T(8,128)(2,1)S(1)} %convolution_convert_fusion.1) | copy-start | bytes 3145732
  35.6 73.8 %copy-start.2 = (bf16[256,512]{1,0:T(8,128)(2,1)S(1)}, bf16[256,512]{1,0:T(8,128)(2,1)}, u32[]{:S(2)}) copy-start(bf16[256,512]{1,0:T(8,128)(2,1)} %param.20) | copy-start | bytes 786436
  36.4 82.2 %collective-permute-start = (bf16[12,512]{1,0:T(8,128)(2,1)S(1)}, bf16[12,512]{1,0:T(8,128)(2,1)S(1)}, u32[]{:S(2)}, u32[]{:S(2)}) collective-permute-start(bf16[12,512]{1,0:T(8,128)(2,1)S(1)} %get-tuple-element.31), channel_id=1, source_target_pairs={{508,0},{0,4},{4,8},{8,12},{12,16},{16,20},{20,24},{24,28},{28,32}... | collective-permute-start | bytes 36872 | tf_op jit(solution)/shard_map/ppermute | solution.py:15
  47.0 84.9 %collective-permute-start.1 = (bf16[12,512]{1,0:T(8,128)(2,1)S(1)}, bf16[12,512]{1,0:T(8,128)(2,1)S(1)}, u32[]{:S(2)}, u32[]{:S(2)}) collective-permute-start(bf16[12,512]{1,0:T(8,128)(2,1)S(1)} %get-tuple-element.30), channel_id=1, source_target_pairs={{4,0},{8,4},{12,8},{16,12},{20,16},{24,20},{28,24},{32,28},{36,32}... | collective-permute-start | bytes 36872 | tf_op jit(solution)/shard_map/ppermute | solution.py:15
  52.4 79.6 %collective-permute-start.2 = (bf16[12,512]{1,0:T(8,128)(2,1)S(1)}, bf16[12,512]{1,0:T(8,128)(2,1)S(1)}, u32[]{:S(2)}, u32[]{:S(2)}) collective-permute-start(bf16[12,512]{1,0:T(8,128)(2,1)S(1)} %get-tuple-element.29), channel_id=1, source_target_pairs={{504,0},{508,4},{0,8},{4,12},{8,16},{12,20},{16,24},{20,28},{24,32... | collective-permute-start | bytes 36872 | tf_op jit(solution)/shard_map/ppermute | solution.py:15
  54.3 77.7 %collective-permute-start.3 = (bf16[12,512]{1,0:T(8,128)(2,1)S(1)}, bf16[12,512]{1,0:T(8,128)(2,1)S(1)}, u32[]{:S(2)}, u32[]{:S(2)}) collective-permute-start(bf16[12,512]{1,0:T(8,128)(2,1)S(1)} %get-tuple-element.28), channel_id=1, source_target_pairs={{8,0},{12,4},{16,8},{20,12},{24,16},{28,20},{32,24},{36,28},{40,32... | collective-permute-start | bytes 36872 | tf_op jit(solution)/shard_map/ppermute | solution.py:15
  64.7 67.3 %collective-permute-start.4 = (bf16[12,512]{1,0:T(8,128)(2,1)S(1)}, bf16[12,512]{1,0:T(8,128)(2,1)S(1)}, u32[]{:S(2)}, u32[]{:S(2)}) collective-permute-start(bf16[12,512]{1,0:T(8,128)(2,1)S(1)} %get-tuple-element.27), channel_id=1, source_target_pairs={{500,0},{504,4},{508,8},{0,12},{4,16},{8,20},{12,24},{16,28},{20,3... | collective-permute-start | bytes 36872 | tf_op jit(solution)/shard_map/ppermute | solution.py:15
  75.6 43.0 %copy-start.15 = (bf16[512,227]{0,1:T(8,128)(2,1)}, bf16[512,227]{0,1:T(8,128)(2,1)S(1)}, u32[]{:S(2)}) copy-start(bf16[512,227]{0,1:T(8,128)(2,1)S(1)} %all_gather.27) | copy-start | bytes 697348
  104.9 57.2 %copy-start.12 = (bf16[512,512]{1,0:T(8,128)(2,1)}, bf16[512,512]{1,0:T(8,128)(2,1)S(1)}, u32[]{:S(2)}) copy-start(bf16[512,512]{1,0:T(8,128)(2,1)S(1)} %all_gather.23) | copy-start | bytes 1572868
  118.6 14.2 %collective-permute-start.5 = (bf16[12,512]{1,0:T(8,128)(2,1)S(1)}, bf16[12,512]{1,0:T(8,128)(2,1)S(1)}, u32[]{:S(2)}, u32[]{:S(2)}) collective-permute-start(bf16[12,512]{1,0:T(8,128)(2,1)S(1)} %get-tuple-element.26), channel_id=1, source_target_pairs={{12,0},{16,4},{20,8},{24,12},{28,16},{32,20},{36,24},{40,28},{44,3... | collective-permute-start | bytes 36872 | tf_op jit(solution)/shard_map/ppermute | solution.py:15
  166.5 24.7 %collective-permute-start.6 = (bf16[8,512]{1,0:T(8,128)(2,1)S(1)}, bf16[8,512]{1,0:T(8,128)(2,1)S(1)}, u32[]{:S(2)}, u32[]{:S(2)}) collective-permute-start(bf16[8,512]{1,0:T(8,128)(2,1)S(1)} %get-tuple-element.49), channel_id=1, source_target_pairs={{508,0},{0,4},{4,8},{8,12},{12,16},{16,20},{20,24},{24,28},{28,32}... | collective-permute-start | bytes 24584 | tf_op jit(solution)/shard_map/ppermute | solution.py:15
  177.7 20.6 %collective-permute-start.7 = (bf16[8,512]{1,0:T(8,128)(2,1)S(1)}, bf16[8,512]{1,0:T(8,128)(2,1)S(1)}, u32[]{:S(2)}, u32[]{:S(2)}) collective-permute-start(bf16[8,512]{1,0:T(8,128)(2,1)S(1)} %get-tuple-element.48), channel_id=1, source_target_pairs={{4,0},{8,4},{12,8},{16,12},{20,16},{24,20},{28,24},{32,28},{36,32}... | collective-permute-start | bytes 24584 | tf_op jit(solution)/shard_map/ppermute | solution.py:15
  180.1 18.2 %collective-permute-start.8 = (bf16[8,512]{1,0:T(8,128)(2,1)S(1)}, bf16[8,512]{1,0:T(8,128)(2,1)S(1)}, u32[]{:S(2)}, u32[]{:S(2)}) collective-permute-start(bf16[8,512]{1,0:T(8,128)(2,1)S(1)} %get-tuple-element.47), channel_id=1, source_target_pairs={{504,0},{508,4},{0,8},{4,12},{8,16},{12,20},{16,24},{20,28},{24,32... | collective-permute-start | bytes 24584 | tf_op jit(solution)/shard_map/ppermute | solution.py:15
  182.1 16.3 %collective-permute-start.9 = (bf16[8,512]{1,0:T(8,128)(2,1)S(1)}, bf16[8,512]{1,0:T(8,128)(2,1)S(1)}, u32[]{:S(2)}, u32[]{:S(2)}) collective-permute-start(bf16[8,512]{1,0:T(8,128)(2,1)S(1)} %get-tuple-element.46), channel_id=1, source_target_pairs={{8,0},{12,4},{16,8},{20,12},{24,16},{28,20},{32,24},{36,28},{40,32... | collective-permute-start | bytes 24584 | tf_op jit(solution)/shard_map/ppermute | solution.py:15
  189.2 9.2 %collective-permute-start.10 = (bf16[8,512]{1,0:T(8,128)(2,1)S(1)}, bf16[8,512]{1,0:T(8,128)(2,1)S(1)}, u32[]{:S(2)}, u32[]{:S(2)}) collective-permute-start(bf16[8,512]{1,0:T(8,128)(2,1)S(1)} %get-tuple-element.45), channel_id=1, source_target_pairs={{500,0},{504,4},{508,8},{0,12},{4,16},{8,20},{12,24},{16,28},{20,3... | collective-permute-start | bytes 24584 | tf_op jit(solution)/shard_map/ppermute | solution.py:15
  191.2 7.7 %collective-permute-start.11 = (bf16[8,512]{1,0:T(8,128)(2,1)S(1)}, bf16[8,512]{1,0:T(8,128)(2,1)S(1)}, u32[]{:S(2)}, u32[]{:S(2)}) collective-permute-start(bf16[8,512]{1,0:T(8,128)(2,1)S(1)} %get-tuple-element.44), channel_id=1, source_target_pairs={{12,0},{16,4},{20,8},{24,12},{28,16},{32,20},{36,24},{40,28},{44,3... | collective-permute-start | bytes 24584 | tf_op jit(solution)/shard_map/ppermute | solution.py:15
  228.8 29.1 %collective-permute-start.12 = (bf16[8,512]{1,0:T(8,128)(2,1)S(1)}, bf16[8,512]{1,0:T(8,128)(2,1)S(1)}, u32[]{:S(2)}, u32[]{:S(2)}) collective-permute-start(bf16[8,512]{1,0:T(8,128)(2,1)S(1)} %get-tuple-element.43), channel_id=1, source_target_pairs={{508,0},{0,4},{4,8},{8,12},{12,16},{16,20},{20,24},{24,28},{28,32}... | collective-permute-start | bytes 24584 | tf_op jit(solution)/shard_map/ppermute | solution.py:15
  241.7 23.3 %collective-permute-start.13 = (bf16[8,512]{1,0:T(8,128)(2,1)S(1)}, bf16[8,512]{1,0:T(8,128)(2,1)S(1)}, u32[]{:S(2)}, u32[]{:S(2)}) collective-permute-start(bf16[8,512]{1,0:T(8,128)(2,1)S(1)} %get-tuple-element.42), channel_id=1, source_target_pairs={{4,0},{8,4},{12,8},{16,12},{20,16},{24,20},{28,24},{32,28},{36,32}... | collective-permute-start | bytes 24584 | tf_op jit(solution)/shard_map/ppermute | solution.py:15
  247.3 17.7 %collective-permute-start.14 = (bf16[8,512]{1,0:T(8,128)(2,1)S(1)}, bf16[8,512]{1,0:T(8,128)(2,1)S(1)}, u32[]{:S(2)}, u32[]{:S(2)}) collective-permute-start(bf16[8,512]{1,0:T(8,128)(2,1)S(1)} %get-tuple-element.41), channel_id=1, source_target_pairs={{504,0},{508,4},{0,8},{4,12},{8,16},{12,20},{16,24},{20,28},{24,32... | collective-permute-start | bytes 24584 | tf_op jit(solution)/shard_map/ppermute | solution.py:15
  249.3 15.8 %collective-permute-start.15 = (bf16[8,512]{1,0:T(8,128)(2,1)S(1)}, bf16[8,512]{1,0:T(8,128)(2,1)S(1)}, u32[]{:S(2)}, u32[]{:S(2)}) collective-permute-start(bf16[8,512]{1,0:T(8,128)(2,1)S(1)} %get-tuple-element.40), channel_id=1, source_target_pairs={{8,0},{12,4},{16,8},{20,12},{24,16},{28,20},{32,24},{36,28},{40,32... | collective-permute-start | bytes 24584 | tf_op jit(solution)/shard_map/ppermute | solution.py:15
  256.0 9.2 %collective-permute-start.16 = (bf16[8,512]{1,0:T(8,128)(2,1)S(1)}, bf16[8,512]{1,0:T(8,128)(2,1)S(1)}, u32[]{:S(2)}, u32[]{:S(2)}) collective-permute-start(bf16[8,512]{1,0:T(8,128)(2,1)S(1)} %get-tuple-element.39), channel_id=1, source_target_pairs={{500,0},{504,4},{508,8},{0,12},{4,16},{8,20},{12,24},{16,28},{20,3... | collective-permute-start | bytes 24584 | tf_op jit(solution)/shard_map/ppermute | solution.py:15
  257.9 7.9 %collective-permute-start.17 = (bf16[8,512]{1,0:T(8,128)(2,1)S(1)}, bf16[8,512]{1,0:T(8,128)(2,1)S(1)}, u32[]{:S(2)}, u32[]{:S(2)}) collective-permute-start(bf16[8,512]{1,0:T(8,128)(2,1)S(1)} %get-tuple-element.38), channel_id=1, source_target_pairs={{12,0},{16,4},{20,8},{24,12},{28,16},{32,20},{36,24},{40,28},{44,3... | collective-permute-start | bytes 24584 | tf_op jit(solution)/shard_map/ppermute | solution.py:15
  295.0 48.2 %collective-permute-start.18 = (bf16[8,512]{1,0:T(8,128)(2,1)S(1)}, bf16[8,512]{1,0:T(8,128)(2,1)S(1)}, u32[]{:S(2)}, u32[]{:S(2)}) collective-permute-start(bf16[8,512]{1,0:T(8,128)(2,1)S(1)} %get-tuple-element.37), channel_id=1, source_target_pairs={{508,0},{0,4},{4,8},{8,12},{12,16},{16,20},{20,24},{24,28},{28,32}... | collective-permute-start | bytes 24584 | tf_op jit(solution)/shard_map/ppermute | solution.py:15
  327.0 23.8 %collective-permute-start.19 = (bf16[8,512]{1,0:T(8,128)(2,1)S(1)}, bf16[8,512]{1,0:T(8,128)(2,1)S(1)}, u32[]{:S(2)}, u32[]{:S(2)}) collective-permute-start(bf16[8,512]{1,0:T(8,128)(2,1)S(1)} %get-tuple-element.36), channel_id=1, source_target_pairs={{4,0},{8,4},{12,8},{16,12},{20,16},{24,20},{28,24},{32,28},{36,32}... | collective-permute-start | bytes 24584 | tf_op jit(solution)/shard_map/ppermute | solution.py:15
  332.6 18.1 %collective-permute-start.20 = (bf16[8,512]{1,0:T(8,128)(2,1)S(1)}, bf16[8,512]{1,0:T(8,128)(2,1)S(1)}, u32[]{:S(2)}, u32[]{:S(2)}) collective-permute-start(bf16[8,512]{1,0:T(8,128)(2,1)S(1)} %get-tuple-element.35), channel_id=1, source_target_pairs={{504,0},{508,4},{0,8},{4,12},{8,16},{12,20},{16,24},{20,28},{24,32... | collective-permute-start | bytes 24584 | tf_op jit(solution)/shard_map/ppermute | solution.py:15
  334.5 16.2 %collective-permute-start.21 = (bf16[8,512]{1,0:T(8,128)(2,1)S(1)}, bf16[8,512]{1,0:T(8,128)(2,1)S(1)}, u32[]{:S(2)}, u32[]{:S(2)}) collective-permute-start(bf16[8,512]{1,0:T(8,128)(2,1)S(1)} %get-tuple-element.34), channel_id=1, source_target_pairs={{8,0},{12,4},{16,8},{20,12},{24,16},{28,20},{32,24},{36,28},{40,32... | collective-permute-start | bytes 24584 | tf_op jit(solution)/shard_map/ppermute | solution.py:15
  341.2 9.6 %collective-permute-start.22 = (bf16[8,512]{1,0:T(8,128)(2,1)S(1)}, bf16[8,512]{1,0:T(8,128)(2,1)S(1)}, u32[]{:S(2)}, u32[]{:S(2)}) collective-permute-start(bf16[8,512]{1,0:T(8,128)(2,1)S(1)} %get-tuple-element.33), channel_id=1, source_target_pairs={{500,0},{504,4},{508,8},{0,12},{4,16},{8,20},{12,24},{16,28},{20,3... | collective-permute-start | bytes 24584 | tf_op jit(solution)/shard_map/ppermute | solution.py:15
  343.2 7.9 %collective-permute-start.23 = (bf16[8,512]{1,0:T(8,128)(2,1)S(1)}, bf16[8,512]{1,0:T(8,128)(2,1)S(1)}, u32[]{:S(2)}, u32[]{:S(2)}) collective-permute-start(bf16[8,512]{1,0:T(8,128)(2,1)S(1)} %get-tuple-element.32), channel_id=1, source_target_pairs={{12,0},{16,4},{20,8},{24,12},{28,16},{32,20},{36,24},{40,28},{44,3... | collective-permute-start | bytes 24584 | tf_op jit(solution)/shard_map/ppermute | solution.py:15
  412.9 29.2 %collective-permute-start.24 = (bf16[8,512]{1,0:T(8,128)(2,1)S(1)}, bf16[8,512]{1,0:T(8,128)(2,1)S(1)}, u32[]{:S(2)}, u32[]{:S(2)}) collective-permute-start(bf16[8,512]{1,0:T(8,128)(2,1)S(1)} %get-tuple-element.25), channel_id=1, source_target_pairs={{4,0},{8,4},{12,8},{16,12},{20,16},{24,20},{28,24},{32,28},{36,32}... | collective-permute-start | bytes 24584 | tf_op jit(solution)/shard_map/ppermute | solution.py:15
  422.9 21.1 %collective-permute-start.25 = (bf16[8,512]{1,0:T(8,128)(2,1)S(1)}, bf16[8,512]{1,0:T(8,128)(2,1)S(1)}, u32[]{:S(2)}, u32[]{:S(2)}) collective-permute-start(bf16[8,512]{1,0:T(8,128)(2,1)S(1)} %get-tuple-element.24), channel_id=1, source_target_pairs={{508,0},{0,4},{4,8},{8,12},{12,16},{16,20},{20,24},{24,28},{28,32}... | collective-permute-start | bytes 24584 | tf_op jit(solution)/shard_map/ppermute | solution.py:15
  424.9 19.2 %collective-permute-start.26 = (bf16[8,512]{1,0:T(8,128)(2,1)S(1)}, bf16[8,512]{1,0:T(8,128)(2,1)S(1)}, u32[]{:S(2)}, u32[]{:S(2)}) collective-permute-start(bf16[8,512]{1,0:T(8,128)(2,1)S(1)} %get-tuple-element.23), channel_id=1, source_target_pairs={{8,0},{12,4},{16,8},{20,12},{24,16},{28,20},{32,24},{36,28},{40,32... | collective-permute-start | bytes 24584 | tf_op jit(solution)/shard_map/ppermute | solution.py:15
  432.6 11.4 %collective-permute-start.27 = (bf16[8,512]{1,0:T(8,128)(2,1)S(1)}, bf16[8,512]{1,0:T(8,128)(2,1)S(1)}, u32[]{:S(2)}, u32[]{:S(2)}) collective-permute-start(bf16[8,512]{1,0:T(8,128)(2,1)S(1)} %get-tuple-element.22), channel_id=1, source_target_pairs={{504,0},{508,4},{0,8},{4,12},{8,16},{12,20},{16,24},{20,28},{24,32... | collective-permute-start | bytes 24584 | tf_op jit(solution)/shard_map/ppermute | solution.py:15
  434.5 9.5 %collective-permute-start.28 = (bf16[8,512]{1,0:T(8,128)(2,1)S(1)}, bf16[8,512]{1,0:T(8,128)(2,1)S(1)}, u32[]{:S(2)}, u32[]{:S(2)}) collective-permute-start(bf16[8,512]{1,0:T(8,128)(2,1)S(1)} %get-tuple-element.21), channel_id=1, source_target_pairs={{12,0},{16,4},{20,8},{24,12},{28,16},{32,20},{36,24},{40,28},{44,3... | collective-permute-start | bytes 24584 | tf_op jit(solution)/shard_map/ppermute | solution.py:15
  442.1 8.3 %collective-permute-start.29 = (bf16[8,512]{1,0:T(8,128)(2,1)S(1)}, bf16[8,512]{1,0:T(8,128)(2,1)S(1)}, u32[]{:S(2)}, u32[]{:S(2)}) collective-permute-start(bf16[8,512]{1,0:T(8,128)(2,1)S(1)} %get-tuple-element.20), channel_id=1, source_target_pairs={{500,0},{504,4},{508,8},{0,12},{4,16},{8,20},{12,24},{16,28},{20,3... | collective-permute-start | bytes 24584 | tf_op jit(solution)/shard_map/ppermute | solution.py:15
  471.6 43.6 %copy-start.6 = (bf16[2048,512]{1,0:T(8,128)(2,1)S(1)}, bf16[2048,512]{1,0:T(8,128)(2,1)}, u32[]{:S(2)}) copy-start(bf16[2048,512]{1,0:T(8,128)(2,1)} %multiply_convert_fusion.4) | copy-start | bytes 6291460
  485.3 45.9 %copy-start.10 = (f32[256,512]{1,0:T(8,128)S(1)}, f32[256,512]{1,0:T(8,128)}, u32[]{:S(2)}) copy-start(f32[256,512]{1,0:T(8,128)} %copy-done.9) | copy-start | bytes 1572868
  485.3 16.4 %collective-permute-start.30 = (bf16[8,512]{1,0:T(8,128)(2,1)S(1)}, bf16[8,512]{1,0:T(8,128)(2,1)S(1)}, u32[]{:S(2)}, u32[]{:S(2)}) collective-permute-start(bf16[8,512]{1,0:T(8,128)(2,1)S(1)} %get-tuple-element.19), channel_id=1, source_target_pairs={{4,0},{8,4},{12,8},{16,12},{20,16},{24,20},{28,24},{32,28},{36,32}... | collective-permute-start | bytes 24584 | tf_op jit(solution)/shard_map/ppermute | solution.py:15
  488.2 16.8 %collective-permute-start.31 = (bf16[8,512]{1,0:T(8,128)(2,1)S(1)}, bf16[8,512]{1,0:T(8,128)(2,1)S(1)}, u32[]{:S(2)}, u32[]{:S(2)}) collective-permute-start(bf16[8,512]{1,0:T(8,128)(2,1)S(1)} %get-tuple-element.18), channel_id=1, source_target_pairs={{508,0},{0,4},{4,8},{8,12},{12,16},{16,20},{20,24},{24,28},{28,32}... | collective-permute-start | bytes 24584 | tf_op jit(solution)/shard_map/ppermute | solution.py:15
  491.8 13.2 %collective-permute-start.32 = (bf16[8,512]{1,0:T(8,128)(2,1)S(1)}, bf16[8,512]{1,0:T(8,128)(2,1)S(1)}, u32[]{:S(2)}, u32[]{:S(2)}) collective-permute-start(bf16[8,512]{1,0:T(8,128)(2,1)S(1)} %get-tuple-element.17), channel_id=1, source_target_pairs={{8,0},{12,4},{16,8},{20,12},{24,16},{28,20},{32,24},{36,28},{40,32... | collective-permute-start | bytes 24584 | tf_op jit(solution)/shard_map/ppermute | solution.py:15
  496.6 8.5 %collective-permute-start.33 = (bf16[8,512]{1,0:T(8,128)(2,1)S(1)}, bf16[8,512]{1,0:T(8,128)(2,1)S(1)}, u32[]{:S(2)}, u32[]{:S(2)}) collective-permute-start(bf16[8,512]{1,0:T(8,128)(2,1)S(1)} %get-tuple-element.16), channel_id=1, source_target_pairs={{504,0},{508,4},{0,8},{4,12},{8,16},{12,20},{16,24},{20,28},{24,32... | collective-permute-start | bytes 24584 | tf_op jit(solution)/shard_map/ppermute | solution.py:15
  498.5 6.6 collective-permute-start.34
  501.7 8.3 %collective-permute-start.35 = (bf16[8,512]{1,0:T(8,128)(2,1)S(1)}, bf16[8,512]{1,0:T(8,128)(2,1)S(1)}, u32[]{:S(2)}, u32[]{:S(2)}) collective-permute-start(bf16[8,512]{1,0:T(8,128)(2,1)S(1)} %get-tuple-element.14), channel_id=1, source_target_pairs={{500,0},{504,4},{508,8},{0,12},{4,16},{8,20},{12,24},{16,28},{20,3... | collective-permute-start | bytes 24584 | tf_op jit(solution)/shard_map/ppermute | solution.py:15
  548.5 42.5 %copy-start.11 = (f32[256,512]{1,0:T(8,128)S(1)}, f32[256,512]{1,0:T(8,128)}, u32[]{:S(2)}) copy-start(f32[256,512]{1,0:T(8,128)} %scatter_custom_fusion.8) | copy-start | bytes 1572868
  548.5 42.5 %copy-start.19 = (bf16[2,512,512]{2,1,0:T(8,128)(2,1)S(1)}, bf16[2,512,512]{2,1,0:T(8,128)(2,1)}, u32[]{:S(2)}) copy-start(bf16[2,512,512]{2,1,0:T(8,128)(2,1)} %all-gather.3.cloned.1.call-done) | copy-start | bytes 3145732
  562.2 46.5 %copy-start.8 = (f32[256,512]{1,0:T(8,128)S(1)}, f32[256,512]{1,0:T(8,128)}, u32[]{:S(2)}) copy-start(f32[256,512]{1,0:T(8,128)} %copy-done.7) | copy-start | bytes 1572868
  562.2 19.4 %collective-permute-start.36 = (bf16[8,512]{1,0:T(8,128)(2,1)S(1)}, bf16[8,512]{1,0:T(8,128)(2,1)S(1)}, u32[]{:S(2)}, u32[]{:S(2)}) collective-permute-start(bf16[8,512]{1,0:T(8,128)(2,1)S(1)} %get-tuple-element.13), channel_id=1, source_target_pairs={{4,0},{8,4},{12,8},{16,12},{20,16},{24,20},{28,24},{32,28},{36,32}... | collective-permute-start | bytes 24584 | tf_op jit(solution)/shard_map/ppermute | solution.py:15
  565.5 20.0 %collective-permute-start.37 = (bf16[8,512]{1,0:T(8,128)(2,1)S(1)}, bf16[8,512]{1,0:T(8,128)(2,1)S(1)}, u32[]{:S(2)}, u32[]{:S(2)}) collective-permute-start(bf16[8,512]{1,0:T(8,128)(2,1)S(1)} %get-tuple-element.12), channel_id=1, source_target_pairs={{508,0},{0,4},{4,8},{8,12},{12,16},{16,20},{20,24},{24,28},{28,32}... | collective-permute-start | bytes 24584 | tf_op jit(solution)/shard_map/ppermute | solution.py:15
  572.1 13.4 %collective-permute-start.38 = (bf16[8,512]{1,0:T(8,128)(2,1)S(1)}, bf16[8,512]{1,0:T(8,128)(2,1)S(1)}, u32[]{:S(2)}, u32[]{:S(2)}) collective-permute-start(bf16[8,512]{1,0:T(8,128)(2,1)S(1)} %get-tuple-element.11), channel_id=1, source_target_pairs={{8,0},{12,4},{16,8},{20,12},{24,16},{28,20},{32,24},{36,28},{40,32... | collective-permute-start | bytes 24584 | tf_op jit(solution)/shard_map/ppermute | solution.py:15
  577.1 8.5 %collective-permute-start.39 = (bf16[8,512]{1,0:T(8,128)(2,1)S(1)}, bf16[8,512]{1,0:T(8,128)(2,1)S(1)}, u32[]{:S(2)}, u32[]{:S(2)}) collective-permute-start(bf16[8,512]{1,0:T(8,128)(2,1)S(1)} %get-tuple-element.10), channel_id=1, source_target_pairs={{504,0},{508,4},{0,8},{4,12},{8,16},{12,20},{16,24},{20,28},{24,32... | collective-permute-start | bytes 24584 | tf_op jit(solution)/shard_map/ppermute | solution.py:15
  579.0 6.6 collective-permute-start.40
  581.6 8.3 %collective-permute-start.41 = (bf16[8,512]{1,0:T(8,128)(2,1)S(1)}, bf16[8,512]{1,0:T(8,128)(2,1)S(1)}, u32[]{:S(2)}, u32[]{:S(2)}) collective-permute-start(bf16[8,512]{1,0:T(8,128)(2,1)S(1)} %get-tuple-element.8), channel_id=1, source_target_pairs={{500,0},{504,4},{508,8},{0,12},{4,16},{8,20},{12,24},{16,28},{20,3... | collective-permute-start | bytes 24584 | tf_op jit(solution)/shard_map/ppermute | solution.py:15
  639.2 20.2 %collective-permute-start.42 = (bf16[12,512]{1,0:T(8,128)(2,1)S(1)}, bf16[12,512]{1,0:T(8,128)(2,1)S(1)}, u32[]{:S(2)}, u32[]{:S(2)}) collective-permute-start(bf16[12,512]{1,0:T(8,128)(2,1)S(1)} %get-tuple-element.7), channel_id=1, source_target_pairs={{4,0},{8,4},{12,8},{16,12},{20,16},{24,20},{28,24},{32,28},{36,32}... | collective-permute-start | bytes 36872 | tf_op jit(solution)/shard_map/ppermute | solution.py:15
  643.3 20.0 %collective-permute-start.43 = (bf16[12,512]{1,0:T(8,128)(2,1)S(1)}, bf16[12,512]{1,0:T(8,128)(2,1)S(1)}, u32[]{:S(2)}, u32[]{:S(2)}) collective-permute-start(bf16[12,512]{1,0:T(8,128)(2,1)S(1)} %get-tuple-element.6), channel_id=1, source_target_pairs={{508,0},{0,4},{4,8},{8,12},{12,16},{16,20},{20,24},{24,28},{28,32}... | collective-permute-start | bytes 36872 | tf_op jit(solution)/shard_map/ppermute | solution.py:15
  649.9 13.4 %collective-permute-start.44 = (bf16[12,512]{1,0:T(8,128)(2,1)S(1)}, bf16[12,512]{1,0:T(8,128)(2,1)S(1)}, u32[]{:S(2)}, u32[]{:S(2)}) collective-permute-start(bf16[12,512]{1,0:T(8,128)(2,1)S(1)} %get-tuple-element.5), channel_id=1, source_target_pairs={{8,0},{12,4},{16,8},{20,12},{24,16},{28,20},{32,24},{36,28},{40,32... | collective-permute-start | bytes 36872 | tf_op jit(solution)/shard_map/ppermute | solution.py:15
  654.8 8.5 %collective-permute-start.45 = (bf16[12,512]{1,0:T(8,128)(2,1)S(1)}, bf16[12,512]{1,0:T(8,128)(2,1)S(1)}, u32[]{:S(2)}, u32[]{:S(2)}) collective-permute-start(bf16[12,512]{1,0:T(8,128)(2,1)S(1)} %get-tuple-element.4), channel_id=1, source_target_pairs={{504,0},{508,4},{0,8},{4,12},{8,16},{12,20},{16,24},{20,28},{24,32... | collective-permute-start | bytes 36872 | tf_op jit(solution)/shard_map/ppermute | solution.py:15
  656.8 6.6 collective-permute-start.46
  659.4 8.4 %collective-permute-start.47 = (bf16[12,512]{1,0:T(8,128)(2,1)S(1)}, bf16[12,512]{1,0:T(8,128)(2,1)S(1)}, u32[]{:S(2)}, u32[]{:S(2)}) collective-permute-start(bf16[12,512]{1,0:T(8,128)(2,1)S(1)} %get-tuple-element.2), channel_id=1, source_target_pairs={{500,0},{504,4},{508,8},{0,12},{4,16},{8,20},{12,24},{16,28},{20,3... | collective-permute-start | bytes 36872 | tf_op jit(solution)/shard_map/ppermute | solution.py:15
  (16 other events, 232.4 us)
Sparse Core Ops, SparseCore 0:
  10.1 39.9 all-gather.2
  66.7 33.9 all-gather.4
where the time goes:
time: 718 us; the launch traced here: 706 us
  other arithmetic  236 us (33%)
  starting transfers between devices  217 us (30%)
  local copies, waits for them, and re-layouts  121 us (17%)
  blocking collectives  62 us (9%)
  matrix products  30.6 us (4%)
  waiting for transfers between devices  22.9 us (3%)
  between operations  16.2 us (2%)
    ppermute x48, starting transfers between devices, from_behind(): return lax.ppermute(block, axis, route)  217 us
    scatter-add x4, other arithmetic, return_rows(): jax.ops.segment_sum(single(edge_grad), sources, num_segments=span)  72.7 us
    scatter-add x2, other arithmetic, per_device(): jax.ops.segment_sum(single(edge_msg), mesh_receiver, num_segments=mesh_co...  32.6 us
    scatter-add x2, other arithmetic, per_device(): jax.ops.segment_sum(single(edge_grad), mesh_receiver, num_segments=mesh_c...  32.5 us
    gather x2, local copies, waits for them, and re-layouts, per_device(): dec_pre = single(dec_extended[dec_source]) + single(hidden[dec_receiver])  26.5 us
    scatter-add x1, other arithmetic, per_device(): jax.ops.segment_sum(single(dec_edge_grad), dec_receiver, num_segments=gri...  22.4 us
    ppermute x48, waiting for transfers between devices, from_behind(): return lax.ppermute(block, axis, route)  22.1 us
    scatter-add x1, other arithmetic, per_device(): jax.ops.segment_sum(single(dec_msg), dec_receiver, num_segments=grid_coun...  21.6 us
  transfers between devices with their start and end apart: 50, of which 8 were waited for; matrix products, arithmetic and copies ran while one was open for 18% of the time, Pallas kernels for 0%

commit v1 on v0

v1 whole, which is shorter than its diff:
```python
import functools

import jax
import jax.numpy as jnp
import numpy as np
from jax import lax
from jax.experimental import pallas as pl
from jax.experimental.pallas import tpu as pltpu
from jax.sharding import PartitionSpec as P

EPSILON = 1e-06
LANES = 128
BF = jnp.bfloat16
F32 = jnp.float32
EVEN = (0, 4, 1, 5, 2, 3)
ODD = (1, 0, 5, 4, 2, 3)
SWAP = (0, 2, 1, 3, 5, 4)
NEIGHBOURS = 6
BLOCK = 256
HALF = 128


def shape(rows, columns, dtype=BF):
    return jax.ShapeDtypeStruct((rows, columns), dtype)


def call(body, outs, args, flops, scratch=(), small=None):
    vmem = pl.BlockSpec(memory_space=pltpu.VMEM)
    smem = pl.BlockSpec(memory_space=pltpu.SMEM)
    moved = sum(a.size * a.dtype.itemsize for a in args)
    moved += sum(o.size * jnp.dtype(o.dtype).itemsize for o in outs)
    return pl.pallas_call(
        body,
        out_shape=tuple(outs),
        in_specs=[smem if i == small else vmem for i in range(len(args))],
        out_specs=tuple([vmem] * len(outs)),
        scratch_shapes=list(scratch),
        compiler_params=pltpu.CompilerParams(vmem_limit_bytes=48 << 20),
        cost_estimate=pl.CostEstimate(flops=flops, bytes_accessed=moved, transcendentals=0),
    )(*args)


def mm(left, right):
    return jnp.dot(left, right, preferred_element_type=F32)


def mm_back(left, right):
    return lax.dot_general(left, right, (((1,), (1,)), ((), ())), preferred_element_type=F32)


def gate(values):
    return 0.5 * jnp.tanh(0.5 * values) + 0.5


def gate_slope(values, sigmoid):
    return sigmoid * (1.0 + values * (1.0 - sigmoid))


def column(row):
    return jnp.broadcast_to(row, (LANES, row.shape[1])).T


def pick(col, count):
    lane = lax.broadcasted_iota(jnp.int32, col.shape, 1)
    tiles = [
        jnp.where(lane + LANES * t == col, 1.0, 0.0).astype(BF) for t in range(count // LANES)
    ]
    return tiles[0] if len(tiles) == 1 else jnp.concatenate(tiles, axis=1)


def spread(row, count):
    own = lax.broadcasted_iota(jnp.int32, (count, row.shape[1]), 0)
    return jnp.where(own == row, 1.0, 0.0).astype(BF)


def weight(ref, start, rows):
    return jnp.concatenate([ref[j, start : start + rows, :] for j in range(ref.shape[0])], axis=1)


def stack_rows(refs):
    rows = jnp.concatenate([r[...].astype(F32) for r in refs], axis=0)
    short = LANES - rows.shape[0]
    return jnp.concatenate([rows, jnp.zeros((short, rows.shape[1]), F32)], axis=0).astype(BF)


def put_rows(refs, rows):
    each = refs[0].shape[0]
    for k, ref in enumerate(refs):
        ref[...] = rows[k * each : (k + 1) * each, :].astype(BF)


def inverse_rms(values):
    return lax.rsqrt(jnp.mean(values * values, axis=-1, keepdims=True) + EPSILON)


def norm_grad(grad, update, scale):
    mixed = jnp.mean(grad * update, axis=-1, keepdims=True)
    return (scale * grad - update * (scale * scale * scale) * mixed).astype(BF)


def prepare_kernel(gs, gd, ms, md, ds, dd, entries, tables, grid_in, cotangent, cols, rows, *sends):
    lists = ((gs, gd), (ms, md), (ds, dd))
    for which, (src, dst) in enumerate(lists):
        blocks, width = src.shape
        slots = column(entries[which : which + 1, :])
        entry = jnp.concatenate([slots] * (width // LANES), axis=1)
        found = jnp.zeros((LANES, width), F32)
        for b in range(blocks):
            dst_row = jnp.broadcast_to(dst[b : b + 1, :], (LANES, width)).astype(F32)
            found += jnp.where(entry == src[b : b + 1, :], dst_row, 0.0)
        total = jnp.sum(found, axis=1, keepdims=True)
        wide = jnp.broadcast_to(total, (LANES, LANES)).astype(jnp.int32)
        wide = jnp.where(slots >= 0, wide, -1)
        cols[which] = wide
        rows[which] = wide.T
    for t in range(3):
        wide = jnp.broadcast_to(tables[t : t + 1, :], (LANES, LANES))
        rows[3 + t] = wide
        cols[3 + t] = wide.T
    sent = mm(pick(cols[3], grid_in.shape[0]), grid_in[...])
    at = pick(cols[2], grid_in.shape[0])
    back = mm(at, grid_in[...])
    back_cot = mm(at, cotangent[...])
    pad_in = jnp.zeros((8, 512 - grid_in.shape[1]), F32)
    pad_cot = jnp.zeros((8, 512 - cotangent.shape[1]), F32)
    for k in range(NEIGHBOURS):
        j = SWAP[k]
        first = jnp.concatenate([sent[16 * k : 16 * k + 8], pad_in], axis=1)
        second = jnp.concatenate([sent[16 * k + 8 : 16 * k + 16], pad_in], axis=1)
        third = jnp.concatenate([back[8 * j : 8 * j + 8], pad_in], axis=1)
        fourth = jnp.concatenate([back_cot[8 * j : 8 * j + 8], pad_cot], axis=1)
        sends[k][...] = jnp.concatenate([first, second, third, fourth], axis=0).astype(BF)


def embed_kernel(grid_in, cotangent, w, *refs):
    early = refs[:NEIGHBOURS]
    slope, hidden, ext, own_grad, b_hidden, b_grad = refs[NEIGHBOURS:]
    rows, f_in = grid_in.shape
    f_out = cotangent.shape[1]
    embed = weight(w, 0, f_in)
    mix = weight(w, 480, 512)
    halves = [[w[j, r : r + LANES, :] for j in range(4)] for r in (992, 992 + LANES)]
    out = jnp.concatenate([jnp.concatenate(h, axis=0) for h in halves], axis=1)[:, :f_out]
    received = [r[...].astype(F32) for r in early]

    def gathered(start, count, order, width):
        parts = [received[k][start : start + count, :width] for k in order]
        short = LANES - count * len(parts)
        return jnp.concatenate(parts + [jnp.zeros((short, width), F32)], axis=0).astype(BF)

    halo = gathered(0, 16, range(6), f_in)
    back = gathered(16, 8, SWAP, f_in)
    back_cot = gathered(24, 8, SWAP, f_out)
    pre = mm(halo, embed)
    ext[rows:, :] = mm((pre * gate(pre)).astype(BF), mix).astype(BF)
    pre = mm(back, embed)
    b_hidden[...] = (pre * gate(pre)).astype(BF)
    b_grad[...] = mm_back(back_cot, out).astype(BF)

    @pl.loop(0, rows // BLOCK)
    def _(b):
        at = pl.ds(pl.multiple_of(b * BLOCK, BLOCK), BLOCK)
        pre = mm(grid_in[at, :], embed)
        sig = gate(pre)
        slope[at, :] = gate_slope(pre, sig).astype(BF)
        own = (pre * sig).astype(BF)
        hidden[at, :] = own
        ext[at, :] = mm(own, mix).astype(BF)
        own_grad[at, :] = mm_back(cotangent[at, :], out).astype(BF)


def encode_kernel(ext, static, src, moves, dst, cols, w, *refs):
    slope, h_slope, encoded, scale, latent, proj = refs[:6]
    sends = refs[6:12]
    total = refs[12]
    count = ext.shape[0]
    meshes = static.shape[0]
    total[...] = jnp.zeros_like(total)

    @pl.loop(0, src.shape[0])
    def _(b):
        at = pl.ds(pl.multiple_of(b * BLOCK, BLOCK), BLOCK)
        dst_row = dst[pl.ds(b, 1), :]
        src_row = src[pl.ds(b, 1), :]
        for k in range(NEIGHBOURS):
            src_row += jnp.where(src[pl.ds(b, 1), :] >= count - LANES + 12 * k, moves[k], 0)
        pre = mm(pick(column(src_row), count), ext[...])
        pre += mm(pick(column(dst_row), meshes), static[...])
        sig = gate(pre)
        slope[at, :] = gate_slope(pre, sig).astype(BF)
        total[...] += mm(spread(dst_row, meshes), (pre * sig).astype(BF))

    pre = ext[count - LANES :, :].astype(F32) + mm(pick(cols[0], meshes), static[...])
    h_slope[...] = gate_slope(pre, gate(pre)).astype(BF)
    made = mm(total[...].astype(BF), weight(w, 0, 512))
    inverse = inverse_rms(made)
    encoded[...] = made
    scale[...] = jnp.broadcast_to(inverse, scale.shape)
    start = (static[...].astype(F32) + made * inverse).astype(BF)
    latent[...] = start
    sent = mm(start, weight(w, 512, 512)).astype(BF)
    proj[...] = sent
    put_rows(sends, mm(pick(cols[4], meshes), sent))


def edges_kernel(proj, latent, src, dst, total, slope):
    count = proj.shape[0]
    total[...] = jnp.zeros_like(total)

    @pl.loop(0, src.shape[0])
    def _(b):
        at = pl.ds(pl.multiple_of(b * BLOCK, BLOCK), BLOCK)
        dst_row = dst[pl.ds(b, 1), :]
        src_row = src[pl.ds(b, 1), :]
        pre = mm(pick(column(src_row), count), proj[...])
        pre += mm(pick(column(dst_row), count), latent[...])
        sig = gate(pre)
        slope[at, :] = gate_slope(pre, sig).astype(BF)
        own_row = jnp.where(src_row < count, dst_row, -1)
        total[...] += mm(spread(own_row, count), (pre * sig).astype(BF))


def layer_kernel(total, latent, cols, rows, w, *refs, last, starts):
    halo = refs[:NEIGHBOURS]
    h_slope, update, scale, new, proj = refs[NEIGHBOURS : NEIGHBOURS + 5]
    sends = refs[NEIGHBOURS + 5 :]
    count = latent.shape[0]
    old = latent[...]
    pre = stack_rows(halo).astype(F32) + mm(pick(cols[1], count), old)
    sig = gate(pre)
    h_slope[...] = gate_slope(pre, sig).astype(BF)
    summed = total[...] + mm(spread(rows[1][0:1, :], count), (pre * sig).astype(BF))
    made = mm(summed.astype(BF), weight(w, starts[0], 512))
    inverse = inverse_rms(made)
    update[...] = made
    scale[...] = jnp.broadcast_to(inverse, scale.shape)
    after = (old.astype(F32) + made * inverse).astype(BF)
    new[...] = after
    sent = mm(after, weight(w, starts[1], 512)).astype(BF)
    proj[...] = sent
    if not last:
        put_rows(sends, mm(pick(cols[4], count), sent))


def outgoing_grad(grad, cols, h_slope, count):
    return (mm(pick(cols, count), grad) * h_slope[...].astype(F32)).astype(BF)


def decode_kernel(proj, hidden, own_grad, b_hidden, b_grad, starts, src, dst, cols, rows, dec_w, node_w, update, scale, h_slope, *refs, where):
    messages, grads, latent_grad, sum_grad = refs[:4]
    sends = refs[4:10]
    entry = refs[10]
    count = proj.shape[0]
    entry[...] = jnp.zeros_like(entry)

    @pl.loop(0, src.shape[0])
    def _(b):
        at = pl.ds(pl.multiple_of(b * BLOCK, BLOCK), BLOCK)
        src_row = src[pl.ds(b, 1), :]
        dst_row = dst[pl.ds(b, 1), :]
        pre = mm(pick(column(src_row), count), proj[...])
        near, grad = [], []
        for half in range(BLOCK // HALF):
            start = pl.multiple_of(starts[2 * b + half], 16)
            window = pl.ds(start, BLOCK)
            local = column(dst_row[:, half * HALF : (half + 1) * HALF] - start)
            chosen = pick(local, BLOCK)
            near.append(mm(chosen, hidden[window, :]))
            grad.append(mm(chosen, own_grad[window, :]))
        pre += jnp.concatenate(near, axis=0)
        sig = gate(pre)
        messages[at, :] = (pre * sig).astype(BF)
        edge = (jnp.concatenate(grad, axis=0) * gate_slope(pre, sig)).astype(BF)
        grads[at, :] = edge
        entry[...] += mm(spread(src_row, count), edge)

    sent = mm(pick(cols[5], count), proj[...])
    pre = sent + b_hidden[...].astype(F32)
    far = (b_grad[...].astype(F32) * gate_slope(pre, gate(pre))).astype(BF)
    own = entry[...].astype(BF).astype(F32)
    row_grad = (own + mm(spread(rows[5][0:1, :], count), far)).astype(BF)
    grad = mm_back(row_grad, weight(dec_w, where[0], 512))
    latent_grad[...] = grad
    step = norm_grad(grad, update[...], scale[:, 0:1])
    back = mm_back(step, weight(node_w, where[1], 512)).astype(BF)
    sum_grad[...] = back
    out = outgoing_grad(back, cols[1], h_slope, count).astype(F32)
    for k in range(NEIGHBOURS):
        j = SWAP[k]
        both = jnp.concatenate([sent[8 * k : 8 * k + 8], out[8 * j : 8 * j + 8]], axis=0)
        sends[k][...] = both.astype(BF)


def predict_kernel(messages, grads, hidden, own_grad, starts, src, dst, cols, rows, w, *refs):
    halo = refs[:NEIGHBOURS]
    pred, skip = refs[NEIGHBOURS : NEIGHBOURS + 2]
    total = refs[NEIGHBOURS + 2]
    count, features = hidden.shape
    f_out = pred.shape[1]
    halves = [[w[j, r : r + LANES, :] for j in range(4)] for r in (992, 992 + LANES)]
    out = jnp.concatenate([jnp.concatenate(h, axis=0) for h in halves], axis=1)[:, :f_out]
    near = pick(cols[2], count)
    got = jnp.concatenate([r[...].astype(F32)[:8] for r in halo] + [jnp.zeros((80, features), F32)], axis=0)
    pre = got + mm(near, hidden[...])
    sig = gate(pre)
    place = spread(rows[2][0:1, :], count)
    total[...] = mm(place, (pre * sig).astype(BF))
    skip[...] = mm(place, (mm(near, own_grad[...]) * gate_slope(pre, sig)).astype(BF))

    @pl.loop(0, src.shape[0])
    def _(b):
        src_row = src[pl.ds(b, 1), :]
        dst_row = jnp.where(src_row < 256, dst[pl.ds(b, 1), :], -(1 << 20))
        for half in range(BLOCK // HALF):
            at = pl.ds(pl.multiple_of(b * BLOCK + half * HALF, HALF), HALF)
            start = pl.multiple_of(starts[2 * b + half], 16)
            window = pl.ds(start, BLOCK)
            chosen = spread(dst_row[:, half * HALF : (half + 1) * HALF] - start, BLOCK)
            total[window, :] += mm(chosen, messages[at, :])
            skip[window, :] += mm(chosen, grads[at, :])

    @pl.loop(0, count // BLOCK)
    def _(b):
        at = pl.ds(pl.multiple_of(b * BLOCK, BLOCK), BLOCK)
        pred[at, :] = mm(total[at, :].astype(BF), out).astype(BF)


def edges_back_kernel(sum_grad, slope, src, dst, rows, *refs):
    far = refs[:NEIGHBOURS]
    entry, into = refs[NEIGHBOURS : NEIGHBOURS + 2]
    acc = refs[NEIGHBOURS + 2]
    count = sum_grad.shape[0]
    keep = far[0].shape[0] - 8
    order = SWAP if keep else range(NEIGHBOURS)
    parts = [far[k][...].astype(F32)[keep:] for k in order]
    short = jnp.zeros((LANES - 8 * NEIGHBOURS, sum_grad.shape[1]), F32)
    outside = jnp.concatenate(parts + [short], axis=0).astype(BF)
    acc[...] = jnp.zeros_like(acc)
    into[...] = mm(spread(rows[1][0:1, :], count), outside)

    @pl.loop(0, src.shape[0])
    def _(b):
        at = pl.ds(pl.multiple_of(b * BLOCK, BLOCK), BLOCK)
        src_row = src[pl.ds(b, 1), :]
        dst_row = dst[pl.ds(b, 1), :]
        edge = mm(pick(column(dst_row), count), sum_grad[...]) * slope[at, :].astype(F32)
        edge = edge.astype(BF)
        acc[...] += mm(spread(src_row, count), edge)
        into[...] += mm(spread(jnp.where(src_row < count, dst_row, -1), count), edge)

    entry[...] = acc[...].astype(BF)


def layer_back_kernel(entry, into, latent_grad, cols, rows, src_w, next_w, update, scale, h_slope, *refs, where, first):
    returned = refs[:NEIGHBOURS]
    outs = refs[NEIGHBOURS:]
    count = entry.shape[0]
    keep = returned[0].shape[0] - 8
    order = SWAP if keep else range(NEIGHBOURS)
    parts = [returned[k][...].astype(F32)[keep:] for k in order]
    short = jnp.zeros((LANES - 8 * NEIGHBOURS, entry.shape[1]), F32)
    back = jnp.concatenate(parts + [short], axis=0).astype(BF)
    row_grad = entry[...].astype(F32) + mm(spread(rows[4][0:1, :], count), back)
    grad = latent_grad[...] + into[...]
    grad += mm_back(row_grad.astype(BF), weight(src_w, where[0], 512))
    step = norm_grad(grad, update[...], scale[:, 0:1])
    summed = mm_back(step, weight(next_w, where[1], 512)).astype(BF)
    if first:
        sum_grad, sends = outs[0], outs[1:]
        which = 0
    else:
        outs[0][...] = grad
        sum_grad, sends = outs[1], outs[2:]
        which = 1
    sum_grad[...] = summed
    put_rows(sends, outgoing_grad(summed, cols[which], h_slope, count).astype(F32))


def encode_back_kernel(sum_grad, slope, src, src_line, dst, entry, edge):
    count = sum_grad.shape[0]

    @pl.loop(0, src.shape[0])
    def _(b):
        at = pl.ds(pl.multiple_of(b * BLOCK, BLOCK), BLOCK)
        grad = mm(pick(column(dst[pl.ds(b, 1), :]), count), sum_grad[...])
        edge[at, :] = (grad * slope[at, :].astype(F32)).astype(BF)

    @pl.loop(0, entry.shape[0] // BLOCK)
    def _(b):
        at = pl.ds(pl.multiple_of(b * BLOCK, BLOCK), BLOCK)
        entry[at, :] = mm(spread(src_line[...] - b * BLOCK, BLOCK), edge[...]).astype(BF)


def input_kernel(entry, skip, slope, rows, w, *refs):
    returned = refs[:NEIGHBOURS]
    out = refs[NEIGHBOURS]
    f_in = out.shape[1]
    embed = weight(w, 0, f_in)
    mix = weight(w, 480, 512)
    back = stack_rows(returned)

    @pl.loop(0, entry.shape[0] // BLOCK)
    def _(b):
        at = pl.ds(pl.multiple_of(b * BLOCK, BLOCK), BLOCK)
        place = spread(rows[3][0:1, :] - b * BLOCK, BLOCK)
        row_grad = (entry[at, :].astype(F32) + mm(place, back)).astype(BF)
        grad = mm_back(row_grad, mix) + skip[at, :]
        grad = (grad * slope[at, :].astype(F32)).astype(BF)
        out[at, :] = mm_back(grad, embed).astype(BF)


def slot_entries(sizes, order):
    table = np.full((8, LANES), -1, np.int32)
    for row, (own, used, apart) in enumerate(sizes):
        for place, k in enumerate(order):
            table[row, place * apart : place * apart + used] = own + k * used + np.arange(used)
    return table


def slot_moves(order):
    shifts = [16 * order.index(k) - 12 * k for k in range(NEIGHBOURS)]
    return np.diff(np.array([0] + shifts)).astype(np.int32)


def permuted(block, route):
    return lax.ppermute(block, "dom", [(i, route(i) % lax.axis_size("dom")) for i in range(lax.axis_size("dom"))])


def exchange(groups, sign):
    each = groups[0].shape[0]
    beside = permuted(jnp.concatenate(groups[:3], axis=0), lambda i: i ^ 1)
    far = permuted(groups[3], lambda i: i + 3 if i % 2 else i - 3)
    up = permuted(jnp.concatenate([beside[each : 2 * each], groups[4]], axis=0), lambda i: i + 2 * sign)
    down = permuted(jnp.concatenate([beside[2 * each :], groups[5]], axis=0), lambda i: i - 2 * sign)
    return [beside[:each], up[:each], down[:each], far, up[each:], down[each:]]


def forward(groups):
    return exchange(groups, 1)


def backward(groups):
    return exchange(groups, -1)


def per_device(
    grid_in,
    mesh_static,
    embed_w,
    grid_w,
    enc_w,
    src_w,
    node_w,
    dec_w,
    out_w,
    cotangent,
    grid_send,
    g2m_src,
    g2m_dst,
    mesh_send,
    mesh_src,
    mesh_dst,
    dec_send,
    m2g_src,
    m2g_dst,
):
    x = grid_in[0]
    cot = cotangent[0]
    grid, f_in = x.shape
    mesh, d = mesh_static.shape
    f_out = cot.shape[1]
    out_pad = jnp.pad(out_w, ((0, 0), (0, 2 * LANES - f_out)))
    first = jnp.concatenate(
        [jnp.pad(embed_w, ((0, 480 - f_in), (0, 0))), grid_w, out_pad[:, :LANES], out_pad[:, LANES:]],
        axis=0,
    )
    w_first = lax.all_gather(first, "phase")
    w_enc = lax.all_gather(jnp.concatenate([enc_w, src_w[0]], axis=0), "phase")
    w_one = lax.all_gather(jnp.concatenate([node_w[0], src_w[1]], axis=0), "phase")
    w_two = lax.all_gather(jnp.concatenate([node_w[1], dec_w], axis=0), "phase")

    gs, gd = g2m_src.reshape(-1, BLOCK), g2m_dst.reshape(-1, BLOCK)
    ms, md = mesh_src.reshape(-1, BLOCK), mesh_dst.reshape(-1, BLOCK)
    ds, dd = m2g_src.reshape(-1, BLOCK), m2g_dst.reshape(-1, BLOCK)
    even = lax.axis_index("dom") % 2 == 0

    def order(table):
        in_even, in_odd = (jnp.stack([table[k] for k in ks]) for ks in (EVEN, ODD))
        return jnp.where(even, in_even, in_odd).reshape(1, -1)

    grid_table = jnp.pad(grid_send[0], ((0, 0), (0, 4)), constant_values=-1)
    tables = [order(grid_table), order(mesh_send[0]), order(dec_send[0])]
    sizes = ((grid, 12, 16), (mesh, 8, 8), (mesh, 8, 8))
    entries = jnp.where(even, slot_entries(sizes, ODD), slot_entries(sizes, EVEN))
    moves = jnp.where(even, slot_moves(ODD), slot_moves(EVEN))
    tables = jnp.concatenate(
        [jnp.pad(t, ((0, 0), (0, LANES - t.shape[1])), constant_values=-1) for t in tables]
        + [jnp.full((5, LANES), -1, jnp.int32)],
        axis=0,
    )
    starts = jnp.minimum(m2g_dst[0, ::HALF] // 16 * 16, grid - BLOCK)
    cols, rows, *sends = call(
        prepare_kernel,
        [jax.ShapeDtypeStruct((6, LANES, LANES), jnp.int32)] * 2 + [shape(32, d)] * 6,
        [gs, gd, ms, md, ds, dd, entries, tables, x, cot],
        400_000_000,
    )
    early = forward(sends)
    slope_in, hidden, ext, own_grad, b_hidden, b_grad = call(
        embed_kernel,
        [shape(grid, d)] * 2 + [shape(grid + LANES, d), shape(grid, d)] + [shape(LANES, d)] * 2,
        [x, cot, w_first, *early],
        1_500_000_000,
    )
    eight = [shape(8, d)] * 6
    enc_slope, enc_far, encoded, enc_scale, latent, proj, *sends = call(
        encode_kernel,
        [shape(gs.size, d), shape(LANES, d), shape(mesh, d, F32), shape(mesh, LANES, F32), shape(mesh, d), shape(mesh, d)]
        + eight,
        [ext, mesh_static, gs, moves, gd, cols, w_enc],
        5_000_000_000,
        [pltpu.VMEM((mesh, d), F32)],
        small=3,
    )
    stored = []
    for layer, w_layer in enumerate((w_one, w_two)):
        halo = forward(sends)
        total, slope = call(
            edges_kernel,
            [shape(mesh, d, F32), shape(ms.size, d)],
            [proj, latent, ms, md],
            3_000_000_000,
        )
        last = layer == 1
        far, update, scale, latent, proj, *sends = call(
            functools.partial(layer_kernel, last=last, starts=(0, d)),
            [shape(LANES, d), shape(mesh, d, F32), shape(mesh, LANES, F32), shape(mesh, d), shape(mesh, d)]
            + ([] if last else eight),
            [total, latent, cols, rows, w_layer, *halo],
            400_000_000,
        )
        stored.append((slope, far, update, scale))

    slope, far, update, scale = stored[1]
    messages, grads, latent_grad, sum_grad, *sends = call(
        functools.partial(decode_kernel, where=(d, 0)),
        [shape(ds.size, d)] * 2 + [shape(mesh, d, F32), shape(mesh, d)] + [shape(16, d)] * 6,
        [proj, hidden, own_grad, b_hidden, b_grad, starts, ds, dd, cols, rows, w_two, w_two, update, scale, far],
        6_000_000_000,
        [pltpu.VMEM((mesh, d), F32)],
        small=5,
    )
    returned = forward(sends)
    halo = returned
    entry, into = call(
        edges_back_kernel,
        [shape(mesh, d), shape(mesh, d, F32)],
        [sum_grad, slope, ms, md, rows, *sends],
        3_000_000_000,
        [pltpu.VMEM((mesh, d), F32)],
    )
    below = stored[0]
    latent_grad, sum_grad, *sends = call(
        functools.partial(layer_back_kernel, where=(d, 0), first=False),
        [shape(mesh, d, F32), shape(mesh, d)] + eight,
        [entry, into, latent_grad, cols, rows, w_one, w_one, below[2], below[3], below[1], *returned],
        400_000_000,
    )
    returned = backward(sends)
    entry, into = call(
        edges_back_kernel,
        [shape(mesh, d), shape(mesh, d, F32)],
        [sum_grad, below[0], ms, md, rows, *sends],
        3_000_000_000,
        [pltpu.VMEM((mesh, d), F32)],
    )
    pred, skip = call(
        predict_kernel,
        [shape(grid, f_out), shape(grid, d, F32)],
        [messages, grads, hidden, own_grad, starts, ds, dd, cols, rows, w_first, *halo],
        5_000_000_000,
        [pltpu.VMEM((grid, d), F32)],
        small=4,
    )
    sum_grad, *sends = call(
        functools.partial(layer_back_kernel, where=(d, 0), first=True),
        [shape(mesh, d)] + [shape(16, d)] * 6,
        [entry, into, latent_grad, cols, rows, w_enc, w_enc, encoded, enc_scale, enc_far, *returned],
        400_000_000,
    )
    returned = backward(sends)
    (entry,) = call(
        encode_back_kernel,
        [shape(grid, d)],
        [sum_grad, enc_slope, gs, g2m_src, gd],
        4_000_000_000,
        [pltpu.VMEM((gs.size, d), BF)],
    )
    (input_grad,) = call(
        input_kernel,
        [shape(grid, f_in)],
        [entry, skip, slope_in, rows, w_first, *returned],
        1_500_000_000,
    )
    return pred[None], input_grad[None]


def solution(mesh):
    placed = (
        P("phase", "dom", None),
        P("dom", None),
        P(None, "phase"),
        P(None, "phase"),
        P(None, "phase"),
        P(None, None, "phase"),
        P(None, None, "phase"),
        P(None, "phase"),
        P("phase", None),
        P("phase", "dom", None),
        P("dom", None, None),
        P("dom", None),
        P("dom", None),
        P("dom", None, None),
        P("dom", None),
        P("dom", None),
        P("dom", None, None),
        P("dom", None),
        P("dom", None),
    )
    return jax.shard_map(
        per_device,
        mesh=mesh,
        in_specs=placed,
        out_specs=(P("phase", "dom", None), P("phase", "dom", None)),
        check_vma=False,
    )
```

time: 718 us -> 271 us (0.38); the launches traced: 706 us -> 269 us
  other arithmetic: 236 us -> 11.3 us
  starting transfers between devices: 217 us -> 100 us
  local copies, waits for them, and re-layouts: 121 us -> 28.9 us
  Pallas kernels: 0 us -> 77.2 us
  blocking collectives: 62 us -> 0 us
  matrix products: 30.6 us -> 0 us
  waiting for transfers between devices: 22.9 us -> 36.8 us
    scatter-add x15 -> x0, other arithmetic: 206 us -> none  [the longest x4 72.7 us: return_rows(): jax.ops.segment_sum(single(edge_grad), sources, num_segments=span)]
    gather x15 -> x0, local copies, waits for them, and re-layouts: 118 us -> none  [the longest x2 26.5 us: per_device(): dec_pre = single(dec_extended[dec_source]) + single(hidden[dec_receiver])]
    ppermute x48 -> x24, starting transfers between devices: 217 us -> 100 us  [permuted(): lax.ppermute(block, 'dom', [(i, route(i) % lax.axis_size('dom')) for i in...]
    pallas_call x0 -> x15, Pallas kernels: none -> 77.2 us  [call(): pl.pallas_call(body, out_shape=tuple(outs), in_specs=[smem if i == small...]
    all_gather x5 -> x0, blocking collectives: 62 us -> none  [the longest x1 14.7 us: per_device(): lax.all_gather(enc_w, 'phase', axis=1, tiled=True)]
    dot_general x18 -> x0, matrix products: 30.6 us -> none  [the longest x9 17.7 us: backward_product(): lax.dot_general(left, right, (((1,), (1,)), ((), ())), preferred_element_...]
    unnamed x100 -> x116, local copies, waits for them, and re-layouts: 2.46 us -> 24.5 us
    convert_element_type x13 -> x0, other arithmetic: 21.3 us -> none  [the longest x9 19.3 us: bfloat(): return values.astype(jnp.bfloat16)]
  transfers between devices with their start and end apart: 50 -> 28, of which waited for: 8 -> 8; matrix products, arithmetic and copies ran while one was open for 18% -> 6% of each run, Pallas kernels for 0% -> 21%
where the time goes in v1:
time: 271 us; the launch traced here: 269 us
  starting transfers between devices  100 us (37%)
  Pallas kernels  77.2 us (28%)
  waiting for transfers between devices  36.8 us (14%)
  local copies, waits for them, and re-layouts  28.9 us (11%)
  between operations  15 us (6%)
  other arithmetic  11.3 us (4%)
    ppermute x24, starting transfers between devices, permuted(): lax.ppermute(block, 'dom', [(i, route(i) % lax.axis_size('dom')) for i in...  100 us
    pallas_call x15, Pallas kernels, call(): pl.pallas_call(body, out_shape=tuple(outs), in_specs=[smem if i == small...  77.2 us
    unnamed x116, local copies, waits for them, and re-layouts  24.5 us
    all_gather x1, waiting for transfers between devices, per_device(): w_enc = lax.all_gather(jnp.concatenate([enc_w, src_w[0]], axis=0), 'phase')  19.6 us
    ppermute x24, waiting for transfers between devices, permuted(): lax.ppermute(block, 'dom', [(i, route(i) % lax.axis_size('dom')) for i in...  17.1 us
  transfers between devices with their start and end apart: 28, of which 8 were waited for; matrix products, arithmetic and copies ran while one was open for 6% of the time, Pallas kernels for 21%

profile of v1, /device:TPU:1, one launch (start us, length us, event | category | flops | bytes accessed | tf_op | source)
XLA Modules:
  0.0 269.2 jit_solution(2217142796270030121)
XLA Ops:
  8.4 1.7 fusion.3
  10.2 1.2 slice_bitcast_fusion
  19.6 0.9 shard_map.230
  20.5 7.2 %collective-permute-start.3 = (bf16[32,512]{1,0:T(8,128)(2,1)S(1)}, bf16[32,512]{1,0:T(8,128)(2,1)S(1)}, u32[]{:S(2)}, u32[]{:S(2)}) collective-permute-start(bf16[32,512]{1,0:T(8,128)(2,1)S(1)} %get-tuple-element.83), channel_id=1, source_target_pairs={{0,500},{4,16},{8,508},{12,24},{16,4},{20,32},{24,12},{28,40},{32,... | collective-permute-start | bytes 98312 | tf_op jit(solution)/shard_map/ppermute | solution.py:426
  27.7 9.5 %collective-permute-start = (bf16[96,512]{1,0:T(8,128)(2,1)S(1)}, bf16[96,512]{1,0:T(8,128)(2,1)S(1)}, u32[]{:S(2)}, u32[]{:S(2)}) collective-permute-start(bf16[96,512]{1,0:T(8,128)(2,1)S(1)} %pad_maximum_fusion.3), channel_id=1, source_target_pairs={{0,4},{4,0},{8,12},{12,8},{16,20},{20,16},{24,28},{28,24},{32,36},... | collective-permute-start | bytes 294920 | tf_op jit(solution)/shard_map/ppermute | solution.py:426
  37.2 1.6 pad_maximum_fusion.2
  39.8 3.1 %collective-permute-start.1 = (bf16[64,512]{1,0:T(8,128)(2,1)S(1)}, bf16[64,512]{1,0:T(8,128)(2,1)S(1)}, u32[]{:S(2)}, u32[]{:S(2)}) collective-permute-start(bf16[64,512]{1,0:T(8,128)(2,1)S(1)} %pad_maximum_fusion.4), channel_id=1, source_target_pairs={{0,8},{4,12},{8,16},{12,20},{16,24},{20,28},{24,32},{28,36},{32,40... | collective-permute-start | bytes 196616 | tf_op jit(solution)/shard_map/ppermute | solution.py:426
  42.9 5.5 %collective-permute-start.2 = (bf16[64,512]{1,0:T(8,128)(2,1)S(1)}, bf16[64,512]{1,0:T(8,128)(2,1)S(1)}, u32[]{:S(2)}, u32[]{:S(2)}) collective-permute-start(bf16[64,512]{1,0:T(8,128)(2,1)S(1)} %pad_maximum_fusion.5), channel_id=1, source_target_pairs={{0,504},{4,508},{8,0},{12,4},{16,8},{20,12},{24,16},{28,20},{32,24... | collective-permute-start | bytes 196616 | tf_op jit(solution)/shard_map/ppermute | solution.py:426
  48.8 1.0 collective-permute-done.2
  49.8 5.8 %shard_map.231 = (bf16[1024,512]{1,0:T(8,128)(2,1)S(1)}, bf16[1024,512]{1,0:T(8,128)(2,1)S(1)}, bf16[1152,512]{1,0:T(8,128)(2,1)}, bf16[1024,512]{1,0:T(8,128)(2...) custom-call(bf16[1024,474]{1,0:T(8,128)(2,1)S(1)} %bitcast.60, bf16[1024,227]{1,0:T(8,128)(2,1)S(1)} %bitcast.63, ...), custom_call_target="tpu_custom_call" | custom-call | flops 1500000000 | bytes 7497728 | tf_op jit(solution)/shard_map/pallas_call | solution.py:32
  55.6 1.0 copy-done.5
  56.5 1.0 copy-done.30
  57.5 1.0 copy-done.32
  58.5 19.6 %all-gather.11.cloned.1.call-done = bf16[4096,128]{1,0:T(8,128)(2,1)} async-done(((bf16[1024,128]{1,0:T(8,128)(2,1)}), bf16[4096,128]{1,0:T(8,128)(2,1)}) %all-gather.11.cloned.1.call-update) | async-done | bytes 1048592 | tf_op jit(solution)/shard_map/all_gather | solution.py:478
  78.1 1.2 copy-done.2
  79.3 1.3 copy-done.29
  80.6 10.3 %shard_map.232 = (bf16[2048,512]{1,0:T(8,128)(2,1)}, bf16[128,512]{1,0:T(8,128)(2,1)S(1)}, f32[256,512]{1,0:T(8,128)S(1)}, f32[256,128]{1,0:T(8,128)S(1)}, bf16[...) custom-call(bf16[1152,512]{1,0:T(8,128)(2,1)S(1)} %copy-done.29, ...), custom_call_target="tpu_custom_call" | custom-call | flops 5000000000 | bytes 6357016 | tf_op jit(solution)/shard_map/pallas_call | solution.py:32
  92.3 5.8 %collective-permute-start.7 = (bf16[8,512]{1,0:T(8,128)(2,1)S(1)}, bf16[8,512]{1,0:T(8,128)(2,1)S(1)}, u32[]{:S(2)}, u32[]{:S(2)}) collective-permute-start(bf16[8,512]{1,0:T(8,128)(2,1)S(1)} %get-tuple-element.95), channel_id=1, source_target_pairs={{0,500},{4,16},{8,508},{12,24},{16,4},{20,32},{24,12},{28,40},{32,... | collective-permute-start | bytes 24584 | tf_op jit(solution)/shard_map/ppermute | solution.py:426
  98.2 5.0 %collective-permute-start.4 = (bf16[24,512]{1,0:T(8,128)(2,1)S(1)}, bf16[24,512]{1,0:T(8,128)(2,1)S(1)}, u32[]{:S(2)}, u32[]{:S(2)}) collective-permute-start(bf16[24,512]{1,0:T(8,128)(2,1)S(1)} %pad_maximum_fusion.12), channel_id=1, source_target_pairs={{0,4},{4,0},{8,12},{12,8},{16,20},{20,16},{24,28},{28,24},{32,36},... | collective-permute-start | bytes 73736 | tf_op jit(solution)/shard_map/ppermute | solution.py:426
  103.2 5.4 %shard_map.233 = (f32[256,512]{1,0:T(8,128)S(1)}, bf16[2048,512]{1,0:T(8,128)(2,1)S(1)}) custom-call(bf16[256,512]{1,0:T(8,128)(2,1)S(1)} %get-tuple-element.86.proj, bf16[256,512]{1,0:T(8,128)(2,1)S(1)} %get-tuple-element.87.latent, s32[8,256]{1,0:T(8,128)S(1)} %reshape.96.ms.src, s32[8,256]{1,0:T(8,128)S(1)} %reshape.97.md.dst), custom_call_target="tpu_custom_call" | custom-call | flops 3000000000 | bytes 3162112 | tf_op jit(solution)/shard_map/pallas_call | solution.py:32
  108.6 1.3 copy-done.37
  109.9 2.4 collective-permute-start.5
  112.3 6.2 %collective-permute-start.6 = (bf16[16,512]{1,0:T(8,128)(2,1)S(1)}, bf16[16,512]{1,0:T(8,128)(2,1)S(1)}, u32[]{:S(2)}, u32[]{:S(2)}) collective-permute-start(bf16[16,512]{1,0:T(8,128)(2,1)S(1)} %pad_maximum_fusion.16), channel_id=1, source_target_pairs={{0,504},{4,508},{8,0},{12,4},{16,8},{20,12},{24,16},{28,20},{32,24... | collective-permute-start | bytes 49160 | tf_op jit(solution)/shard_map/ppermute | solution.py:426
  119.4 1.2 copy-done
  120.6 1.1 shard_map.234
  121.7 1.9 collective-permute-start.11
  123.6 3.7 %collective-permute-start.8 = (bf16[24,512]{1,0:T(8,128)(2,1)S(1)}, bf16[24,512]{1,0:T(8,128)(2,1)S(1)}, u32[]{:S(2)}, u32[]{:S(2)}) collective-permute-start(bf16[24,512]{1,0:T(8,128)(2,1)S(1)} %pad_maximum_fusion.13), channel_id=1, source_target_pairs={{0,4},{4,0},{8,12},{12,8},{16,20},{20,16},{24,28},{28,24},{32,36},... | collective-permute-start | bytes 73736 | tf_op jit(solution)/shard_map/ppermute | solution.py:426
  127.4 5.4 %shard_map.235 = (f32[256,512]{1,0:T(8,128)S(1)}, bf16[2048,512]{1,0:T(8,128)(2,1)S(1)}) custom-call(bf16[256,512]{1,0:T(8,128)(2,1)S(1)} %get-tuple-element.96.proj, bf16[256,512]{1,0:T(8,128)(2,1)S(1)} %get-tuple-element.97.latent, s32[8,256]{1,0:T(8,128)S(1)} %reshape.96.ms.src, s32[8,256]{1,0:T(8,128)S(1)} %reshape.97.md.dst), custom_call_target="tpu_custom_call" | custom-call | flops 3000000000 | bytes 3162112 | tf_op jit(solution)/shard_map/pallas_call | solution.py:32
  132.8 1.3 copy-done.35
  134.1 6.7 %collective-permute-start.9 = (bf16[16,512]{1,0:T(8,128)(2,1)S(1)}, bf16[16,512]{1,0:T(8,128)(2,1)S(1)}, u32[]{:S(2)}, u32[]{:S(2)}) collective-permute-start(bf16[16,512]{1,0:T(8,128)(2,1)S(1)} %pad_maximum_fusion.17), channel_id=1, source_target_pairs={{0,8},{4,12},{8,16},{12,20},{16,24},{20,28},{24,32},{28,36},{32,40... | collective-permute-start | bytes 49160 | tf_op jit(solution)/shard_map/ppermute | solution.py:426
  140.8 1.9 collective-permute-start.10
  142.8 2.5 collective-permute-done.10
  145.3 1.2 copy-done.7
  146.6 1.4 shard_map.236
  148.1 1.2 copy-done.33
  149.3 13.0 %shard_map.237 = (bf16[3072,512]{1,0:T(8,128)(2,1)}, bf16[3072,512]{1,0:T(8,128)(2,1)}, f32[256,512]{1,0:T(8,128)S(1)}, bf16[256,512]{1,0:T(8,128)(2,1)S(1)}, bf...) custom-call(bf16[256,512]{1,0:T(8,128)(2,1)S(1)} %get-tuple-element., ...), custom_call_target="tpu_custom_call" | custom-call | flops 6000000000 | bytes 13492320 | tf_op jit(solution)/shard_map/pallas_call | solution.py:32
  162.4 2.4 collective-permute-start.15
  164.8 4.9 %collective-permute-start.12 = (bf16[48,512]{1,0:T(8,128)(2,1)S(1)}, bf16[48,512]{1,0:T(8,128)(2,1)S(1)}, u32[]{:S(2)}, u32[]{:S(2)}) collective-permute-start(bf16[48,512]{1,0:T(8,128)(2,1)S(1)} %pad_maximum_fusion.6), channel_id=1, source_target_pairs={{0,4},{4,0},{8,12},{12,8},{16,20},{20,16},{24,28},{28,24},{32,36},... | collective-permute-start | bytes 147464 | tf_op jit(solution)/shard_map/ppermute | solution.py:426
  169.8 4.6 %shard_map.239 = (bf16[256,512]{1,0:T(8,128)(2,1)S(1)}, f32[256,512]{1,0:T(8,128)S(1)}) custom-call(bf16[256,512]{1,0:T(8,128)(2,1)S(1)} %get-tuple-element.122.sum_grad, bf16[2048,512]{1,0:T(8,128)(2,1)S(1)} %copy-done.36, s32[8,256]{1,0:T(8,128)S(1)} %reshape.96.ms.src, s32[8,256]{1,0:T(8,128)S(1)} %reshape.97.md.dst, ...), custom_call_target="tpu_custom_call" | custom-call | flops 3000000000 | bytes 3653632 | tf_op jit(solution)/shard_map/pallas_call | solution.py:32
  174.5 3.3 %collective-permute-start.13 = (bf16[32,512]{1,0:T(8,128)(2,1)S(1)}, bf16[32,512]{1,0:T(8,128)(2,1)S(1)}, u32[]{:S(2)}, u32[]{:S(2)}) collective-permute-start(bf16[32,512]{1,0:T(8,128)(2,1)S(1)} %pad_maximum_fusion.8), channel_id=1, source_target_pairs={{0,8},{4,12},{8,16},{12,20},{16,24},{20,28},{24,32},{28,36},{32,40... | collective-permute-start | bytes 98312 | tf_op jit(solution)/shard_map/ppermute | solution.py:426
  177.8 5.3 %collective-permute-start.14 = (bf16[32,512]{1,0:T(8,128)(2,1)S(1)}, bf16[32,512]{1,0:T(8,128)(2,1)S(1)}, u32[]{:S(2)}, u32[]{:S(2)}) collective-permute-start(bf16[32,512]{1,0:T(8,128)(2,1)S(1)} %pad_maximum_fusion.9), channel_id=1, source_target_pairs={{0,504},{4,508},{8,0},{12,4},{16,8},{20,12},{24,16},{28,20},{32,24... | collective-permute-start | bytes 98312 | tf_op jit(solution)/shard_map/ppermute | solution.py:426
  183.1 1.0 collective-permute-done.14
  184.1 1.5 shard_map.240
  186.5 1.9 collective-permute-start.19
  189.0 3.9 %collective-permute-start.16 = (bf16[24,512]{1,0:T(8,128)(2,1)}, bf16[24,512]{1,0:T(8,128)(2,1)}, u32[]{:S(2)}, u32[]{:S(2)}) collective-permute-start(bf16[24,512]{1,0:T(8,128)(2,1)} %pad_maximum_fusion.14), channel_id=1, source_target_pairs={{0,4},{4,0},{8,12},{12,8},{16,20},{20,16},{24,28},{28,24},{32,36},... | collective-permute-start | bytes 73736 | tf_op jit(solution)/shard_map/ppermute | solution.py:426
  193.0 11.4 %shard_map.238 = (bf16[1024,227]{1,0:T(8,128)(2,1)S(1)}, f32[1024,512]{1,0:T(8,128)}) custom-call(bf16[3072,512]{1,0:T(8,128)(2,1)} %get-tuple-element.113.messages, bf16[3072,512]{1,0:T(8,128)(2,1)} %get-tuple-element.114.grads, bf16[1024,512]{1,0:T(8,128)(2,1)S(1)} %copy-done.31, bf16[1024,512]{1,0:T(8,128)(2,1)S(1)} %copy-done.34, s32[24]{0:T(128)S(1)} %copy-done.28, ...), custom_call_target="tpu_custom_call" | custom-call | flops 5000000000 | bytes 13138016 | tf_op jit(solution)/shard_map/pallas_call | solution.py:32
  205.2 5.4 %shard_map.241 = (bf16[256,512]{1,0:T(8,128)(2,1)S(1)}, f32[256,512]{1,0:T(8,128)S(1)}) custom-call(bf16[256,512]{1,0:T(8,128)(2,1)S(1)} %get-tuple-element.130.sum_grad, bf16[2048,512]{1,0:T(8,128)(2,1)S(1)} %copy-done.38, s32[8,256]{1,0:T(8,128)S(1)} %copy-done.19, s32[8,256]{1,0:T(8,128)S(1)} %copy-done.21, s32[6,128,128]{2,1,0:T(8,128)S(1)} %get-tuple-element.89.rows, ...), custom_call_target="tpu_custom_call" | custom-call | flops 3000000000 | bytes 3604480 | tf_op jit(solution)/shard_map/pallas_call | solution.py:32
  211.5 2.0 copy.29
  214.9 6.5 %collective-permute-start.17 = (bf16[16,512]{1,0:T(8,128)(2,1)S(1)}, bf16[16,512]{1,0:T(8,128)(2,1)S(1)}, u32[]{:S(2)}, u32[]{:S(2)}) collective-permute-start(bf16[16,512]{1,0:T(8,128)(2,1)S(1)} %pad_maximum_fusion.19), channel_id=1, source_target_pairs={{0,504},{4,508},{8,0},{12,4},{16,8},{20,12},{24,16},{28,20},{32,24... | collective-permute-start | bytes 49160 | tf_op jit(solution)/shard_map/ppermute | solution.py:426
  222.2 2.0 collective-permute-start.18
  224.2 5.7 %collective-permute-done.18 = bf16[16,512]{1,0:T(8,128)(2,1)S(1)} collective-permute-done((bf16[16,512]{1,0:T(8,128)(2,1)S(1)}, bf16[16,512]{1,0:T(8,128)(2,1)S(1)}, u32[]{:S(2)}, u32[]{:S(2)}) %collective-permute-start.18) | collective-permute-done | bytes 16416 | tf_op jit(solution)/shard_map/ppermute | solution.py:426
  230.0 1.0 copy-done.10
  231.0 1.0 copy-done.12
  232.1 1.0 copy-done.14
  233.1 0.9 copy-done.17
  234.0 1.7 shard_map.242
  235.8 1.9 collective-permute-start.23
  237.7 3.4 %collective-permute-start.20 = (bf16[48,512]{1,0:T(8,128)(2,1)S(1)}, bf16[48,512]{1,0:T(8,128)(2,1)S(1)}, u32[]{:S(2)}, u32[]{:S(2)}) collective-permute-start(bf16[48,512]{1,0:T(8,128)(2,1)S(1)} %pad_maximum_fusion.7), channel_id=1, source_target_pairs={{0,4},{4,0},{8,12},{12,8},{16,20},{20,16},{24,28},{28,24},{32,36},... | collective-permute-start | bytes 147464 | tf_op jit(solution)/shard_map/ppermute | solution.py:426
  241.1 5.0 %shard_map.243.entry = bf16[1024,512]{1,0:T(8,128)(2,1)S(1)} custom-call(bf16[256,512]{1,0:T(8,128)(2,1)S(1)} %get-tuple-element.144.sum_grad, bf16[2048,512]{1,0:T(8,128)(2,1)S(1)} %copy-done.39, s32[8,256]{1,0:T(8,128)S(1)} %reshape.94.gs.src, s32[1,2048]{1,0:T(1,128)S(1)} %copy-done.23, s32[8,256]{1,0:T(8,128)S(1)} %reshape.95.gd.dst), custom_call_target="tpu_custom_call" | custom-call | flops 4000000000 | bytes 3432448 | tf_op jit(solution)/shard_map/pallas_call | solution.py:32
  246.2 2.8 %collective-permute-start.21 = (bf16[32,512]{1,0:T(8,128)(2,1)S(1)}, bf16[32,512]{1,0:T(8,128)(2,1)S(1)}, u32[]{:S(2)}, u32[]{:S(2)}) collective-permute-start(bf16[32,512]{1,0:T(8,128)(2,1)S(1)} %pad_maximum_fusion.10), channel_id=1, source_target_pairs={{0,504},{4,508},{8,0},{12,4},{16,8},{20,12},{24,16},{28,20},{32,24... | collective-permute-start | bytes 98312 | tf_op jit(solution)/shard_map/ppermute | solution.py:426
  249.0 2.5 collective-permute-start.22
  251.5 5.7 %collective-permute-done.22 = bf16[32,512]{1,0:T(8,128)(2,1)S(1)} collective-permute-done((bf16[32,512]{1,0:T(8,128)(2,1)S(1)}, bf16[32,512]{1,0:T(8,128)(2,1)S(1)}, u32[]{:S(2)}, u32[]{:S(2)}) %collective-permute-start.22) | collective-permute-done | bytes 32800 | tf_op jit(solution)/shard_map/ppermute | solution.py:426
  257.2 4.2 %shard_map.244 = bf16[1024,474]{1,0:T(8,128)(2,1)S(1)} custom-call(bf16[1024,512]{1,0:T(8,128)(2,1)S(1)} %shard_map.243.entry, f32[1024,512]{1,0:T(8,128)} %get-tuple-element.146.skip, bf16[1024,512]{1,0:T(8,128)(2,1)S(1)} %copy-done.6, s32[6,128,128]{2,1,0:T(8,128)S(1)} %get-tuple-element.89.rows, bf16[4,1248,128]{2,1,0:T(8,128)(2,1)S(1)} %bitcast.66, ...), custom_call_target="tpu_custom_call" | custom-call | flops 1500000000 | bytes 6934528 | tf_op jit(solution)/shard_map/pallas_call | solution.py:32
  261.4 1.3 copy.30
  (205 shorter events, 18.0 us)
Async XLA Ops:
  7.2 4.2 %copy-start.42 = (bf16[512,128]{1,0:T(8,128)(2,1)S(1)}, bf16[512,128]{1,0:T(8,128)(2,1)}, u32[]{:S(2)}) copy-start(bf16[512,128]{1,0:T(8,128)(2,1)} %param.27) | copy-start | bytes 393220
  7.2 5.9 %copy-start.51 = (s32[1,6,8]{2,0,1:T(1,128)S(1)}, s32[1,6,8]{2,0,1:T(1,128)}, u32[]{:S(2)}) copy-start(s32[1,6,8]{2,0,1:T(1,128)} %param.39) | copy-start | bytes 580
  7.2 5.9 %copy-start.52 = (s32[1,6,8]{2,0,1:T(1,128)S(1)}, s32[1,6,8]{2,0,1:T(1,128)}, u32[]{:S(2)}) copy-start(s32[1,6,8]{2,0,1:T(1,128)} %param.36) | copy-start | bytes 580
  7.2 6.0 %copy-start.50 = (s32[1,6,12]{2,0,1:T(1,128)S(1)}, s32[1,6,12]{2,0,1:T(1,128)}, u32[]{:S(2)}) copy-start(s32[1,6,12]{2,0,1:T(1,128)} %param.33) | copy-start | bytes 868
  7.2 7.0 %copy-start.45 = (s32[1,2048]{1,0:T(1,128)S(1)}, s32[1,2048]{1,0:T(1,128)}, u32[]{:S(2)}) copy-start(s32[1,2048]{1,0:T(1,128)} %param.35) | copy-start | bytes 24580
  7.2 7.8 %copy-start.46 = (s32[1,2048]{1,0:T(1,128)S(1)}, s32[1,2048]{1,0:T(1,128)}, u32[]{:S(2)}) copy-start(s32[1,2048]{1,0:T(1,128)} %param.37) | copy-start | bytes 24580
  7.2 8.5 %copy-start.47 = (s32[1,2048]{1,0:T(1,128)S(1)}, s32[1,2048]{1,0:T(1,128)}, u32[]{:S(2)}) copy-start(s32[1,2048]{1,0:T(1,128)} %param.38) | copy-start | bytes 24580
  7.2 9.2 %copy-start.22 = (s32[1,2048]{1,0:T(1,128)S(1)}, s32[1,2048]{1,0:T(1,128)}, u32[]{:S(2)}) copy-start(s32[1,2048]{1,0:T(1,128)} %src_line.1) | copy-start | bytes 24580
  7.2 10.0 %copy-start.43 = (s32[1,3072]{1,0:T(1,128)S(1)}, s32[1,3072]{1,0:T(1,128)}, u32[]{:S(2)}) copy-start(s32[1,3072]{1,0:T(1,128)} %param.40) | copy-start | bytes 36868
  7.3 42.5 %all-gather.9.cloned.1.call-start = ((), (), s32[]{:S(2)}) async-start(), calls=%async_computation | async-start | bytes 1597440 | tf_op jit(solution)/shard_map/all_gather | solution.py:477
  8.1 9.8 %copy-start.44 = (s32[1,3072]{1,0:T(1,128)S(1)}, s32[1,3072]{1,0:T(1,128)}, u32[]{:S(2)}) copy-start(s32[1,3072]{1,0:T(1,128)} %param.41) | copy-start | bytes 36868
  8.1 10.6 %copy-start.41 = (bf16[1,1024,227]{1,2,0:T(8,128)(2,1)S(1)}, bf16[1,1024,227]{1,2,0:T(8,128)(2,1)}, u32[]{:S(2)}) copy-start(bf16[1,1024,227]{1,2,0:T(8,128)(2,1)} %param.32) | copy-start | bytes 1394692
  10.1 8.8 %copy-start.40 = (bf16[1,1024,474]{1,2,0:T(8,128)(2,1)S(1)}, bf16[1,1024,474]{1,2,0:T(8,128)(2,1)}, u32[]{:S(2)}) copy-start(bf16[1,1024,474]{1,2,0:T(8,128)(2,1)} %param.23) | copy-start | bytes 2912260
  10.1 68.0 %all-gather.11.cloned.1.call-start = ((), (), s32[]{:S(2)}) async-start(), calls=%async_computation.1 | async-start | bytes 1310720 | tf_op jit(solution)/shard_map/all_gather | solution.py:478
  12.2 107.2 %all-gather.13.cloned.1.call-start = ((), (), s32[]{:S(2)}) async-start(), calls=%async_computation.2 | async-start | bytes 1310720 | tf_op jit(solution)/shard_map/all_gather | solution.py:479
  12.2 7.4 %copy-start.48 = (s32[8,128]{1,0:T(8,128)S(1)}, s32[8,128]{1,0:T(8,128)}, u32[]{:S(2)}) copy-start(s32[8,128]{1,0:T(8,128)} %constant.51.clone) | copy-start | bytes 12292
  12.2 7.4 %copy-start.49 = (s32[8,128]{1,0:T(8,128)S(1)}, s32[8,128]{1,0:T(8,128)}, u32[]{:S(2)}) copy-start(s32[8,128]{1,0:T(8,128)} %constant.50.clone) | copy-start | bytes 12292
  13.0 132.3 %all-gather.15.cloned.1.call-start = ((), (), s32[]{:S(2)}) async-start(), calls=%async_computation.3 | async-start | bytes 1310720 | tf_op jit(solution)/shard_map/all_gather | solution.py:480
  15.7 154.0 %copy-start.18 = (s32[8,256]{1,0:T(8,128)}, s32[8,256]{1,0:T(8,128)S(1)}, u32[]{:S(2)}) copy-start(s32[8,256]{1,0:T(8,128)S(1)} %reshape.96.ms.src) | copy-start | bytes 24580
  16.5 153.3 %copy-start.20 = (s32[8,256]{1,0:T(8,128)}, s32[8,256]{1,0:T(8,128)S(1)}, u32[]{:S(2)}) copy-start(s32[8,256]{1,0:T(8,128)S(1)} %reshape.97.md.dst) | copy-start | bytes 24580
  18.9 20.8 %copy-start.53 = (s32[6]{0:T(128)S(1)}, s32[6]{0:T(128)}, u32[]{:S(2)}) copy-start(s32[6]{0:T(128)} %constant.53.clone) | copy-start | bytes 76
  19.0 20.8 %copy-start.54 = (s32[6]{0:T(128)S(1)}, s32[6]{0:T(128)}, u32[]{:S(2)}) copy-start(s32[6]{0:T(128)} %constant.52.clone) | copy-start | bytes 76
  20.5 29.3 %collective-permute-start.3 = (bf16[32,512]{1,0:T(8,128)(2,1)S(1)}, bf16[32,512]{1,0:T(8,128)(2,1)S(1)}, u32[]{:S(2)}, u32[]{:S(2)}) collective-permute-start(bf16[32,512]{1,0:T(8,128)(2,1)S(1)} %get-tuple-element.83), channel_id=1, source_target_pairs={{0,500},{4,16},{8,508},{12,24},{16,4},{20,32},{24,12},{28,40},{32,... | collective-permute-start | bytes 98312 | tf_op jit(solution)/shard_map/ppermute | solution.py:426
  27.7 12.1 %collective-permute-start = (bf16[96,512]{1,0:T(8,128)(2,1)S(1)}, bf16[96,512]{1,0:T(8,128)(2,1)S(1)}, u32[]{:S(2)}, u32[]{:S(2)}) collective-permute-start(bf16[96,512]{1,0:T(8,128)(2,1)S(1)} %pad_maximum_fusion.3), channel_id=1, source_target_pairs={{0,4},{4,0},{8,12},{12,8},{16,20},{20,16},{24,28},{28,24},{32,36},... | collective-permute-start | bytes 294920 | tf_op jit(solution)/shard_map/ppermute | solution.py:426
  39.8 108.2 %copy-start.27 = (s32[24]{0:T(128)}, s32[24]{0:T(128)S(1)}, u32[]{:S(2)}) copy-start(s32[24]{0:T(128)S(1)} %multiply_minimum_fusion.starts) | copy-start | bytes 292
  39.8 8.9 %collective-permute-start.1 = (bf16[64,512]{1,0:T(8,128)(2,1)S(1)}, bf16[64,512]{1,0:T(8,128)(2,1)S(1)}, u32[]{:S(2)}, u32[]{:S(2)}) collective-permute-start(bf16[64,512]{1,0:T(8,128)(2,1)S(1)} %pad_maximum_fusion.4), channel_id=1, source_target_pairs={{0,8},{4,12},{8,16},{12,20},{16,24},{20,28},{24,32},{28,36},{32,40... | collective-permute-start | bytes 196616 | tf_op jit(solution)/shard_map/ppermute | solution.py:426
  42.9 6.8 %collective-permute-start.2 = (bf16[64,512]{1,0:T(8,128)(2,1)S(1)}, bf16[64,512]{1,0:T(8,128)(2,1)S(1)}, u32[]{:S(2)}, u32[]{:S(2)}) collective-permute-start(bf16[64,512]{1,0:T(8,128)(2,1)S(1)} %pad_maximum_fusion.5), channel_id=1, source_target_pairs={{0,504},{4,508},{8,0},{12,4},{16,8},{20,12},{24,16},{28,20},{32,24... | collective-permute-start | bytes 196616 | tf_op jit(solution)/shard_map/ppermute | solution.py:426
  49.8 28.3 %copy-start.26 = (bf16[256,512]{1,0:T(8,128)(2,1)S(1)}, bf16[256,512]{1,0:T(8,128)(2,1)}, u32[]{:S(2)}) copy-start(bf16[256,512]{1,0:T(8,128)(2,1)} %static.1) | copy-start | bytes 786436
  92.3 27.1 %collective-permute-start.7 = (bf16[8,512]{1,0:T(8,128)(2,1)S(1)}, bf16[8,512]{1,0:T(8,128)(2,1)S(1)}, u32[]{:S(2)}, u32[]{:S(2)}) collective-permute-start(bf16[8,512]{1,0:T(8,128)(2,1)S(1)} %get-tuple-element.95), channel_id=1, source_target_pairs={{0,500},{4,16},{8,508},{12,24},{16,4},{20,32},{24,12},{28,40},{32,... | collective-permute-start | bytes 24584 | tf_op jit(solution)/shard_map/ppermute | solution.py:426
  98.2 11.7 %collective-permute-start.4 = (bf16[24,512]{1,0:T(8,128)(2,1)S(1)}, bf16[24,512]{1,0:T(8,128)(2,1)S(1)}, u32[]{:S(2)}, u32[]{:S(2)}) collective-permute-start(bf16[24,512]{1,0:T(8,128)(2,1)S(1)} %pad_maximum_fusion.12), channel_id=1, source_target_pairs={{0,4},{4,0},{8,12},{12,8},{16,20},{20,16},{24,28},{28,24},{32,36},... | collective-permute-start | bytes 73736 | tf_op jit(solution)/shard_map/ppermute | solution.py:426
  109.9 8.6 %collective-permute-start.5 = (bf16[16,512]{1,0:T(8,128)(2,1)S(1)}, bf16[16,512]{1,0:T(8,128)(2,1)S(1)}, u32[]{:S(2)}, u32[]{:S(2)}) collective-permute-start(bf16[16,512]{1,0:T(8,128)(2,1)S(1)} %pad_maximum_fusion.15), channel_id=1, source_target_pairs={{0,8},{4,12},{8,16},{12,20},{16,24},{20,28},{24,32},{28,36},{32,40... | collective-permute-start | bytes 49160 | tf_op jit(solution)/shard_map/ppermute | solution.py:426
  112.3 7.1 %collective-permute-start.6 = (bf16[16,512]{1,0:T(8,128)(2,1)S(1)}, bf16[16,512]{1,0:T(8,128)(2,1)S(1)}, u32[]{:S(2)}, u32[]{:S(2)}) collective-permute-start(bf16[16,512]{1,0:T(8,128)(2,1)S(1)} %pad_maximum_fusion.16), channel_id=1, source_target_pairs={{0,504},{4,508},{8,0},{12,4},{16,8},{20,12},{24,16},{28,20},{32,24... | collective-permute-start | bytes 49160 | tf_op jit(solution)/shard_map/ppermute | solution.py:426
  121.7 23.6 %collective-permute-start.11 = (bf16[8,512]{1,0:T(8,128)(2,1)S(1)}, bf16[8,512]{1,0:T(8,128)(2,1)S(1)}, u32[]{:S(2)}, u32[]{:S(2)}) collective-permute-start(bf16[8,512]{1,0:T(8,128)(2,1)S(1)} %get-tuple-element.104), channel_id=1, source_target_pairs={{0,500},{4,16},{8,508},{12,24},{16,4},{20,32},{24,12},{28,40},{32,... | collective-permute-start | bytes 24584 | tf_op jit(solution)/shard_map/ppermute | solution.py:426
  123.6 10.5 %collective-permute-start.8 = (bf16[24,512]{1,0:T(8,128)(2,1)S(1)}, bf16[24,512]{1,0:T(8,128)(2,1)S(1)}, u32[]{:S(2)}, u32[]{:S(2)}) collective-permute-start(bf16[24,512]{1,0:T(8,128)(2,1)S(1)} %pad_maximum_fusion.13), channel_id=1, source_target_pairs={{0,4},{4,0},{8,12},{12,8},{16,20},{20,16},{24,28},{28,24},{32,36},... | collective-permute-start | bytes 73736 | tf_op jit(solution)/shard_map/ppermute | solution.py:426
  134.1 8.6 %collective-permute-start.9 = (bf16[16,512]{1,0:T(8,128)(2,1)S(1)}, bf16[16,512]{1,0:T(8,128)(2,1)S(1)}, u32[]{:S(2)}, u32[]{:S(2)}) collective-permute-start(bf16[16,512]{1,0:T(8,128)(2,1)S(1)} %pad_maximum_fusion.17), channel_id=1, source_target_pairs={{0,8},{4,12},{8,16},{12,20},{16,24},{20,28},{24,32},{28,36},{32,40... | collective-permute-start | bytes 49160 | tf_op jit(solution)/shard_map/ppermute | solution.py:426
  140.8 4.5 %collective-permute-start.10 = (bf16[16,512]{1,0:T(8,128)(2,1)S(1)}, bf16[16,512]{1,0:T(8,128)(2,1)S(1)}, u32[]{:S(2)}, u32[]{:S(2)}) collective-permute-start(bf16[16,512]{1,0:T(8,128)(2,1)S(1)} %pad_maximum_fusion.18), channel_id=1, source_target_pairs={{0,504},{4,508},{8,0},{12,4},{16,8},{20,12},{24,16},{28,20},{32,24... | collective-permute-start | bytes 49160 | tf_op jit(solution)/shard_map/ppermute | solution.py:426
  146.6 1.4 copy-start.8
  146.6 1.5 copy-start.31
  149.3 20.4 %copy-start.36 = (bf16[2048,512]{1,0:T(8,128)(2,1)S(1)}, bf16[2048,512]{1,0:T(8,128)(2,1)}, u32[]{:S(2)}) copy-start(bf16[2048,512]{1,0:T(8,128)(2,1)} %copy-done.35) | copy-start | bytes 6291460
  162.4 21.7 %collective-permute-start.15 = (bf16[16,512]{1,0:T(8,128)(2,1)S(1)}, bf16[16,512]{1,0:T(8,128)(2,1)S(1)}, u32[]{:S(2)}, u32[]{:S(2)}) collective-permute-start(bf16[16,512]{1,0:T(8,128)(2,1)S(1)} %get-tuple-element.120.refs_3_), channel_id=1, source_target_pairs={{0,500},{4,16},{8,508},{12,24},{16,4},{20,32},{24,12},{28,40},{32,... | collective-permute-start | bytes 49160 | tf_op jit(solution)/shard_map/ppermute | solution.py:426
  164.8 9.6 %collective-permute-start.12 = (bf16[48,512]{1,0:T(8,128)(2,1)S(1)}, bf16[48,512]{1,0:T(8,128)(2,1)S(1)}, u32[]{:S(2)}, u32[]{:S(2)}) collective-permute-start(bf16[48,512]{1,0:T(8,128)(2,1)S(1)} %pad_maximum_fusion.6), channel_id=1, source_target_pairs={{0,4},{4,0},{8,12},{12,8},{16,20},{20,16},{24,28},{28,24},{32,36},... | collective-permute-start | bytes 147464 | tf_op jit(solution)/shard_map/ppermute | solution.py:426
  169.8 14.3 %copy-start.1 = (bf16[4096,128]{1,0:T(8,128)(2,1)S(1)}, bf16[4096,128]{1,0:T(8,128)(2,1)}, u32[]{:S(2)}) copy-start(bf16[4096,128]{1,0:T(8,128)(2,1)} %all-gather.13.cloned.1.call-done) | copy-start | bytes 3145732
  174.5 8.6 %collective-permute-start.13 = (bf16[32,512]{1,0:T(8,128)(2,1)S(1)}, bf16[32,512]{1,0:T(8,128)(2,1)S(1)}, u32[]{:S(2)}, u32[]{:S(2)}) collective-permute-start(bf16[32,512]{1,0:T(8,128)(2,1)S(1)} %pad_maximum_fusion.8), channel_id=1, source_target_pairs={{0,8},{4,12},{8,16},{12,20},{16,24},{20,28},{24,32},{28,36},{32,40... | collective-permute-start | bytes 98312 | tf_op jit(solution)/shard_map/ppermute | solution.py:426
  177.8 6.3 %collective-permute-start.14 = (bf16[32,512]{1,0:T(8,128)(2,1)S(1)}, bf16[32,512]{1,0:T(8,128)(2,1)S(1)}, u32[]{:S(2)}, u32[]{:S(2)}) collective-permute-start(bf16[32,512]{1,0:T(8,128)(2,1)S(1)} %pad_maximum_fusion.9), channel_id=1, source_target_pairs={{0,504},{4,508},{8,0},{12,4},{16,8},{20,12},{24,16},{28,20},{32,24... | collective-permute-start | bytes 98312 | tf_op jit(solution)/shard_map/ppermute | solution.py:426
  184.1 8.8 %copy-start.4 = (bf16[4992,128]{1,0:T(8,128)(2,1)S(1)}, bf16[4992,128]{1,0:T(8,128)(2,1)}, u32[]{:S(2)}) copy-start(bf16[4992,128]{1,0:T(8,128)(2,1)} %all-gather.9.cloned.1.call-done) | copy-start | bytes 3833860
  184.1 8.8 %copy-start.28 = (s32[24]{0:T(128)S(1)}, s32[24]{0:T(128)}, u32[]{:S(2)}) copy-start(s32[24]{0:T(128)} %copy-done.27) | copy-start | bytes 292
  184.1 8.8 %copy-start.34 = (bf16[1024,512]{1,0:T(8,128)(2,1)S(1)}, bf16[1024,512]{1,0:T(8,128)(2,1)}, u32[]{:S(2)}) copy-start(bf16[1024,512]{1,0:T(8,128)(2,1)} %copy-done.32) | copy-start | bytes 3145732
  186.5 18.7 %copy-start.24 = (bf16[8,512]{1,0:T(8,128)(2,1)}, bf16[8,512]{1,0:T(8,128)(2,1)S(1)}, u32[]{:S(2)}) copy-start(bf16[8,512]{1,0:T(8,128)(2,1)S(1)} %get-tuple-element.137.refs_5_) | copy-start | bytes 24580
  186.5 18.7 %copy-start.25 = (bf16[8,512]{1,0:T(8,128)(2,1)}, bf16[8,512]{1,0:T(8,128)(2,1)S(1)}, u32[]{:S(2)}) copy-start(bf16[8,512]{1,0:T(8,128)(2,1)S(1)} %get-tuple-element.136.refs_4_) | copy-start | bytes 24580
  186.5 43.5 %collective-permute-start.19 = (bf16[8,512]{1,0:T(8,128)(2,1)}, bf16[8,512]{1,0:T(8,128)(2,1)}, u32[]{:S(2)}, u32[]{:S(2)}) collective-permute-start(bf16[8,512]{1,0:T(8,128)(2,1)} %get-tuple-element.135.refs_3_), channel_id=1, source_target_pairs={{0,500},{4,16},{8,508},{12,24},{16,4},{20,32},{24,12},{28,40},{32,... | collective-permute-start | bytes 24584 | tf_op jit(solution)/shard_map/ppermute | solution.py:426
  189.0 24.5 %collective-permute-start.16 = (bf16[24,512]{1,0:T(8,128)(2,1)}, bf16[24,512]{1,0:T(8,128)(2,1)}, u32[]{:S(2)}, u32[]{:S(2)}) collective-permute-start(bf16[24,512]{1,0:T(8,128)(2,1)} %pad_maximum_fusion.14), channel_id=1, source_target_pairs={{0,4},{4,0},{8,12},{12,8},{16,20},{20,16},{24,28},{28,24},{32,36},... | collective-permute-start | bytes 73736 | tf_op jit(solution)/shard_map/ppermute | solution.py:426
  193.0 12.2 %copy-start.19 = (s32[8,256]{1,0:T(8,128)S(1)}, s32[8,256]{1,0:T(8,128)}, u32[]{:S(2)}) copy-start(s32[8,256]{1,0:T(8,128)} %copy-done.18) | copy-start | bytes 24580
  193.0 12.2 %copy-start.21 = (s32[8,256]{1,0:T(8,128)S(1)}, s32[8,256]{1,0:T(8,128)}, u32[]{:S(2)}) copy-start(s32[8,256]{1,0:T(8,128)} %copy-done.20) | copy-start | bytes 24580
  193.0 12.2 %copy-start.38 = (bf16[2048,512]{1,0:T(8,128)(2,1)S(1)}, bf16[2048,512]{1,0:T(8,128)(2,1)}, u32[]{:S(2)}) copy-start(bf16[2048,512]{1,0:T(8,128)(2,1)} %copy-done.37) | copy-start | bytes 6291460
  205.2 24.8 %copy-start.3 = (bf16[4096,128]{1,0:T(8,128)(2,1)S(1)}, bf16[4096,128]{1,0:T(8,128)(2,1)}, u32[]{:S(2)}) copy-start(bf16[4096,128]{1,0:T(8,128)(2,1)} %all-gather.11.cloned.1.call-done) | copy-start | bytes 3145732
  214.9 9.3 %collective-permute-start.17 = (bf16[16,512]{1,0:T(8,128)(2,1)S(1)}, bf16[16,512]{1,0:T(8,128)(2,1)S(1)}, u32[]{:S(2)}, u32[]{:S(2)}) collective-permute-start(bf16[16,512]{1,0:T(8,128)(2,1)S(1)} %pad_maximum_fusion.19), channel_id=1, source_target_pairs={{0,504},{4,508},{8,0},{12,4},{16,8},{20,12},{24,16},{28,20},{32,24... | collective-permute-start | bytes 49160 | tf_op jit(solution)/shard_map/ppermute | solution.py:426
  222.2 7.8 %collective-permute-start.18 = (bf16[16,512]{1,0:T(8,128)(2,1)S(1)}, bf16[16,512]{1,0:T(8,128)(2,1)S(1)}, u32[]{:S(2)}, u32[]{:S(2)}) collective-permute-start(bf16[16,512]{1,0:T(8,128)(2,1)S(1)} %pad_maximum_fusion.20), channel_id=1, source_target_pairs={{0,8},{4,12},{8,16},{12,20},{16,24},{20,28},{24,32},{28,36},{32,40... | collective-permute-start | bytes 49160 | tf_op jit(solution)/shard_map/ppermute | solution.py:426
  234.0 7.1 %copy-start.23 = (s32[1,2048]{1,0:T(1,128)S(1)}, s32[1,2048]{1,0:T(1,128)}, u32[]{:S(2)}) copy-start(s32[1,2048]{1,0:T(1,128)} %src_line.1) | copy-start | bytes 24580
  234.0 7.1 %copy-start.39 = (bf16[2048,512]{1,0:T(8,128)(2,1)S(1)}, bf16[2048,512]{1,0:T(8,128)(2,1)}, u32[]{:S(2)}) copy-start(bf16[2048,512]{1,0:T(8,128)(2,1)} %get-tuple-element.145.slope) | copy-start | bytes 6291460
  235.8 21.4 %collective-permute-start.23 = (bf16[16,512]{1,0:T(8,128)(2,1)S(1)}, bf16[16,512]{1,0:T(8,128)(2,1)S(1)}, u32[]{:S(2)}, u32[]{:S(2)}) collective-permute-start(bf16[16,512]{1,0:T(8,128)(2,1)S(1)} %get-tuple-element.153), channel_id=1, source_target_pairs={{0,500},{4,16},{8,508},{12,24},{16,4},{20,32},{24,12},{28,40},{32,... | collective-permute-start | bytes 49160 | tf_op jit(solution)/shard_map/ppermute | solution.py:426
  237.7 8.5 %collective-permute-start.20 = (bf16[48,512]{1,0:T(8,128)(2,1)S(1)}, bf16[48,512]{1,0:T(8,128)(2,1)S(1)}, u32[]{:S(2)}, u32[]{:S(2)}) collective-permute-start(bf16[48,512]{1,0:T(8,128)(2,1)S(1)} %pad_maximum_fusion.7), channel_id=1, source_target_pairs={{0,4},{4,0},{8,12},{12,8},{16,20},{20,16},{24,28},{28,24},{32,36},... | collective-permute-start | bytes 147464 | tf_op jit(solution)/shard_map/ppermute | solution.py:426
  241.1 16.1 %copy-start.6 = (bf16[1024,512]{1,0:T(8,128)(2,1)S(1)}, bf16[1024,512]{1,0:T(8,128)(2,1)}, u32[]{:S(2)}) copy-start(bf16[1024,512]{1,0:T(8,128)(2,1)} %copy-done.5) | copy-start | bytes 3145732
  246.2 5.3 %collective-permute-start.21 = (bf16[32,512]{1,0:T(8,128)(2,1)S(1)}, bf16[32,512]{1,0:T(8,128)(2,1)S(1)}, u32[]{:S(2)}, u32[]{:S(2)}) collective-permute-start(bf16[32,512]{1,0:T(8,128)(2,1)S(1)} %pad_maximum_fusion.10), channel_id=1, source_target_pairs={{0,504},{4,508},{8,0},{12,4},{16,8},{20,12},{24,16},{28,20},{32,24... | collective-permute-start | bytes 98312 | tf_op jit(solution)/shard_map/ppermute | solution.py:426
  249.0 8.1 %collective-permute-start.22 = (bf16[32,512]{1,0:T(8,128)(2,1)S(1)}, bf16[32,512]{1,0:T(8,128)(2,1)S(1)}, u32[]{:S(2)}, u32[]{:S(2)}) collective-permute-start(bf16[32,512]{1,0:T(8,128)(2,1)S(1)} %pad_maximum_fusion.11), channel_id=1, source_target_pairs={{0,8},{4,12},{8,16},{12,20},{16,24},{20,28},{24,32},{28,36},{32,40... | collective-permute-start | bytes 98312 | tf_op jit(solution)/shard_map/ppermute | solution.py:426
  (19 other events, 19.7 us)
Sparse Core Ops, SparseCore 0:
  10.8 34.4 all-gather.8
  47.9 30.1 all-gather.10
  80.2 29.6 all-gather.12
  111.9 29.6 all-gather.14

commit v2 on v0

v2 whole, which is shorter than its diff:
```python
import functools

import jax
import jax.numpy as jnp
import numpy as np
from jax import lax
from jax.experimental import pallas as pl
from jax.experimental.pallas import tpu as pltpu
from jax.sharding import PartitionSpec as P

EPSILON = 1e-06
LANES = 128
NEIGHBOURS = 6
BLOCK = 256
HALF = 128
BF = jnp.bfloat16
F32 = jnp.float32
EVEN = (0, 4, 1, 5, 2, 3)
ODD = (1, 0, 5, 4, 2, 3)
SWAP = (0, 2, 1, 3, 5, 4)


def shape(rows, columns, dtype=BF):
    return jax.ShapeDtypeStruct((rows, columns), dtype)


def smem(array):
    return pltpu.SMEM, array


def call(body, outs, args, flops, scratch=(), ties=()):
    outs = [o if isinstance(o, tuple) else (pltpu.VMEM, o) for o in outs]
    args = [a if isinstance(a, tuple) else (pltpu.VMEM, a) for a in args]
    moved = sum(a.size * a.dtype.itemsize for _, a in args)
    moved += sum(o.size * jnp.dtype(o.dtype).itemsize for _, o in outs)

    def kernel(*refs):
        body(*refs[: len(args)], *refs[len(args) + len(ties) :])

    return pl.pallas_call(
        kernel,
        out_shape=tuple(o for _, o in outs),
        in_specs=[pl.BlockSpec(memory_space=m) for m, _ in args]
        + [pl.BlockSpec(memory_space=pl.ANY)] * len(ties),
        out_specs=tuple(pl.BlockSpec(memory_space=m) for m, _ in outs),
        scratch_shapes=list(scratch),
        compiler_params=pltpu.CompilerParams(vmem_limit_bytes=20 << 20),
        cost_estimate=pl.CostEstimate(flops=flops, bytes_accessed=moved, transcendentals=0),
    )(*[a for _, a in args], *ties)


def vmem(rows, columns, dtype=BF):
    return pltpu.VMEM((rows, columns), dtype)


def mm(left, right):
    return jnp.dot(left, right, preferred_element_type=F32)


def mm_back(left, right):
    return lax.dot_general(left, right, (((1,), (1,)), ((), ())), preferred_element_type=F32)


def gate(values):
    return 0.5 * jnp.tanh(0.5 * values) + 0.5


def gate_slope(values, sigmoid):
    return sigmoid * (1.0 + values * (1.0 - sigmoid))


def column(row):
    return jnp.broadcast_to(row, (LANES, row.shape[1])).T


def pick(col, count):
    lane = lax.broadcasted_iota(jnp.int32, col.shape, 1)
    tiles = [
        jnp.where(lane + LANES * t == col, 1.0, 0.0).astype(BF) for t in range(count // LANES)
    ]
    return tiles[0] if len(tiles) == 1 else jnp.concatenate(tiles, axis=1)


def spread(row, count):
    own = lax.broadcasted_iota(jnp.int32, (count, row.shape[1]), 0)
    return jnp.where(own == row, 1.0, 0.0).astype(BF)


def mm_first(left, right):
    return lax.dot_general(left, right, (((0,), (0,)), ((), ())), preferred_element_type=F32)


def section(ref, place):
    return ref[place * 512 : (place + 1) * 512, :]


def assemble(shards, phase, target):
    for away, shard in enumerate(shards):
        block = pl.ds(pl.multiple_of(lax.rem(phase[0] - away + 4, 4) * LANES, LANES), LANES)
        target[:, block] = shard[...]


def at_block(b, size=BLOCK):
    return pl.ds(pl.multiple_of(b * size, size), size)


def line(ref, b, size=BLOCK):
    return ref[:, at_block(b, size)]


def received(refs):
    beside, far, up, down = [r[...].astype(F32) for r in refs]
    each = far.shape[0]
    return [beside[:each], up[:each], down[:each], far, up[each:], down[each:]]


def stacked(groups):
    rows = jnp.concatenate(groups, axis=0)
    short = LANES - rows.shape[0]
    return jnp.concatenate([rows, jnp.zeros((short, rows.shape[1]), F32)], axis=0).astype(BF)


def put(refs, groups):
    beside, far, up, down = refs
    beside[...] = jnp.concatenate(groups[:3], axis=0).astype(BF)
    far[...] = groups[3].astype(BF)
    up[...] = groups[4].astype(BF)
    down[...] = groups[5].astype(BF)


def cut(rows, each):
    return [rows[k * each : (k + 1) * each] for k in range(NEIGHBOURS)]


def inverse_rms(values):
    return lax.rsqrt(jnp.mean(values * values, axis=-1, keepdims=True) + EPSILON)


def norm_grad(grad, update, scale):
    mixed = jnp.mean(grad * update, axis=-1, keepdims=True)
    return (scale * grad - update * (scale * scale * scale) * mixed).astype(BF)


def prepare_kernel(gs, gd, ms, md, ds, dd, dd_small, entries, tables, grid_in, cotangent, cols, rows, starts, *sends):
    last_start = grid_in.shape[1] - HALF - 16
    for b in range(starts.shape[0]):
        starts[b] = jnp.minimum(lax.shift_left(lax.shift_right_logical(dd_small[0, b * HALF], 4), 4), last_start)
    lists = ((gs, gd), (ms, md), (ds, dd))
    for which, (src, dst) in enumerate(lists):
        slots = column(entries[which : which + 1, :])
        entry = jnp.concatenate([slots] * (BLOCK // LANES), axis=1)
        found = jnp.zeros((LANES, BLOCK), F32)
        for b in range(src.shape[1] // BLOCK):
            piece = slice(b * BLOCK, (b + 1) * BLOCK)
            dst_row = jnp.broadcast_to(dst[:, piece], (LANES, BLOCK)).astype(F32)
            found += jnp.where(entry == src[:, piece], dst_row, 0.0)
        total = jnp.sum(found, axis=1, keepdims=True)
        wide = jnp.broadcast_to(total, (LANES, LANES)).astype(jnp.int32)
        wide = jnp.where(slots >= 0, wide, -1)
        cols[which] = wide
        rows[which] = wide.T[:8, :]
    for t in range(3):
        wide = jnp.broadcast_to(tables[t : t + 1, :], (LANES, LANES))
        rows[3 + t] = wide[:8, :]
        cols[3 + t] = wide.T
    count = grid_in.shape[1]
    sent = mm_back(pick(cols[3], count), grid_in[...])
    at = pick(cols[2], count)
    back = mm_back(at, grid_in[...])
    back_cot = mm_back(at, cotangent[...])

    def padded(piece):
        return jnp.concatenate([piece, jnp.zeros((piece.shape[0], 512 - piece.shape[1]), F32)], axis=1)

    groups = []
    for k in range(NEIGHBOURS):
        j = SWAP[k]
        parts = [sent[16 * k : 16 * k + 16], back[8 * j : 8 * j + 8], back_cot[8 * j : 8 * j + 8]]
        groups.append(jnp.concatenate([padded(piece) for piece in parts], axis=0))
    put(sends, groups)


def embed_kernel(grid_in, own, from_1, from_2, from_3, phase, *refs):
    early = refs[:4]
    ext, slope, hidden, b_hidden, b_cot, w = refs[4:]
    f_in, rows = grid_in.shape
    assemble((own, from_1, from_2, from_3), phase, w)
    embed = w[:f_in, :]
    mix = w[480:992, :]
    groups = received(early)
    b_cot[...] = stacked([groups[k][24:32, :256] for k in SWAP])
    pre = mm(stacked([groups[k][16:24, :f_in] for k in SWAP]), embed)
    b_hidden[...] = (pre * gate(pre)).astype(BF)
    pre = mm(stacked([g[:16, :f_in] for g in groups]), embed)
    ext[rows:, :] = mm((pre * gate(pre)).astype(BF), mix).astype(BF)
    size = 512
    for b in range(rows // size):
        at = slice(b * size, (b + 1) * size)
        pre = mm_first(grid_in[:, at], embed)
        sig = gate(pre)
        slope[at, :] = gate_slope(pre, sig).astype(BF)
        own_rows = (pre * sig).astype(BF)
        hidden[at, :] = own_rows
        ext[at, :] = mm(own_rows, mix).astype(BF)


def assemble_kernel(own, from_1, from_2_low, from_2_high, from_3, phase, w):
    half = from_2_low.shape[0]
    low, high = w.at[:half, :], w.at[half:, :]
    assemble((own.at[:half, :], from_1.at[:half, :], from_2_low, from_3.at[:half, :]), phase, low)
    assemble((own.at[half:, :], from_1.at[half:, :], from_2_high, from_3.at[half:, :]), phase, high)


def cotangent_kernel(cotangent, b_cot, w, own_grad, b_grad):
    f_out = cotangent.shape[0]
    out = w[2048 : 2048 + f_out, :]
    own_grad[...] = mm_first(cotangent[...], out).astype(BF)
    b_grad[...] = mm(b_cot[:, :f_out], out).astype(BF)


def encode_edges_kernel(ext, static, src, moves, dst, cols, slope, h_slope, total, messages):
    count = ext.shape[0]
    meshes = static.shape[0]
    pre = ext[count - LANES :, :].astype(F32) + mm(pick(cols[0], meshes), static[...])
    h_slope[...] = gate_slope(pre, gate(pre)).astype(BF)
    size = src.shape[1] // 2
    for b in range(2):
        at = slice(b * size, (b + 1) * size)
        entry = src[:, at]
        src_row = entry
        for k in range(NEIGHBOURS):
            src_row += jnp.where(entry >= count - LANES + 12 * k, moves[k], 0)
        pre = mm(pick(column(src_row), count), ext[...])
        pre += mm(pick(column(dst[:, at]), meshes), static[...])
        sig = gate(pre)
        slope[at, :] = gate_slope(pre, sig).astype(BF)
        messages[at, :] = (pre * sig).astype(BF)
    total[...] = mm(spread(dst[...], meshes), messages[...])


def encode_rows_kernel(total, static, cols, w, *refs):
    encoded, latent, proj = refs[:3]
    made = mm(total[...].astype(BF), w[992:1504, :])
    encoded[...] = made
    start = (static[...].astype(F32) + made * inverse_rms(made)).astype(BF)
    latent[...] = start
    sent = mm(start, w[1504:, :]).astype(BF)
    proj[...] = sent
    put(refs[3:], cut(mm(pick(cols[4], static.shape[0]), sent), 8))


def edges_kernel(proj, latent, src, dst, total, slope, messages):
    count = proj.shape[0]
    size = src.shape[1] // 2
    for b in range(2):
        at = slice(b * size, (b + 1) * size)
        pre = mm(pick(column(src[:, at]), count), proj[...])
        pre += mm(pick(column(dst[:, at]), count), latent[...])
        sig = gate(pre)
        slope[at, :] = gate_slope(pre, sig).astype(BF)
        messages[at, :] = (pre * sig).astype(BF)
    own_row = jnp.where(src[...] < count, dst[...], -1)
    total[...] = mm(spread(own_row, count), messages[...])


def layer_kernel(total, latent, cols, rows, w, *refs, places):
    halo = refs[:4]
    h_slope, update, new, proj = refs[4:8]
    sends = refs[8:]
    count = latent.shape[0]
    old = latent[...]
    pre = stacked(received(halo)).astype(F32) + mm(pick(cols[1], count), old)
    sig = gate(pre)
    h_slope[...] = gate_slope(pre, sig).astype(BF)
    summed = total[...] + mm(spread(rows[1][0:1, :], count), (pre * sig).astype(BF))
    made = mm(summed.astype(BF), section(w, places[0]))
    update[...] = made
    after = (old.astype(F32) + made * inverse_rms(made)).astype(BF)
    new[...] = after
    sent = mm(after, section(w, places[1])).astype(BF)
    proj[...] = sent
    if sends:
        put(sends, cut(mm(pick(cols[4], count), sent), 8))


def outgoing_grad(grad, cols, h_slope, count):
    return (mm(pick(cols, count), grad) * h_slope[...].astype(F32)).astype(BF).astype(F32)


def decode_kernel(proj, hidden, own_grad, b_hidden, b_grad, starts, src, dst, cols, rows, w, update, h_slope, *refs):
    messages, grads, latent_grad, sum_grad = refs[:4]
    sends = refs[4:]
    count = proj.shape[0]
    last_start = hidden.shape[0] - BLOCK

    @pl.loop(0, src.shape[1] // BLOCK, unroll=4)
    def _(b):
        at = at_block(b)
        dst_row = line(dst, b)
        pre = mm(pick(column(line(src, b)), count), proj[...])
        near, grad = [], []
        for half in range(BLOCK // HALF):
            start = pl.multiple_of(jnp.minimum(starts[2 * b + half], last_start), 16)
            window = pl.ds(start, BLOCK)
            chosen = pick(column(dst_row[:, half * HALF : (half + 1) * HALF] - start), BLOCK)
            near.append(mm(chosen, hidden[window, :]))
            grad.append(mm(chosen, own_grad[window, :]))
        pre += jnp.concatenate(near, axis=0)
        sig = gate(pre)
        messages[at, :] = (pre * sig).astype(BF)
        grads[at, :] = (jnp.concatenate(grad, axis=0) * gate_slope(pre, sig)).astype(BF)

    own = mm(spread(src[...], count), grads[...]).astype(BF).astype(F32)
    sent = mm(pick(cols[5], count), proj[...])
    pre = sent + b_hidden[...].astype(F32)
    far = (b_grad[...].astype(F32) * gate_slope(pre, gate(pre))).astype(BF)
    row_grad = (own + mm(spread(rows[5][0:1, :], count), far)).astype(BF)
    grad = mm_back(row_grad, section(w, 3))
    latent_grad[...] = grad
    made = update[...]
    step = norm_grad(grad, made, inverse_rms(made))
    back = mm_back(step, section(w, 2)).astype(BF)
    sum_grad[...] = back
    out = cut(outgoing_grad(back, cols[1], h_slope, count), 8)
    put(sends, [jnp.concatenate([a, out[j]], axis=0) for a, j in zip(cut(sent, 8), SWAP)])


def add_by_row(total, values, starts, src, dst, own):
    rows = HALF + 16

    @pl.loop(0, src.shape[1] // HALF, unroll=4)
    def _(b):
        dst_row = jnp.where(line(src, b, HALF) < own, line(dst, b, HALF), -(1 << 20))
        start = pl.multiple_of(starts[b], 16)
        total[pl.ds(start, rows), :] += mm(spread(dst_row - start, rows), values[at_block(b, HALF), :])


def skip_kernel(grads, hidden, own_grad, starts, src, dst, cols, rows, *refs, own):
    halo = refs[:4]
    skip, message, total = refs[4:]
    count = hidden.shape[0]
    near = pick(cols[2], count)
    far = stacked([g[:8] for g in received(halo)]).astype(F32)
    pre = far + mm(near, hidden[...])
    sig = gate(pre)
    message[...] = (pre * sig).astype(BF)
    edge = (mm(near, own_grad[...]) * gate_slope(pre, sig)).astype(BF)
    total[...] = mm(spread(rows[2][0:1, :], count), edge)
    add_by_row(total, grads, starts, src, dst, own)
    skip[...] = total[...].astype(BF)


def predict_kernel(messages, message, starts, src, dst, rows, w, pred, total, *, own):
    f_out, count = pred.shape
    total[...] = mm(spread(rows[2][0:1, :], count), message[...])
    add_by_row(total, messages, starts, src, dst, own)
    pred[...] = mm_back(w[2048 : 2048 + f_out, :], total[...].astype(BF)).astype(BF)


def edges_back_kernel(sum_grad, slope, src, dst, rows, *refs, both):
    far = refs[:4]
    entry, into, edge = refs[4:]
    count = sum_grad.shape[0]
    size = src.shape[1] // 2
    beside, beyond, up, down = [r[...].astype(F32) for r in far]
    each = beyond.shape[0]
    groups = [beside[k * each : (k + 1) * each] for k in range(3)] + [beyond, up, down]
    if both:
        groups = [groups[k][8:] for k in SWAP]
    for b in range(2):
        at = slice(b * size, (b + 1) * size)
        grad = mm(pick(column(dst[:, at]), count), sum_grad[...])
        edge[at, :] = (grad * slope[at, :].astype(F32)).astype(BF)
    own_row = jnp.where(src[...] < count, dst[...], -1)
    into[...] = mm(spread(rows[1][0:1, :], count), stacked(groups)) + mm(spread(own_row, count), edge[...])
    entry[...] = mm(spread(src[...], count), edge[...]).astype(BF)


def layer_back_kernel(entry, into, latent_grad, cols, rows, src_w, next_w, update, h_slope, *refs, where, both, first):
    groups = received(refs[:4])
    outs = refs[4:]
    count = entry.shape[0]
    if both:
        groups = [groups[k][8:] for k in SWAP]
    row_grad = entry[...].astype(F32) + mm(spread(rows[4][0:1, :], count), stacked(groups))
    grad = latent_grad[...] + into[...] + mm_back(row_grad.astype(BF), src_w[where[0] : where[0] + 512, :])
    made = update[...]
    step = norm_grad(grad, made, inverse_rms(made))
    summed = mm_back(step, next_w[where[1] : where[1] + 512, :]).astype(BF)
    if first:
        sum_grad, sends = outs[0], outs[1:]
    else:
        outs[0][...] = grad
        sum_grad, sends = outs[1], outs[2:]
    sum_grad[...] = summed
    each = sends[1].shape[0]
    put(sends, cut(outgoing_grad(summed, cols[0 if first else 1], h_slope, count), each))


def encode_back_kernel(sum_grad, slope, src, dst, entry, edge):
    count = sum_grad.shape[0]
    size = src.shape[1] // 2
    for b in range(2):
        at = slice(b * size, (b + 1) * size)
        grad = mm(pick(column(dst[:, at]), count), sum_grad[...])
        edge[at, :] = (grad * slope[at, :].astype(F32)).astype(BF)

    @pl.loop(0, entry.shape[0] // BLOCK)
    def _(b):
        entry[at_block(b), :] = mm(spread(src[...] - b * BLOCK, BLOCK), edge[...]).astype(BF)


def input_kernel(entry, w, slope, skip, rows, *refs):
    returned = refs[:4]
    out = refs[4]
    f_in, count = out.shape
    back = stacked(received(returned))
    mix = w[480:992, :]
    size = 512
    for b in range(count // size):
        at = slice(b * size, (b + 1) * size)
        place = spread(rows[3][0:1, :] - b * size, size)
        row_grad = (entry[at, :].astype(F32) + mm(place, back)).astype(BF)
        grad = mm_back(row_grad, mix) + skip[at, :].astype(F32)
        grad = (grad * slope[at, :].astype(F32)).astype(BF)
        out[:, at] = mm_back(w[:f_in, :], grad).astype(BF)


def slot_entries(sizes, order):
    table = np.full((8, LANES), -1, np.int32)
    for row, (own, used, apart) in enumerate(sizes):
        for place, k in enumerate(order):
            table[row, place * apart : place * apart + used] = own + k * used + np.arange(used)
    return table


def slot_moves(order):
    shifts = [16 * order.index(k) - 12 * k for k in range(NEIGHBOURS)]
    return np.diff(np.array([0] + shifts)).astype(np.int32)


def permuted(block, route):
    size = lax.axis_size("dom")
    return lax.ppermute(block, "dom", [(i, route(i) % size) for i in range(size)])


class Exchange:
    def __init__(self, sends, sign):
        beside, far, up, down = sends
        each = far.shape[0]
        self.beside = permuted(beside, lambda i: i ^ 1)
        self.far = permuted(far, lambda i: i + 3 if i % 2 else i - 3)
        up = jnp.concatenate([self.beside[each : 2 * each], up], axis=0)
        down = jnp.concatenate([self.beside[2 * each :], down], axis=0)
        self.ties = (up, down)
        self.up = permuted(up, lambda i: i + 2 * sign)
        self.down = permuted(down, lambda i: i - 2 * sign)

    def rows(self):
        return [self.beside, self.far, self.up, self.down]


def send_shapes(each, d):
    return [shape(3 * each, d)] + [shape(each, d)] * 3


def per_device(
    grid_in,
    mesh_static,
    embed_w,
    grid_w,
    enc_w,
    src_w,
    node_w,
    dec_w,
    out_w,
    cotangent,
    grid_send,
    g2m_src,
    g2m_dst,
    mesh_send,
    mesh_src,
    mesh_dst,
    dec_send,
    m2g_src,
    m2g_dst,
):
    x = grid_in[0].T
    cot = cotangent[0].T
    f_in, grid = x.shape
    mesh, d = mesh_static.shape
    f_out = cot.shape[0]
    edges = mesh_src.size
    phase = lax.axis_index("phase").reshape(1)

    def along(block, away):
        return lax.ppermute(block, "phase", [(i, (i + away) % 4) for i in range(4)])

    w_first = jnp.concatenate([jnp.pad(embed_w, ((0, 480 - f_in), (0, 0))), grid_w, enc_w, src_w[0]], axis=0)
    w_second = jnp.concatenate(
        [src_w[1], node_w[0], node_w[1], dec_w, jnp.pad(out_w.T, ((0, 256 - f_out), (0, 0)))], axis=0
    )
    even = lax.axis_index("dom") % 2 == 0

    def order(table, apart):
        flat = [jnp.pad(table[k], (0, apart - table.shape[1]), constant_values=-1) for k in range(NEIGHBOURS)]
        in_even, in_odd = (jnp.concatenate([flat[k] for k in ks]) for ks in (EVEN, ODD))
        row = jnp.where(even, in_even, in_odd)
        return jnp.pad(row, (0, LANES - row.shape[0]), constant_values=-1)

    tables = [order(grid_send[0], 16), order(mesh_send[0], 8), order(dec_send[0], 8)]
    tables = jnp.stack(tables + [tables[2]] * 5)
    sizes = ((grid, 12, 16), (mesh, 8, 8), (mesh, 8, 8))
    entries = jnp.where(even, slot_entries(sizes, ODD), slot_entries(sizes, EVEN))
    moves = jnp.where(even, slot_moves(ODD), slot_moves(EVEN))
    w_first, w_second, phase, moves, tables = lax.optimization_barrier((w_first, w_second, phase, moves, tables))
    first_1, first_3 = along(w_first, 1), along(w_first, -1)
    first_shards = [w_first, first_1, along(first_1, 1), first_3]
    cols, rows, starts, *sends = call(
        prepare_kernel,
        [
            jax.ShapeDtypeStruct((6, LANES, LANES), jnp.int32),
            jax.ShapeDtypeStruct((6, 8, LANES), jnp.int32),
            smem(jax.ShapeDtypeStruct((m2g_dst.size // HALF,), jnp.int32)),
        ]
        + send_shapes(32, d),
        [g2m_src, g2m_dst, mesh_src, mesh_dst, m2g_src, m2g_dst, smem(m2g_dst), entries, tables, x, cot],
        400_000_000,
        ties=(w_second, phase, moves),
    )
    early = Exchange(sends, 1)
    w_second, _ = lax.optimization_barrier((w_second, early.ties))
    half = w_second.shape[0] // 2
    second_1, second_3 = along(w_second, 1), along(w_second, -1)
    second_2 = (along(second_1[:half], 1), along(second_3[half:], -1))
    ext, slope_in, hidden, b_hidden, b_cot, w_enc = call(
        embed_kernel,
        [shape(grid + LANES, d), shape(grid, d), shape(grid, d), shape(LANES, d), shape(LANES, 256), shape(w_first.shape[0], d)],
        [x, *first_shards, smem(phase), *early.rows()],
        1_500_000_000,
    )
    enc_slope, enc_far, total = call(
        encode_edges_kernel,
        [shape(edges, d), shape(LANES, d), shape(mesh, d, F32)],
        [ext, mesh_static, g2m_src, smem(moves), g2m_dst, cols],
        5_000_000_000,
        [vmem(edges, d)],
        ties=(second_1, second_3),
    )
    encoded, latent, proj, *sends = call(
        encode_rows_kernel,
        [shape(mesh, d, F32), shape(mesh, d), shape(mesh, d)] + send_shapes(8, d),
        [total, mesh_static, cols, w_enc],
        300_000_000,
        ties=second_2,
    )
    stored = []
    for layer in range(2):
        moving = Exchange(sends, 1)
        total, slope = call(
            edges_kernel,
            [shape(mesh, d, F32), shape(edges, d)],
            [proj, latent, mesh_src, mesh_dst],
            3_000_000_000,
            [vmem(edges, d)],
            ties=moving.ties,
        )
        if layer == 0:
            (w,) = call(
                assemble_kernel,
                [shape(w_second.shape[0], d)],
                [w_second, second_1, *second_2, second_3, smem(phase)],
                1_000_000_000,
                ties=moving.ties,
            )
        else:
            own_grad, b_grad = call(
                cotangent_kernel,
                [shape(grid, d), shape(LANES, d)],
                [cot, b_cot, w],
                500_000_000,
                ties=moving.ties,
            )
        far, update, latent, proj, *sends = call(
            functools.partial(layer_kernel, places=(1 + layer, 3 * layer)),
            [shape(LANES, d), shape(mesh, d, F32), shape(mesh, d), shape(mesh, d)]
            + (send_shapes(8, d) if layer == 0 else []),
            [total, latent, cols, rows, w, *moving.rows()],
            400_000_000,
        )
        stored.append((slope, far, update))

    messages, grads, latent_grad, sum_grad, *sends = call(
        decode_kernel,
        [shape(m2g_src.size, d)] * 2 + [shape(mesh, d, F32), shape(mesh, d)] + send_shapes(16, d),
        [proj, hidden, own_grad, b_hidden, b_grad, smem(starts), m2g_src, m2g_dst, cols, rows, w, update, far],
        6_000_000_000,
    )

    def edges_back(sum_grad, slope, sends, both, ties):
        return call(
            functools.partial(edges_back_kernel, both=both),
            [shape(mesh, d), shape(mesh, d, F32)],
            [sum_grad, slope, mesh_src, mesh_dst, rows, *sends],
            3_000_000_000,
            [vmem(edges, d)],
            ties=ties,
        )

    moving = Exchange(sends, 1)
    halo = moving.rows()
    entry, into = edges_back(sum_grad, stored[1][0], sends, True, moving.ties)
    latent_grad, sum_grad, *sends = call(
        functools.partial(layer_back_kernel, where=(0, d), both=True, first=False),
        [shape(mesh, d, F32), shape(mesh, d)] + send_shapes(8, d),
        [entry, into, latent_grad, cols, rows, w, w, stored[0][2], stored[0][1], *halo],
        400_000_000,
    )
    moving = Exchange(sends, -1)
    entry, into = edges_back(sum_grad, stored[0][0], sends, False, moving.ties)
    skip, message = call(
        functools.partial(skip_kernel, own=mesh),
        [shape(grid, d), shape(LANES, d)],
        [grads, hidden, own_grad, smem(starts), m2g_src, m2g_dst, cols, rows, *halo],
        2_500_000_000,
        [vmem(grid, d, F32)],
        ties=moving.ties,
    )
    sum_grad, *sends = call(
        functools.partial(layer_back_kernel, where=(1504, 992), both=False, first=True),
        [shape(mesh, d)] + send_shapes(16, d),
        [entry, into, latent_grad, cols, rows, w_enc, w_enc, encoded, enc_far, *moving.rows()],
        400_000_000,
    )
    moving = Exchange(sends, -1)
    (pred,) = call(
        functools.partial(predict_kernel, own=mesh),
        [shape(f_out, grid)],
        [messages, message, smem(starts), m2g_src, m2g_dst, rows, w],
        2_500_000_000,
        [vmem(grid, d, F32)],
        ties=moving.ties,
    )
    (entry,) = call(
        encode_back_kernel,
        [shape(grid, d)],
        [sum_grad, enc_slope, g2m_src, g2m_dst],
        4_000_000_000,
        [vmem(edges, d)],
        ties=moving.ties,
    )
    (input_grad,) = call(
        input_kernel,
        [shape(f_in, grid)],
        [entry, w_enc, slope_in, skip, rows, *moving.rows()],
        1_500_000_000,
    )
    return pred.T[None], input_grad.T[None]


def solution(mesh):
    placed = (
        P("phase", "dom", None),
        P("dom", None),
        P(None, "phase"),
        P(None, "phase"),
        P(None, "phase"),
        P(None, None, "phase"),
        P(None, None, "phase"),
        P(None, "phase"),
        P("phase", None),
        P("phase", "dom", None),
        P("dom", None, None),
        P("dom", None),
        P("dom", None),
        P("dom", None, None),
        P("dom", None),
        P("dom", None),
        P("dom", None, None),
        P("dom", None),
        P("dom", None),
    )
    return jax.shard_map(
        per_device,
        mesh=mesh,
        in_specs=placed,
        out_specs=(P("phase", "dom", None), P("phase", "dom", None)),
        check_vma=False,
    )
```

time: 718 us -> 189 us (0.26); the launches traced: 706 us -> 188 us
  other arithmetic: 236 us -> 1.81 us
  local copies, waits for them, and re-layouts: 121 us -> 8.45 us
  starting transfers between devices: 217 us -> 117 us
  blocking collectives: 62 us -> 0 us
  Pallas kernels: 0 us -> 46.5 us
  matrix products: 30.6 us -> 0 us
  between operations: 16.2 us -> 1.66 us
  waiting for transfers between devices: 22.9 us -> 12.4 us
    scatter-add x15 -> x0, other arithmetic: 206 us -> none  [the longest x4 72.7 us: return_rows(): jax.ops.segment_sum(single(edge_grad), sources, num_segments=span)]
    gather x15 -> x0, local copies, waits for them, and re-layouts: 118 us -> none  [the longest x2 26.5 us: per_device(): dec_pre = single(dec_extended[dec_source]) + single(hidden[dec_receiver])]
    ppermute x48 -> x31, starting transfers between devices: 217 us -> 117 us  [the longest x24 96.2 us: permuted(): lax.ppermute(block, 'dom', [(i, route(i) % size) for i in range(size)])]
    all_gather x5 -> x0, blocking collectives: 62 us -> none  [the longest x1 14.7 us: per_device(): lax.all_gather(enc_w, 'phase', axis=1, tiled=True)]
    pallas_call x0 -> x19, Pallas kernels: none -> 46.5 us  [call(): pl.pallas_call(kernel, out_shape=tuple((o for _, o in outs)), in_specs=[p...]
    dot_general x18 -> x0, matrix products: 30.6 us -> none  [the longest x9 17.7 us: backward_product(): lax.dot_general(left, right, (((1,), (1,)), ((), ())), preferred_element_...]
    convert_element_type x13 -> x0, other arithmetic: 21.3 us -> none  [the longest x9 19.3 us: bfloat(): return values.astype(jnp.bfloat16)]
    ppermute x48 -> x31, waiting for transfers between devices: 22.1 us -> 12.4 us  [the longest x24 8.42 us: permuted(): lax.ppermute(block, 'dom', [(i, route(i) % size) for i in range(size)])]
  transfers between devices with their start and end apart: 50 -> 31, of which waited for: 8 -> 4; matrix products, arithmetic and copies ran while one was open for 18% -> 0% of each run, Pallas kernels for 0% -> 16%
where the time goes in v2:
time: 189 us; the launch traced here: 188 us
  starting transfers between devices  117 us (62%)
  Pallas kernels  46.5 us (25%)
  waiting for transfers between devices  12.4 us (7%)
  local copies, waits for them, and re-layouts  8.45 us (4%)
    ppermute x24, starting transfers between devices, permuted(): lax.ppermute(block, 'dom', [(i, route(i) % size) for i in range(size)])  96.2 us
    pallas_call x19, Pallas kernels, call(): pl.pallas_call(kernel, out_shape=tuple((o for _, o in outs)), in_specs=[p...  46.5 us
    ppermute x7, starting transfers between devices, along(): return lax.ppermute(block, 'phase', [(i, (i + away) % 4) for i in range(4)])  20.5 us
    ppermute x24, waiting for transfers between devices, permuted(): lax.ppermute(block, 'dom', [(i, route(i) % size) for i in range(size)])  8.42 us
    ppermute x7, waiting for transfers between devices, along(): return lax.ppermute(block, 'phase', [(i, (i + away) % 4) for i in range(4)])  3.99 us
  transfers between devices with their start and end apart: 31, of which 4 were waited for; matrix products, arithmetic and copies ran while one was open for 0% of the time, Pallas kernels for 16%

profile of v2, /device:TPU:1, one launch (start us, length us, event | category | flops | bytes accessed | tf_op | source)
XLA Modules:
  0.0 187.6 jit_solution(11517614410500574529)
XLA Ops:
  0.7 0.9 slice_bitcast_fusion.13
  1.8 0.7 slice_bitcast_fusion.7
  2.7 0.7 slice_bitcast_fusion.1
  3.6 0.9 slice_bitcast_fusion
  4.5 0.9 bitcast_dynamic-update-slice_fusion.2
  5.5 0.9 bitcast_dynamic-update-slice_fusion.1
  6.5 0.9 bitcast_dynamic-update-slice_fusion
  7.4 0.7 broadcast_select_fusion.4.refs_13_.refs_3_
  8.1 0.9 constant_dynamic-update-slice_fusion
  9.0 0.8 pad_dynamic-update-slice_fusion.refs_11_.refs_0_
  9.9 1.1 fusion.3.refs_1_
  11.0 2.4 %shard_map.230 = (s32[6,128,128]{2,1,0:T(8,128)S(1)}, s32[6,8,128]{2,1,0:T(8,128)S(1)}, s32[24]{0:T(128)S(1)}, bf16[96,512]{1,0:T(8,128)(2,1)S(1)}, bf16[32,512]...) custom-call(s32[1,2048]{1,0:T(1,128)S(1)} %copy-done.7, s32[1,2048]{1,0:T(1,128)S(1)} %copy-done.8, ...), custom_call_target="tpu_custom_call" | custom-call | flops 400000000 | bytes 2127968 | tf_op jit(solution)/shard_map/pallas_call | solution.py:40
  13.4 8.8 %collective-permute-start.3 = (bf16[96,512]{1,0:T(8,128)(2,1)S(1)}, bf16[96,512]{1,0:T(8,128)(2,1)S(1)}, u32[]{:S(2)}, u32[]{:S(2)}) collective-permute-start(bf16[96,512]{1,0:T(8,128)(2,1)S(1)} %get-tuple-element.78), channel_id=1, source_target_pairs={{0,4},{4,0},{8,12},{12,8},{16,20},{20,16},{24,28},{28,24},{32,36},... | collective-permute-start | bytes 294920 | tf_op jit(solution)/shard_map/ppermute | solution.py:444
  22.2 1.9 %collective-permute-start = (bf16[2016,128]{1,0:T(8,128)(2,1)S(1)}, bf16[2016,128]{1,0:T(8,128)(2,1)S(1)}, u32[]{:S(2)}, u32[]{:S(2)}) collective-permute-start(bf16[2016,128]{1,0:T(8,128)(2,1)S(1)} %fusion.3.refs_1_), channel_id=1, source_target_pairs={{0,1},{1,2},{2,3},{3,0},{4,5},{5,6},{6,7},{7,4},{8,9},{9,10},{10,1... | collective-permute-start | bytes 1548296 | tf_op jit(solution)/shard_map/ppermute | solution.py:497
  24.2 4.6 %collective-permute-start.8 = (bf16[2304,128]{1,0:T(8,128)(2,1)S(1)}, bf16[2304,128]{1,0:T(8,128)(2,1)S(1)}, u32[]{:S(2)}, u32[]{:S(2)}) collective-permute-start(bf16[2304,128]{1,0:T(8,128)(2,1)S(1)} %pad_dynamic-update-slice_fusion.refs_11_.refs_0_), channel_id=1, source_target_pairs={{0,3},{1,0},{2,1},{3,2},{4,7},{5,4},{6,5},{7,6},{8,11},{9,8},{10,9... | collective-permute-start | bytes 1769480 | tf_op jit(solution)/shard_map/ppermute | solution.py:497
  28.8 1.9 %collective-permute-start.7 = (bf16[2304,128]{1,0:T(8,128)(2,1)S(1)}, bf16[2304,128]{1,0:T(8,128)(2,1)S(1)}, u32[]{:S(2)}, u32[]{:S(2)}) collective-permute-start(bf16[2304,128]{1,0:T(8,128)(2,1)S(1)} %pad_dynamic-update-slice_fusion.refs_11_.refs_0_), channel_id=1, source_target_pairs={{0,1},{1,2},{2,3},{3,0},{4,5},{5,6},{6,7},{7,4},{8,9},{9,10},{10,1... | collective-permute-start | bytes 1769480 | tf_op jit(solution)/shard_map/ppermute | solution.py:497
  30.7 4.6 %collective-permute-start.2 = (bf16[2016,128]{1,0:T(8,128)(2,1)S(1)}, bf16[2016,128]{1,0:T(8,128)(2,1)S(1)}, u32[]{:S(2)}, u32[]{:S(2)}) collective-permute-start(bf16[2016,128]{1,0:T(8,128)(2,1)S(1)} %fusion.3.refs_1_), channel_id=1, source_target_pairs={{0,3},{1,0},{2,1},{3,2},{4,7},{5,4},{6,5},{7,6},{8,11},{9,8},{10,9... | collective-permute-start | bytes 1548296 | tf_op jit(solution)/shard_map/ppermute | solution.py:497
  35.3 3.4 %collective-permute-done.refs_2_ = bf16[2016,128]{1,0:T(8,128)(2,1)S(1)} collective-permute-done((bf16[2016,128]{1,0:T(8,128)(2,1)S(1)}, bf16[2016,128]{1,0:T(8,128)(2,1)S(1)}, u32[]{:S(2)}, u32[]{:S(2)}) %collective-permute-start) | collective-permute-done | bytes 516128 | tf_op jit(solution)/shard_map/ppermute | solution.py:497
  38.7 1.9 %collective-permute-start.1 = (bf16[2016,128]{1,0:T(8,128)(2,1)S(1)}, bf16[2016,128]{1,0:T(8,128)(2,1)S(1)}, u32[]{:S(2)}, u32[]{:S(2)}) collective-permute-start(bf16[2016,128]{1,0:T(8,128)(2,1)S(1)} %collective-permute-done.refs_2_), channel_id=1, source_target_pairs={{0,1},{1,2},{2,3},{3,0},{4,5},{5,6},{6,7},{7,4},{8,9},{9,10},{10,1... | collective-permute-start | bytes 1548296 | tf_op jit(solution)/shard_map/ppermute | solution.py:497
  40.6 1.9 %collective-permute-start.5 = (bf16[64,512]{1,0:T(8,128)(2,1)S(1)}, bf16[64,512]{1,0:T(8,128)(2,1)S(1)}, u32[]{:S(2)}, u32[]{:S(2)}) collective-permute-start(bf16[64,512]{1,0:T(8,128)(2,1)S(1)} %pad_maximum_fusion), channel_id=1, source_target_pairs={{0,8},{4,12},{8,16},{12,20},{16,24},{20,28},{24,32},{28,36},{32,40... | collective-permute-start | bytes 196616 | tf_op jit(solution)/shard_map/ppermute | solution.py:444
  42.5 8.2 %collective-permute-start.6 = (bf16[64,512]{1,0:T(8,128)(2,1)S(1)}, bf16[64,512]{1,0:T(8,128)(2,1)S(1)}, u32[]{:S(2)}, u32[]{:S(2)}) collective-permute-start(bf16[64,512]{1,0:T(8,128)(2,1)S(1)} %pad_maximum_fusion.1), channel_id=1, source_target_pairs={{0,504},{4,508},{8,0},{12,4},{16,8},{20,12},{24,16},{28,20},{32,24... | collective-permute-start | bytes 196616 | tf_op jit(solution)/shard_map/ppermute | solution.py:444
  50.8 0.6 collective-permute-done.7.refs_6_.refs_1_
  51.3 1.9 %collective-permute-start.4 = (bf16[32,512]{1,0:T(8,128)(2,1)S(1)}, bf16[32,512]{1,0:T(8,128)(2,1)S(1)}, u32[]{:S(2)}, u32[]{:S(2)}) collective-permute-start(bf16[32,512]{1,0:T(8,128)(2,1)S(1)} %get-tuple-element.79), channel_id=1, source_target_pairs={{0,500},{4,16},{8,508},{12,24},{16,4},{20,32},{24,12},{28,40},{32,... | collective-permute-start | bytes 98312 | tf_op jit(solution)/shard_map/ppermute | solution.py:444
  53.3 4.4 %collective-permute-done.4.refs_7_ = bf16[32,512]{1,0:T(8,128)(2,1)S(1)} collective-permute-done((bf16[32,512]{1,0:T(8,128)(2,1)S(1)}, bf16[32,512]{1,0:T(8,128)(2,1)S(1)}, u32[]{:S(2)}, u32[]{:S(2)}) %collective-permute-start.4) | collective-permute-done | bytes 32800 | tf_op jit(solution)/shard_map/ppermute | solution.py:444
  57.7 3.7 %collective-permute-start.10 = (bf16[1152,128]{1,0:T(8,128)(2,1)S(1)}, bf16[1152,128]{1,0:T(8,128)(2,1)S(1)}, u32[]{:S(2)}, u32[]{:S(2)}) collective-permute-start(bf16[1152,128]{1,0:T(8,128)(2,1)S(1)} %slice.165), channel_id=1, source_target_pairs={{0,3},{1,0},{2,1},{3,2},{4,7},{5,4},{6,5},{7,6},{8,11},{9,8},{10,9... | collective-permute-start | bytes 884744 | tf_op jit(solution)/shard_map/ppermute | solution.py:497
  61.5 1.9 %collective-permute-start.9 = (bf16[1152,128]{1,0:T(8,128)(2,1)S(1)}, bf16[1152,128]{1,0:T(8,128)(2,1)S(1)}, u32[]{:S(2)}, u32[]{:S(2)}) collective-permute-start(bf16[1152,128]{1,0:T(8,128)(2,1)S(1)} %slice.164), channel_id=1, source_target_pairs={{0,1},{1,2},{2,3},{3,0},{4,5},{5,6},{6,7},{7,4},{8,9},{9,10},{10,1... | collective-permute-start | bytes 884744 | tf_op jit(solution)/shard_map/ppermute | solution.py:497
  63.4 2.6 %shard_map.231 = (bf16[1152,512]{1,0:T(8,128)(2,1)S(1)}, bf16[1024,512]{1,0:T(8,128)(2,1)S(1)}, bf16[1024,512]{1,0:T(8,128)(2,1)S(1)}, bf16[128,512]{1,0:T(8,128...) custom-call(bf16[474,1024]{1,0:T(8,128)(2,1)S(1)} %bitcast.67, ...), custom_call_target="tpu_custom_call" | custom-call | flops 1500000000 | bytes 8835076 | tf_op jit(solution)/shard_map/pallas_call | solution.py:40
  66.1 5.2 %shard_map.232 = (bf16[2048,512]{1,0:T(8,128)(2,1)S(1)}, bf16[128,512]{1,0:T(8,128)(2,1)S(1)}, f32[256,512]{1,0:T(8,128)S(1)}) custom-call(bf16[1152,512]{1,0:T(8,128)(2,1)S(1)} %get-tuple-element.82.refs_0_, bf16[256,512]{1,0:T(8,128)(2,1)S(1)} %copy-done.2, s32[1,2048]{1,0:T(1,128)S(1)} %copy-done.7, s32[6]{0:T(128)S(1)} %broadcast_select_fusion.4.refs_13_.refs_3_, ...), custom_call_target="tpu_custom_call" | custom-call | flops 5000000000 | bytes 4603928 | tf_op jit(solution)/shard_map/pallas_call | solution.py:40
  71.3 0.8 shard_map.233
  72.1 7.3 %collective-permute-start.11 = (bf16[24,512]{1,0:T(8,128)(2,1)S(1)}, bf16[24,512]{1,0:T(8,128)(2,1)S(1)}, u32[]{:S(2)}, u32[]{:S(2)}) collective-permute-start(bf16[24,512]{1,0:T(8,128)(2,1)S(1)} %get-tuple-element.89), channel_id=1, source_target_pairs={{0,4},{4,0},{8,12},{12,8},{16,20},{20,16},{24,28},{28,24},{32,36},... | collective-permute-start | bytes 73736 | tf_op jit(solution)/shard_map/ppermute | solution.py:444
  79.4 1.9 %collective-permute-start.12 = (bf16[8,512]{1,0:T(8,128)(2,1)S(1)}, bf16[8,512]{1,0:T(8,128)(2,1)S(1)}, u32[]{:S(2)}, u32[]{:S(2)}) collective-permute-start(bf16[8,512]{1,0:T(8,128)(2,1)S(1)} %get-tuple-element.94), channel_id=1, source_target_pairs={{0,500},{4,16},{8,508},{12,24},{16,4},{20,32},{24,12},{28,40},{32,... | collective-permute-start | bytes 24584 | tf_op jit(solution)/shard_map/ppermute | solution.py:444
  81.3 1.9 %collective-permute-start.13 = (bf16[16,512]{1,0:T(8,128)(2,1)S(1)}, bf16[16,512]{1,0:T(8,128)(2,1)S(1)}, u32[]{:S(2)}, u32[]{:S(2)}) collective-permute-start(bf16[16,512]{1,0:T(8,128)(2,1)S(1)} %pad_maximum_fusion.6.refs_4_.refs_6_), channel_id=1, source_target_pairs={{0,8},{4,12},{8,16},{12,20},{16,24},{20,28},{24,32},{28,36},{32,40... | collective-permute-start | bytes 49160 | tf_op jit(solution)/shard_map/ppermute | solution.py:444
  83.3 6.9 %collective-permute-start.14 = (bf16[16,512]{1,0:T(8,128)(2,1)S(1)}, bf16[16,512]{1,0:T(8,128)(2,1)S(1)}, u32[]{:S(2)}, u32[]{:S(2)}) collective-permute-start(bf16[16,512]{1,0:T(8,128)(2,1)S(1)} %pad_maximum_fusion.7.refs_5_.refs_7_), channel_id=1, source_target_pairs={{0,504},{4,508},{8,0},{12,4},{16,8},{20,12},{24,16},{28,20},{32,24... | collective-permute-start | bytes 49160 | tf_op jit(solution)/shard_map/ppermute | solution.py:444
  90.1 2.7 %shard_map.234 = (f32[256,512]{1,0:T(8,128)S(1)}, bf16[2048,512]{1,0:T(8,128)(2,1)S(1)}) custom-call(bf16[256,512]{1,0:T(8,128)(2,1)S(1)} %get-tuple-element.87.refs_0_, bf16[256,512]{1,0:T(8,128)(2,1)S(1)} %get-tuple-element.88.refs_1_, s32[1,2048]{1,0:T(1,128)S(1)} %copy-done.5, s32[1,2048]{1,0:T(1,128)S(1)} %copy-done.6, ...), custom_call_target="tpu_custom_call" | custom-call | flops 3000000000 | bytes 3162112 | tf_op jit(solution)/shard_map/pallas_call | solution.py:40
  92.8 0.6 shard_map.235.refs_4_.refs_2_.refs_10_.refs_5_.refs_6_
  93.5 1.1 shard_map.236
  94.6 6.9 %collective-permute-start.15 = (bf16[24,512]{1,0:T(8,128)(2,1)S(1)}, bf16[24,512]{1,0:T(8,128)(2,1)S(1)}, u32[]{:S(2)}, u32[]{:S(2)}) collective-permute-start(bf16[24,512]{1,0:T(8,128)(2,1)S(1)} %get-tuple-element.97), channel_id=1, source_target_pairs={{0,4},{4,0},{8,12},{12,8},{16,20},{20,16},{24,28},{28,24},{32,36},... | collective-permute-start | bytes 73736 | tf_op jit(solution)/shard_map/ppermute | solution.py:444
  101.5 1.9 %collective-permute-start.16 = (bf16[8,512]{1,0:T(8,128)(2,1)S(1)}, bf16[8,512]{1,0:T(8,128)(2,1)S(1)}, u32[]{:S(2)}, u32[]{:S(2)}) collective-permute-start(bf16[8,512]{1,0:T(8,128)(2,1)S(1)} %get-tuple-element.101), channel_id=1, source_target_pairs={{0,500},{4,16},{8,508},{12,24},{16,4},{20,32},{24,12},{28,40},{32,... | collective-permute-start | bytes 24584 | tf_op jit(solution)/shard_map/ppermute | solution.py:444
  103.5 1.9 %collective-permute-start.17 = (bf16[16,512]{1,0:T(8,128)(2,1)S(1)}, bf16[16,512]{1,0:T(8,128)(2,1)S(1)}, u32[]{:S(2)}, u32[]{:S(2)}) collective-permute-start(bf16[16,512]{1,0:T(8,128)(2,1)S(1)} %pad_maximum_fusion.8.refs_4_.refs_3_), channel_id=1, source_target_pairs={{0,8},{4,12},{8,16},{12,20},{16,24},{20,28},{24,32},{28,36},{32,40... | collective-permute-start | bytes 49160 | tf_op jit(solution)/shard_map/ppermute | solution.py:444
  105.4 6.7 %collective-permute-start.18 = (bf16[16,512]{1,0:T(8,128)(2,1)S(1)}, bf16[16,512]{1,0:T(8,128)(2,1)S(1)}, u32[]{:S(2)}, u32[]{:S(2)}) collective-permute-start(bf16[16,512]{1,0:T(8,128)(2,1)S(1)} %pad_maximum_fusion.9.refs_5_.refs_4_), channel_id=1, source_target_pairs={{0,504},{4,508},{8,0},{12,4},{16,8},{20,12},{24,16},{28,20},{32,24... | collective-permute-start | bytes 49160 | tf_op jit(solution)/shard_map/ppermute | solution.py:444
  112.1 2.7 %shard_map.237 = (f32[256,512]{1,0:T(8,128)S(1)}, bf16[2048,512]{1,0:T(8,128)(2,1)S(1)}) custom-call(bf16[256,512]{1,0:T(8,128)(2,1)S(1)} %get-tuple-element.95.refs_0_, bf16[256,512]{1,0:T(8,128)(2,1)S(1)} %get-tuple-element.96.refs_1_, s32[1,2048]{1,0:T(1,128)S(1)} %copy-done.5, s32[1,2048]{1,0:T(1,128)S(1)} %copy-done.6, ...), custom_call_target="tpu_custom_call" | custom-call | flops 3000000000 | bytes 3162112 | tf_op jit(solution)/shard_map/pallas_call | solution.py:40
  115.3 1.5 shard_map.238
  116.8 7.3 %shard_map.240 = (bf16[3072,512]{1,0:T(8,128)(2,1)S(1)}, bf16[3072,512]{1,0:T(8,128)(2,1)S(1)}, f32[256,512]{1,0:T(8,128)S(1)}, bf16[256,512]{1,0:T(8,128)(2,1)S...) custom-call(bf16[256,512]{1,0:T(8,128)(2,1)S(1)} %get-tuple-element., ...), custom_call_target="tpu_custom_call" | custom-call | flops 6000000000 | bytes 13254752 | tf_op jit(solution)/shard_map/pallas_call | solution.py:40
  124.1 2.7 %collective-permute-start.19 = (bf16[48,512]{1,0:T(8,128)(2,1)S(1)}, bf16[48,512]{1,0:T(8,128)(2,1)S(1)}, u32[]{:S(2)}, u32[]{:S(2)}) collective-permute-start(bf16[48,512]{1,0:T(8,128)(2,1)S(1)} %get-tuple-element.113.refs_5_), channel_id=1, source_target_pairs={{0,4},{4,0},{8,12},{12,8},{16,20},{20,16},{24,28},{28,24},{32,36},... | collective-permute-start | bytes 147464 | tf_op jit(solution)/shard_map/ppermute | solution.py:444
  126.8 2.5 %collective-permute-start.20 = (bf16[16,512]{1,0:T(8,128)(2,1)S(1)}, bf16[16,512]{1,0:T(8,128)(2,1)S(1)}, u32[]{:S(2)}, u32[]{:S(2)}) collective-permute-start(bf16[16,512]{1,0:T(8,128)(2,1)S(1)} %get-tuple-element.114.refs_6_), channel_id=1, source_target_pairs={{0,500},{4,16},{8,508},{12,24},{16,4},{20,32},{24,12},{28,40},{32,... | collective-permute-start | bytes 49160 | tf_op jit(solution)/shard_map/ppermute | solution.py:444
  129.3 2.6 %collective-permute-start.21 = (bf16[32,512]{1,0:T(8,128)(2,1)S(1)}, bf16[32,512]{1,0:T(8,128)(2,1)S(1)}, u32[]{:S(2)}, u32[]{:S(2)}) collective-permute-start(bf16[32,512]{1,0:T(8,128)(2,1)S(1)} %pad_maximum_fusion.2.refs_9_), channel_id=1, source_target_pairs={{0,8},{4,12},{8,16},{12,20},{16,24},{20,28},{24,32},{28,36},{32,40... | collective-permute-start | bytes 98312 | tf_op jit(solution)/shard_map/ppermute | solution.py:444
  131.9 6.5 %collective-permute-start.22 = (bf16[32,512]{1,0:T(8,128)(2,1)S(1)}, bf16[32,512]{1,0:T(8,128)(2,1)S(1)}, u32[]{:S(2)}, u32[]{:S(2)}) collective-permute-start(bf16[32,512]{1,0:T(8,128)(2,1)S(1)} %pad_maximum_fusion.3.refs_10_), channel_id=1, source_target_pairs={{0,504},{4,508},{8,0},{12,4},{16,8},{20,12},{24,16},{28,20},{32,24... | collective-permute-start | bytes 98312 | tf_op jit(solution)/shard_map/ppermute | solution.py:444
  138.5 1.9 %shard_map.241 = (bf16[256,512]{1,0:T(8,128)(2,1)S(1)}, f32[256,512]{1,0:T(8,128)S(1)}) custom-call(bf16[256,512]{1,0:T(8,128)(2,1)S(1)} %get-tuple-element.117.refs_0_, bf16[2048,512]{1,0:T(8,128)(2,1)S(1)} %get-tuple-element.118.refs_1_, s32[1,2048]{1,0:T(1,128)S(1)} %copy-done.5, s32[1,2048]{1,0:T(1,128)S(1)} %copy-done.6, ...), custom_call_target="tpu_custom_call" | custom-call | flops 3000000000 | bytes 3284992 | tf_op jit(solution)/shard_map/pallas_call | solution.py:40
  140.4 0.9 shard_map.242
  141.3 3.4 %collective-permute-start.23 = (bf16[24,512]{1,0:T(8,128)(2,1)S(1)}, bf16[24,512]{1,0:T(8,128)(2,1)S(1)}, u32[]{:S(2)}, u32[]{:S(2)}) collective-permute-start(bf16[24,512]{1,0:T(8,128)(2,1)S(1)} %get-tuple-element.124.refs_5_), channel_id=1, source_target_pairs={{0,4},{4,0},{8,12},{12,8},{16,20},{20,16},{24,28},{28,24},{32,36},... | collective-permute-start | bytes 73736 | tf_op jit(solution)/shard_map/ppermute | solution.py:444
  144.8 1.9 %collective-permute-start.24 = (bf16[8,512]{1,0:T(8,128)(2,1)S(1)}, bf16[8,512]{1,0:T(8,128)(2,1)S(1)}, u32[]{:S(2)}, u32[]{:S(2)}) collective-permute-start(bf16[8,512]{1,0:T(8,128)(2,1)S(1)} %get-tuple-element.130.refs_6_), channel_id=1, source_target_pairs={{0,500},{4,16},{8,508},{12,24},{16,4},{20,32},{24,12},{28,40},{32,... | collective-permute-start | bytes 24584 | tf_op jit(solution)/shard_map/ppermute | solution.py:444
  146.8 6.7 %collective-permute-start.25 = (bf16[16,512]{1,0:T(8,128)(2,1)S(1)}, bf16[16,512]{1,0:T(8,128)(2,1)S(1)}, u32[]{:S(2)}, u32[]{:S(2)}) collective-permute-start(bf16[16,512]{1,0:T(8,128)(2,1)S(1)} %pad_maximum_fusion.10.refs_12_.refs_9_), channel_id=1, source_target_pairs={{0,504},{4,508},{8,0},{12,4},{16,8},{20,12},{24,16},{28,20},{32,24... | collective-permute-start | bytes 49160 | tf_op jit(solution)/shard_map/ppermute | solution.py:444
  153.4 1.9 %collective-permute-start.26 = (bf16[16,512]{1,0:T(8,128)(2,1)S(1)}, bf16[16,512]{1,0:T(8,128)(2,1)S(1)}, u32[]{:S(2)}, u32[]{:S(2)}) collective-permute-start(bf16[16,512]{1,0:T(8,128)(2,1)S(1)} %pad_maximum_fusion.11.refs_13_.refs_10_), channel_id=1, source_target_pairs={{0,8},{4,12},{8,16},{12,20},{16,24},{20,28},{24,32},{28,36},{32,40... | collective-permute-start | bytes 49160 | tf_op jit(solution)/shard_map/ppermute | solution.py:444
  155.4 1.9 %shard_map.244 = (bf16[256,512]{1,0:T(8,128)(2,1)S(1)}, f32[256,512]{1,0:T(8,128)S(1)}) custom-call(bf16[256,512]{1,0:T(8,128)(2,1)S(1)} %get-tuple-element.128.refs_0_, bf16[2048,512]{1,0:T(8,128)(2,1)S(1)} %get-tuple-element.129.refs_1_, s32[1,2048]{1,0:T(1,128)S(1)} %copy-done.5, s32[1,2048]{1,0:T(1,128)S(1)} %copy-done.6, ...), custom_call_target="tpu_custom_call" | custom-call | flops 3000000000 | bytes 3235840 | tf_op jit(solution)/shard_map/pallas_call | solution.py:40
  157.3 3.9 %collective-permute-done.26.refs_12_ = bf16[16,512]{1,0:T(8,128)(2,1)S(1)} collective-permute-done((bf16[16,512]{1,0:T(8,128)(2,1)S(1)}, bf16[16,512]{1,0:T(8,128)(2,1)S(1)}, u32[]{:S(2)}, u32[]{:S(2)}) %collective-permute-start.26) | collective-permute-done | bytes 16416 | tf_op jit(solution)/shard_map/ppermute | solution.py:444
  161.2 0.9 shard_map.245
  162.2 3.4 %collective-permute-start.27 = (bf16[48,512]{1,0:T(8,128)(2,1)S(1)}, bf16[48,512]{1,0:T(8,128)(2,1)S(1)}, u32[]{:S(2)}, u32[]{:S(2)}) collective-permute-start(bf16[48,512]{1,0:T(8,128)(2,1)S(1)} %get-tuple-element.136), channel_id=1, source_target_pairs={{0,4},{4,0},{8,12},{12,8},{16,20},{20,16},{24,28},{28,24},{32,36},... | collective-permute-start | bytes 147464 | tf_op jit(solution)/shard_map/ppermute | solution.py:444
  165.5 3.3 %shard_map.243 = (bf16[1024,512]{1,0:T(8,128)(2,1)S(1)}, bf16[128,512]{1,0:T(8,128)(2,1)S(1)}) custom-call(bf16[3072,512]{1,0:T(8,128)(2,1)S(1)} %get-tuple-element.112.refs_0_, bf16[1024,512]{1,0:T(8,128)(2,1)S(1)} %get-tuple-element.103.refs_1_, bf16[1024,512]{1,0:T(8,128)(2,1)S(1)} %get-tuple-element.105.refs_2_, ...), custom_call_target="tpu_custom_call" | custom-call | flops 2500000000 | bytes 6996064 | tf_op jit(solution)/shard_map/pallas_call | solution.py:40
  168.8 1.9 %collective-permute-start.28 = (bf16[16,512]{1,0:T(8,128)(2,1)S(1)}, bf16[16,512]{1,0:T(8,128)(2,1)S(1)}, u32[]{:S(2)}, u32[]{:S(2)}) collective-permute-start(bf16[16,512]{1,0:T(8,128)(2,1)S(1)} %get-tuple-element.143), channel_id=1, source_target_pairs={{0,500},{4,16},{8,508},{12,24},{16,4},{20,32},{24,12},{28,40},{32,... | collective-permute-start | bytes 49160 | tf_op jit(solution)/shard_map/ppermute | solution.py:444
  170.8 4.5 %collective-permute-start.29 = (bf16[32,512]{1,0:T(8,128)(2,1)S(1)}, bf16[32,512]{1,0:T(8,128)(2,1)S(1)}, u32[]{:S(2)}, u32[]{:S(2)}) collective-permute-start(bf16[32,512]{1,0:T(8,128)(2,1)S(1)} %pad_maximum_fusion.4.refs_7_.refs_4_), channel_id=1, source_target_pairs={{0,504},{4,508},{8,0},{12,4},{16,8},{20,12},{24,16},{28,20},{32,24... | collective-permute-start | bytes 98312 | tf_op jit(solution)/shard_map/ppermute | solution.py:444
  175.3 1.9 %collective-permute-start.30 = (bf16[32,512]{1,0:T(8,128)(2,1)S(1)}, bf16[32,512]{1,0:T(8,128)(2,1)S(1)}, u32[]{:S(2)}, u32[]{:S(2)}) collective-permute-start(bf16[32,512]{1,0:T(8,128)(2,1)S(1)} %pad_maximum_fusion.5.refs_8_.refs_5_), channel_id=1, source_target_pairs={{0,8},{4,12},{8,16},{12,20},{16,24},{20,28},{24,32},{28,36},{32,40... | collective-permute-start | bytes 98312 | tf_op jit(solution)/shard_map/ppermute | solution.py:444
  177.3 3.6 %shard_map.247.refs_0_ = bf16[1024,512]{1,0:T(8,128)(2,1)S(1)} custom-call(bf16[256,512]{1,0:T(8,128)(2,1)S(1)} %get-tuple-element.139.refs_0_, bf16[2048,512]{1,0:T(8,128)(2,1)S(1)} %get-tuple-element.140.refs_1_, s32[1,2048]{1,0:T(1,128)S(1)} %copy-done.7, s32[1,2048]{1,0:T(1,128)S(1)} %copy-done.8, bf16[32,512]{1,0:T(8,128)(2,1)S(1)} %pad_maximum_fusion.4.refs_7_.refs_4_, ...), custom_call_target="tpu_custom_call" | custom-call | flops 4000000000 | bytes 3424256 | tf_op jit(solution)/shard_map/pallas_call | solution.py:40
  180.9 4.0 %shard_map.246 = bf16[227,1024]{1,0:T(8,128)(2,1)} custom-call(bf16[3072,512]{1,0:T(8,128)(2,1)S(1)} %get-tuple-element.111.refs_0_, bf16[128,512]{1,0:T(8,128)(2,1)S(1)} %get-tuple-element.127.refs_1_, s32[24]{0:T(128)S(1)} %get-tuple-element.108.refs_5_.refs_3_.refs_2_, s32[1,3072]{1,0:T(1,128)S(1)} %copy-done.4, s32[1,3072]{1,0:T(1,128)S(1)} %copy-done.3, ...), custom_call_target="tpu_custom_call" | custom-call | flops 2500000000 | bytes 6150240 | tf_op jit(solution)/shard_map/pallas_call | solution.py:40
  184.9 2.7 %shard_map.248 = bf16[474,1024]{1,0:T(8,128)(2,1)} custom-call(bf16[1024,512]{1,0:T(8,128)(2,1)S(1)} %shard_map.247.refs_0_, bf16[2016,512]{1,0:T(8,128)(2,1)S(1)} %get-tuple-element.86.refs_3_.refs_5_.refs_6_.refs_1_, bf16[1024,512]{1,0:T(8,128)(2,1)S(1)} %get-tuple-element.141.refs_2_, bf16[1024,512]{1,0:T(8,128)(2,1)S(1)} %get-tuple-element.142.refs_3_, ...), custom_call_target="tpu_custom_call" | custom-call | flops 1500000000 | bytes 6336512 | tf_op jit(solution)/shard_map/pallas_call | solution.py:40
  (89 shorter events, 1.3 us)
Async XLA Ops:
  0.6 10.3 %copy-start.9 = (s32[8,128]{1,0:T(8,128)S(1)}, s32[8,128]{1,0:T(8,128)}, u32[]{:S(2)}) copy-start(s32[8,128]{1,0:T(8,128)} %constant.36.clone) | copy-start | bytes 12292
  0.6 10.3 %copy-start.10 = (s32[8,128]{1,0:T(8,128)S(1)}, s32[8,128]{1,0:T(8,128)}, u32[]{:S(2)}) copy-start(s32[8,128]{1,0:T(8,128)} %constant.35.clone) | copy-start | bytes 12292
  0.7 10.3 %copy-start.6 = (s32[1,2048]{1,0:T(1,128)S(1)}, s32[1,2048]{1,0:T(1,128)}, u32[]{:S(2)}) copy-start(s32[1,2048]{1,0:T(1,128)} %refs_3_.11) | copy-start | bytes 24580
  0.7 10.3 %copy-start.5 = (s32[1,2048]{1,0:T(1,128)S(1)}, s32[1,2048]{1,0:T(1,128)}, u32[]{:S(2)}) copy-start(s32[1,2048]{1,0:T(1,128)} %refs_2_.12) | copy-start | bytes 24580
  0.7 10.3 %copy-start.3 = (s32[1,3072]{1,0:T(1,128)S(1)}, s32[1,3072]{1,0:T(1,128)}, u32[]{:S(2)}) copy-start(s32[1,3072]{1,0:T(1,128)} %refs_4_.7) | copy-start | bytes 36868
  0.7 10.3 %copy-start.4 = (s32[1,3072]{1,0:T(1,128)S(1)}, s32[1,3072]{1,0:T(1,128)}, u32[]{:S(2)}) copy-start(s32[1,3072]{1,0:T(1,128)} %refs_3_.12) | copy-start | bytes 36868
  0.7 10.3 %copy-start.8 = (s32[1,2048]{1,0:T(1,128)S(1)}, s32[1,2048]{1,0:T(1,128)}, u32[]{:S(2)}) copy-start(s32[1,2048]{1,0:T(1,128)} %refs_3_.13) | copy-start | bytes 24580
  0.7 10.3 %copy-start.7 = (s32[1,2048]{1,0:T(1,128)S(1)}, s32[1,2048]{1,0:T(1,128)}, u32[]{:S(2)}) copy-start(s32[1,2048]{1,0:T(1,128)} %refs_2_.13) | copy-start | bytes 24580
  0.7 10.3 %copy-start = (bf16[1,1024,227]{1,2,0:T(8,128)(2,1)S(1)}, bf16[1,1024,227]{1,2,0:T(8,128)(2,1)}, u32[]{:S(2)}) copy-start(bf16[1,1024,227]{1,2,0:T(8,128)(2,1)} %param.32) | copy-start | bytes 1394692
  0.7 10.3 %copy-start.1 = (bf16[1,1024,474]{1,2,0:T(8,128)(2,1)S(1)}, bf16[1,1024,474]{1,2,0:T(8,128)(2,1)}, u32[]{:S(2)}) copy-start(bf16[1,1024,474]{1,2,0:T(8,128)(2,1)} %param.23) | copy-start | bytes 2912260
  13.4 10.7 %collective-permute-start.3 = (bf16[96,512]{1,0:T(8,128)(2,1)S(1)}, bf16[96,512]{1,0:T(8,128)(2,1)S(1)}, u32[]{:S(2)}, u32[]{:S(2)}) collective-permute-start(bf16[96,512]{1,0:T(8,128)(2,1)S(1)} %get-tuple-element.78), channel_id=1, source_target_pairs={{0,4},{4,0},{8,12},{12,8},{16,20},{20,16},{24,28},{28,24},{32,36},... | collective-permute-start | bytes 294920 | tf_op jit(solution)/shard_map/ppermute | solution.py:444
  22.2 16.5 %collective-permute-start = (bf16[2016,128]{1,0:T(8,128)(2,1)S(1)}, bf16[2016,128]{1,0:T(8,128)(2,1)S(1)}, u32[]{:S(2)}, u32[]{:S(2)}) collective-permute-start(bf16[2016,128]{1,0:T(8,128)(2,1)S(1)} %fusion.3.refs_1_), channel_id=1, source_target_pairs={{0,1},{1,2},{2,3},{3,0},{4,5},{5,6},{6,7},{7,4},{8,9},{9,10},{10,1... | collective-permute-start | bytes 1548296 | tf_op jit(solution)/shard_map/ppermute | solution.py:497
  24.2 18.3 %collective-permute-start.8 = (bf16[2304,128]{1,0:T(8,128)(2,1)S(1)}, bf16[2304,128]{1,0:T(8,128)(2,1)S(1)}, u32[]{:S(2)}, u32[]{:S(2)}) collective-permute-start(bf16[2304,128]{1,0:T(8,128)(2,1)S(1)} %pad_dynamic-update-slice_fusion.refs_11_.refs_0_), channel_id=1, source_target_pairs={{0,3},{1,0},{2,1},{3,2},{4,7},{5,4},{6,5},{7,6},{8,11},{9,8},{10,9... | collective-permute-start | bytes 1769480 | tf_op jit(solution)/shard_map/ppermute | solution.py:497
  28.8 22.5 %collective-permute-start.7 = (bf16[2304,128]{1,0:T(8,128)(2,1)S(1)}, bf16[2304,128]{1,0:T(8,128)(2,1)S(1)}, u32[]{:S(2)}, u32[]{:S(2)}) collective-permute-start(bf16[2304,128]{1,0:T(8,128)(2,1)S(1)} %pad_dynamic-update-slice_fusion.refs_11_.refs_0_), channel_id=1, source_target_pairs={{0,1},{1,2},{2,3},{3,0},{4,5},{5,6},{6,7},{7,4},{8,9},{9,10},{10,1... | collective-permute-start | bytes 1769480 | tf_op jit(solution)/shard_map/ppermute | solution.py:497
  30.7 32.7 %collective-permute-start.2 = (bf16[2016,128]{1,0:T(8,128)(2,1)S(1)}, bf16[2016,128]{1,0:T(8,128)(2,1)S(1)}, u32[]{:S(2)}, u32[]{:S(2)}) collective-permute-start(bf16[2016,128]{1,0:T(8,128)(2,1)S(1)} %fusion.3.refs_1_), channel_id=1, source_target_pairs={{0,3},{1,0},{2,1},{3,2},{4,7},{5,4},{6,5},{7,6},{8,11},{9,8},{10,9... | collective-permute-start | bytes 1548296 | tf_op jit(solution)/shard_map/ppermute | solution.py:497
  38.7 24.7 %collective-permute-start.1 = (bf16[2016,128]{1,0:T(8,128)(2,1)S(1)}, bf16[2016,128]{1,0:T(8,128)(2,1)S(1)}, u32[]{:S(2)}, u32[]{:S(2)}) collective-permute-start(bf16[2016,128]{1,0:T(8,128)(2,1)S(1)} %collective-permute-done.refs_2_), channel_id=1, source_target_pairs={{0,1},{1,2},{2,3},{3,0},{4,5},{5,6},{6,7},{7,4},{8,9},{9,10},{10,1... | collective-permute-start | bytes 1548296 | tf_op jit(solution)/shard_map/ppermute | solution.py:497
  40.6 20.9 %collective-permute-start.5 = (bf16[64,512]{1,0:T(8,128)(2,1)S(1)}, bf16[64,512]{1,0:T(8,128)(2,1)S(1)}, u32[]{:S(2)}, u32[]{:S(2)}) collective-permute-start(bf16[64,512]{1,0:T(8,128)(2,1)S(1)} %pad_maximum_fusion), channel_id=1, source_target_pairs={{0,8},{4,12},{8,16},{12,20},{16,24},{20,28},{24,32},{28,36},{32,40... | collective-permute-start | bytes 196616 | tf_op jit(solution)/shard_map/ppermute | solution.py:444
  42.5 20.9 %collective-permute-start.6 = (bf16[64,512]{1,0:T(8,128)(2,1)S(1)}, bf16[64,512]{1,0:T(8,128)(2,1)S(1)}, u32[]{:S(2)}, u32[]{:S(2)}) collective-permute-start(bf16[64,512]{1,0:T(8,128)(2,1)S(1)} %pad_maximum_fusion.1), channel_id=1, source_target_pairs={{0,504},{4,508},{8,0},{12,4},{16,8},{20,12},{24,16},{28,20},{32,24... | collective-permute-start | bytes 196616 | tf_op jit(solution)/shard_map/ppermute | solution.py:444
  51.3 6.4 %collective-permute-start.4 = (bf16[32,512]{1,0:T(8,128)(2,1)S(1)}, bf16[32,512]{1,0:T(8,128)(2,1)S(1)}, u32[]{:S(2)}, u32[]{:S(2)}) collective-permute-start(bf16[32,512]{1,0:T(8,128)(2,1)S(1)} %get-tuple-element.79), channel_id=1, source_target_pairs={{0,500},{4,16},{8,508},{12,24},{16,4},{20,32},{24,12},{28,40},{32,... | collective-permute-start | bytes 98312 | tf_op jit(solution)/shard_map/ppermute | solution.py:444
  53.3 12.8 %copy-start.2 = (bf16[256,512]{1,0:T(8,128)(2,1)S(1)}, bf16[256,512]{1,0:T(8,128)(2,1)}, u32[]{:S(2)}) copy-start(bf16[256,512]{1,0:T(8,128)(2,1)} %refs_1_.5) | copy-start | bytes 786436
  57.7 13.6 %collective-permute-start.10 = (bf16[1152,128]{1,0:T(8,128)(2,1)S(1)}, bf16[1152,128]{1,0:T(8,128)(2,1)S(1)}, u32[]{:S(2)}, u32[]{:S(2)}) collective-permute-start(bf16[1152,128]{1,0:T(8,128)(2,1)S(1)} %slice.165), channel_id=1, source_target_pairs={{0,3},{1,0},{2,1},{3,2},{4,7},{5,4},{6,5},{7,6},{8,11},{9,8},{10,9... | collective-permute-start | bytes 884744 | tf_op jit(solution)/shard_map/ppermute | solution.py:497
  61.5 9.8 %collective-permute-start.9 = (bf16[1152,128]{1,0:T(8,128)(2,1)S(1)}, bf16[1152,128]{1,0:T(8,128)(2,1)S(1)}, u32[]{:S(2)}, u32[]{:S(2)}) collective-permute-start(bf16[1152,128]{1,0:T(8,128)(2,1)S(1)} %slice.164), channel_id=1, source_target_pairs={{0,1},{1,2},{2,3},{3,0},{4,5},{5,6},{6,7},{7,4},{8,9},{9,10},{10,1... | collective-permute-start | bytes 884744 | tf_op jit(solution)/shard_map/ppermute | solution.py:497
  72.1 9.2 %collective-permute-start.11 = (bf16[24,512]{1,0:T(8,128)(2,1)S(1)}, bf16[24,512]{1,0:T(8,128)(2,1)S(1)}, u32[]{:S(2)}, u32[]{:S(2)}) collective-permute-start(bf16[24,512]{1,0:T(8,128)(2,1)S(1)} %get-tuple-element.89), channel_id=1, source_target_pairs={{0,4},{4,0},{8,12},{12,8},{16,20},{20,16},{24,28},{28,24},{32,36},... | collective-permute-start | bytes 73736 | tf_op jit(solution)/shard_map/ppermute | solution.py:444
  79.4 14.1 %collective-permute-start.12 = (bf16[8,512]{1,0:T(8,128)(2,1)S(1)}, bf16[8,512]{1,0:T(8,128)(2,1)S(1)}, u32[]{:S(2)}, u32[]{:S(2)}) collective-permute-start(bf16[8,512]{1,0:T(8,128)(2,1)S(1)} %get-tuple-element.94), channel_id=1, source_target_pairs={{0,500},{4,16},{8,508},{12,24},{16,4},{20,32},{24,12},{28,40},{32,... | collective-permute-start | bytes 24584 | tf_op jit(solution)/shard_map/ppermute | solution.py:444
  81.3 12.1 %collective-permute-start.13 = (bf16[16,512]{1,0:T(8,128)(2,1)S(1)}, bf16[16,512]{1,0:T(8,128)(2,1)S(1)}, u32[]{:S(2)}, u32[]{:S(2)}) collective-permute-start(bf16[16,512]{1,0:T(8,128)(2,1)S(1)} %pad_maximum_fusion.6.refs_4_.refs_6_), channel_id=1, source_target_pairs={{0,8},{4,12},{8,16},{12,20},{16,24},{20,28},{24,32},{28,36},{32,40... | collective-permute-start | bytes 49160 | tf_op jit(solution)/shard_map/ppermute | solution.py:444
  83.3 10.2 %collective-permute-start.14 = (bf16[16,512]{1,0:T(8,128)(2,1)S(1)}, bf16[16,512]{1,0:T(8,128)(2,1)S(1)}, u32[]{:S(2)}, u32[]{:S(2)}) collective-permute-start(bf16[16,512]{1,0:T(8,128)(2,1)S(1)} %pad_maximum_fusion.7.refs_5_.refs_7_), channel_id=1, source_target_pairs={{0,504},{4,508},{8,0},{12,4},{16,8},{20,12},{24,16},{28,20},{32,24... | collective-permute-start | bytes 49160 | tf_op jit(solution)/shard_map/ppermute | solution.py:444
  94.6 8.8 %collective-permute-start.15 = (bf16[24,512]{1,0:T(8,128)(2,1)S(1)}, bf16[24,512]{1,0:T(8,128)(2,1)S(1)}, u32[]{:S(2)}, u32[]{:S(2)}) collective-permute-start(bf16[24,512]{1,0:T(8,128)(2,1)S(1)} %get-tuple-element.97), channel_id=1, source_target_pairs={{0,4},{4,0},{8,12},{12,8},{16,20},{20,16},{24,28},{28,24},{32,36},... | collective-permute-start | bytes 73736 | tf_op jit(solution)/shard_map/ppermute | solution.py:444
  101.5 13.8 %collective-permute-start.16 = (bf16[8,512]{1,0:T(8,128)(2,1)S(1)}, bf16[8,512]{1,0:T(8,128)(2,1)S(1)}, u32[]{:S(2)}, u32[]{:S(2)}) collective-permute-start(bf16[8,512]{1,0:T(8,128)(2,1)S(1)} %get-tuple-element.101), channel_id=1, source_target_pairs={{0,500},{4,16},{8,508},{12,24},{16,4},{20,32},{24,12},{28,40},{32,... | collective-permute-start | bytes 24584 | tf_op jit(solution)/shard_map/ppermute | solution.py:444
  103.5 11.8 %collective-permute-start.17 = (bf16[16,512]{1,0:T(8,128)(2,1)S(1)}, bf16[16,512]{1,0:T(8,128)(2,1)S(1)}, u32[]{:S(2)}, u32[]{:S(2)}) collective-permute-start(bf16[16,512]{1,0:T(8,128)(2,1)S(1)} %pad_maximum_fusion.8.refs_4_.refs_3_), channel_id=1, source_target_pairs={{0,8},{4,12},{8,16},{12,20},{16,24},{20,28},{24,32},{28,36},{32,40... | collective-permute-start | bytes 49160 | tf_op jit(solution)/shard_map/ppermute | solution.py:444
  105.4 9.9 %collective-permute-start.18 = (bf16[16,512]{1,0:T(8,128)(2,1)S(1)}, bf16[16,512]{1,0:T(8,128)(2,1)S(1)}, u32[]{:S(2)}, u32[]{:S(2)}) collective-permute-start(bf16[16,512]{1,0:T(8,128)(2,1)S(1)} %pad_maximum_fusion.9.refs_5_.refs_4_), channel_id=1, source_target_pairs={{0,504},{4,508},{8,0},{12,4},{16,8},{20,12},{24,16},{28,20},{32,24... | collective-permute-start | bytes 49160 | tf_op jit(solution)/shard_map/ppermute | solution.py:444
  124.1 5.2 %collective-permute-start.19 = (bf16[48,512]{1,0:T(8,128)(2,1)S(1)}, bf16[48,512]{1,0:T(8,128)(2,1)S(1)}, u32[]{:S(2)}, u32[]{:S(2)}) collective-permute-start(bf16[48,512]{1,0:T(8,128)(2,1)S(1)} %get-tuple-element.113.refs_5_), channel_id=1, source_target_pairs={{0,4},{4,0},{8,12},{12,8},{16,20},{20,16},{24,28},{28,24},{32,36},... | collective-permute-start | bytes 147464 | tf_op jit(solution)/shard_map/ppermute | solution.py:444
  126.8 13.6 %collective-permute-start.20 = (bf16[16,512]{1,0:T(8,128)(2,1)S(1)}, bf16[16,512]{1,0:T(8,128)(2,1)S(1)}, u32[]{:S(2)}, u32[]{:S(2)}) collective-permute-start(bf16[16,512]{1,0:T(8,128)(2,1)S(1)} %get-tuple-element.114.refs_6_), channel_id=1, source_target_pairs={{0,500},{4,16},{8,508},{12,24},{16,4},{20,32},{24,12},{28,40},{32,... | collective-permute-start | bytes 49160 | tf_op jit(solution)/shard_map/ppermute | solution.py:444
  129.3 11.1 %collective-permute-start.21 = (bf16[32,512]{1,0:T(8,128)(2,1)S(1)}, bf16[32,512]{1,0:T(8,128)(2,1)S(1)}, u32[]{:S(2)}, u32[]{:S(2)}) collective-permute-start(bf16[32,512]{1,0:T(8,128)(2,1)S(1)} %pad_maximum_fusion.2.refs_9_), channel_id=1, source_target_pairs={{0,8},{4,12},{8,16},{12,20},{16,24},{20,28},{24,32},{28,36},{32,40... | collective-permute-start | bytes 98312 | tf_op jit(solution)/shard_map/ppermute | solution.py:444
  131.9 8.5 %collective-permute-start.22 = (bf16[32,512]{1,0:T(8,128)(2,1)S(1)}, bf16[32,512]{1,0:T(8,128)(2,1)S(1)}, u32[]{:S(2)}, u32[]{:S(2)}) collective-permute-start(bf16[32,512]{1,0:T(8,128)(2,1)S(1)} %pad_maximum_fusion.3.refs_10_), channel_id=1, source_target_pairs={{0,504},{4,508},{8,0},{12,4},{16,8},{20,12},{24,16},{28,20},{32,24... | collective-permute-start | bytes 98312 | tf_op jit(solution)/shard_map/ppermute | solution.py:444
  141.3 5.4 %collective-permute-start.23 = (bf16[24,512]{1,0:T(8,128)(2,1)S(1)}, bf16[24,512]{1,0:T(8,128)(2,1)S(1)}, u32[]{:S(2)}, u32[]{:S(2)}) collective-permute-start(bf16[24,512]{1,0:T(8,128)(2,1)S(1)} %get-tuple-element.124.refs_5_), channel_id=1, source_target_pairs={{0,4},{4,0},{8,12},{12,8},{16,20},{20,16},{24,28},{28,24},{32,36},... | collective-permute-start | bytes 73736 | tf_op jit(solution)/shard_map/ppermute | solution.py:444
  144.8 12.5 %collective-permute-start.24 = (bf16[8,512]{1,0:T(8,128)(2,1)S(1)}, bf16[8,512]{1,0:T(8,128)(2,1)S(1)}, u32[]{:S(2)}, u32[]{:S(2)}) collective-permute-start(bf16[8,512]{1,0:T(8,128)(2,1)S(1)} %get-tuple-element.130.refs_6_), channel_id=1, source_target_pairs={{0,500},{4,16},{8,508},{12,24},{16,4},{20,32},{24,12},{28,40},{32,... | collective-permute-start | bytes 24584 | tf_op jit(solution)/shard_map/ppermute | solution.py:444
  146.8 10.5 %collective-permute-start.25 = (bf16[16,512]{1,0:T(8,128)(2,1)S(1)}, bf16[16,512]{1,0:T(8,128)(2,1)S(1)}, u32[]{:S(2)}, u32[]{:S(2)}) collective-permute-start(bf16[16,512]{1,0:T(8,128)(2,1)S(1)} %pad_maximum_fusion.10.refs_12_.refs_9_), channel_id=1, source_target_pairs={{0,504},{4,508},{8,0},{12,4},{16,8},{20,12},{24,16},{28,20},{32,24... | collective-permute-start | bytes 49160 | tf_op jit(solution)/shard_map/ppermute | solution.py:444
  153.4 7.8 %collective-permute-start.26 = (bf16[16,512]{1,0:T(8,128)(2,1)S(1)}, bf16[16,512]{1,0:T(8,128)(2,1)S(1)}, u32[]{:S(2)}, u32[]{:S(2)}) collective-permute-start(bf16[16,512]{1,0:T(8,128)(2,1)S(1)} %pad_maximum_fusion.11.refs_13_.refs_10_), channel_id=1, source_target_pairs={{0,8},{4,12},{8,16},{12,20},{16,24},{20,28},{24,32},{28,36},{32,40... | collective-permute-start | bytes 49160 | tf_op jit(solution)/shard_map/ppermute | solution.py:444
  162.2 8.6 %collective-permute-start.27 = (bf16[48,512]{1,0:T(8,128)(2,1)S(1)}, bf16[48,512]{1,0:T(8,128)(2,1)S(1)}, u32[]{:S(2)}, u32[]{:S(2)}) collective-permute-start(bf16[48,512]{1,0:T(8,128)(2,1)S(1)} %get-tuple-element.136), channel_id=1, source_target_pairs={{0,4},{4,0},{8,12},{12,8},{16,20},{20,16},{24,28},{28,24},{32,36},... | collective-permute-start | bytes 147464 | tf_op jit(solution)/shard_map/ppermute | solution.py:444
  168.8 16.1 %collective-permute-start.28 = (bf16[16,512]{1,0:T(8,128)(2,1)S(1)}, bf16[16,512]{1,0:T(8,128)(2,1)S(1)}, u32[]{:S(2)}, u32[]{:S(2)}) collective-permute-start(bf16[16,512]{1,0:T(8,128)(2,1)S(1)} %get-tuple-element.143), channel_id=1, source_target_pairs={{0,500},{4,16},{8,508},{12,24},{16,4},{20,32},{24,12},{28,40},{32,... | collective-permute-start | bytes 49160 | tf_op jit(solution)/shard_map/ppermute | solution.py:444
  170.8 14.1 %collective-permute-start.29 = (bf16[32,512]{1,0:T(8,128)(2,1)S(1)}, bf16[32,512]{1,0:T(8,128)(2,1)S(1)}, u32[]{:S(2)}, u32[]{:S(2)}) collective-permute-start(bf16[32,512]{1,0:T(8,128)(2,1)S(1)} %pad_maximum_fusion.4.refs_7_.refs_4_), channel_id=1, source_target_pairs={{0,504},{4,508},{8,0},{12,4},{16,8},{20,12},{24,16},{28,20},{32,24... | collective-permute-start | bytes 98312 | tf_op jit(solution)/shard_map/ppermute | solution.py:444
  175.3 9.6 %collective-permute-start.30 = (bf16[32,512]{1,0:T(8,128)(2,1)S(1)}, bf16[32,512]{1,0:T(8,128)(2,1)S(1)}, u32[]{:S(2)}, u32[]{:S(2)}) collective-permute-start(bf16[32,512]{1,0:T(8,128)(2,1)S(1)} %pad_maximum_fusion.5.refs_8_.refs_5_), channel_id=1, source_target_pairs={{0,8},{4,12},{8,16},{12,20},{16,24},{20,28},{24,32},{28,36},{32,40... | collective-permute-start | bytes 98312 | tf_op jit(solution)/shard_map/ppermute | solution.py:444

commit v3 on v2

--- a/solution.py
+++ b/solution.py
@@ -2,7 +2,6 @@
 
 import jax
 import jax.numpy as jnp
-import numpy as np
 from jax import lax
 from jax.experimental import pallas as pl
 from jax.experimental.pallas import tpu as pltpu
@@ -28,7 +27,7 @@
     return pltpu.SMEM, array
 
 
-def call(body, outs, args, flops, scratch=(), ties=()):
+def call(body, outs, args, flops, scratch=(), ties=(), limit=20):
     outs = [o if isinstance(o, tuple) else (pltpu.VMEM, o) for o in outs]
     args = [a if isinstance(a, tuple) else (pltpu.VMEM, a) for a in args]
     moved = sum(a.size * a.dtype.itemsize for _, a in args)
@@ -44,7 +43,7 @@
         + [pl.BlockSpec(memory_space=pl.ANY)] * len(ties),
         out_specs=tuple(pl.BlockSpec(memory_space=m) for m, _ in outs),
         scratch_shapes=list(scratch),
-        compiler_params=pltpu.CompilerParams(vmem_limit_bytes=20 << 20),
+        compiler_params=pltpu.CompilerParams(vmem_limit_bytes=limit << 20),
         cost_estimate=pl.CostEstimate(flops=flops, bytes_accessed=moved, transcendentals=0),
     )(*[a for _, a in args], *ties)
 
@@ -94,9 +93,10 @@
     return ref[place * 512 : (place + 1) * 512, :]
 
 
-def assemble(shards, phase, target):
+def assemble(shards, target):
+    phase = lax.axis_index("phase")
     for away, shard in enumerate(shards):
-        block = pl.ds(pl.multiple_of(lax.rem(phase[0] - away + 4, 4) * LANES, LANES), LANES)
+        block = pl.ds(pl.multiple_of(lax.rem(phase - away + 4, 4) * LANES, LANES), LANES)
         target[:, block] = shard[...]
 
 
@@ -141,13 +141,64 @@
     return (scale * grad - update * (scale * scale * scale) * mixed).astype(BF)
 
 
-def prepare_kernel(gs, gd, ms, md, ds, dd, dd_small, entries, tables, grid_in, cotangent, cols, rows, starts, *sends):
+def is_even():
+    return lax.rem(lax.axis_index("dom"), 2) == 0
+
+
+def group_at(place, sent):
+    mine, other = (EVEN, ODD) if sent else (ODD, EVEN)
+    return jnp.where(is_even(), jnp.int32(mine[place]), jnp.int32(other[place]))
+
+
+def slot_entries(own, used, apart):
+    slot = lax.broadcasted_iota(jnp.int32, (LANES, LANES), 0)
+    entry = jnp.full((LANES, LANES), -1, jnp.int32)
+    for place in range(NEIGHBOURS):
+        inner = slot - place * apart
+        first = own + group_at(place, False) * used
+        entry = jnp.where((inner >= 0) & (inner < used), first + inner, entry)
+    return entry
+
+
+def sent_rows(table, used, apart):
+    lane = lax.broadcasted_iota(jnp.int32, (8, LANES), 1)
+    row = jnp.full((8, LANES), -1, jnp.int32)
+    for place in range(NEIGHBOURS):
+        group = group_at(place, True)
+        for s in range(used):
+            row = jnp.where(lane == place * apart + s, table[group, 0, s], row)
+    return row
+
+
+def prepare_kernel(
+    dd_small, grid_send, mesh_send, dec_send,
+    grid_in, cotangent, embed_w, out_w,
+    g_src, g_dst, m_src, m_dst, d_src, d_dst,
+    grid_w, enc_w, src_w, node_w, dec_w,
+    cols, rows, starts, w_first, w_second, *refs,
+):
+    sends, held, sem = refs[:4], refs[4:10], refs[10]
+    sources = [g_src, g_dst, m_src, m_dst, d_src, d_dst]
+    targets = list(held)
+    sources += [grid_w, enc_w, src_w.at[0], src_w.at[1], node_w.at[0], node_w.at[1], dec_w]
+    targets += [w_first.at[pl.ds(512 * k + 480, 512), :] for k in range(3)]
+    targets += [w_second.at[pl.ds(512 * k, 512), :] for k in range(4)]
+    copies = [pltpu.make_async_copy(a, b, sem.at[i]) for i, (a, b) in enumerate(zip(sources, targets))]
+    for copy in copies:
+        copy.start()
+    for copy in copies[: len(held)]:
+        copy.wait()
+    gs, gd, ms, md, ds, dd = held
+    w_first[:480, :] = jnp.concatenate([embed_w[...].astype(F32), jnp.zeros((480 - embed_w.shape[0], LANES), F32)], axis=0).astype(BF)
+    w_second[2048:, :] = jnp.concatenate([out_w[...].astype(F32), jnp.zeros((256 - out_w.shape[0], LANES), F32)], axis=0).astype(BF)
+    lists = ((gs, gd), (ms, md), (ds, dd))
+    grid, mesh = grid_in.shape[1], 256
+    sizes = ((grid, 12, 16), (mesh, 8, 8), (mesh, 8, 8))
     last_start = grid_in.shape[1] - HALF - 16
     for b in range(starts.shape[0]):
         starts[b] = jnp.minimum(lax.shift_left(lax.shift_right_logical(dd_small[0, b * HALF], 4), 4), last_start)
-    lists = ((gs, gd), (ms, md), (ds, dd))
     for which, (src, dst) in enumerate(lists):
-        slots = column(entries[which : which + 1, :])
+        slots = slot_entries(*sizes[which])
         entry = jnp.concatenate([slots] * (BLOCK // LANES), axis=1)
         found = jnp.zeros((LANES, BLOCK), F32)
         for b in range(src.shape[1] // BLOCK):
@@ -159,10 +210,10 @@
         wide = jnp.where(slots >= 0, wide, -1)
         cols[which] = wide
         rows[which] = wide.T[:8, :]
-    for t in range(3):
-        wide = jnp.broadcast_to(tables[t : t + 1, :], (LANES, LANES))
-        rows[3 + t] = wide[:8, :]
-        cols[3 + t] = wide.T
+    for t, table in enumerate((grid_send, mesh_send, dec_send)):
+        row = sent_rows(table, *sizes[t][1:])
+        rows[3 + t] = row
+        cols[3 + t] = column(row[:1, :])
     count = grid_in.shape[1]
     sent = mm_back(pick(cols[3], count), grid_in[...])
     at = pick(cols[2], count)
@@ -178,13 +229,15 @@
         parts = [sent[16 * k : 16 * k + 16], back[8 * j : 8 * j + 8], back_cot[8 * j : 8 * j + 8]]
         groups.append(jnp.concatenate([padded(piece) for piece in parts], axis=0))
     put(sends, groups)
-
-
-def embed_kernel(grid_in, own, from_1, from_2, from_3, phase, *refs):
+    for copy in copies[len(held) :]:
+        copy.wait()
+
+
+def embed_kernel(grid_in, own, from_1, from_2, from_3, *refs):
     early = refs[:4]
     ext, slope, hidden, b_hidden, b_cot, w = refs[4:]
     f_in, rows = grid_in.shape
-    assemble((own, from_1, from_2, from_3), phase, w)
+    assemble((own, from_1, from_2, from_3), w)
     embed = w[:f_in, :]
     mix = w[480:992, :]
     groups = received(early)
@@ -204,11 +257,11 @@
         ext[at, :] = mm(own_rows, mix).astype(BF)
 
 
-def assemble_kernel(own, from_1, from_2_low, from_2_high, from_3, phase, w):
+def assemble_kernel(own, from_1, from_2_low, from_2_high, from_3, w):
     half = from_2_low.shape[0]
     low, high = w.at[:half, :], w.at[half:, :]
-    assemble((own.at[:half, :], from_1.at[:half, :], from_2_low, from_3.at[:half, :]), phase, low)
-    assemble((own.at[half:, :], from_1.at[half:, :], from_2_high, from_3.at[half:, :]), phase, high)
+    assemble((own.at[:half, :], from_1.at[:half, :], from_2_low, from_3.at[:half, :]), low)
+    assemble((own.at[half:, :], from_1.at[half:, :], from_2_high, from_3.at[half:, :]), high)
 
 
 def cotangent_kernel(cotangent, b_cot, w, own_grad, b_grad):
@@ -218,7 +271,7 @@
     b_grad[...] = mm(b_cot[:, :f_out], out).astype(BF)
 
 
-def encode_edges_kernel(ext, static, src, moves, dst, cols, slope, h_slope, total, messages):
+def encode_edges_kernel(ext, static, src, dst, cols, slope, h_slope, total, messages):
     count = ext.shape[0]
     meshes = static.shape[0]
     pre = ext[count - LANES :, :].astype(F32) + mm(pick(cols[0], meshes), static[...])
@@ -229,7 +282,10 @@
         entry = src[:, at]
         src_row = entry
         for k in range(NEIGHBOURS):
-            src_row += jnp.where(entry >= count - LANES + 12 * k, moves[k], 0)
+            to = [16 * order.index(k) - 12 * k for order in (ODD, EVEN)]
+            by = jnp.where(is_even(), jnp.int32(to[0]), jnp.int32(to[1]))
+            first = count - LANES + 12 * k
+            src_row = jnp.where((entry >= first) & (entry < first + 12), entry + by, src_row)
         pre = mm(pick(column(src_row), count), ext[...])
         pre += mm(pick(column(dst[:, at]), meshes), static[...])
         sig = gate(pre)
@@ -350,11 +406,15 @@
     skip[...] = total[...].astype(BF)
 
 
-def predict_kernel(messages, message, starts, src, dst, rows, w, pred, total, *, own):
+def grid_sum_kernel(messages, starts, src, dst, total, *, own):
+    total[...] = jnp.zeros_like(total)
+    add_by_row(total, messages, starts, src, dst, own)
+
+
+def predict_kernel(total, message, rows, w, pred):
     f_out, count = pred.shape
-    total[...] = mm(spread(rows[2][0:1, :], count), message[...])
-    add_by_row(total, messages, starts, src, dst, own)
-    pred[...] = mm_back(w[2048 : 2048 + f_out, :], total[...].astype(BF)).astype(BF)
+    summed = total[...] + mm(spread(rows[2][0:1, :], count), message[...])
+    pred[...] = mm_back(w[2048 : 2048 + f_out, :], summed.astype(BF)).astype(BF)
 
 
 def edges_back_kernel(sum_grad, slope, src, dst, rows, *refs, both):
@@ -424,19 +484,6 @@
         grad = mm_back(row_grad, mix) + skip[at, :].astype(F32)
         grad = (grad * slope[at, :].astype(F32)).astype(BF)
         out[:, at] = mm_back(w[:f_in, :], grad).astype(BF)
-
-
-def slot_entries(sizes, order):
-    table = np.full((8, LANES), -1, np.int32)
-    for row, (own, used, apart) in enumerate(sizes):
-        for place, k in enumerate(order):
-            table[row, place * apart : place * apart + used] = own + k * used + np.arange(used)
-    return table
-
-
-def slot_moves(order):
-    shifts = [16 * order.index(k) - 12 * k for k in range(NEIGHBOURS)]
-    return np.diff(np.array([0] + shifts)).astype(np.int32)
 
 
 def permuted(block, route):
@@ -491,43 +538,30 @@
     mesh, d = mesh_static.shape
     f_out = cot.shape[0]
     edges = mesh_src.size
-    phase = lax.axis_index("phase").reshape(1)
 
     def along(block, away):
         return lax.ppermute(block, "phase", [(i, (i + away) % 4) for i in range(4)])
 
-    w_first = jnp.concatenate([jnp.pad(embed_w, ((0, 480 - f_in), (0, 0))), grid_w, enc_w, src_w[0]], axis=0)
-    w_second = jnp.concatenate(
-        [src_w[1], node_w[0], node_w[1], dec_w, jnp.pad(out_w.T, ((0, 256 - f_out), (0, 0)))], axis=0
-    )
-    even = lax.axis_index("dom") % 2 == 0
-
-    def order(table, apart):
-        flat = [jnp.pad(table[k], (0, apart - table.shape[1]), constant_values=-1) for k in range(NEIGHBOURS)]
-        in_even, in_odd = (jnp.concatenate([flat[k] for k in ks]) for ks in (EVEN, ODD))
-        row = jnp.where(even, in_even, in_odd)
-        return jnp.pad(row, (0, LANES - row.shape[0]), constant_values=-1)
-
-    tables = [order(grid_send[0], 16), order(mesh_send[0], 8), order(dec_send[0], 8)]
-    tables = jnp.stack(tables + [tables[2]] * 5)
-    sizes = ((grid, 12, 16), (mesh, 8, 8), (mesh, 8, 8))
-    entries = jnp.where(even, slot_entries(sizes, ODD), slot_entries(sizes, EVEN))
-    moves = jnp.where(even, slot_moves(ODD), slot_moves(EVEN))
-    w_first, w_second, phase, moves, tables = lax.optimization_barrier((w_first, w_second, phase, moves, tables))
-    first_1, first_3 = along(w_first, 1), along(w_first, -1)
-    first_shards = [w_first, first_1, along(first_1, 1), first_3]
-    cols, rows, starts, *sends = call(
+    lists = (g2m_src, g2m_dst, mesh_src, mesh_dst, m2g_src, m2g_dst)
+    far_away = [(pl.ANY, a) for a in lists + (grid_w, enc_w, src_w, node_w, dec_w)]
+    cols, rows, starts, w_first, w_second, *sends = call(
         prepare_kernel,
         [
             jax.ShapeDtypeStruct((6, LANES, LANES), jnp.int32),
             jax.ShapeDtypeStruct((6, 8, LANES), jnp.int32),
             smem(jax.ShapeDtypeStruct((m2g_dst.size // HALF,), jnp.int32)),
+            shape(2016, LANES),
+            shape(2304, LANES),
         ]
         + send_shapes(32, d),
-        [g2m_src, g2m_dst, mesh_src, mesh_dst, m2g_src, m2g_dst, smem(m2g_dst), entries, tables, x, cot],
+        [smem(m2g_dst)] + [smem(jnp.swapaxes(table, 0, 1)) for table in (grid_send, mesh_send, dec_send)]
+        + [x, cot, embed_w, out_w.T]
+        + far_away,
         400_000_000,
-        ties=(w_second, phase, moves),
-    )
+        [pltpu.VMEM(a.shape, a.dtype) for a in lists] + [pltpu.SemaphoreType.DMA((13,))],
+        limit=56,
+    )
+    first_shards = [w_first] + [along(w_first, away) for away in (1, 2, 3)]
     early = Exchange(sends, 1)
     w_second, _ = lax.optimization_barrier((w_second, early.ties))
     half = w_second.shape[0] // 2
@@ -536,23 +570,22 @@
     ext, slope_in, hidden, b_hidden, b_cot, w_enc = call(
         embed_kernel,
         [shape(grid + LANES, d), shape(grid, d), shape(grid, d), shape(LANES, d), shape(LANES, 256), shape(w_first.shape[0], d)],
-        [x, *first_shards, smem(phase), *early.rows()],
+        [x, *first_shards, *early.rows()],
         1_500_000_000,
     )
     enc_slope, enc_far, total = call(
         encode_edges_kernel,
         [shape(edges, d), shape(LANES, d), shape(mesh, d, F32)],
-        [ext, mesh_static, g2m_src, smem(moves), g2m_dst, cols],
+        [ext, mesh_static, g2m_src, g2m_dst, cols],
         5_000_000_000,
         [vmem(edges, d)],
-        ties=(second_1, second_3),
     )
     encoded, latent, proj, *sends = call(
         encode_rows_kernel,
         [shape(mesh, d, F32), shape(mesh, d), shape(mesh, d)] + send_shapes(8, d),
         [total, mesh_static, cols, w_enc],
         300_000_000,
-        ties=second_2,
+        ties=(second_1, second_3),
     )
     stored = []
     for layer in range(2):
@@ -569,7 +602,7 @@
             (w,) = call(
                 assemble_kernel,
                 [shape(w_second.shape[0], d)],
-                [w_second, second_1, *second_2, second_3, smem(phase)],
+                [w_second, second_1, *second_2, second_3],
                 1_000_000_000,
                 ties=moving.ties,
             )
@@ -610,11 +643,19 @@
     moving = Exchange(sends, 1)
     halo = moving.rows()
     entry, into = edges_back(sum_grad, stored[1][0], sends, True, moving.ties)
+    (dec_total,) = call(
+        functools.partial(grid_sum_kernel, own=mesh),
+        [shape(grid, d, F32)],
+        [messages, smem(starts), m2g_src, m2g_dst],
+        2_000_000_000,
+        ties=moving.ties,
+    )
     latent_grad, sum_grad, *sends = call(
         functools.partial(layer_back_kernel, where=(0, d), both=True, first=False),
         [shape(mesh, d, F32), shape(mesh, d)] + send_shapes(8, d),
         [entry, into, latent_grad, cols, rows, w, w, stored[0][2], stored[0][1], *halo],
         400_000_000,
+        ties=(dec_total,),
     )
     moving = Exchange(sends, -1)
     entry, into = edges_back(sum_grad, stored[0][0], sends, False, moving.ties)
@@ -631,14 +672,14 @@
         [shape(mesh, d)] + send_shapes(16, d),
         [entry, into, latent_grad, cols, rows, w_enc, w_enc, encoded, enc_far, *moving.rows()],
         400_000_000,
+        ties=(skip,),
     )
     moving = Exchange(sends, -1)
     (pred,) = call(
-        functools.partial(predict_kernel, own=mesh),
+        predict_kernel,
         [shape(f_out, grid)],
-        [messages, message, smem(starts), m2g_src, m2g_dst, rows, w],
-        2_500_000_000,
-        [vmem(grid, d, F32)],
+        [dec_total, message, rows, w],
+        500_000_000,
         ties=moving.ties,
     )
     (entry,) = call(

time: 189 us -> 178 us (0.942)
  local copies, waits for them, and re-layouts: 8.45 us -> 1.21 us
  waiting for transfers between devices: 12.4 us -> 7.69 us
    ppermute x24, waiting for transfers between devices: 8.42 us -> 1.6 us  [permuted(): lax.ppermute(block, 'dom', [(i, route(i) % size) for i in range(size)])]
    squeeze x4 -> x0, local copies, waits for them, and re-layouts: 3.26 us -> none  [the longest x3 2.34 us: order(): table[k]]
    unnamed x26 -> x28, local copies, waits for them, and re-layouts: 3.74 us -> 1.14 us
    ppermute x24, starting transfers between devices: 96.2 us -> 98.3 us  [permuted(): lax.ppermute(block, 'dom', [(i, route(i) % size) for i in range(size)])]
    ppermute x7, waiting for transfers between devices: 3.99 us -> 6.09 us  [along(): return lax.ppermute(block, 'phase', [(i, (i + away) % 4) for i in range(4)])]
    ppermute x7, starting transfers between devices: 20.5 us -> 18.5 us  [along(): return lax.ppermute(block, 'phase', [(i, (i + away) % 4) for i in range(4)])]
    pallas_call x19 -> x20, Pallas kernels: 46.5 us -> 48.2 us  [call(): pl.pallas_call(kernel, out_shape=tuple((o for _, o in outs)), in_specs=[p...]
  transfers between devices with their start and end apart: 31 -> 31, of which waited for: 4 -> 4; matrix products, arithmetic and copies ran while one was open for 0% -> 1% of each run, Pallas kernels for 16% -> 16%
where the time goes in v3:
time: 178 us; the launch traced here: 177 us
  starting transfers between devices  117 us (66%)
  Pallas kernels  48.2 us (27%)
  waiting for transfers between devices  7.69 us (4%)
    ppermute x24, starting transfers between devices, permuted(): lax.ppermute(block, 'dom', [(i, route(i) % size) for i in range(size)])  98.3 us
    pallas_call x20, Pallas kernels, call(): pl.pallas_call(kernel, out_shape=tuple((o for _, o in outs)), in_specs=[p...  48.2 us
    ppermute x7, starting transfers between devices, along(): return lax.ppermute(block, 'phase', [(i, (i + away) % 4) for i in range(4)])  18.5 us
    ppermute x7, waiting for transfers between devices, along(): return lax.ppermute(block, 'phase', [(i, (i + away) % 4) for i in range(4)])  6.09 us
  transfers between devices with their start and end apart: 31, of which 4 were waited for; matrix products, arithmetic and copies ran while one was open for 1% of the time, Pallas kernels for 16%

profile of v3, /device:TPU:1, one launch (start us, length us, event | category | flops | bytes accessed | tf_op | source)
XLA Modules:
  0.0 177.1 jit_solution(9371190004521173103)
XLA Ops:
  0.6 4.7 %shard_map.194 = (s32[6,128,128]{2,1,0:T(8,128)}, s32[6,8,128]{2,1,0:T(8,128)}, s32[24]{0:T(128)}, bf16[2016,128]{1,0:T(8,128)(2,1)}, bf16[2304,128]{1,0:T(8,128...) custom-call(s32[1,3072]{1,0:T(1,128)} %refs_5_.1, ...), custom_call_target="tpu_custom_call" | custom-call | flops 400000000 | bytes 4323328 | tf_op jit(solution)/shard_map/pallas_call | solution.py:39
  5.3 8.8 %collective-permute-start.3 = (bf16[96,512]{1,0:T(8,128)(2,1)}, bf16[96,512]{1,0:T(8,128)(2,1)S(1)}, u32[]{:S(2)}, u32[]{:S(2)}) collective-permute-start(bf16[96,512]{1,0:T(8,128)(2,1)} %get-tuple-element.71), channel_id=1, source_target_pairs={{0,4},{4,0},{8,12},{12,8},{16,20},{20,16},{24,28},{28,24},{32,36},... | collective-permute-start | bytes 294920 | tf_op jit(solution)/shard_map/ppermute | solution.py:491
  14.1 1.9 %collective-permute-start.2 = (bf16[2016,128]{1,0:T(8,128)(2,1)}, bf16[2016,128]{1,0:T(8,128)(2,1)S(1)}, u32[]{:S(2)}, u32[]{:S(2)}) collective-permute-start(bf16[2016,128]{1,0:T(8,128)(2,1)} %get-tuple-element.70.refs_1_), channel_id=1, source_target_pairs={{0,3},{1,0},{2,1},{3,2},{4,7},{5,4},{6,5},{7,6},{8,11},{9,8},{10,9... | collective-permute-start | bytes 1548296 | tf_op jit(solution)/shard_map/ppermute | solution.py:543
  16.1 1.9 %collective-permute-start.1 = (bf16[2016,128]{1,0:T(8,128)(2,1)}, bf16[2016,128]{1,0:T(8,128)(2,1)S(1)}, u32[]{:S(2)}, u32[]{:S(2)}) collective-permute-start(bf16[2016,128]{1,0:T(8,128)(2,1)} %get-tuple-element.70.refs_1_), channel_id=1, source_target_pairs={{0,2},{1,3},{2,0},{3,1},{4,6},{5,7},{6,4},{7,5},{8,10},{9,11},{10,... | collective-permute-start | bytes 1548296 | tf_op jit(solution)/shard_map/ppermute | solution.py:543
  18.0 3.4 %collective-permute-start = (bf16[2016,128]{1,0:T(8,128)(2,1)}, bf16[2016,128]{1,0:T(8,128)(2,1)S(1)}, u32[]{:S(2)}, u32[]{:S(2)}) collective-permute-start(bf16[2016,128]{1,0:T(8,128)(2,1)} %get-tuple-element.70.refs_1_), channel_id=1, source_target_pairs={{0,1},{1,2},{2,3},{3,0},{4,5},{5,6},{6,7},{7,4},{8,9},{9,10},{10,1... | collective-permute-start | bytes 1548296 | tf_op jit(solution)/shard_map/ppermute | solution.py:543
  21.3 3.3 %collective-permute-start.4 = (bf16[32,512]{1,0:T(8,128)(2,1)}, bf16[32,512]{1,0:T(8,128)(2,1)S(1)}, u32[]{:S(2)}, u32[]{:S(2)}) collective-permute-start(bf16[32,512]{1,0:T(8,128)(2,1)} %get-tuple-element.72), channel_id=1, source_target_pairs={{0,500},{4,16},{8,508},{12,24},{16,4},{20,32},{24,12},{28,40},{32,... | collective-permute-start | bytes 98312 | tf_op jit(solution)/shard_map/ppermute | solution.py:491
  24.7 0.8 pad_maximum_fusion
  25.4 4.0 %collective-permute-start.5 = (bf16[64,512]{1,0:T(8,128)(2,1)S(1)}, bf16[64,512]{1,0:T(8,128)(2,1)S(1)}, u32[]{:S(2)}, u32[]{:S(2)}) collective-permute-start(bf16[64,512]{1,0:T(8,128)(2,1)S(1)} %pad_maximum_fusion), channel_id=1, source_target_pairs={{0,8},{4,12},{8,16},{12,20},{16,24},{20,28},{24,32},{28,36},{32,40... | collective-permute-start | bytes 196616 | tf_op jit(solution)/shard_map/ppermute | solution.py:491
  29.4 0.8 pad_maximum_fusion.1
  30.2 11.1 %collective-permute-start.6 = (bf16[64,512]{1,0:T(8,128)(2,1)S(1)}, bf16[64,512]{1,0:T(8,128)(2,1)S(1)}, u32[]{:S(2)}, u32[]{:S(2)}) collective-permute-start(bf16[64,512]{1,0:T(8,128)(2,1)S(1)} %pad_maximum_fusion.1), channel_id=1, source_target_pairs={{0,504},{4,508},{8,0},{12,4},{16,8},{20,12},{24,16},{28,20},{32,24... | collective-permute-start | bytes 196616 | tf_op jit(solution)/shard_map/ppermute | solution.py:491
  41.3 0.0 copy-start
  41.3 0.0 copy-start.5
  41.4 0.0 copy-start.10
  41.4 0.0 copy-start.11
  41.4 4.1 %collective-permute-start.8 = (bf16[2304,128]{1,0:T(8,128)(2,1)}, bf16[2304,128]{1,0:T(8,128)(2,1)S(1)}, u32[]{:S(2)}, u32[]{:S(2)}) collective-permute-start(bf16[2304,128]{1,0:T(8,128)(2,1)} %get-tuple-element.80.refs_0_), channel_id=1, source_target_pairs={{0,3},{1,0},{2,1},{3,2},{4,7},{5,4},{6,5},{7,6},{8,11},{9,8},{10,9... | collective-permute-start | bytes 1769480 | tf_op jit(solution)/shard_map/ppermute | solution.py:543
  45.5 1.9 %collective-permute-start.7 = (bf16[2304,128]{1,0:T(8,128)(2,1)}, bf16[2304,128]{1,0:T(8,128)(2,1)S(1)}, u32[]{:S(2)}, u32[]{:S(2)}) collective-permute-start(bf16[2304,128]{1,0:T(8,128)(2,1)} %get-tuple-element.80.refs_0_), channel_id=1, source_target_pairs={{0,1},{1,2},{2,3},{3,0},{4,5},{5,6},{6,7},{7,4},{8,9},{9,10},{10,1... | collective-permute-start | bytes 1769480 | tf_op jit(solution)/shard_map/ppermute | solution.py:543
  47.5 1.0 copy-done.12
  48.5 2.6 %shard_map.195 = (bf16[1152,512]{1,0:T(8,128)(2,1)S(1)}, bf16[1024,512]{1,0:T(8,128)(2,1)S(1)}, bf16[1024,512]{1,0:T(8,128)(2,1)S(1)}, bf16[128,512]{1,0:T(8,128...) custom-call(bf16[474,1024]{1,0:T(8,128)(2,1)S(1)} %bitcast.19, bf16[2016,128]{1,0:T(8,128)(2,1)S(1)} %copy-done.12, ...), custom_call_target="tpu_custom_call" | custom-call | flops 1500000000 | bytes 8835072 | tf_op jit(solution)/shard_map/pallas_call | solution.py:39
  51.2 4.6 %shard_map.196 = (bf16[2048,512]{1,0:T(8,128)(2,1)S(1)}, bf16[128,512]{1,0:T(8,128)(2,1)S(1)}, f32[256,512]{1,0:T(8,128)S(1)}) custom-call(bf16[1152,512]{1,0:T(8,128)(2,1)S(1)} %get-tuple-element.75.refs_0_, bf16[256,512]{1,0:T(8,128)(2,1)S(1)} %copy-done.5, s32[1,2048]{1,0:T(1,128)S(1)} %copy-done.10, s32[1,2048]{1,0:T(1,128)S(1)} %copy-done.11, ...), custom_call_target="tpu_custom_call" | custom-call | flops 5000000000 | bytes 4603904 | tf_op jit(solution)/shard_map/pallas_call | solution.py:39
  55.9 1.3 collective-permute-done.8.refs_5_.refs_4_
  57.1 4.8 %collective-permute-done.7.refs_4_.refs_1_ = bf16[2304,128]{1,0:T(8,128)(2,1)S(1)} collective-permute-done((bf16[2304,128]{1,0:T(8,128)(2,1)}, bf16[2304,128]{1,0:T(8,128)(2,1)S(1)}, u32[]{:S(2)}, u32[]{:S(2)}) %collective-permute-start.7) | collective-permute-done | bytes 589856 | tf_op jit(solution)/shard_map/ppermute | solution.py:543
  61.9 0.8 shard_map.197
  62.7 4.6 %collective-permute-start.9 = (bf16[24,512]{1,0:T(8,128)(2,1)S(1)}, bf16[24,512]{1,0:T(8,128)(2,1)S(1)}, u32[]{:S(2)}, u32[]{:S(2)}) collective-permute-start(bf16[24,512]{1,0:T(8,128)(2,1)S(1)} %get-tuple-element.83), channel_id=1, source_target_pairs={{0,4},{4,0},{8,12},{12,8},{16,20},{20,16},{24,28},{28,24},{32,36},... | collective-permute-start | bytes 73736 | tf_op jit(solution)/shard_map/ppermute | solution.py:491
  67.3 1.9 %collective-permute-start.11 = (bf16[1152,128]{1,0:T(8,128)(2,1)S(1)}, bf16[1152,128]{1,0:T(8,128)(2,1)S(1)}, u32[]{:S(2)}, u32[]{:S(2)}) collective-permute-start(bf16[1152,128]{1,0:T(8,128)(2,1)S(1)} %slice.61), channel_id=1, source_target_pairs={{0,3},{1,0},{2,1},{3,2},{4,7},{5,4},{6,5},{7,6},{8,11},{9,8},{10,9... | collective-permute-start | bytes 884744 | tf_op jit(solution)/shard_map/ppermute | solution.py:543
  69.3 3.4 %collective-permute-start.10 = (bf16[1152,128]{1,0:T(8,128)(2,1)S(1)}, bf16[1152,128]{1,0:T(8,128)(2,1)S(1)}, u32[]{:S(2)}, u32[]{:S(2)}) collective-permute-start(bf16[1152,128]{1,0:T(8,128)(2,1)S(1)} %slice.60), channel_id=1, source_target_pairs={{0,1},{1,2},{2,3},{3,0},{4,5},{5,6},{6,7},{7,4},{8,9},{9,10},{10,1... | collective-permute-start | bytes 884744 | tf_op jit(solution)/shard_map/ppermute | solution.py:543
  72.6 1.9 %collective-permute-start.12 = (bf16[8,512]{1,0:T(8,128)(2,1)S(1)}, bf16[8,512]{1,0:T(8,128)(2,1)S(1)}, u32[]{:S(2)}, u32[]{:S(2)}) collective-permute-start(bf16[8,512]{1,0:T(8,128)(2,1)S(1)} %get-tuple-element.88), channel_id=1, source_target_pairs={{0,500},{4,16},{8,508},{12,24},{16,4},{20,32},{24,12},{28,40},{32,... | collective-permute-start | bytes 24584 | tf_op jit(solution)/shard_map/ppermute | solution.py:491
  74.6 1.9 %collective-permute-start.13 = (bf16[16,512]{1,0:T(8,128)(2,1)S(1)}, bf16[16,512]{1,0:T(8,128)(2,1)S(1)}, u32[]{:S(2)}, u32[]{:S(2)}) collective-permute-start(bf16[16,512]{1,0:T(8,128)(2,1)S(1)} %pad_maximum_fusion.6.refs_4_.refs_5_), channel_id=1, source_target_pairs={{0,8},{4,12},{8,16},{12,20},{16,24},{20,28},{24,32},{28,36},{32,40... | collective-permute-start | bytes 49160 | tf_op jit(solution)/shard_map/ppermute | solution.py:491
  76.5 6.9 %collective-permute-start.14 = (bf16[16,512]{1,0:T(8,128)(2,1)S(1)}, bf16[16,512]{1,0:T(8,128)(2,1)S(1)}, u32[]{:S(2)}, u32[]{:S(2)}) collective-permute-start(bf16[16,512]{1,0:T(8,128)(2,1)S(1)} %pad_maximum_fusion.7.refs_5_.refs_6_), channel_id=1, source_target_pairs={{0,504},{4,508},{8,0},{12,4},{16,8},{20,12},{24,16},{28,20},{32,24... | collective-permute-start | bytes 49160 | tf_op jit(solution)/shard_map/ppermute | solution.py:491
  83.4 2.7 %shard_map.198 = (f32[256,512]{1,0:T(8,128)S(1)}, bf16[2048,512]{1,0:T(8,128)(2,1)S(1)}) custom-call(bf16[256,512]{1,0:T(8,128)(2,1)S(1)} %get-tuple-element.81.refs_0_, bf16[256,512]{1,0:T(8,128)(2,1)S(1)} %get-tuple-element.82.refs_1_, s32[1,2048]{1,0:T(1,128)S(1)} %copy-done.8, s32[1,2048]{1,0:T(1,128)S(1)} %copy-done.9, ...), custom_call_target="tpu_custom_call" | custom-call | flops 3000000000 | bytes 3162112 | tf_op jit(solution)/shard_map/pallas_call | solution.py:39
  86.1 0.6 shard_map.199.refs_4_.refs_2_.refs_10_.refs_5_.refs_6_.refs_3_
  86.8 0.0 copy-done.3
  86.8 1.1 shard_map.200
  87.9 4.5 %collective-permute-start.15 = (bf16[24,512]{1,0:T(8,128)(2,1)S(1)}, bf16[24,512]{1,0:T(8,128)(2,1)S(1)}, u32[]{:S(2)}, u32[]{:S(2)}) collective-permute-start(bf16[24,512]{1,0:T(8,128)(2,1)S(1)} %get-tuple-element.91), channel_id=1, source_target_pairs={{0,4},{4,0},{8,12},{12,8},{16,20},{20,16},{24,28},{28,24},{32,36},... | collective-permute-start | bytes 73736 | tf_op jit(solution)/shard_map/ppermute | solution.py:491
  92.5 1.9 %collective-permute-start.16 = (bf16[8,512]{1,0:T(8,128)(2,1)S(1)}, bf16[8,512]{1,0:T(8,128)(2,1)S(1)}, u32[]{:S(2)}, u32[]{:S(2)}) collective-permute-start(bf16[8,512]{1,0:T(8,128)(2,1)S(1)} %get-tuple-element.95), channel_id=1, source_target_pairs={{0,500},{4,16},{8,508},{12,24},{16,4},{20,32},{24,12},{28,40},{32,... | collective-permute-start | bytes 24584 | tf_op jit(solution)/shard_map/ppermute | solution.py:491
  94.4 1.9 %collective-permute-start.17 = (bf16[16,512]{1,0:T(8,128)(2,1)S(1)}, bf16[16,512]{1,0:T(8,128)(2,1)S(1)}, u32[]{:S(2)}, u32[]{:S(2)}) collective-permute-start(bf16[16,512]{1,0:T(8,128)(2,1)S(1)} %pad_maximum_fusion.8.refs_4_.refs_3_), channel_id=1, source_target_pairs={{0,8},{4,12},{8,16},{12,20},{16,24},{20,28},{24,32},{28,36},{32,40... | collective-permute-start | bytes 49160 | tf_op jit(solution)/shard_map/ppermute | solution.py:491
  96.4 6.7 %collective-permute-start.18 = (bf16[16,512]{1,0:T(8,128)(2,1)S(1)}, bf16[16,512]{1,0:T(8,128)(2,1)S(1)}, u32[]{:S(2)}, u32[]{:S(2)}) collective-permute-start(bf16[16,512]{1,0:T(8,128)(2,1)S(1)} %pad_maximum_fusion.9.refs_5_.refs_4_), channel_id=1, source_target_pairs={{0,504},{4,508},{8,0},{12,4},{16,8},{20,12},{24,16},{28,20},{32,24... | collective-permute-start | bytes 49160 | tf_op jit(solution)/shard_map/ppermute | solution.py:491
  103.1 2.7 %shard_map.201 = (f32[256,512]{1,0:T(8,128)S(1)}, bf16[2048,512]{1,0:T(8,128)(2,1)S(1)}) custom-call(bf16[256,512]{1,0:T(8,128)(2,1)S(1)} %get-tuple-element.89.refs_0_, bf16[256,512]{1,0:T(8,128)(2,1)S(1)} %get-tuple-element.90.refs_1_, s32[1,2048]{1,0:T(1,128)S(1)} %copy-done.8, s32[1,2048]{1,0:T(1,128)S(1)} %copy-done.9, ...), custom_call_target="tpu_custom_call" | custom-call | flops 3000000000 | bytes 3162112 | tf_op jit(solution)/shard_map/pallas_call | solution.py:39
  105.8 0.5 shard_map.203
  106.3 0.0 copy-start.7
  106.4 1.5 shard_map.202
  107.8 7.2 %shard_map.204 = (bf16[3072,512]{1,0:T(8,128)(2,1)S(1)}, bf16[3072,512]{1,0:T(8,128)(2,1)S(1)}, f32[256,512]{1,0:T(8,128)S(1)}, bf16[256,512]{1,0:T(8,128)(2,1)S...) custom-call(bf16[256,512]{1,0:T(8,128)(2,1)S(1)} %get-tuple-element., ...), custom_call_target="tpu_custom_call" | custom-call | flops 6000000000 | bytes 13254752 | tf_op jit(solution)/shard_map/pallas_call | solution.py:39
  115.1 3.1 %collective-permute-start.19 = (bf16[48,512]{1,0:T(8,128)(2,1)S(1)}, bf16[48,512]{1,0:T(8,128)(2,1)S(1)}, u32[]{:S(2)}, u32[]{:S(2)}) collective-permute-start(bf16[48,512]{1,0:T(8,128)(2,1)S(1)} %get-tuple-element.106.refs_5_), channel_id=1, source_target_pairs={{0,4},{4,0},{8,12},{12,8},{16,20},{20,16},{24,28},{28,24},{32,36},... | collective-permute-start | bytes 147464 | tf_op jit(solution)/shard_map/ppermute | solution.py:491
  118.2 2.0 %collective-permute-start.20 = (bf16[16,512]{1,0:T(8,128)(2,1)S(1)}, bf16[16,512]{1,0:T(8,128)(2,1)S(1)}, u32[]{:S(2)}, u32[]{:S(2)}) collective-permute-start(bf16[16,512]{1,0:T(8,128)(2,1)S(1)} %get-tuple-element.110.refs_6_), channel_id=1, source_target_pairs={{0,500},{4,16},{8,508},{12,24},{16,4},{20,32},{24,12},{28,40},{32,... | collective-permute-start | bytes 49160 | tf_op jit(solution)/shard_map/ppermute | solution.py:491
  120.2 2.6 %collective-permute-start.21 = (bf16[32,512]{1,0:T(8,128)(2,1)S(1)}, bf16[32,512]{1,0:T(8,128)(2,1)S(1)}, u32[]{:S(2)}, u32[]{:S(2)}) collective-permute-start(bf16[32,512]{1,0:T(8,128)(2,1)S(1)} %pad_maximum_fusion.2.refs_4_.refs_9_), channel_id=1, source_target_pairs={{0,8},{4,12},{8,16},{12,20},{16,24},{20,28},{24,32},{28,36},{32,40... | collective-permute-start | bytes 98312 | tf_op jit(solution)/shard_map/ppermute | solution.py:491
  122.8 6.5 %collective-permute-start.22 = (bf16[32,512]{1,0:T(8,128)(2,1)S(1)}, bf16[32,512]{1,0:T(8,128)(2,1)S(1)}, u32[]{:S(2)}, u32[]{:S(2)}) collective-permute-start(bf16[32,512]{1,0:T(8,128)(2,1)S(1)} %pad_maximum_fusion.3.refs_5_.refs_10_), channel_id=1, source_target_pairs={{0,504},{4,508},{8,0},{12,4},{16,8},{20,12},{24,16},{28,20},{32,24... | collective-permute-start | bytes 98312 | tf_op jit(solution)/shard_map/ppermute | solution.py:491
  129.4 1.9 %shard_map.206 = (bf16[256,512]{1,0:T(8,128)(2,1)S(1)}, f32[256,512]{1,0:T(8,128)S(1)}) custom-call(bf16[256,512]{1,0:T(8,128)(2,1)S(1)} %get-tuple-element.111.refs_0_, bf16[2048,512]{1,0:T(8,128)(2,1)S(1)} %get-tuple-element.112.refs_1_, s32[1,2048]{1,0:T(1,128)S(1)} %copy-done.8, s32[1,2048]{1,0:T(1,128)S(1)} %copy-done.9, s32[6,8,128]{2,1,0:T(8,128)S(1)} %copy-done.3, ...), custom_call_target="tpu_custom_call" | custom-call | flops 3000000000 | bytes 3284992 | tf_op jit(solution)/shard_map/pallas_call | solution.py:39
  131.3 2.5 %shard_map.205.refs_13_.refs_0_ = f32[1024,512]{1,0:T(8,128)S(1)} custom-call(bf16[3072,512]{1,0:T(8,128)(2,1)S(1)} %get-tuple-element.105.refs_0_, s32[24]{0:T(128)S(1)} %copy-done.13, s32[1,3072]{1,0:T(1,128)S(1)} %copy-done.7, s32[1,3072]{1,0:T(1,128)S(1)} %copy-done.6, bf16[32,512]{1,0:T(8,128)(2,1)S(1)} %pad_maximum_fusion.2.refs_4_.refs_9_, ...), custom_call_target="tpu_custom_call" | custom-call | flops 2000000000 | bytes 5267552 | tf_op jit(solution)/shard_map/pallas_call | solution.py:39
  133.8 0.9 shard_map.207
  134.8 3.6 %collective-permute-start.23 = (bf16[24,512]{1,0:T(8,128)(2,1)S(1)}, bf16[24,512]{1,0:T(8,128)(2,1)S(1)}, u32[]{:S(2)}, u32[]{:S(2)}) collective-permute-start(bf16[24,512]{1,0:T(8,128)(2,1)S(1)} %get-tuple-element.118.refs_5_), channel_id=1, source_target_pairs={{0,4},{4,0},{8,12},{12,8},{16,20},{20,16},{24,28},{28,24},{32,36},... | collective-permute-start | bytes 73736 | tf_op jit(solution)/shard_map/ppermute | solution.py:491
  138.3 1.9 %collective-permute-start.24 = (bf16[8,512]{1,0:T(8,128)(2,1)S(1)}, bf16[8,512]{1,0:T(8,128)(2,1)S(1)}, u32[]{:S(2)}, u32[]{:S(2)}) collective-permute-start(bf16[8,512]{1,0:T(8,128)(2,1)S(1)} %get-tuple-element.124.refs_6_), channel_id=1, source_target_pairs={{0,500},{4,16},{8,508},{12,24},{16,4},{20,32},{24,12},{28,40},{32,... | collective-permute-start | bytes 24584 | tf_op jit(solution)/shard_map/ppermute | solution.py:491
  140.3 6.5 %collective-permute-start.25 = (bf16[16,512]{1,0:T(8,128)(2,1)S(1)}, bf16[16,512]{1,0:T(8,128)(2,1)S(1)}, u32[]{:S(2)}, u32[]{:S(2)}) collective-permute-start(bf16[16,512]{1,0:T(8,128)(2,1)S(1)} %pad_maximum_fusion.10.refs_12_.refs_9_), channel_id=1, source_target_pairs={{0,504},{4,508},{8,0},{12,4},{16,8},{20,12},{24,16},{28,20},{32,24... | collective-permute-start | bytes 49160 | tf_op jit(solution)/shard_map/ppermute | solution.py:491
  146.8 1.9 %collective-permute-start.26 = (bf16[16,512]{1,0:T(8,128)(2,1)S(1)}, bf16[16,512]{1,0:T(8,128)(2,1)S(1)}, u32[]{:S(2)}, u32[]{:S(2)}) collective-permute-start(bf16[16,512]{1,0:T(8,128)(2,1)S(1)} %pad_maximum_fusion.11.refs_13_.refs_10_), channel_id=1, source_target_pairs={{0,8},{4,12},{8,16},{12,20},{16,24},{20,28},{24,32},{28,36},{32,40... | collective-permute-start | bytes 49160 | tf_op jit(solution)/shard_map/ppermute | solution.py:491
  148.8 1.9 %shard_map.209 = (bf16[256,512]{1,0:T(8,128)(2,1)S(1)}, f32[256,512]{1,0:T(8,128)S(1)}) custom-call(bf16[256,512]{1,0:T(8,128)(2,1)S(1)} %get-tuple-element.122.refs_0_, bf16[2048,512]{1,0:T(8,128)(2,1)S(1)} %get-tuple-element.123.refs_1_, s32[1,2048]{1,0:T(1,128)S(1)} %copy-done.8, s32[1,2048]{1,0:T(1,128)S(1)} %copy-done.9, s32[6,8,128]{2,1,0:T(8,128)S(1)} %copy-done.3, ...), custom_call_target="tpu_custom_call" | custom-call | flops 3000000000 | bytes 3235840 | tf_op jit(solution)/shard_map/pallas_call | solution.py:39
  150.7 3.3 %shard_map.208 = (bf16[1024,512]{1,0:T(8,128)(2,1)S(1)}, bf16[128,512]{1,0:T(8,128)(2,1)S(1)}) custom-call(bf16[3072,512]{1,0:T(8,128)(2,1)S(1)} %get-tuple-element.109.refs_0_, bf16[1024,512]{1,0:T(8,128)(2,1)S(1)} %get-tuple-element.97.refs_1_, bf16[1024,512]{1,0:T(8,128)(2,1)S(1)} %get-tuple-element.99.refs_2_, s32[24]{0:T(128)S(1)} %copy-done.13, ...), custom_call_target="tpu_custom_call" | custom-call | flops 2500000000 | bytes 6996064 | tf_op jit(solution)/shard_map/pallas_call | solution.py:39
  154.0 0.6 collective-permute-done.26.refs_12_
  154.6 0.9 shard_map.210
  155.6 1.9 %collective-permute-start.27 = (bf16[48,512]{1,0:T(8,128)(2,1)S(1)}, bf16[48,512]{1,0:T(8,128)(2,1)S(1)}, u32[]{:S(2)}, u32[]{:S(2)}) collective-permute-start(bf16[48,512]{1,0:T(8,128)(2,1)S(1)} %get-tuple-element.131), channel_id=1, source_target_pairs={{0,4},{4,0},{8,12},{12,8},{16,20},{20,16},{24,28},{28,24},{32,36},... | collective-permute-start | bytes 147464 | tf_op jit(solution)/shard_map/ppermute | solution.py:491
  157.5 1.9 %collective-permute-start.28 = (bf16[16,512]{1,0:T(8,128)(2,1)S(1)}, bf16[16,512]{1,0:T(8,128)(2,1)S(1)}, u32[]{:S(2)}, u32[]{:S(2)}) collective-permute-start(bf16[16,512]{1,0:T(8,128)(2,1)S(1)} %get-tuple-element.137), channel_id=1, source_target_pairs={{0,500},{4,16},{8,508},{12,24},{16,4},{20,32},{24,12},{28,40},{32,... | collective-permute-start | bytes 49160 | tf_op jit(solution)/shard_map/ppermute | solution.py:491
  159.4 6.9 %collective-permute-start.29 = (bf16[32,512]{1,0:T(8,128)(2,1)S(1)}, bf16[32,512]{1,0:T(8,128)(2,1)S(1)}, u32[]{:S(2)}, u32[]{:S(2)}) collective-permute-start(bf16[32,512]{1,0:T(8,128)(2,1)S(1)} %pad_maximum_fusion.4.refs_4_), channel_id=1, source_target_pairs={{0,504},{4,508},{8,0},{12,4},{16,8},{20,12},{24,16},{28,20},{32,24... | collective-permute-start | bytes 98312 | tf_op jit(solution)/shard_map/ppermute | solution.py:491
  166.4 1.9 %collective-permute-start.30 = (bf16[32,512]{1,0:T(8,128)(2,1)S(1)}, bf16[32,512]{1,0:T(8,128)(2,1)S(1)}, u32[]{:S(2)}, u32[]{:S(2)}) collective-permute-start(bf16[32,512]{1,0:T(8,128)(2,1)S(1)} %pad_maximum_fusion.5.refs_5_), channel_id=1, source_target_pairs={{0,8},{4,12},{8,16},{12,20},{16,24},{20,28},{24,32},{28,36},{32,40... | collective-permute-start | bytes 98312 | tf_op jit(solution)/shard_map/ppermute | solution.py:491
  168.3 3.6 %shard_map.212.refs_0_ = bf16[1024,512]{1,0:T(8,128)(2,1)S(1)} custom-call(bf16[256,512]{1,0:T(8,128)(2,1)S(1)} %get-tuple-element.134.refs_0_, bf16[2048,512]{1,0:T(8,128)(2,1)S(1)} %get-tuple-element.135.refs_1_, s32[1,2048]{1,0:T(1,128)S(1)} %copy-done.10, s32[1,2048]{1,0:T(1,128)S(1)} %copy-done.11, bf16[32,512]{1,0:T(8,128)(2,1)S(1)} %pad_maximum_fusion.4.refs_4_, ...), custom_call_target="tpu_custom_call" | custom-call | flops 4000000000 | bytes 3424256 | tf_op jit(solution)/shard_map/pallas_call | solution.py:39
  171.9 1.5 shard_map.211
  173.4 0.9 collective-permute-done.30.refs_8_
  174.4 2.7 %shard_map.213 = bf16[474,1024]{1,0:T(8,128)(2,1)} custom-call(bf16[1024,512]{1,0:T(8,128)(2,1)S(1)} %shard_map.212.refs_0_, bf16[2016,512]{1,0:T(8,128)(2,1)S(1)} %get-tuple-element.78.refs_3_.refs_5_.refs_6_.refs_1_, bf16[1024,512]{1,0:T(8,128)(2,1)S(1)} %get-tuple-element.136.refs_2_, bf16[1024,512]{1,0:T(8,128)(2,1)S(1)} %get-tuple-element.130.refs_13_.refs_3_, ...), custom_call_target="tpu_custom_call" | custom-call | flops 1500000000 | bytes 6336512 | tf_op jit(solution)/shard_map/pallas_call | solution.py:39
  (66 shorter events, 0.2 us)
Async XLA Ops:
  0.6 46.8 %copy-start.2 = (bf16[1,1024,474]{1,2,0:T(8,128)(2,1)S(1)}, bf16[1,1024,474]{1,2,0:T(8,128)(2,1)}, u32[]{:S(2)}) copy-start(bf16[1,1024,474]{1,2,0:T(8,128)(2,1)} %param.19) | copy-start | bytes 2912260
  5.3 19.3 %collective-permute-start.3 = (bf16[96,512]{1,0:T(8,128)(2,1)}, bf16[96,512]{1,0:T(8,128)(2,1)S(1)}, u32[]{:S(2)}, u32[]{:S(2)}) collective-permute-start(bf16[96,512]{1,0:T(8,128)(2,1)} %get-tuple-element.71), channel_id=1, source_target_pairs={{0,4},{4,0},{8,12},{12,8},{16,20},{20,16},{24,28},{28,24},{32,36},... | collective-permute-start | bytes 294920 | tf_op jit(solution)/shard_map/ppermute | solution.py:491
  14.1 33.3 %collective-permute-start.2 = (bf16[2016,128]{1,0:T(8,128)(2,1)}, bf16[2016,128]{1,0:T(8,128)(2,1)S(1)}, u32[]{:S(2)}, u32[]{:S(2)}) collective-permute-start(bf16[2016,128]{1,0:T(8,128)(2,1)} %get-tuple-element.70.refs_1_), channel_id=1, source_target_pairs={{0,3},{1,0},{2,1},{3,2},{4,7},{5,4},{6,5},{7,6},{8,11},{9,8},{10,9... | collective-permute-start | bytes 1548296 | tf_op jit(solution)/shard_map/ppermute | solution.py:543
  16.1 31.4 %collective-permute-start.1 = (bf16[2016,128]{1,0:T(8,128)(2,1)}, bf16[2016,128]{1,0:T(8,128)(2,1)S(1)}, u32[]{:S(2)}, u32[]{:S(2)}) collective-permute-start(bf16[2016,128]{1,0:T(8,128)(2,1)} %get-tuple-element.70.refs_1_), channel_id=1, source_target_pairs={{0,2},{1,3},{2,0},{3,1},{4,6},{5,7},{6,4},{7,5},{8,10},{9,11},{10,... | collective-permute-start | bytes 1548296 | tf_op jit(solution)/shard_map/ppermute | solution.py:543
  18.0 29.5 %collective-permute-start = (bf16[2016,128]{1,0:T(8,128)(2,1)}, bf16[2016,128]{1,0:T(8,128)(2,1)S(1)}, u32[]{:S(2)}, u32[]{:S(2)}) collective-permute-start(bf16[2016,128]{1,0:T(8,128)(2,1)} %get-tuple-element.70.refs_1_), channel_id=1, source_target_pairs={{0,1},{1,2},{2,3},{3,0},{4,5},{5,6},{6,7},{7,4},{8,9},{9,10},{10,1... | collective-permute-start | bytes 1548296 | tf_op jit(solution)/shard_map/ppermute | solution.py:543
  21.3 8.9 %collective-permute-start.4 = (bf16[32,512]{1,0:T(8,128)(2,1)}, bf16[32,512]{1,0:T(8,128)(2,1)S(1)}, u32[]{:S(2)}, u32[]{:S(2)}) collective-permute-start(bf16[32,512]{1,0:T(8,128)(2,1)} %get-tuple-element.72), channel_id=1, source_target_pairs={{0,500},{4,16},{8,508},{12,24},{16,4},{20,32},{24,12},{28,40},{32,... | collective-permute-start | bytes 98312 | tf_op jit(solution)/shard_map/ppermute | solution.py:491
  25.4 15.9 %collective-permute-start.5 = (bf16[64,512]{1,0:T(8,128)(2,1)S(1)}, bf16[64,512]{1,0:T(8,128)(2,1)S(1)}, u32[]{:S(2)}, u32[]{:S(2)}) collective-permute-start(bf16[64,512]{1,0:T(8,128)(2,1)S(1)} %pad_maximum_fusion), channel_id=1, source_target_pairs={{0,8},{4,12},{8,16},{12,20},{16,24},{20,28},{24,32},{28,36},{32,40... | collective-permute-start | bytes 196616 | tf_op jit(solution)/shard_map/ppermute | solution.py:491
  30.2 15.3 %collective-permute-start.6 = (bf16[64,512]{1,0:T(8,128)(2,1)S(1)}, bf16[64,512]{1,0:T(8,128)(2,1)S(1)}, u32[]{:S(2)}, u32[]{:S(2)}) collective-permute-start(bf16[64,512]{1,0:T(8,128)(2,1)S(1)} %pad_maximum_fusion.1), channel_id=1, source_target_pairs={{0,504},{4,508},{8,0},{12,4},{16,8},{20,12},{24,16},{28,20},{32,24... | collective-permute-start | bytes 196616 | tf_op jit(solution)/shard_map/ppermute | solution.py:491
  41.3 9.8 %copy-start = (s32[6,128,128]{2,1,0:T(8,128)S(1)}, s32[6,128,128]{2,1,0:T(8,128)}, u32[]{:S(2)}) copy-start(s32[6,128,128]{2,1,0:T(8,128)} %get-tuple-element.76.refs_4_.refs_2_.refs_8_.refs_3_.refs_6_) | copy-start | bytes 1179652
  41.3 9.8 %copy-start.5 = (bf16[256,512]{1,0:T(8,128)(2,1)S(1)}, bf16[256,512]{1,0:T(8,128)(2,1)}, u32[]{:S(2)}) copy-start(bf16[256,512]{1,0:T(8,128)(2,1)} %refs_1_.3) | copy-start | bytes 786436
  41.4 9.8 %copy-start.10 = (s32[1,2048]{1,0:T(1,128)S(1)}, s32[1,2048]{1,0:T(1,128)}, u32[]{:S(2)}) copy-start(s32[1,2048]{1,0:T(1,128)} %refs_2_.13) | copy-start | bytes 24580
  41.4 9.8 %copy-start.11 = (s32[1,2048]{1,0:T(1,128)S(1)}, s32[1,2048]{1,0:T(1,128)}, u32[]{:S(2)}) copy-start(s32[1,2048]{1,0:T(1,128)} %refs_3_.13) | copy-start | bytes 24580
  41.4 15.7 %collective-permute-start.8 = (bf16[2304,128]{1,0:T(8,128)(2,1)}, bf16[2304,128]{1,0:T(8,128)(2,1)S(1)}, u32[]{:S(2)}, u32[]{:S(2)}) collective-permute-start(bf16[2304,128]{1,0:T(8,128)(2,1)} %get-tuple-element.80.refs_0_), channel_id=1, source_target_pairs={{0,3},{1,0},{2,1},{3,2},{4,7},{5,4},{6,5},{7,6},{8,11},{9,8},{10,9... | collective-permute-start | bytes 1769480 | tf_op jit(solution)/shard_map/ppermute | solution.py:543
  45.5 16.4 %collective-permute-start.7 = (bf16[2304,128]{1,0:T(8,128)(2,1)}, bf16[2304,128]{1,0:T(8,128)(2,1)S(1)}, u32[]{:S(2)}, u32[]{:S(2)}) collective-permute-start(bf16[2304,128]{1,0:T(8,128)(2,1)} %get-tuple-element.80.refs_0_), channel_id=1, source_target_pairs={{0,1},{1,2},{2,3},{3,0},{4,5},{5,6},{6,7},{7,4},{8,9},{9,10},{10,1... | collective-permute-start | bytes 1769480 | tf_op jit(solution)/shard_map/ppermute | solution.py:543
  47.5 1.0 copy-start.12
  61.9 21.5 %copy-start.8 = (s32[1,2048]{1,0:T(1,128)S(1)}, s32[1,2048]{1,0:T(1,128)}, u32[]{:S(2)}) copy-start(s32[1,2048]{1,0:T(1,128)} %refs_2_.12) | copy-start | bytes 24580
  61.9 21.5 %copy-start.9 = (s32[1,2048]{1,0:T(1,128)S(1)}, s32[1,2048]{1,0:T(1,128)}, u32[]{:S(2)}) copy-start(s32[1,2048]{1,0:T(1,128)} %refs_3_.12) | copy-start | bytes 24580
  62.7 11.9 %collective-permute-start.9 = (bf16[24,512]{1,0:T(8,128)(2,1)S(1)}, bf16[24,512]{1,0:T(8,128)(2,1)S(1)}, u32[]{:S(2)}, u32[]{:S(2)}) collective-permute-start(bf16[24,512]{1,0:T(8,128)(2,1)S(1)} %get-tuple-element.83), channel_id=1, source_target_pairs={{0,4},{4,0},{8,12},{12,8},{16,20},{20,16},{24,28},{28,24},{32,36},... | collective-permute-start | bytes 73736 | tf_op jit(solution)/shard_map/ppermute | solution.py:491
  67.3 18.8 %collective-permute-start.11 = (bf16[1152,128]{1,0:T(8,128)(2,1)S(1)}, bf16[1152,128]{1,0:T(8,128)(2,1)S(1)}, u32[]{:S(2)}, u32[]{:S(2)}) collective-permute-start(bf16[1152,128]{1,0:T(8,128)(2,1)S(1)} %slice.61), channel_id=1, source_target_pairs={{0,3},{1,0},{2,1},{3,2},{4,7},{5,4},{6,5},{7,6},{8,11},{9,8},{10,9... | collective-permute-start | bytes 884744 | tf_op jit(solution)/shard_map/ppermute | solution.py:543
  69.3 16.9 %collective-permute-start.10 = (bf16[1152,128]{1,0:T(8,128)(2,1)S(1)}, bf16[1152,128]{1,0:T(8,128)(2,1)S(1)}, u32[]{:S(2)}, u32[]{:S(2)}) collective-permute-start(bf16[1152,128]{1,0:T(8,128)(2,1)S(1)} %slice.60), channel_id=1, source_target_pairs={{0,1},{1,2},{2,3},{3,0},{4,5},{5,6},{6,7},{7,4},{8,9},{9,10},{10,1... | collective-permute-start | bytes 884744 | tf_op jit(solution)/shard_map/ppermute | solution.py:543
  72.6 14.1 %collective-permute-start.12 = (bf16[8,512]{1,0:T(8,128)(2,1)S(1)}, bf16[8,512]{1,0:T(8,128)(2,1)S(1)}, u32[]{:S(2)}, u32[]{:S(2)}) collective-permute-start(bf16[8,512]{1,0:T(8,128)(2,1)S(1)} %get-tuple-element.88), channel_id=1, source_target_pairs={{0,500},{4,16},{8,508},{12,24},{16,4},{20,32},{24,12},{28,40},{32,... | collective-permute-start | bytes 24584 | tf_op jit(solution)/shard_map/ppermute | solution.py:491
  74.6 12.2 %collective-permute-start.13 = (bf16[16,512]{1,0:T(8,128)(2,1)S(1)}, bf16[16,512]{1,0:T(8,128)(2,1)S(1)}, u32[]{:S(2)}, u32[]{:S(2)}) collective-permute-start(bf16[16,512]{1,0:T(8,128)(2,1)S(1)} %pad_maximum_fusion.6.refs_4_.refs_5_), channel_id=1, source_target_pairs={{0,8},{4,12},{8,16},{12,20},{16,24},{20,28},{24,32},{28,36},{32,40... | collective-permute-start | bytes 49160 | tf_op jit(solution)/shard_map/ppermute | solution.py:491
  76.5 10.3 %collective-permute-start.14 = (bf16[16,512]{1,0:T(8,128)(2,1)S(1)}, bf16[16,512]{1,0:T(8,128)(2,1)S(1)}, u32[]{:S(2)}, u32[]{:S(2)}) collective-permute-start(bf16[16,512]{1,0:T(8,128)(2,1)S(1)} %pad_maximum_fusion.7.refs_5_.refs_6_), channel_id=1, source_target_pairs={{0,504},{4,508},{8,0},{12,4},{16,8},{20,12},{24,16},{28,20},{32,24... | collective-permute-start | bytes 49160 | tf_op jit(solution)/shard_map/ppermute | solution.py:491
  83.4 2.7 %copy-start.4 = (bf16[2304,128]{1,0:T(8,128)(2,1)S(1)}, bf16[2304,128]{1,0:T(8,128)(2,1)}, u32[]{:S(2)}) copy-start(bf16[2304,128]{1,0:T(8,128)(2,1)} %get-tuple-element.80.refs_0_) | copy-start | bytes 1769476
  86.1 0.7 copy-start.3
  87.9 6.5 %collective-permute-start.15 = (bf16[24,512]{1,0:T(8,128)(2,1)S(1)}, bf16[24,512]{1,0:T(8,128)(2,1)S(1)}, u32[]{:S(2)}, u32[]{:S(2)}) collective-permute-start(bf16[24,512]{1,0:T(8,128)(2,1)S(1)} %get-tuple-element.91), channel_id=1, source_target_pairs={{0,4},{4,0},{8,12},{12,8},{16,20},{20,16},{24,28},{28,24},{32,36},... | collective-permute-start | bytes 73736 | tf_op jit(solution)/shard_map/ppermute | solution.py:491
  92.5 13.9 %collective-permute-start.16 = (bf16[8,512]{1,0:T(8,128)(2,1)S(1)}, bf16[8,512]{1,0:T(8,128)(2,1)S(1)}, u32[]{:S(2)}, u32[]{:S(2)}) collective-permute-start(bf16[8,512]{1,0:T(8,128)(2,1)S(1)} %get-tuple-element.95), channel_id=1, source_target_pairs={{0,500},{4,16},{8,508},{12,24},{16,4},{20,32},{24,12},{28,40},{32,... | collective-permute-start | bytes 24584 | tf_op jit(solution)/shard_map/ppermute | solution.py:491
  94.4 11.9 %collective-permute-start.17 = (bf16[16,512]{1,0:T(8,128)(2,1)S(1)}, bf16[16,512]{1,0:T(8,128)(2,1)S(1)}, u32[]{:S(2)}, u32[]{:S(2)}) collective-permute-start(bf16[16,512]{1,0:T(8,128)(2,1)S(1)} %pad_maximum_fusion.8.refs_4_.refs_3_), channel_id=1, source_target_pairs={{0,8},{4,12},{8,16},{12,20},{16,24},{20,28},{24,32},{28,36},{32,40... | collective-permute-start | bytes 49160 | tf_op jit(solution)/shard_map/ppermute | solution.py:491
  96.4 10.0 %collective-permute-start.18 = (bf16[16,512]{1,0:T(8,128)(2,1)S(1)}, bf16[16,512]{1,0:T(8,128)(2,1)S(1)}, u32[]{:S(2)}, u32[]{:S(2)}) collective-permute-start(bf16[16,512]{1,0:T(8,128)(2,1)S(1)} %pad_maximum_fusion.9.refs_5_.refs_4_), channel_id=1, source_target_pairs={{0,504},{4,508},{8,0},{12,4},{16,8},{20,12},{24,16},{28,20},{32,24... | collective-permute-start | bytes 49160 | tf_op jit(solution)/shard_map/ppermute | solution.py:491
  103.1 2.7 %copy-start.1 = (bf16[1,1024,227]{1,2,0:T(8,128)(2,1)S(1)}, bf16[1,1024,227]{1,2,0:T(8,128)(2,1)}, u32[]{:S(2)}) copy-start(bf16[1,1024,227]{1,2,0:T(8,128)(2,1)} %param.28) | copy-start | bytes 1394692
  106.3 1.5 copy-start.6
  106.3 1.5 copy-start.7
  106.3 1.5 copy-start.13
  115.1 5.1 %collective-permute-start.19 = (bf16[48,512]{1,0:T(8,128)(2,1)S(1)}, bf16[48,512]{1,0:T(8,128)(2,1)S(1)}, u32[]{:S(2)}, u32[]{:S(2)}) collective-permute-start(bf16[48,512]{1,0:T(8,128)(2,1)S(1)} %get-tuple-element.106.refs_5_), channel_id=1, source_target_pairs={{0,4},{4,0},{8,12},{12,8},{16,20},{20,16},{24,28},{28,24},{32,36},... | collective-permute-start | bytes 147464 | tf_op jit(solution)/shard_map/ppermute | solution.py:491
  118.2 15.6 %collective-permute-start.20 = (bf16[16,512]{1,0:T(8,128)(2,1)S(1)}, bf16[16,512]{1,0:T(8,128)(2,1)S(1)}, u32[]{:S(2)}, u32[]{:S(2)}) collective-permute-start(bf16[16,512]{1,0:T(8,128)(2,1)S(1)} %get-tuple-element.110.refs_6_), channel_id=1, source_target_pairs={{0,500},{4,16},{8,508},{12,24},{16,4},{20,32},{24,12},{28,40},{32,... | collective-permute-start | bytes 49160 | tf_op jit(solution)/shard_map/ppermute | solution.py:491
  120.2 13.6 %collective-permute-start.21 = (bf16[32,512]{1,0:T(8,128)(2,1)S(1)}, bf16[32,512]{1,0:T(8,128)(2,1)S(1)}, u32[]{:S(2)}, u32[]{:S(2)}) collective-permute-start(bf16[32,512]{1,0:T(8,128)(2,1)S(1)} %pad_maximum_fusion.2.refs_4_.refs_9_), channel_id=1, source_target_pairs={{0,8},{4,12},{8,16},{12,20},{16,24},{20,28},{24,32},{28,36},{32,40... | collective-permute-start | bytes 98312 | tf_op jit(solution)/shard_map/ppermute | solution.py:491
  122.8 11.0 %collective-permute-start.22 = (bf16[32,512]{1,0:T(8,128)(2,1)S(1)}, bf16[32,512]{1,0:T(8,128)(2,1)S(1)}, u32[]{:S(2)}, u32[]{:S(2)}) collective-permute-start(bf16[32,512]{1,0:T(8,128)(2,1)S(1)} %pad_maximum_fusion.3.refs_5_.refs_10_), channel_id=1, source_target_pairs={{0,504},{4,508},{8,0},{12,4},{16,8},{20,12},{24,16},{28,20},{32,24... | collective-permute-start | bytes 98312 | tf_op jit(solution)/shard_map/ppermute | solution.py:491
  134.8 5.5 %collective-permute-start.23 = (bf16[24,512]{1,0:T(8,128)(2,1)S(1)}, bf16[24,512]{1,0:T(8,128)(2,1)S(1)}, u32[]{:S(2)}, u32[]{:S(2)}) collective-permute-start(bf16[24,512]{1,0:T(8,128)(2,1)S(1)} %get-tuple-element.118.refs_5_), channel_id=1, source_target_pairs={{0,4},{4,0},{8,12},{12,8},{16,20},{20,16},{24,28},{28,24},{32,36},... | collective-permute-start | bytes 73736 | tf_op jit(solution)/shard_map/ppermute | solution.py:491
  138.3 15.7 %collective-permute-start.24 = (bf16[8,512]{1,0:T(8,128)(2,1)S(1)}, bf16[8,512]{1,0:T(8,128)(2,1)S(1)}, u32[]{:S(2)}, u32[]{:S(2)}) collective-permute-start(bf16[8,512]{1,0:T(8,128)(2,1)S(1)} %get-tuple-element.124.refs_6_), channel_id=1, source_target_pairs={{0,500},{4,16},{8,508},{12,24},{16,4},{20,32},{24,12},{28,40},{32,... | collective-permute-start | bytes 24584 | tf_op jit(solution)/shard_map/ppermute | solution.py:491
  140.3 13.7 %collective-permute-start.25 = (bf16[16,512]{1,0:T(8,128)(2,1)S(1)}, bf16[16,512]{1,0:T(8,128)(2,1)S(1)}, u32[]{:S(2)}, u32[]{:S(2)}) collective-permute-start(bf16[16,512]{1,0:T(8,128)(2,1)S(1)} %pad_maximum_fusion.10.refs_12_.refs_9_), channel_id=1, source_target_pairs={{0,504},{4,508},{8,0},{12,4},{16,8},{20,12},{24,16},{28,20},{32,24... | collective-permute-start | bytes 49160 | tf_op jit(solution)/shard_map/ppermute | solution.py:491
  146.8 7.8 %collective-permute-start.26 = (bf16[16,512]{1,0:T(8,128)(2,1)S(1)}, bf16[16,512]{1,0:T(8,128)(2,1)S(1)}, u32[]{:S(2)}, u32[]{:S(2)}) collective-permute-start(bf16[16,512]{1,0:T(8,128)(2,1)S(1)} %pad_maximum_fusion.11.refs_13_.refs_10_), channel_id=1, source_target_pairs={{0,8},{4,12},{8,16},{12,20},{16,24},{20,28},{24,32},{28,36},{32,40... | collective-permute-start | bytes 49160 | tf_op jit(solution)/shard_map/ppermute | solution.py:491
  155.6 3.9 %collective-permute-start.27 = (bf16[48,512]{1,0:T(8,128)(2,1)S(1)}, bf16[48,512]{1,0:T(8,128)(2,1)S(1)}, u32[]{:S(2)}, u32[]{:S(2)}) collective-permute-start(bf16[48,512]{1,0:T(8,128)(2,1)S(1)} %get-tuple-element.131), channel_id=1, source_target_pairs={{0,4},{4,0},{8,12},{12,8},{16,20},{20,16},{24,28},{28,24},{32,36},... | collective-permute-start | bytes 147464 | tf_op jit(solution)/shard_map/ppermute | solution.py:491
  157.5 16.0 %collective-permute-start.28 = (bf16[16,512]{1,0:T(8,128)(2,1)S(1)}, bf16[16,512]{1,0:T(8,128)(2,1)S(1)}, u32[]{:S(2)}, u32[]{:S(2)}) collective-permute-start(bf16[16,512]{1,0:T(8,128)(2,1)S(1)} %get-tuple-element.137), channel_id=1, source_target_pairs={{0,500},{4,16},{8,508},{12,24},{16,4},{20,32},{24,12},{28,40},{32,... | collective-permute-start | bytes 49160 | tf_op jit(solution)/shard_map/ppermute | solution.py:491
  159.4 14.0 %collective-permute-start.29 = (bf16[32,512]{1,0:T(8,128)(2,1)S(1)}, bf16[32,512]{1,0:T(8,128)(2,1)S(1)}, u32[]{:S(2)}, u32[]{:S(2)}) collective-permute-start(bf16[32,512]{1,0:T(8,128)(2,1)S(1)} %pad_maximum_fusion.4.refs_4_), channel_id=1, source_target_pairs={{0,504},{4,508},{8,0},{12,4},{16,8},{20,12},{24,16},{28,20},{32,24... | collective-permute-start | bytes 98312 | tf_op jit(solution)/shard_map/ppermute | solution.py:491
  166.4 8.0 %collective-permute-start.30 = (bf16[32,512]{1,0:T(8,128)(2,1)S(1)}, bf16[32,512]{1,0:T(8,128)(2,1)S(1)}, u32[]{:S(2)}, u32[]{:S(2)}) collective-permute-start(bf16[32,512]{1,0:T(8,128)(2,1)S(1)} %pad_maximum_fusion.5.refs_5_), channel_id=1, source_target_pairs={{0,8},{4,12},{8,16},{12,20},{16,24},{20,28},{24,32},{28,36},{32,40... | collective-permute-start | bytes 98312 | tf_op jit(solution)/shard_map/ppermute | solution.py:491

commit v4 on v3

--- a/solution.py
+++ b/solution.py
@@ -170,27 +170,32 @@
     return row
 
 
-def prepare_kernel(
-    dd_small, grid_send, mesh_send, dec_send,
-    grid_in, cotangent, embed_w, out_w,
-    g_src, g_dst, m_src, m_dst, d_src, d_dst,
-    grid_w, enc_w, src_w, node_w, dec_w,
-    cols, rows, starts, w_first, w_second, *refs,
-):
-    sends, held, sem = refs[:4], refs[4:10], refs[10]
-    sources = [g_src, g_dst, m_src, m_dst, d_src, d_dst]
-    targets = list(held)
-    sources += [grid_w, enc_w, src_w.at[0], src_w.at[1], node_w.at[0], node_w.at[1], dec_w]
-    targets += [w_first.at[pl.ds(512 * k + 480, 512), :] for k in range(3)]
+def pack_kernel(embed_w, out_w, grid_w, enc_w, src_w, node_w, dec_w, w_first, w_second, sem):
+    sources = [grid_w, enc_w, src_w.at[0], src_w.at[1], node_w.at[0], node_w.at[1], dec_w]
+    targets = [w_first.at[pl.ds(512 * k + 480, 512), :] for k in range(3)]
     targets += [w_second.at[pl.ds(512 * k, 512), :] for k in range(4)]
     copies = [pltpu.make_async_copy(a, b, sem.at[i]) for i, (a, b) in enumerate(zip(sources, targets))]
     for copy in copies:
         copy.start()
-    for copy in copies[: len(held)]:
+    for ref, target in ((embed_w, w_first.at[:480, :]), (out_w, w_second.at[2048:, :])):
+        short = target.shape[0] - ref.shape[0]
+        target[...] = jnp.concatenate([ref[...].astype(F32), jnp.zeros((short, LANES), F32)], axis=0).astype(BF)
+    for copy in copies:
+        copy.wait()
+
+
+def prepare_kernel(
+    dd_small, grid_send, mesh_send, dec_send, grid_in, cotangent,
+    g_src, g_dst, m_src, m_dst, d_src, d_dst, cols, rows, starts, *refs,
+):
+    sends, held, sem = refs[:4], refs[4:10], refs[10]
+    sources = [g_src, g_dst, m_src, m_dst, d_src, d_dst]
+    copies = [pltpu.make_async_copy(a, b, sem.at[i]) for i, (a, b) in enumerate(zip(sources, held))]
+    for copy in copies:
+        copy.start()
+    for copy in copies:
         copy.wait()
     gs, gd, ms, md, ds, dd = held
-    w_first[:480, :] = jnp.concatenate([embed_w[...].astype(F32), jnp.zeros((480 - embed_w.shape[0], LANES), F32)], axis=0).astype(BF)
-    w_second[2048:, :] = jnp.concatenate([out_w[...].astype(F32), jnp.zeros((256 - out_w.shape[0], LANES), F32)], axis=0).astype(BF)
     lists = ((gs, gd), (ms, md), (ds, dd))
     grid, mesh = grid_in.shape[1], 256
     sizes = ((grid, 12, 16), (mesh, 8, 8), (mesh, 8, 8))
@@ -229,8 +234,6 @@
         parts = [sent[16 * k : 16 * k + 16], back[8 * j : 8 * j + 8], back_cot[8 * j : 8 * j + 8]]
         groups.append(jnp.concatenate([padded(piece) for piece in parts], axis=0))
     put(sends, groups)
-    for copy in copies[len(held) :]:
-        copy.wait()
 
 
 def embed_kernel(grid_in, own, from_1, from_2, from_3, *refs):
@@ -349,7 +352,7 @@
     count = proj.shape[0]
     last_start = hidden.shape[0] - BLOCK
 
-    @pl.loop(0, src.shape[1] // BLOCK, unroll=4)
+    @pl.loop(0, src.shape[1] // BLOCK, unroll=6)
     def _(b):
         at = at_block(b)
         dst_row = line(dst, b)
@@ -384,7 +387,7 @@
 def add_by_row(total, values, starts, src, dst, own):
     rows = HALF + 16
 
-    @pl.loop(0, src.shape[1] // HALF, unroll=4)
+    @pl.loop(0, src.shape[1] // HALF, unroll=8)
     def _(b):
         dst_row = jnp.where(line(src, b, HALF) < own, line(dst, b, HALF), -(1 << 20))
         start = pl.multiple_of(starts[b], 16)
@@ -543,25 +546,31 @@
         return lax.ppermute(block, "phase", [(i, (i + away) % 4) for i in range(4)])
 
     lists = (g2m_src, g2m_dst, mesh_src, mesh_dst, m2g_src, m2g_dst)
-    far_away = [(pl.ANY, a) for a in lists + (grid_w, enc_w, src_w, node_w, dec_w)]
-    cols, rows, starts, w_first, w_second, *sends = call(
+    w_first, w_second = call(
+        pack_kernel,
+        [shape(2016, LANES), shape(2304, LANES)],
+        [embed_w, out_w.T] + [(pl.ANY, w) for w in (grid_w, enc_w, src_w, node_w, dec_w)],
+        1_000_000,
+        [pltpu.SemaphoreType.DMA((7,))],
+        limit=56,
+    )
+    first_shards = [w_first] + [along(w_first, away) for away in (1, 2, 3)]
+    cols, rows, starts, *sends = call(
         prepare_kernel,
         [
             jax.ShapeDtypeStruct((6, LANES, LANES), jnp.int32),
             jax.ShapeDtypeStruct((6, 8, LANES), jnp.int32),
             smem(jax.ShapeDtypeStruct((m2g_dst.size // HALF,), jnp.int32)),
-            shape(2016, LANES),
-            shape(2304, LANES),
         ]
         + send_shapes(32, d),
         [smem(m2g_dst)] + [smem(jnp.swapaxes(table, 0, 1)) for table in (grid_send, mesh_send, dec_send)]
-        + [x, cot, embed_w, out_w.T]
-        + far_away,
+        + [x, cot]
+        + [(pl.ANY, a) for a in lists],
         400_000_000,
-        [pltpu.VMEM(a.shape, a.dtype) for a in lists] + [pltpu.SemaphoreType.DMA((13,))],
+        [pltpu.VMEM(a.shape, a.dtype) for a in lists] + [pltpu.SemaphoreType.DMA((6,))],
+        ties=(w_first,),
         limit=56,
     )
-    first_shards = [w_first] + [along(w_first, away) for away in (1, 2, 3)]
     early = Exchange(sends, 1)
     w_second, _ = lax.optimization_barrier((w_second, early.ties))
     half = w_second.shape[0] // 2

time: 178 us -> 180 us (1.011)
    pallas_call x20 -> x21, Pallas kernels: 48.2 us -> 49.8 us  [call(): pl.pallas_call(kernel, out_shape=tuple((o for _, o in outs)), in_specs=[p...]
  transfers between devices with their start and end apart: 31 -> 31, of which waited for: 4 -> 4; matrix products, arithmetic and copies ran while one was open for 1% -> 1% of each run, Pallas kernels for 16% -> 15%
where the time goes in v4:
time: 180 us; the launch traced here: 179 us
  starting transfers between devices  117 us (65%)
  Pallas kernels  49.8 us (28%)
  waiting for transfers between devices  9.03 us (5%)
    ppermute x24, starting transfers between devices, permuted(): lax.ppermute(block, 'dom', [(i, route(i) % size) for i in range(size)])  98.5 us
    pallas_call x21, Pallas kernels, call(): pl.pallas_call(kernel, out_shape=tuple((o for _, o in outs)), in_specs=[p...  49.8 us
    ppermute x7, starting transfers between devices, along(): return lax.ppermute(block, 'phase', [(i, (i + away) % 4) for i in range(4)])  18.5 us
    ppermute x7, waiting for transfers between devices, along(): return lax.ppermute(block, 'phase', [(i, (i + away) % 4) for i in range(4)])  6.9 us
  transfers between devices with their start and end apart: 31, of which 4 were waited for; matrix products, arithmetic and copies ran while one was open for 1% of the time, Pallas kernels for 15%

profile of v4, /device:TPU:1, one launch (start us, length us, event | category | flops | bytes accessed | tf_op | source)
XLA Modules:
  0.0 179.2 jit_solution(8863001368737803545)
XLA Ops:
  0.6 0.0 copy-start.2
  0.6 3.3 %shard_map.194 = (bf16[2016,128]{1,0:T(8,128)(2,1)}, bf16[2304,128]{1,0:T(8,128)(2,1)}) custom-call(bf16[474,128]{1,0:T(8,128)(2,1)} %refs_0_.2, bf16[227,128]{1,0:T(8,128)(2,1)} %bitcast.22, bf16[512,128]{1,0:T(8,128)(2,1)} %refs_2_.8, bf16[512,128]{1,0:T(8,128)(2,1)} %refs_3_.8, bf16[2,512,128]{2,1,0:T(8,128)(2,1)} %refs_4_.2, ...), custom_call_target="tpu_custom_call" | custom-call | flops 1000000 | bytes 2202880 | tf_op jit(solution)/shard_map/pallas_call | solution.py:39
  3.9 4.1 %shard_map.195 = (s32[6,128,128]{2,1,0:T(8,128)}, s32[6,8,128]{2,1,0:T(8,128)}, s32[24]{0:T(128)}, bf16[96,512]{1,0:T(8,128)(2,1)}, bf16[32,512]{1,0:T(8,128)(2,...) custom-call(s32[1,3072]{1,0:T(1,128)} %refs_5_.3, s32[6,1,12]{2,1,0:T(1,128)} %bitcast.23, s32[6,1,8]{2,1,0:T(1,128)} %bitcast.24, ...), custom_call_target="tpu_custom_call" | custom-call | flops 400000000 | bytes 2120448 | tf_op jit(solution)/shard_map/pallas_call | solution.py:39
  8.1 8.8 %collective-permute-start.3 = (bf16[96,512]{1,0:T(8,128)(2,1)}, bf16[96,512]{1,0:T(8,128)(2,1)S(1)}, u32[]{:S(2)}, u32[]{:S(2)}) collective-permute-start(bf16[96,512]{1,0:T(8,128)(2,1)} %get-tuple-element.71), channel_id=1, source_target_pairs={{0,4},{4,0},{8,12},{12,8},{16,20},{20,16},{24,28},{28,24},{32,36},... | collective-permute-start | bytes 294920 | tf_op jit(solution)/shard_map/ppermute | solution.py:494
  16.9 1.9 %collective-permute-start.2 = (bf16[2016,128]{1,0:T(8,128)(2,1)}, bf16[2016,128]{1,0:T(8,128)(2,1)S(1)}, u32[]{:S(2)}, u32[]{:S(2)}) collective-permute-start(bf16[2016,128]{1,0:T(8,128)(2,1)} %get-tuple-element.70.refs_12_.refs_1_), channel_id=1, source_target_pairs={{0,3},{1,0},{2,1},{3,2},{4,7},{5,4},{6,5},{7,6},{8,11},{9,8},{10,9... | collective-permute-start | bytes 1548296 | tf_op jit(solution)/shard_map/ppermute | solution.py:546
  18.8 1.9 %collective-permute-start.1 = (bf16[2016,128]{1,0:T(8,128)(2,1)}, bf16[2016,128]{1,0:T(8,128)(2,1)S(1)}, u32[]{:S(2)}, u32[]{:S(2)}) collective-permute-start(bf16[2016,128]{1,0:T(8,128)(2,1)} %get-tuple-element.70.refs_12_.refs_1_), channel_id=1, source_target_pairs={{0,2},{1,3},{2,0},{3,1},{4,6},{5,7},{6,4},{7,5},{8,10},{9,11},{10,... | collective-permute-start | bytes 1548296 | tf_op jit(solution)/shard_map/ppermute | solution.py:546
  20.7 3.4 %collective-permute-start = (bf16[2016,128]{1,0:T(8,128)(2,1)}, bf16[2016,128]{1,0:T(8,128)(2,1)S(1)}, u32[]{:S(2)}, u32[]{:S(2)}) collective-permute-start(bf16[2016,128]{1,0:T(8,128)(2,1)} %get-tuple-element.70.refs_12_.refs_1_), channel_id=1, source_target_pairs={{0,1},{1,2},{2,3},{3,0},{4,5},{5,6},{6,7},{7,4},{8,9},{9,10},{10,1... | collective-permute-start | bytes 1548296 | tf_op jit(solution)/shard_map/ppermute | solution.py:546
  24.1 3.3 %collective-permute-start.4 = (bf16[32,512]{1,0:T(8,128)(2,1)}, bf16[32,512]{1,0:T(8,128)(2,1)S(1)}, u32[]{:S(2)}, u32[]{:S(2)}) collective-permute-start(bf16[32,512]{1,0:T(8,128)(2,1)} %get-tuple-element.72), channel_id=1, source_target_pairs={{0,500},{4,16},{8,508},{12,24},{16,4},{20,32},{24,12},{28,40},{32,... | collective-permute-start | bytes 98312 | tf_op jit(solution)/shard_map/ppermute | solution.py:494
  27.4 0.8 pad_maximum_fusion
  28.2 4.0 %collective-permute-start.5 = (bf16[64,512]{1,0:T(8,128)(2,1)S(1)}, bf16[64,512]{1,0:T(8,128)(2,1)S(1)}, u32[]{:S(2)}, u32[]{:S(2)}) collective-permute-start(bf16[64,512]{1,0:T(8,128)(2,1)S(1)} %pad_maximum_fusion), channel_id=1, source_target_pairs={{0,8},{4,12},{8,16},{12,20},{16,24},{20,28},{24,32},{28,36},{32,40... | collective-permute-start | bytes 196616 | tf_op jit(solution)/shard_map/ppermute | solution.py:494
  32.2 0.8 pad_maximum_fusion.1
  33.0 11.1 %collective-permute-start.6 = (bf16[64,512]{1,0:T(8,128)(2,1)S(1)}, bf16[64,512]{1,0:T(8,128)(2,1)S(1)}, u32[]{:S(2)}, u32[]{:S(2)}) collective-permute-start(bf16[64,512]{1,0:T(8,128)(2,1)S(1)} %pad_maximum_fusion.1), channel_id=1, source_target_pairs={{0,504},{4,508},{8,0},{12,4},{16,8},{20,12},{24,16},{28,20},{32,24... | collective-permute-start | bytes 196616 | tf_op jit(solution)/shard_map/ppermute | solution.py:494
  44.1 0.0 copy-start.6
  44.1 0.0 copy-start.11
  44.2 4.1 %collective-permute-start.8 = (bf16[2304,128]{1,0:T(8,128)(2,1)S(1)}, bf16[2304,128]{1,0:T(8,128)(2,1)S(1)}, u32[]{:S(2)}, u32[]{:S(2)}) collective-permute-start(bf16[2304,128]{1,0:T(8,128)(2,1)S(1)} %copy-done.4), channel_id=1, source_target_pairs={{0,3},{1,0},{2,1},{3,2},{4,7},{5,4},{6,5},{7,6},{8,11},{9,8},{10,9... | collective-permute-start | bytes 1769480 | tf_op jit(solution)/shard_map/ppermute | solution.py:546
  48.3 1.9 %collective-permute-start.7 = (bf16[2304,128]{1,0:T(8,128)(2,1)S(1)}, bf16[2304,128]{1,0:T(8,128)(2,1)S(1)}, u32[]{:S(2)}, u32[]{:S(2)}) collective-permute-start(bf16[2304,128]{1,0:T(8,128)(2,1)S(1)} %copy-done.4), channel_id=1, source_target_pairs={{0,1},{1,2},{2,3},{3,0},{4,5},{5,6},{6,7},{7,4},{8,9},{9,10},{10,1... | collective-permute-start | bytes 1769480 | tf_op jit(solution)/shard_map/ppermute | solution.py:546
  50.3 2.6 %shard_map.196 = (bf16[1152,512]{1,0:T(8,128)(2,1)S(1)}, bf16[1024,512]{1,0:T(8,128)(2,1)S(1)}, bf16[1024,512]{1,0:T(8,128)(2,1)S(1)}, bf16[128,512]{1,0:T(8,128...) custom-call(bf16[474,1024]{1,0:T(8,128)(2,1)S(1)} %bitcast.19, bf16[2016,128]{1,0:T(8,128)(2,1)S(1)} %copy-done.5, ...), custom_call_target="tpu_custom_call" | custom-call | flops 1500000000 | bytes 8835072 | tf_op jit(solution)/shard_map/pallas_call | solution.py:39
  53.0 4.6 %shard_map.197 = (bf16[2048,512]{1,0:T(8,128)(2,1)S(1)}, bf16[128,512]{1,0:T(8,128)(2,1)S(1)}, f32[256,512]{1,0:T(8,128)S(1)}) custom-call(bf16[1152,512]{1,0:T(8,128)(2,1)S(1)} %get-tuple-element.75.refs_0_, bf16[256,512]{1,0:T(8,128)(2,1)S(1)} %copy-done.6, s32[1,2048]{1,0:T(1,128)S(1)} %copy-done.11, s32[1,2048]{1,0:T(1,128)S(1)} %copy-done.12, ...), custom_call_target="tpu_custom_call" | custom-call | flops 5000000000 | bytes 4603904 | tf_op jit(solution)/shard_map/pallas_call | solution.py:39
  57.6 2.1 %collective-permute-done.8.refs_5_.refs_4_ = bf16[2304,128]{1,0:T(8,128)(2,1)S(1)} collective-permute-done((bf16[2304,128]{1,0:T(8,128)(2,1)S(1)}, bf16[2304,128]{1,0:T(8,128)(2,1)S(1)}, u32[]{:S(2)}, u32[]{:S(2)}) %collective-permute-start.8) | collective-permute-done | bytes 589856 | tf_op jit(solution)/shard_map/ppermute | solution.py:546
  59.7 4.8 %collective-permute-done.7.refs_4_.refs_1_ = bf16[2304,128]{1,0:T(8,128)(2,1)S(1)} collective-permute-done((bf16[2304,128]{1,0:T(8,128)(2,1)S(1)}, bf16[2304,128]{1,0:T(8,128)(2,1)S(1)}, u32[]{:S(2)}, u32[]{:S(2)}) %collective-permute-start.7) | collective-permute-done | bytes 589856 | tf_op jit(solution)/shard_map/ppermute | solution.py:546
  64.5 0.8 shard_map.198
  65.2 4.6 %collective-permute-start.9 = (bf16[24,512]{1,0:T(8,128)(2,1)S(1)}, bf16[24,512]{1,0:T(8,128)(2,1)S(1)}, u32[]{:S(2)}, u32[]{:S(2)}) collective-permute-start(bf16[24,512]{1,0:T(8,128)(2,1)S(1)} %get-tuple-element.83), channel_id=1, source_target_pairs={{0,4},{4,0},{8,12},{12,8},{16,20},{20,16},{24,28},{28,24},{32,36},... | collective-permute-start | bytes 73736 | tf_op jit(solution)/shard_map/ppermute | solution.py:494
  69.8 1.9 %collective-permute-start.11 = (bf16[1152,128]{1,0:T(8,128)(2,1)S(1)}, bf16[1152,128]{1,0:T(8,128)(2,1)S(1)}, u32[]{:S(2)}, u32[]{:S(2)}) collective-permute-start(bf16[1152,128]{1,0:T(8,128)(2,1)S(1)} %slice.61), channel_id=1, source_target_pairs={{0,3},{1,0},{2,1},{3,2},{4,7},{5,4},{6,5},{7,6},{8,11},{9,8},{10,9... | collective-permute-start | bytes 884744 | tf_op jit(solution)/shard_map/ppermute | solution.py:546
  71.8 3.4 %collective-permute-start.10 = (bf16[1152,128]{1,0:T(8,128)(2,1)S(1)}, bf16[1152,128]{1,0:T(8,128)(2,1)S(1)}, u32[]{:S(2)}, u32[]{:S(2)}) collective-permute-start(bf16[1152,128]{1,0:T(8,128)(2,1)S(1)} %slice.60), channel_id=1, source_target_pairs={{0,1},{1,2},{2,3},{3,0},{4,5},{5,6},{6,7},{7,4},{8,9},{9,10},{10,1... | collective-permute-start | bytes 884744 | tf_op jit(solution)/shard_map/ppermute | solution.py:546
  75.2 1.9 %collective-permute-start.12 = (bf16[8,512]{1,0:T(8,128)(2,1)S(1)}, bf16[8,512]{1,0:T(8,128)(2,1)S(1)}, u32[]{:S(2)}, u32[]{:S(2)}) collective-permute-start(bf16[8,512]{1,0:T(8,128)(2,1)S(1)} %get-tuple-element.88), channel_id=1, source_target_pairs={{0,500},{4,16},{8,508},{12,24},{16,4},{20,32},{24,12},{28,40},{32,... | collective-permute-start | bytes 24584 | tf_op jit(solution)/shard_map/ppermute | solution.py:494
  77.1 1.9 %collective-permute-start.13 = (bf16[16,512]{1,0:T(8,128)(2,1)S(1)}, bf16[16,512]{1,0:T(8,128)(2,1)S(1)}, u32[]{:S(2)}, u32[]{:S(2)}) collective-permute-start(bf16[16,512]{1,0:T(8,128)(2,1)S(1)} %pad_maximum_fusion.6.refs_4_.refs_5_), channel_id=1, source_target_pairs={{0,8},{4,12},{8,16},{12,20},{16,24},{20,28},{24,32},{28,36},{32,40... | collective-permute-start | bytes 49160 | tf_op jit(solution)/shard_map/ppermute | solution.py:494
  79.1 6.9 %collective-permute-start.14 = (bf16[16,512]{1,0:T(8,128)(2,1)S(1)}, bf16[16,512]{1,0:T(8,128)(2,1)S(1)}, u32[]{:S(2)}, u32[]{:S(2)}) collective-permute-start(bf16[16,512]{1,0:T(8,128)(2,1)S(1)} %pad_maximum_fusion.7.refs_5_.refs_6_), channel_id=1, source_target_pairs={{0,504},{4,508},{8,0},{12,4},{16,8},{20,12},{24,16},{28,20},{32,24... | collective-permute-start | bytes 49160 | tf_op jit(solution)/shard_map/ppermute | solution.py:494
  86.0 2.7 %shard_map.199 = (f32[256,512]{1,0:T(8,128)S(1)}, bf16[2048,512]{1,0:T(8,128)(2,1)S(1)}) custom-call(bf16[256,512]{1,0:T(8,128)(2,1)S(1)} %get-tuple-element.81.refs_0_, bf16[256,512]{1,0:T(8,128)(2,1)S(1)} %get-tuple-element.82.refs_1_, s32[1,2048]{1,0:T(1,128)S(1)} %copy-done.9, s32[1,2048]{1,0:T(1,128)S(1)} %copy-done.10, ...), custom_call_target="tpu_custom_call" | custom-call | flops 3000000000 | bytes 3162112 | tf_op jit(solution)/shard_map/pallas_call | solution.py:39
  88.7 0.6 shard_map.200.refs_4_.refs_2_.refs_10_.refs_5_.refs_6_.refs_3_
  89.4 0.1 copy-done.3
  89.4 1.1 shard_map.201
  90.5 4.7 %collective-permute-start.15 = (bf16[24,512]{1,0:T(8,128)(2,1)S(1)}, bf16[24,512]{1,0:T(8,128)(2,1)S(1)}, u32[]{:S(2)}, u32[]{:S(2)}) collective-permute-start(bf16[24,512]{1,0:T(8,128)(2,1)S(1)} %get-tuple-element.91), channel_id=1, source_target_pairs={{0,4},{4,0},{8,12},{12,8},{16,20},{20,16},{24,28},{28,24},{32,36},... | collective-permute-start | bytes 73736 | tf_op jit(solution)/shard_map/ppermute | solution.py:494
  95.2 1.9 %collective-permute-start.16 = (bf16[8,512]{1,0:T(8,128)(2,1)S(1)}, bf16[8,512]{1,0:T(8,128)(2,1)S(1)}, u32[]{:S(2)}, u32[]{:S(2)}) collective-permute-start(bf16[8,512]{1,0:T(8,128)(2,1)S(1)} %get-tuple-element.95), channel_id=1, source_target_pairs={{0,500},{4,16},{8,508},{12,24},{16,4},{20,32},{24,12},{28,40},{32,... | collective-permute-start | bytes 24584 | tf_op jit(solution)/shard_map/ppermute | solution.py:494
  97.2 1.9 %collective-permute-start.17 = (bf16[16,512]{1,0:T(8,128)(2,1)S(1)}, bf16[16,512]{1,0:T(8,128)(2,1)S(1)}, u32[]{:S(2)}, u32[]{:S(2)}) collective-permute-start(bf16[16,512]{1,0:T(8,128)(2,1)S(1)} %pad_maximum_fusion.8.refs_4_.refs_3_), channel_id=1, source_target_pairs={{0,8},{4,12},{8,16},{12,20},{16,24},{20,28},{24,32},{28,36},{32,40... | collective-permute-start | bytes 49160 | tf_op jit(solution)/shard_map/ppermute | solution.py:494
  99.1 6.7 %collective-permute-start.18 = (bf16[16,512]{1,0:T(8,128)(2,1)S(1)}, bf16[16,512]{1,0:T(8,128)(2,1)S(1)}, u32[]{:S(2)}, u32[]{:S(2)}) collective-permute-start(bf16[16,512]{1,0:T(8,128)(2,1)S(1)} %pad_maximum_fusion.9.refs_5_.refs_4_), channel_id=1, source_target_pairs={{0,504},{4,508},{8,0},{12,4},{16,8},{20,12},{24,16},{28,20},{32,24... | collective-permute-start | bytes 49160 | tf_op jit(solution)/shard_map/ppermute | solution.py:494
  105.8 2.7 %shard_map.202 = (f32[256,512]{1,0:T(8,128)S(1)}, bf16[2048,512]{1,0:T(8,128)(2,1)S(1)}) custom-call(bf16[256,512]{1,0:T(8,128)(2,1)S(1)} %get-tuple-element.89.refs_0_, bf16[256,512]{1,0:T(8,128)(2,1)S(1)} %get-tuple-element.90.refs_1_, s32[1,2048]{1,0:T(1,128)S(1)} %copy-done.9, s32[1,2048]{1,0:T(1,128)S(1)} %copy-done.10, ...), custom_call_target="tpu_custom_call" | custom-call | flops 3000000000 | bytes 3162112 | tf_op jit(solution)/shard_map/pallas_call | solution.py:39
  108.5 0.5 shard_map.204
  109.0 0.0 copy-start.7
  109.1 0.0 copy-start.8
  109.1 1.5 shard_map.203
  110.6 7.0 %shard_map.205 = (bf16[3072,512]{1,0:T(8,128)(2,1)S(1)}, bf16[3072,512]{1,0:T(8,128)(2,1)S(1)}, f32[256,512]{1,0:T(8,128)S(1)}, bf16[256,512]{1,0:T(8,128)(2,1)S...) custom-call(bf16[256,512]{1,0:T(8,128)(2,1)S(1)} %get-tuple-element., ...), custom_call_target="tpu_custom_call" | custom-call | flops 6000000000 | bytes 13254752 | tf_op jit(solution)/shard_map/pallas_call | solution.py:39
  117.6 2.8 %collective-permute-start.19 = (bf16[48,512]{1,0:T(8,128)(2,1)S(1)}, bf16[48,512]{1,0:T(8,128)(2,1)S(1)}, u32[]{:S(2)}, u32[]{:S(2)}) collective-permute-start(bf16[48,512]{1,0:T(8,128)(2,1)S(1)} %get-tuple-element.106.refs_5_), channel_id=1, source_target_pairs={{0,4},{4,0},{8,12},{12,8},{16,20},{20,16},{24,28},{28,24},{32,36},... | collective-permute-start | bytes 147464 | tf_op jit(solution)/shard_map/ppermute | solution.py:494
  120.4 2.3 %collective-permute-start.20 = (bf16[16,512]{1,0:T(8,128)(2,1)S(1)}, bf16[16,512]{1,0:T(8,128)(2,1)S(1)}, u32[]{:S(2)}, u32[]{:S(2)}) collective-permute-start(bf16[16,512]{1,0:T(8,128)(2,1)S(1)} %get-tuple-element.110.refs_6_), channel_id=1, source_target_pairs={{0,500},{4,16},{8,508},{12,24},{16,4},{20,32},{24,12},{28,40},{32,... | collective-permute-start | bytes 49160 | tf_op jit(solution)/shard_map/ppermute | solution.py:494
  122.7 2.6 %collective-permute-start.21 = (bf16[32,512]{1,0:T(8,128)(2,1)S(1)}, bf16[32,512]{1,0:T(8,128)(2,1)S(1)}, u32[]{:S(2)}, u32[]{:S(2)}) collective-permute-start(bf16[32,512]{1,0:T(8,128)(2,1)S(1)} %pad_maximum_fusion.2.refs_4_.refs_9_), channel_id=1, source_target_pairs={{0,8},{4,12},{8,16},{12,20},{16,24},{20,28},{24,32},{28,36},{32,40... | collective-permute-start | bytes 98312 | tf_op jit(solution)/shard_map/ppermute | solution.py:494
  125.3 6.5 %collective-permute-start.22 = (bf16[32,512]{1,0:T(8,128)(2,1)S(1)}, bf16[32,512]{1,0:T(8,128)(2,1)S(1)}, u32[]{:S(2)}, u32[]{:S(2)}) collective-permute-start(bf16[32,512]{1,0:T(8,128)(2,1)S(1)} %pad_maximum_fusion.3.refs_5_.refs_10_), channel_id=1, source_target_pairs={{0,504},{4,508},{8,0},{12,4},{16,8},{20,12},{24,16},{28,20},{32,24... | collective-permute-start | bytes 98312 | tf_op jit(solution)/shard_map/ppermute | solution.py:494
  131.9 1.9 %shard_map.207 = (bf16[256,512]{1,0:T(8,128)(2,1)S(1)}, f32[256,512]{1,0:T(8,128)S(1)}) custom-call(bf16[256,512]{1,0:T(8,128)(2,1)S(1)} %get-tuple-element.111.refs_0_, bf16[2048,512]{1,0:T(8,128)(2,1)S(1)} %get-tuple-element.112.refs_1_, s32[1,2048]{1,0:T(1,128)S(1)} %copy-done.9, s32[1,2048]{1,0:T(1,128)S(1)} %copy-done.10, s32[6,8,128]{2,1,0:T(8,128)S(1)} %copy-done.3, ...), custom_call_target="tpu_custom_call" | custom-call | flops 3000000000 | bytes 3284992 | tf_op jit(solution)/shard_map/pallas_call | solution.py:39
  133.8 2.0 %shard_map.206.refs_13_.refs_0_ = f32[1024,512]{1,0:T(8,128)S(1)} custom-call(bf16[3072,512]{1,0:T(8,128)(2,1)S(1)} %get-tuple-element.105.refs_0_, s32[24]{0:T(128)S(1)} %copy-done.13, s32[1,3072]{1,0:T(1,128)S(1)} %copy-done.8, s32[1,3072]{1,0:T(1,128)S(1)} %copy-done.7, bf16[32,512]{1,0:T(8,128)(2,1)S(1)} %pad_maximum_fusion.2.refs_4_.refs_9_, ...), custom_call_target="tpu_custom_call" | custom-call | flops 2000000000 | bytes 5267552 | tf_op jit(solution)/shard_map/pallas_call | solution.py:39
  135.9 0.9 shard_map.208
  136.8 3.6 %collective-permute-start.23 = (bf16[24,512]{1,0:T(8,128)(2,1)S(1)}, bf16[24,512]{1,0:T(8,128)(2,1)S(1)}, u32[]{:S(2)}, u32[]{:S(2)}) collective-permute-start(bf16[24,512]{1,0:T(8,128)(2,1)S(1)} %get-tuple-element.118.refs_5_), channel_id=1, source_target_pairs={{0,4},{4,0},{8,12},{12,8},{16,20},{20,16},{24,28},{28,24},{32,36},... | collective-permute-start | bytes 73736 | tf_op jit(solution)/shard_map/ppermute | solution.py:494
  140.4 1.9 %collective-permute-start.24 = (bf16[8,512]{1,0:T(8,128)(2,1)S(1)}, bf16[8,512]{1,0:T(8,128)(2,1)S(1)}, u32[]{:S(2)}, u32[]{:S(2)}) collective-permute-start(bf16[8,512]{1,0:T(8,128)(2,1)S(1)} %get-tuple-element.124.refs_6_), channel_id=1, source_target_pairs={{0,500},{4,16},{8,508},{12,24},{16,4},{20,32},{24,12},{28,40},{32,... | collective-permute-start | bytes 24584 | tf_op jit(solution)/shard_map/ppermute | solution.py:494
  142.3 6.3 %collective-permute-start.25 = (bf16[16,512]{1,0:T(8,128)(2,1)S(1)}, bf16[16,512]{1,0:T(8,128)(2,1)S(1)}, u32[]{:S(2)}, u32[]{:S(2)}) collective-permute-start(bf16[16,512]{1,0:T(8,128)(2,1)S(1)} %pad_maximum_fusion.10.refs_12_.refs_9_), channel_id=1, source_target_pairs={{0,504},{4,508},{8,0},{12,4},{16,8},{20,12},{24,16},{28,20},{32,24... | collective-permute-start | bytes 49160 | tf_op jit(solution)/shard_map/ppermute | solution.py:494
  148.6 1.9 %collective-permute-start.26 = (bf16[16,512]{1,0:T(8,128)(2,1)S(1)}, bf16[16,512]{1,0:T(8,128)(2,1)S(1)}, u32[]{:S(2)}, u32[]{:S(2)}) collective-permute-start(bf16[16,512]{1,0:T(8,128)(2,1)S(1)} %pad_maximum_fusion.11.refs_13_.refs_10_), channel_id=1, source_target_pairs={{0,8},{4,12},{8,16},{12,20},{16,24},{20,28},{24,32},{28,36},{32,40... | collective-permute-start | bytes 49160 | tf_op jit(solution)/shard_map/ppermute | solution.py:494
  150.6 1.9 %shard_map.210 = (bf16[256,512]{1,0:T(8,128)(2,1)S(1)}, f32[256,512]{1,0:T(8,128)S(1)}) custom-call(bf16[256,512]{1,0:T(8,128)(2,1)S(1)} %get-tuple-element.122.refs_0_, bf16[2048,512]{1,0:T(8,128)(2,1)S(1)} %get-tuple-element.123.refs_1_, s32[1,2048]{1,0:T(1,128)S(1)} %copy-done.9, s32[1,2048]{1,0:T(1,128)S(1)} %copy-done.10, s32[6,8,128]{2,1,0:T(8,128)S(1)} %copy-done.3, ...), custom_call_target="tpu_custom_call" | custom-call | flops 3000000000 | bytes 3235840 | tf_op jit(solution)/shard_map/pallas_call | solution.py:39
  152.5 2.9 %shard_map.209 = (bf16[1024,512]{1,0:T(8,128)(2,1)S(1)}, bf16[128,512]{1,0:T(8,128)(2,1)S(1)}) custom-call(bf16[3072,512]{1,0:T(8,128)(2,1)S(1)} %get-tuple-element.109.refs_0_, bf16[1024,512]{1,0:T(8,128)(2,1)S(1)} %get-tuple-element.97.refs_1_, bf16[1024,512]{1,0:T(8,128)(2,1)S(1)} %get-tuple-element.99.refs_2_, s32[24]{0:T(128)S(1)} %copy-done.13, ...), custom_call_target="tpu_custom_call" | custom-call | flops 2500000000 | bytes 6996064 | tf_op jit(solution)/shard_map/pallas_call | solution.py:39
  155.4 1.1 collective-permute-done.26.refs_12_
  156.4 0.9 shard_map.211
  157.4 1.9 %collective-permute-start.27 = (bf16[48,512]{1,0:T(8,128)(2,1)S(1)}, bf16[48,512]{1,0:T(8,128)(2,1)S(1)}, u32[]{:S(2)}, u32[]{:S(2)}) collective-permute-start(bf16[48,512]{1,0:T(8,128)(2,1)S(1)} %get-tuple-element.131), channel_id=1, source_target_pairs={{0,4},{4,0},{8,12},{12,8},{16,20},{20,16},{24,28},{28,24},{32,36},... | collective-permute-start | bytes 147464 | tf_op jit(solution)/shard_map/ppermute | solution.py:494
  159.3 2.1 %collective-permute-start.28 = (bf16[16,512]{1,0:T(8,128)(2,1)S(1)}, bf16[16,512]{1,0:T(8,128)(2,1)S(1)}, u32[]{:S(2)}, u32[]{:S(2)}) collective-permute-start(bf16[16,512]{1,0:T(8,128)(2,1)S(1)} %get-tuple-element.137), channel_id=1, source_target_pairs={{0,500},{4,16},{8,508},{12,24},{16,4},{20,32},{24,12},{28,40},{32,... | collective-permute-start | bytes 49160 | tf_op jit(solution)/shard_map/ppermute | solution.py:494
  161.5 7.0 %collective-permute-start.29 = (bf16[32,512]{1,0:T(8,128)(2,1)S(1)}, bf16[32,512]{1,0:T(8,128)(2,1)S(1)}, u32[]{:S(2)}, u32[]{:S(2)}) collective-permute-start(bf16[32,512]{1,0:T(8,128)(2,1)S(1)} %pad_maximum_fusion.4.refs_4_), channel_id=1, source_target_pairs={{0,504},{4,508},{8,0},{12,4},{16,8},{20,12},{24,16},{28,20},{32,24... | collective-permute-start | bytes 98312 | tf_op jit(solution)/shard_map/ppermute | solution.py:494
  168.4 1.9 %collective-permute-start.30 = (bf16[32,512]{1,0:T(8,128)(2,1)S(1)}, bf16[32,512]{1,0:T(8,128)(2,1)S(1)}, u32[]{:S(2)}, u32[]{:S(2)}) collective-permute-start(bf16[32,512]{1,0:T(8,128)(2,1)S(1)} %pad_maximum_fusion.5.refs_5_), channel_id=1, source_target_pairs={{0,8},{4,12},{8,16},{12,20},{16,24},{20,28},{24,32},{28,36},{32,40... | collective-permute-start | bytes 98312 | tf_op jit(solution)/shard_map/ppermute | solution.py:494
  170.4 3.6 %shard_map.213.refs_0_ = bf16[1024,512]{1,0:T(8,128)(2,1)S(1)} custom-call(bf16[256,512]{1,0:T(8,128)(2,1)S(1)} %get-tuple-element.134.refs_0_, bf16[2048,512]{1,0:T(8,128)(2,1)S(1)} %get-tuple-element.135.refs_1_, s32[1,2048]{1,0:T(1,128)S(1)} %copy-done.11, s32[1,2048]{1,0:T(1,128)S(1)} %copy-done.12, bf16[32,512]{1,0:T(8,128)(2,1)S(1)} %pad_maximum_fusion.4.refs_4_, ...), custom_call_target="tpu_custom_call" | custom-call | flops 4000000000 | bytes 3424256 | tf_op jit(solution)/shard_map/pallas_call | solution.py:39
  174.0 1.5 shard_map.212
  175.5 1.0 collective-permute-done.30.refs_8_
  176.5 2.7 %shard_map.214 = bf16[474,1024]{1,0:T(8,128)(2,1)} custom-call(bf16[1024,512]{1,0:T(8,128)(2,1)S(1)} %shard_map.213.refs_0_, bf16[2016,512]{1,0:T(8,128)(2,1)S(1)} %get-tuple-element.78.refs_3_.refs_5_.refs_6_.refs_1_, bf16[1024,512]{1,0:T(8,128)(2,1)S(1)} %get-tuple-element.136.refs_2_, bf16[1024,512]{1,0:T(8,128)(2,1)S(1)} %get-tuple-element.130.refs_13_.refs_3_, ...), custom_call_target="tpu_custom_call" | custom-call | flops 1500000000 | bytes 6336512 | tf_op jit(solution)/shard_map/pallas_call | solution.py:39
  (67 shorter events, 0.2 us)
Async XLA Ops:
  0.6 49.6 %copy-start.2 = (bf16[1,1024,474]{1,2,0:T(8,128)(2,1)S(1)}, bf16[1,1024,474]{1,2,0:T(8,128)(2,1)}, u32[]{:S(2)}) copy-start(bf16[1,1024,474]{1,2,0:T(8,128)(2,1)} %param.19) | copy-start | bytes 2912260
  3.9 40.2 %copy-start.4 = (bf16[2304,128]{1,0:T(8,128)(2,1)S(1)}, bf16[2304,128]{1,0:T(8,128)(2,1)}, u32[]{:S(2)}) copy-start(bf16[2304,128]{1,0:T(8,128)(2,1)} %get-tuple-element.80.refs_0_) | copy-start | bytes 1769476
  3.9 46.3 %copy-start.5 = (bf16[2016,128]{1,0:T(8,128)(2,1)S(1)}, bf16[2016,128]{1,0:T(8,128)(2,1)}, u32[]{:S(2)}) copy-start(bf16[2016,128]{1,0:T(8,128)(2,1)} %get-tuple-element.70.refs_12_.refs_1_) | copy-start | bytes 1548292
  8.1 19.3 %collective-permute-start.3 = (bf16[96,512]{1,0:T(8,128)(2,1)}, bf16[96,512]{1,0:T(8,128)(2,1)S(1)}, u32[]{:S(2)}, u32[]{:S(2)}) collective-permute-start(bf16[96,512]{1,0:T(8,128)(2,1)} %get-tuple-element.71), channel_id=1, source_target_pairs={{0,4},{4,0},{8,12},{12,8},{16,20},{20,16},{24,28},{28,24},{32,36},... | collective-permute-start | bytes 294920 | tf_op jit(solution)/shard_map/ppermute | solution.py:494
  16.9 33.3 %collective-permute-start.2 = (bf16[2016,128]{1,0:T(8,128)(2,1)}, bf16[2016,128]{1,0:T(8,128)(2,1)S(1)}, u32[]{:S(2)}, u32[]{:S(2)}) collective-permute-start(bf16[2016,128]{1,0:T(8,128)(2,1)} %get-tuple-element.70.refs_12_.refs_1_), channel_id=1, source_target_pairs={{0,3},{1,0},{2,1},{3,2},{4,7},{5,4},{6,5},{7,6},{8,11},{9,8},{10,9... | collective-permute-start | bytes 1548296 | tf_op jit(solution)/shard_map/ppermute | solution.py:546
  18.8 31.4 %collective-permute-start.1 = (bf16[2016,128]{1,0:T(8,128)(2,1)}, bf16[2016,128]{1,0:T(8,128)(2,1)S(1)}, u32[]{:S(2)}, u32[]{:S(2)}) collective-permute-start(bf16[2016,128]{1,0:T(8,128)(2,1)} %get-tuple-element.70.refs_12_.refs_1_), channel_id=1, source_target_pairs={{0,2},{1,3},{2,0},{3,1},{4,6},{5,7},{6,4},{7,5},{8,10},{9,11},{10,... | collective-permute-start | bytes 1548296 | tf_op jit(solution)/shard_map/ppermute | solution.py:546
  20.7 29.5 %collective-permute-start = (bf16[2016,128]{1,0:T(8,128)(2,1)}, bf16[2016,128]{1,0:T(8,128)(2,1)S(1)}, u32[]{:S(2)}, u32[]{:S(2)}) collective-permute-start(bf16[2016,128]{1,0:T(8,128)(2,1)} %get-tuple-element.70.refs_12_.refs_1_), channel_id=1, source_target_pairs={{0,1},{1,2},{2,3},{3,0},{4,5},{5,6},{6,7},{7,4},{8,9},{9,10},{10,1... | collective-permute-start | bytes 1548296 | tf_op jit(solution)/shard_map/ppermute | solution.py:546
  24.1 8.9 %collective-permute-start.4 = (bf16[32,512]{1,0:T(8,128)(2,1)}, bf16[32,512]{1,0:T(8,128)(2,1)S(1)}, u32[]{:S(2)}, u32[]{:S(2)}) collective-permute-start(bf16[32,512]{1,0:T(8,128)(2,1)} %get-tuple-element.72), channel_id=1, source_target_pairs={{0,500},{4,16},{8,508},{12,24},{16,4},{20,32},{24,12},{28,40},{32,... | collective-permute-start | bytes 98312 | tf_op jit(solution)/shard_map/ppermute | solution.py:494
  28.2 15.9 %collective-permute-start.5 = (bf16[64,512]{1,0:T(8,128)(2,1)S(1)}, bf16[64,512]{1,0:T(8,128)(2,1)S(1)}, u32[]{:S(2)}, u32[]{:S(2)}) collective-permute-start(bf16[64,512]{1,0:T(8,128)(2,1)S(1)} %pad_maximum_fusion), channel_id=1, source_target_pairs={{0,8},{4,12},{8,16},{12,20},{16,24},{20,28},{24,32},{28,36},{32,40... | collective-permute-start | bytes 196616 | tf_op jit(solution)/shard_map/ppermute | solution.py:494
  33.0 15.3 %collective-permute-start.6 = (bf16[64,512]{1,0:T(8,128)(2,1)S(1)}, bf16[64,512]{1,0:T(8,128)(2,1)S(1)}, u32[]{:S(2)}, u32[]{:S(2)}) collective-permute-start(bf16[64,512]{1,0:T(8,128)(2,1)S(1)} %pad_maximum_fusion.1), channel_id=1, source_target_pairs={{0,504},{4,508},{8,0},{12,4},{16,8},{20,12},{24,16},{28,20},{32,24... | collective-permute-start | bytes 196616 | tf_op jit(solution)/shard_map/ppermute | solution.py:494
  44.1 8.8 %copy-start = (s32[6,128,128]{2,1,0:T(8,128)S(1)}, s32[6,128,128]{2,1,0:T(8,128)}, u32[]{:S(2)}) copy-start(s32[6,128,128]{2,1,0:T(8,128)} %get-tuple-element.76.refs_4_.refs_2_.refs_8_.refs_3_.refs_6_) | copy-start | bytes 1179652
  44.1 8.8 %copy-start.6 = (bf16[256,512]{1,0:T(8,128)(2,1)S(1)}, bf16[256,512]{1,0:T(8,128)(2,1)}, u32[]{:S(2)}) copy-start(bf16[256,512]{1,0:T(8,128)(2,1)} %refs_1_.3) | copy-start | bytes 786436
  44.1 8.8 %copy-start.11 = (s32[1,2048]{1,0:T(1,128)S(1)}, s32[1,2048]{1,0:T(1,128)}, u32[]{:S(2)}) copy-start(s32[1,2048]{1,0:T(1,128)} %refs_2_.15) | copy-start | bytes 24580
  44.1 8.8 %copy-start.12 = (s32[1,2048]{1,0:T(1,128)S(1)}, s32[1,2048]{1,0:T(1,128)}, u32[]{:S(2)}) copy-start(s32[1,2048]{1,0:T(1,128)} %refs_3_.15) | copy-start | bytes 24580
  44.2 15.5 %collective-permute-start.8 = (bf16[2304,128]{1,0:T(8,128)(2,1)S(1)}, bf16[2304,128]{1,0:T(8,128)(2,1)S(1)}, u32[]{:S(2)}, u32[]{:S(2)}) collective-permute-start(bf16[2304,128]{1,0:T(8,128)(2,1)S(1)} %copy-done.4), channel_id=1, source_target_pairs={{0,3},{1,0},{2,1},{3,2},{4,7},{5,4},{6,5},{7,6},{8,11},{9,8},{10,9... | collective-permute-start | bytes 1769480 | tf_op jit(solution)/shard_map/ppermute | solution.py:546
  48.3 16.2 %collective-permute-start.7 = (bf16[2304,128]{1,0:T(8,128)(2,1)S(1)}, bf16[2304,128]{1,0:T(8,128)(2,1)S(1)}, u32[]{:S(2)}, u32[]{:S(2)}) collective-permute-start(bf16[2304,128]{1,0:T(8,128)(2,1)S(1)} %copy-done.4), channel_id=1, source_target_pairs={{0,1},{1,2},{2,3},{3,0},{4,5},{5,6},{6,7},{7,4},{8,9},{9,10},{10,1... | collective-permute-start | bytes 1769480 | tf_op jit(solution)/shard_map/ppermute | solution.py:546
  64.5 21.5 %copy-start.9 = (s32[1,2048]{1,0:T(1,128)S(1)}, s32[1,2048]{1,0:T(1,128)}, u32[]{:S(2)}) copy-start(s32[1,2048]{1,0:T(1,128)} %refs_2_.14) | copy-start | bytes 24580
  64.5 21.5 %copy-start.10 = (s32[1,2048]{1,0:T(1,128)S(1)}, s32[1,2048]{1,0:T(1,128)}, u32[]{:S(2)}) copy-start(s32[1,2048]{1,0:T(1,128)} %refs_3_.14) | copy-start | bytes 24580
  65.2 11.9 %collective-permute-start.9 = (bf16[24,512]{1,0:T(8,128)(2,1)S(1)}, bf16[24,512]{1,0:T(8,128)(2,1)S(1)}, u32[]{:S(2)}, u32[]{:S(2)}) collective-permute-start(bf16[24,512]{1,0:T(8,128)(2,1)S(1)} %get-tuple-element.83), channel_id=1, source_target_pairs={{0,4},{4,0},{8,12},{12,8},{16,20},{20,16},{24,28},{28,24},{32,36},... | collective-permute-start | bytes 73736 | tf_op jit(solution)/shard_map/ppermute | solution.py:494
  69.8 18.8 %collective-permute-start.11 = (bf16[1152,128]{1,0:T(8,128)(2,1)S(1)}, bf16[1152,128]{1,0:T(8,128)(2,1)S(1)}, u32[]{:S(2)}, u32[]{:S(2)}) collective-permute-start(bf16[1152,128]{1,0:T(8,128)(2,1)S(1)} %slice.61), channel_id=1, source_target_pairs={{0,3},{1,0},{2,1},{3,2},{4,7},{5,4},{6,5},{7,6},{8,11},{9,8},{10,9... | collective-permute-start | bytes 884744 | tf_op jit(solution)/shard_map/ppermute | solution.py:546
  71.8 16.9 %collective-permute-start.10 = (bf16[1152,128]{1,0:T(8,128)(2,1)S(1)}, bf16[1152,128]{1,0:T(8,128)(2,1)S(1)}, u32[]{:S(2)}, u32[]{:S(2)}) collective-permute-start(bf16[1152,128]{1,0:T(8,128)(2,1)S(1)} %slice.60), channel_id=1, source_target_pairs={{0,1},{1,2},{2,3},{3,0},{4,5},{5,6},{6,7},{7,4},{8,9},{9,10},{10,1... | collective-permute-start | bytes 884744 | tf_op jit(solution)/shard_map/ppermute | solution.py:546
  75.2 14.2 %collective-permute-start.12 = (bf16[8,512]{1,0:T(8,128)(2,1)S(1)}, bf16[8,512]{1,0:T(8,128)(2,1)S(1)}, u32[]{:S(2)}, u32[]{:S(2)}) collective-permute-start(bf16[8,512]{1,0:T(8,128)(2,1)S(1)} %get-tuple-element.88), channel_id=1, source_target_pairs={{0,500},{4,16},{8,508},{12,24},{16,4},{20,32},{24,12},{28,40},{32,... | collective-permute-start | bytes 24584 | tf_op jit(solution)/shard_map/ppermute | solution.py:494
  77.1 12.2 %collective-permute-start.13 = (bf16[16,512]{1,0:T(8,128)(2,1)S(1)}, bf16[16,512]{1,0:T(8,128)(2,1)S(1)}, u32[]{:S(2)}, u32[]{:S(2)}) collective-permute-start(bf16[16,512]{1,0:T(8,128)(2,1)S(1)} %pad_maximum_fusion.6.refs_4_.refs_5_), channel_id=1, source_target_pairs={{0,8},{4,12},{8,16},{12,20},{16,24},{20,28},{24,32},{28,36},{32,40... | collective-permute-start | bytes 49160 | tf_op jit(solution)/shard_map/ppermute | solution.py:494
  79.1 10.3 %collective-permute-start.14 = (bf16[16,512]{1,0:T(8,128)(2,1)S(1)}, bf16[16,512]{1,0:T(8,128)(2,1)S(1)}, u32[]{:S(2)}, u32[]{:S(2)}) collective-permute-start(bf16[16,512]{1,0:T(8,128)(2,1)S(1)} %pad_maximum_fusion.7.refs_5_.refs_6_), channel_id=1, source_target_pairs={{0,504},{4,508},{8,0},{12,4},{16,8},{20,12},{24,16},{28,20},{32,24... | collective-permute-start | bytes 49160 | tf_op jit(solution)/shard_map/ppermute | solution.py:494
  88.7 0.7 copy-start.3
  90.5 6.7 %collective-permute-start.15 = (bf16[24,512]{1,0:T(8,128)(2,1)S(1)}, bf16[24,512]{1,0:T(8,128)(2,1)S(1)}, u32[]{:S(2)}, u32[]{:S(2)}) collective-permute-start(bf16[24,512]{1,0:T(8,128)(2,1)S(1)} %get-tuple-element.91), channel_id=1, source_target_pairs={{0,4},{4,0},{8,12},{12,8},{16,20},{20,16},{24,28},{28,24},{32,36},... | collective-permute-start | bytes 73736 | tf_op jit(solution)/shard_map/ppermute | solution.py:494
  95.2 13.9 %collective-permute-start.16 = (bf16[8,512]{1,0:T(8,128)(2,1)S(1)}, bf16[8,512]{1,0:T(8,128)(2,1)S(1)}, u32[]{:S(2)}, u32[]{:S(2)}) collective-permute-start(bf16[8,512]{1,0:T(8,128)(2,1)S(1)} %get-tuple-element.95), channel_id=1, source_target_pairs={{0,500},{4,16},{8,508},{12,24},{16,4},{20,32},{24,12},{28,40},{32,... | collective-permute-start | bytes 24584 | tf_op jit(solution)/shard_map/ppermute | solution.py:494
  97.2 11.9 %collective-permute-start.17 = (bf16[16,512]{1,0:T(8,128)(2,1)S(1)}, bf16[16,512]{1,0:T(8,128)(2,1)S(1)}, u32[]{:S(2)}, u32[]{:S(2)}) collective-permute-start(bf16[16,512]{1,0:T(8,128)(2,1)S(1)} %pad_maximum_fusion.8.refs_4_.refs_3_), channel_id=1, source_target_pairs={{0,8},{4,12},{8,16},{12,20},{16,24},{20,28},{24,32},{28,36},{32,40... | collective-permute-start | bytes 49160 | tf_op jit(solution)/shard_map/ppermute | solution.py:494
  99.1 10.0 %collective-permute-start.18 = (bf16[16,512]{1,0:T(8,128)(2,1)S(1)}, bf16[16,512]{1,0:T(8,128)(2,1)S(1)}, u32[]{:S(2)}, u32[]{:S(2)}) collective-permute-start(bf16[16,512]{1,0:T(8,128)(2,1)S(1)} %pad_maximum_fusion.9.refs_5_.refs_4_), channel_id=1, source_target_pairs={{0,504},{4,508},{8,0},{12,4},{16,8},{20,12},{24,16},{28,20},{32,24... | collective-permute-start | bytes 49160 | tf_op jit(solution)/shard_map/ppermute | solution.py:494
  105.8 2.7 %copy-start.1 = (bf16[1,1024,227]{1,2,0:T(8,128)(2,1)S(1)}, bf16[1,1024,227]{1,2,0:T(8,128)(2,1)}, u32[]{:S(2)}) copy-start(bf16[1,1024,227]{1,2,0:T(8,128)(2,1)} %param.28) | copy-start | bytes 1394692
  109.0 1.5 copy-start.7
  109.1 1.5 copy-start.8
  109.1 1.5 copy-start.13
  117.6 5.1 %collective-permute-start.19 = (bf16[48,512]{1,0:T(8,128)(2,1)S(1)}, bf16[48,512]{1,0:T(8,128)(2,1)S(1)}, u32[]{:S(2)}, u32[]{:S(2)}) collective-permute-start(bf16[48,512]{1,0:T(8,128)(2,1)S(1)} %get-tuple-element.106.refs_5_), channel_id=1, source_target_pairs={{0,4},{4,0},{8,12},{12,8},{16,20},{20,16},{24,28},{28,24},{32,36},... | collective-permute-start | bytes 147464 | tf_op jit(solution)/shard_map/ppermute | solution.py:494
  120.4 15.4 %collective-permute-start.20 = (bf16[16,512]{1,0:T(8,128)(2,1)S(1)}, bf16[16,512]{1,0:T(8,128)(2,1)S(1)}, u32[]{:S(2)}, u32[]{:S(2)}) collective-permute-start(bf16[16,512]{1,0:T(8,128)(2,1)S(1)} %get-tuple-element.110.refs_6_), channel_id=1, source_target_pairs={{0,500},{4,16},{8,508},{12,24},{16,4},{20,32},{24,12},{28,40},{32,... | collective-permute-start | bytes 49160 | tf_op jit(solution)/shard_map/ppermute | solution.py:494
  122.7 13.1 %collective-permute-start.21 = (bf16[32,512]{1,0:T(8,128)(2,1)S(1)}, bf16[32,512]{1,0:T(8,128)(2,1)S(1)}, u32[]{:S(2)}, u32[]{:S(2)}) collective-permute-start(bf16[32,512]{1,0:T(8,128)(2,1)S(1)} %pad_maximum_fusion.2.refs_4_.refs_9_), channel_id=1, source_target_pairs={{0,8},{4,12},{8,16},{12,20},{16,24},{20,28},{24,32},{28,36},{32,40... | collective-permute-start | bytes 98312 | tf_op jit(solution)/shard_map/ppermute | solution.py:494
  125.3 10.5 %collective-permute-start.22 = (bf16[32,512]{1,0:T(8,128)(2,1)S(1)}, bf16[32,512]{1,0:T(8,128)(2,1)S(1)}, u32[]{:S(2)}, u32[]{:S(2)}) collective-permute-start(bf16[32,512]{1,0:T(8,128)(2,1)S(1)} %pad_maximum_fusion.3.refs_5_.refs_10_), channel_id=1, source_target_pairs={{0,504},{4,508},{8,0},{12,4},{16,8},{20,12},{24,16},{28,20},{32,24... | collective-permute-start | bytes 98312 | tf_op jit(solution)/shard_map/ppermute | solution.py:494
  136.8 5.5 %collective-permute-start.23 = (bf16[24,512]{1,0:T(8,128)(2,1)S(1)}, bf16[24,512]{1,0:T(8,128)(2,1)S(1)}, u32[]{:S(2)}, u32[]{:S(2)}) collective-permute-start(bf16[24,512]{1,0:T(8,128)(2,1)S(1)} %get-tuple-element.118.refs_5_), channel_id=1, source_target_pairs={{0,4},{4,0},{8,12},{12,8},{16,20},{20,16},{24,28},{28,24},{32,36},... | collective-permute-start | bytes 73736 | tf_op jit(solution)/shard_map/ppermute | solution.py:494
  140.4 15.0 %collective-permute-start.24 = (bf16[8,512]{1,0:T(8,128)(2,1)S(1)}, bf16[8,512]{1,0:T(8,128)(2,1)S(1)}, u32[]{:S(2)}, u32[]{:S(2)}) collective-permute-start(bf16[8,512]{1,0:T(8,128)(2,1)S(1)} %get-tuple-element.124.refs_6_), channel_id=1, source_target_pairs={{0,500},{4,16},{8,508},{12,24},{16,4},{20,32},{24,12},{28,40},{32,... | collective-permute-start | bytes 24584 | tf_op jit(solution)/shard_map/ppermute | solution.py:494
  142.3 13.0 %collective-permute-start.25 = (bf16[16,512]{1,0:T(8,128)(2,1)S(1)}, bf16[16,512]{1,0:T(8,128)(2,1)S(1)}, u32[]{:S(2)}, u32[]{:S(2)}) collective-permute-start(bf16[16,512]{1,0:T(8,128)(2,1)S(1)} %pad_maximum_fusion.10.refs_12_.refs_9_), channel_id=1, source_target_pairs={{0,504},{4,508},{8,0},{12,4},{16,8},{20,12},{24,16},{28,20},{32,24... | collective-permute-start | bytes 49160 | tf_op jit(solution)/shard_map/ppermute | solution.py:494
  148.6 7.8 %collective-permute-start.26 = (bf16[16,512]{1,0:T(8,128)(2,1)S(1)}, bf16[16,512]{1,0:T(8,128)(2,1)S(1)}, u32[]{:S(2)}, u32[]{:S(2)}) collective-permute-start(bf16[16,512]{1,0:T(8,128)(2,1)S(1)} %pad_maximum_fusion.11.refs_13_.refs_10_), channel_id=1, source_target_pairs={{0,8},{4,12},{8,16},{12,20},{16,24},{20,28},{24,32},{28,36},{32,40... | collective-permute-start | bytes 49160 | tf_op jit(solution)/shard_map/ppermute | solution.py:494
  157.4 4.1 %collective-permute-start.27 = (bf16[48,512]{1,0:T(8,128)(2,1)S(1)}, bf16[48,512]{1,0:T(8,128)(2,1)S(1)}, u32[]{:S(2)}, u32[]{:S(2)}) collective-permute-start(bf16[48,512]{1,0:T(8,128)(2,1)S(1)} %get-tuple-element.131), channel_id=1, source_target_pairs={{0,4},{4,0},{8,12},{12,8},{16,20},{20,16},{24,28},{28,24},{32,36},... | collective-permute-start | bytes 147464 | tf_op jit(solution)/shard_map/ppermute | solution.py:494
  159.3 16.2 %collective-permute-start.28 = (bf16[16,512]{1,0:T(8,128)(2,1)S(1)}, bf16[16,512]{1,0:T(8,128)(2,1)S(1)}, u32[]{:S(2)}, u32[]{:S(2)}) collective-permute-start(bf16[16,512]{1,0:T(8,128)(2,1)S(1)} %get-tuple-element.137), channel_id=1, source_target_pairs={{0,500},{4,16},{8,508},{12,24},{16,4},{20,32},{24,12},{28,40},{32,... | collective-permute-start | bytes 49160 | tf_op jit(solution)/shard_map/ppermute | solution.py:494
  161.5 14.0 %collective-permute-start.29 = (bf16[32,512]{1,0:T(8,128)(2,1)S(1)}, bf16[32,512]{1,0:T(8,128)(2,1)S(1)}, u32[]{:S(2)}, u32[]{:S(2)}) collective-permute-start(bf16[32,512]{1,0:T(8,128)(2,1)S(1)} %pad_maximum_fusion.4.refs_4_), channel_id=1, source_target_pairs={{0,504},{4,508},{8,0},{12,4},{16,8},{20,12},{24,16},{28,20},{32,24... | collective-permute-start | bytes 98312 | tf_op jit(solution)/shard_map/ppermute | solution.py:494
  168.4 8.0 %collective-permute-start.30 = (bf16[32,512]{1,0:T(8,128)(2,1)S(1)}, bf16[32,512]{1,0:T(8,128)(2,1)S(1)}, u32[]{:S(2)}, u32[]{:S(2)}) collective-permute-start(bf16[32,512]{1,0:T(8,128)(2,1)S(1)} %pad_maximum_fusion.5.refs_5_), channel_id=1, source_target_pairs={{0,8},{4,12},{8,16},{12,20},{16,24},{20,28},{24,32},{28,36},{32,40... | collective-permute-start | bytes 98312 | tf_op jit(solution)/shard_map/ppermute | solution.py:494

commit v5 on v3

--- a/solution.py
+++ b/solution.py
@@ -349,7 +349,7 @@
     count = proj.shape[0]
     last_start = hidden.shape[0] - BLOCK
 
-    @pl.loop(0, src.shape[1] // BLOCK, unroll=4)
+    @pl.loop(0, src.shape[1] // BLOCK, unroll=6)
     def _(b):
         at = at_block(b)
         dst_row = line(dst, b)
@@ -384,7 +384,7 @@
 def add_by_row(total, values, starts, src, dst, own):
     rows = HALF + 16
 
-    @pl.loop(0, src.shape[1] // HALF, unroll=4)
+    @pl.loop(0, src.shape[1] // HALF, unroll=8)
     def _(b):
         dst_row = jnp.where(line(src, b, HALF) < own, line(dst, b, HALF), -(1 << 20))
         start = pl.multiple_of(starts[b], 16)

time: 178 us -> 178 us (level)
  no operation moved by 1% of the time
where the time goes in v5:
time: 178 us; the launch traced here: 177 us
  starting transfers between devices  117 us (66%)
  Pallas kernels  47 us (26%)
  waiting for transfers between devices  8.67 us (5%)
    ppermute x24, starting transfers between devices, permuted(): lax.ppermute(block, 'dom', [(i, route(i) % size) for i in range(size)])  98.4 us
    pallas_call x20, Pallas kernels, call(): pl.pallas_call(kernel, out_shape=tuple((o for _, o in outs)), in_specs=[p...  47 us
    ppermute x7, starting transfers between devices, along(): return lax.ppermute(block, 'phase', [(i, (i + away) % 4) for i in range(4)])  18.5 us
    ppermute x7, waiting for transfers between devices, along(): return lax.ppermute(block, 'phase', [(i, (i + away) % 4) for i in range(4)])  6.09 us
  transfers between devices with their start and end apart: 31, of which 4 were waited for; matrix products, arithmetic and copies ran while one was open for 1% of the time, Pallas kernels for 16%

profile of v5, /device:TPU:1, one launch (start us, length us, event | category | flops | bytes accessed | tf_op | source)
XLA Modules:
  0.0 176.9 jit_solution(594470048137933821)
XLA Ops:
  0.6 4.7 %shard_map.194 = (s32[6,128,128]{2,1,0:T(8,128)}, s32[6,8,128]{2,1,0:T(8,128)}, s32[24]{0:T(128)}, bf16[2016,128]{1,0:T(8,128)(2,1)}, bf16[2304,128]{1,0:T(8,128...) custom-call(s32[1,3072]{1,0:T(1,128)} %refs_5_.1, ...), custom_call_target="tpu_custom_call" | custom-call | flops 400000000 | bytes 4323328 | tf_op jit(solution)/shard_map/pallas_call | solution.py:39
  5.3 8.8 %collective-permute-start.3 = (bf16[96,512]{1,0:T(8,128)(2,1)}, bf16[96,512]{1,0:T(8,128)(2,1)S(1)}, u32[]{:S(2)}, u32[]{:S(2)}) collective-permute-start(bf16[96,512]{1,0:T(8,128)(2,1)} %get-tuple-element.71), channel_id=1, source_target_pairs={{0,4},{4,0},{8,12},{12,8},{16,20},{20,16},{24,28},{28,24},{32,36},... | collective-permute-start | bytes 294920 | tf_op jit(solution)/shard_map/ppermute | solution.py:491
  14.1 1.9 %collective-permute-start.2 = (bf16[2016,128]{1,0:T(8,128)(2,1)}, bf16[2016,128]{1,0:T(8,128)(2,1)S(1)}, u32[]{:S(2)}, u32[]{:S(2)}) collective-permute-start(bf16[2016,128]{1,0:T(8,128)(2,1)} %get-tuple-element.70.refs_1_), channel_id=1, source_target_pairs={{0,3},{1,0},{2,1},{3,2},{4,7},{5,4},{6,5},{7,6},{8,11},{9,8},{10,9... | collective-permute-start | bytes 1548296 | tf_op jit(solution)/shard_map/ppermute | solution.py:543
  16.1 1.9 %collective-permute-start.1 = (bf16[2016,128]{1,0:T(8,128)(2,1)}, bf16[2016,128]{1,0:T(8,128)(2,1)S(1)}, u32[]{:S(2)}, u32[]{:S(2)}) collective-permute-start(bf16[2016,128]{1,0:T(8,128)(2,1)} %get-tuple-element.70.refs_1_), channel_id=1, source_target_pairs={{0,2},{1,3},{2,0},{3,1},{4,6},{5,7},{6,4},{7,5},{8,10},{9,11},{10,... | collective-permute-start | bytes 1548296 | tf_op jit(solution)/shard_map/ppermute | solution.py:543
  18.0 3.4 %collective-permute-start = (bf16[2016,128]{1,0:T(8,128)(2,1)}, bf16[2016,128]{1,0:T(8,128)(2,1)S(1)}, u32[]{:S(2)}, u32[]{:S(2)}) collective-permute-start(bf16[2016,128]{1,0:T(8,128)(2,1)} %get-tuple-element.70.refs_1_), channel_id=1, source_target_pairs={{0,1},{1,2},{2,3},{3,0},{4,5},{5,6},{6,7},{7,4},{8,9},{9,10},{10,1... | collective-permute-start | bytes 1548296 | tf_op jit(solution)/shard_map/ppermute | solution.py:543
  21.3 3.3 %collective-permute-start.4 = (bf16[32,512]{1,0:T(8,128)(2,1)}, bf16[32,512]{1,0:T(8,128)(2,1)S(1)}, u32[]{:S(2)}, u32[]{:S(2)}) collective-permute-start(bf16[32,512]{1,0:T(8,128)(2,1)} %get-tuple-element.72), channel_id=1, source_target_pairs={{0,500},{4,16},{8,508},{12,24},{16,4},{20,32},{24,12},{28,40},{32,... | collective-permute-start | bytes 98312 | tf_op jit(solution)/shard_map/ppermute | solution.py:491
  24.7 0.8 pad_maximum_fusion
  25.4 4.0 %collective-permute-start.5 = (bf16[64,512]{1,0:T(8,128)(2,1)S(1)}, bf16[64,512]{1,0:T(8,128)(2,1)S(1)}, u32[]{:S(2)}, u32[]{:S(2)}) collective-permute-start(bf16[64,512]{1,0:T(8,128)(2,1)S(1)} %pad_maximum_fusion), channel_id=1, source_target_pairs={{0,8},{4,12},{8,16},{12,20},{16,24},{20,28},{24,32},{28,36},{32,40... | collective-permute-start | bytes 196616 | tf_op jit(solution)/shard_map/ppermute | solution.py:491
  29.4 0.8 pad_maximum_fusion.1
  30.2 11.1 %collective-permute-start.6 = (bf16[64,512]{1,0:T(8,128)(2,1)S(1)}, bf16[64,512]{1,0:T(8,128)(2,1)S(1)}, u32[]{:S(2)}, u32[]{:S(2)}) collective-permute-start(bf16[64,512]{1,0:T(8,128)(2,1)S(1)} %pad_maximum_fusion.1), channel_id=1, source_target_pairs={{0,504},{4,508},{8,0},{12,4},{16,8},{20,12},{24,16},{28,20},{32,24... | collective-permute-start | bytes 196616 | tf_op jit(solution)/shard_map/ppermute | solution.py:491
  41.3 0.0 copy-start
  41.3 0.0 copy-start.5
  41.4 0.0 copy-start.10
  41.4 0.0 copy-start.11
  41.4 4.1 %collective-permute-start.8 = (bf16[2304,128]{1,0:T(8,128)(2,1)}, bf16[2304,128]{1,0:T(8,128)(2,1)S(1)}, u32[]{:S(2)}, u32[]{:S(2)}) collective-permute-start(bf16[2304,128]{1,0:T(8,128)(2,1)} %get-tuple-element.80.refs_0_), channel_id=1, source_target_pairs={{0,3},{1,0},{2,1},{3,2},{4,7},{5,4},{6,5},{7,6},{8,11},{9,8},{10,9... | collective-permute-start | bytes 1769480 | tf_op jit(solution)/shard_map/ppermute | solution.py:543
  45.5 1.9 %collective-permute-start.7 = (bf16[2304,128]{1,0:T(8,128)(2,1)}, bf16[2304,128]{1,0:T(8,128)(2,1)S(1)}, u32[]{:S(2)}, u32[]{:S(2)}) collective-permute-start(bf16[2304,128]{1,0:T(8,128)(2,1)} %get-tuple-element.80.refs_0_), channel_id=1, source_target_pairs={{0,1},{1,2},{2,3},{3,0},{4,5},{5,6},{6,7},{7,4},{8,9},{9,10},{10,1... | collective-permute-start | bytes 1769480 | tf_op jit(solution)/shard_map/ppermute | solution.py:543
  47.5 1.0 copy-done.12
  48.5 2.6 %shard_map.195 = (bf16[1152,512]{1,0:T(8,128)(2,1)S(1)}, bf16[1024,512]{1,0:T(8,128)(2,1)S(1)}, bf16[1024,512]{1,0:T(8,128)(2,1)S(1)}, bf16[128,512]{1,0:T(8,128...) custom-call(bf16[474,1024]{1,0:T(8,128)(2,1)S(1)} %bitcast.19, bf16[2016,128]{1,0:T(8,128)(2,1)S(1)} %copy-done.12, ...), custom_call_target="tpu_custom_call" | custom-call | flops 1500000000 | bytes 8835072 | tf_op jit(solution)/shard_map/pallas_call | solution.py:39
  51.2 4.6 %shard_map.196 = (bf16[2048,512]{1,0:T(8,128)(2,1)S(1)}, bf16[128,512]{1,0:T(8,128)(2,1)S(1)}, f32[256,512]{1,0:T(8,128)S(1)}) custom-call(bf16[1152,512]{1,0:T(8,128)(2,1)S(1)} %get-tuple-element.75.refs_0_, bf16[256,512]{1,0:T(8,128)(2,1)S(1)} %copy-done.5, s32[1,2048]{1,0:T(1,128)S(1)} %copy-done.10, s32[1,2048]{1,0:T(1,128)S(1)} %copy-done.11, ...), custom_call_target="tpu_custom_call" | custom-call | flops 5000000000 | bytes 4603904 | tf_op jit(solution)/shard_map/pallas_call | solution.py:39
  55.9 1.3 collective-permute-done.8.refs_5_.refs_4_
  57.1 4.8 %collective-permute-done.7.refs_4_.refs_1_ = bf16[2304,128]{1,0:T(8,128)(2,1)S(1)} collective-permute-done((bf16[2304,128]{1,0:T(8,128)(2,1)}, bf16[2304,128]{1,0:T(8,128)(2,1)S(1)}, u32[]{:S(2)}, u32[]{:S(2)}) %collective-permute-start.7) | collective-permute-done | bytes 589856 | tf_op jit(solution)/shard_map/ppermute | solution.py:543
  61.9 0.8 shard_map.197
  62.7 4.6 %collective-permute-start.9 = (bf16[24,512]{1,0:T(8,128)(2,1)S(1)}, bf16[24,512]{1,0:T(8,128)(2,1)S(1)}, u32[]{:S(2)}, u32[]{:S(2)}) collective-permute-start(bf16[24,512]{1,0:T(8,128)(2,1)S(1)} %get-tuple-element.83), channel_id=1, source_target_pairs={{0,4},{4,0},{8,12},{12,8},{16,20},{20,16},{24,28},{28,24},{32,36},... | collective-permute-start | bytes 73736 | tf_op jit(solution)/shard_map/ppermute | solution.py:491
  67.3 1.9 %collective-permute-start.11 = (bf16[1152,128]{1,0:T(8,128)(2,1)S(1)}, bf16[1152,128]{1,0:T(8,128)(2,1)S(1)}, u32[]{:S(2)}, u32[]{:S(2)}) collective-permute-start(bf16[1152,128]{1,0:T(8,128)(2,1)S(1)} %slice.61), channel_id=1, source_target_pairs={{0,3},{1,0},{2,1},{3,2},{4,7},{5,4},{6,5},{7,6},{8,11},{9,8},{10,9... | collective-permute-start | bytes 884744 | tf_op jit(solution)/shard_map/ppermute | solution.py:543
  69.3 3.4 %collective-permute-start.10 = (bf16[1152,128]{1,0:T(8,128)(2,1)S(1)}, bf16[1152,128]{1,0:T(8,128)(2,1)S(1)}, u32[]{:S(2)}, u32[]{:S(2)}) collective-permute-start(bf16[1152,128]{1,0:T(8,128)(2,1)S(1)} %slice.60), channel_id=1, source_target_pairs={{0,1},{1,2},{2,3},{3,0},{4,5},{5,6},{6,7},{7,4},{8,9},{9,10},{10,1... | collective-permute-start | bytes 884744 | tf_op jit(solution)/shard_map/ppermute | solution.py:543
  72.6 1.9 %collective-permute-start.12 = (bf16[8,512]{1,0:T(8,128)(2,1)S(1)}, bf16[8,512]{1,0:T(8,128)(2,1)S(1)}, u32[]{:S(2)}, u32[]{:S(2)}) collective-permute-start(bf16[8,512]{1,0:T(8,128)(2,1)S(1)} %get-tuple-element.88), channel_id=1, source_target_pairs={{0,500},{4,16},{8,508},{12,24},{16,4},{20,32},{24,12},{28,40},{32,... | collective-permute-start | bytes 24584 | tf_op jit(solution)/shard_map/ppermute | solution.py:491
  74.6 1.9 %collective-permute-start.13 = (bf16[16,512]{1,0:T(8,128)(2,1)S(1)}, bf16[16,512]{1,0:T(8,128)(2,1)S(1)}, u32[]{:S(2)}, u32[]{:S(2)}) collective-permute-start(bf16[16,512]{1,0:T(8,128)(2,1)S(1)} %pad_maximum_fusion.6.refs_4_.refs_5_), channel_id=1, source_target_pairs={{0,8},{4,12},{8,16},{12,20},{16,24},{20,28},{24,32},{28,36},{32,40... | collective-permute-start | bytes 49160 | tf_op jit(solution)/shard_map/ppermute | solution.py:491
  76.5 6.9 %collective-permute-start.14 = (bf16[16,512]{1,0:T(8,128)(2,1)S(1)}, bf16[16,512]{1,0:T(8,128)(2,1)S(1)}, u32[]{:S(2)}, u32[]{:S(2)}) collective-permute-start(bf16[16,512]{1,0:T(8,128)(2,1)S(1)} %pad_maximum_fusion.7.refs_5_.refs_6_), channel_id=1, source_target_pairs={{0,504},{4,508},{8,0},{12,4},{16,8},{20,12},{24,16},{28,20},{32,24... | collective-permute-start | bytes 49160 | tf_op jit(solution)/shard_map/ppermute | solution.py:491
  83.4 2.7 %shard_map.198 = (f32[256,512]{1,0:T(8,128)S(1)}, bf16[2048,512]{1,0:T(8,128)(2,1)S(1)}) custom-call(bf16[256,512]{1,0:T(8,128)(2,1)S(1)} %get-tuple-element.81.refs_0_, bf16[256,512]{1,0:T(8,128)(2,1)S(1)} %get-tuple-element.82.refs_1_, s32[1,2048]{1,0:T(1,128)S(1)} %copy-done.8, s32[1,2048]{1,0:T(1,128)S(1)} %copy-done.9, ...), custom_call_target="tpu_custom_call" | custom-call | flops 3000000000 | bytes 3162112 | tf_op jit(solution)/shard_map/pallas_call | solution.py:39
  86.1 0.6 shard_map.199.refs_4_.refs_2_.refs_10_.refs_5_.refs_6_.refs_3_
  86.8 0.0 copy-done.3
  86.8 1.1 shard_map.200
  87.9 4.5 %collective-permute-start.15 = (bf16[24,512]{1,0:T(8,128)(2,1)S(1)}, bf16[24,512]{1,0:T(8,128)(2,1)S(1)}, u32[]{:S(2)}, u32[]{:S(2)}) collective-permute-start(bf16[24,512]{1,0:T(8,128)(2,1)S(1)} %get-tuple-element.91), channel_id=1, source_target_pairs={{0,4},{4,0},{8,12},{12,8},{16,20},{20,16},{24,28},{28,24},{32,36},... | collective-permute-start | bytes 73736 | tf_op jit(solution)/shard_map/ppermute | solution.py:491
  92.5 1.9 %collective-permute-start.16 = (bf16[8,512]{1,0:T(8,128)(2,1)S(1)}, bf16[8,512]{1,0:T(8,128)(2,1)S(1)}, u32[]{:S(2)}, u32[]{:S(2)}) collective-permute-start(bf16[8,512]{1,0:T(8,128)(2,1)S(1)} %get-tuple-element.95), channel_id=1, source_target_pairs={{0,500},{4,16},{8,508},{12,24},{16,4},{20,32},{24,12},{28,40},{32,... | collective-permute-start | bytes 24584 | tf_op jit(solution)/shard_map/ppermute | solution.py:491
  94.4 1.9 %collective-permute-start.17 = (bf16[16,512]{1,0:T(8,128)(2,1)S(1)}, bf16[16,512]{1,0:T(8,128)(2,1)S(1)}, u32[]{:S(2)}, u32[]{:S(2)}) collective-permute-start(bf16[16,512]{1,0:T(8,128)(2,1)S(1)} %pad_maximum_fusion.8.refs_4_.refs_3_), channel_id=1, source_target_pairs={{0,8},{4,12},{8,16},{12,20},{16,24},{20,28},{24,32},{28,36},{32,40... | collective-permute-start | bytes 49160 | tf_op jit(solution)/shard_map/ppermute | solution.py:491
  96.4 6.7 %collective-permute-start.18 = (bf16[16,512]{1,0:T(8,128)(2,1)S(1)}, bf16[16,512]{1,0:T(8,128)(2,1)S(1)}, u32[]{:S(2)}, u32[]{:S(2)}) collective-permute-start(bf16[16,512]{1,0:T(8,128)(2,1)S(1)} %pad_maximum_fusion.9.refs_5_.refs_4_), channel_id=1, source_target_pairs={{0,504},{4,508},{8,0},{12,4},{16,8},{20,12},{24,16},{28,20},{32,24... | collective-permute-start | bytes 49160 | tf_op jit(solution)/shard_map/ppermute | solution.py:491
  103.1 2.7 %shard_map.201 = (f32[256,512]{1,0:T(8,128)S(1)}, bf16[2048,512]{1,0:T(8,128)(2,1)S(1)}) custom-call(bf16[256,512]{1,0:T(8,128)(2,1)S(1)} %get-tuple-element.89.refs_0_, bf16[256,512]{1,0:T(8,128)(2,1)S(1)} %get-tuple-element.90.refs_1_, s32[1,2048]{1,0:T(1,128)S(1)} %copy-done.8, s32[1,2048]{1,0:T(1,128)S(1)} %copy-done.9, ...), custom_call_target="tpu_custom_call" | custom-call | flops 3000000000 | bytes 3162112 | tf_op jit(solution)/shard_map/pallas_call | solution.py:39
  105.8 0.5 shard_map.203
  106.3 0.0 copy-start.7
  106.4 1.5 shard_map.202
  107.8 7.0 %shard_map.204 = (bf16[3072,512]{1,0:T(8,128)(2,1)S(1)}, bf16[3072,512]{1,0:T(8,128)(2,1)S(1)}, f32[256,512]{1,0:T(8,128)S(1)}, bf16[256,512]{1,0:T(8,128)(2,1)S...) custom-call(bf16[256,512]{1,0:T(8,128)(2,1)S(1)} %get-tuple-element., ...), custom_call_target="tpu_custom_call" | custom-call | flops 6000000000 | bytes 13254752 | tf_op jit(solution)/shard_map/pallas_call | solution.py:39
  114.8 3.1 %collective-permute-start.19 = (bf16[48,512]{1,0:T(8,128)(2,1)S(1)}, bf16[48,512]{1,0:T(8,128)(2,1)S(1)}, u32[]{:S(2)}, u32[]{:S(2)}) collective-permute-start(bf16[48,512]{1,0:T(8,128)(2,1)S(1)} %get-tuple-element.106.refs_5_), channel_id=1, source_target_pairs={{0,4},{4,0},{8,12},{12,8},{16,20},{20,16},{24,28},{28,24},{32,36},... | collective-permute-start | bytes 147464 | tf_op jit(solution)/shard_map/ppermute | solution.py:491
  117.9 2.1 %collective-permute-start.20 = (bf16[16,512]{1,0:T(8,128)(2,1)S(1)}, bf16[16,512]{1,0:T(8,128)(2,1)S(1)}, u32[]{:S(2)}, u32[]{:S(2)}) collective-permute-start(bf16[16,512]{1,0:T(8,128)(2,1)S(1)} %get-tuple-element.110.refs_6_), channel_id=1, source_target_pairs={{0,500},{4,16},{8,508},{12,24},{16,4},{20,32},{24,12},{28,40},{32,... | collective-permute-start | bytes 49160 | tf_op jit(solution)/shard_map/ppermute | solution.py:491
  120.0 2.6 %collective-permute-start.21 = (bf16[32,512]{1,0:T(8,128)(2,1)S(1)}, bf16[32,512]{1,0:T(8,128)(2,1)S(1)}, u32[]{:S(2)}, u32[]{:S(2)}) collective-permute-start(bf16[32,512]{1,0:T(8,128)(2,1)S(1)} %pad_maximum_fusion.2.refs_4_.refs_9_), channel_id=1, source_target_pairs={{0,8},{4,12},{8,16},{12,20},{16,24},{20,28},{24,32},{28,36},{32,40... | collective-permute-start | bytes 98312 | tf_op jit(solution)/shard_map/ppermute | solution.py:491
  122.6 6.5 %collective-permute-start.22 = (bf16[32,512]{1,0:T(8,128)(2,1)S(1)}, bf16[32,512]{1,0:T(8,128)(2,1)S(1)}, u32[]{:S(2)}, u32[]{:S(2)}) collective-permute-start(bf16[32,512]{1,0:T(8,128)(2,1)S(1)} %pad_maximum_fusion.3.refs_5_.refs_10_), channel_id=1, source_target_pairs={{0,504},{4,508},{8,0},{12,4},{16,8},{20,12},{24,16},{28,20},{32,24... | collective-permute-start | bytes 98312 | tf_op jit(solution)/shard_map/ppermute | solution.py:491
  129.1 1.9 %shard_map.206 = (bf16[256,512]{1,0:T(8,128)(2,1)S(1)}, f32[256,512]{1,0:T(8,128)S(1)}) custom-call(bf16[256,512]{1,0:T(8,128)(2,1)S(1)} %get-tuple-element.111.refs_0_, bf16[2048,512]{1,0:T(8,128)(2,1)S(1)} %get-tuple-element.112.refs_1_, s32[1,2048]{1,0:T(1,128)S(1)} %copy-done.8, s32[1,2048]{1,0:T(1,128)S(1)} %copy-done.9, s32[6,8,128]{2,1,0:T(8,128)S(1)} %copy-done.3, ...), custom_call_target="tpu_custom_call" | custom-call | flops 3000000000 | bytes 3284992 | tf_op jit(solution)/shard_map/pallas_call | solution.py:39
  131.0 2.0 %shard_map.205.refs_13_.refs_0_ = f32[1024,512]{1,0:T(8,128)S(1)} custom-call(bf16[3072,512]{1,0:T(8,128)(2,1)S(1)} %get-tuple-element.105.refs_0_, s32[24]{0:T(128)S(1)} %copy-done.13, s32[1,3072]{1,0:T(1,128)S(1)} %copy-done.7, s32[1,3072]{1,0:T(1,128)S(1)} %copy-done.6, bf16[32,512]{1,0:T(8,128)(2,1)S(1)} %pad_maximum_fusion.2.refs_4_.refs_9_, ...), custom_call_target="tpu_custom_call" | custom-call | flops 2000000000 | bytes 5267552 | tf_op jit(solution)/shard_map/pallas_call | solution.py:39
  133.1 0.9 shard_map.207
  134.0 3.6 %collective-permute-start.23 = (bf16[24,512]{1,0:T(8,128)(2,1)S(1)}, bf16[24,512]{1,0:T(8,128)(2,1)S(1)}, u32[]{:S(2)}, u32[]{:S(2)}) collective-permute-start(bf16[24,512]{1,0:T(8,128)(2,1)S(1)} %get-tuple-element.118.refs_5_), channel_id=1, source_target_pairs={{0,4},{4,0},{8,12},{12,8},{16,20},{20,16},{24,28},{28,24},{32,36},... | collective-permute-start | bytes 73736 | tf_op jit(solution)/shard_map/ppermute | solution.py:491
  137.6 1.9 %collective-permute-start.24 = (bf16[8,512]{1,0:T(8,128)(2,1)S(1)}, bf16[8,512]{1,0:T(8,128)(2,1)S(1)}, u32[]{:S(2)}, u32[]{:S(2)}) collective-permute-start(bf16[8,512]{1,0:T(8,128)(2,1)S(1)} %get-tuple-element.124.refs_6_), channel_id=1, source_target_pairs={{0,500},{4,16},{8,508},{12,24},{16,4},{20,32},{24,12},{28,40},{32,... | collective-permute-start | bytes 24584 | tf_op jit(solution)/shard_map/ppermute | solution.py:491
  139.6 6.5 %collective-permute-start.25 = (bf16[16,512]{1,0:T(8,128)(2,1)S(1)}, bf16[16,512]{1,0:T(8,128)(2,1)S(1)}, u32[]{:S(2)}, u32[]{:S(2)}) collective-permute-start(bf16[16,512]{1,0:T(8,128)(2,1)S(1)} %pad_maximum_fusion.10.refs_12_.refs_9_), channel_id=1, source_target_pairs={{0,504},{4,508},{8,0},{12,4},{16,8},{20,12},{24,16},{28,20},{32,24... | collective-permute-start | bytes 49160 | tf_op jit(solution)/shard_map/ppermute | solution.py:491
  146.1 1.9 %collective-permute-start.26 = (bf16[16,512]{1,0:T(8,128)(2,1)S(1)}, bf16[16,512]{1,0:T(8,128)(2,1)S(1)}, u32[]{:S(2)}, u32[]{:S(2)}) collective-permute-start(bf16[16,512]{1,0:T(8,128)(2,1)S(1)} %pad_maximum_fusion.11.refs_13_.refs_10_), channel_id=1, source_target_pairs={{0,8},{4,12},{8,16},{12,20},{16,24},{20,28},{24,32},{28,36},{32,40... | collective-permute-start | bytes 49160 | tf_op jit(solution)/shard_map/ppermute | solution.py:491
  148.0 1.9 %shard_map.209 = (bf16[256,512]{1,0:T(8,128)(2,1)S(1)}, f32[256,512]{1,0:T(8,128)S(1)}) custom-call(bf16[256,512]{1,0:T(8,128)(2,1)S(1)} %get-tuple-element.122.refs_0_, bf16[2048,512]{1,0:T(8,128)(2,1)S(1)} %get-tuple-element.123.refs_1_, s32[1,2048]{1,0:T(1,128)S(1)} %copy-done.8, s32[1,2048]{1,0:T(1,128)S(1)} %copy-done.9, s32[6,8,128]{2,1,0:T(8,128)S(1)} %copy-done.3, ...), custom_call_target="tpu_custom_call" | custom-call | flops 3000000000 | bytes 3235840 | tf_op jit(solution)/shard_map/pallas_call | solution.py:39
  150.0 2.9 %shard_map.208 = (bf16[1024,512]{1,0:T(8,128)(2,1)S(1)}, bf16[128,512]{1,0:T(8,128)(2,1)S(1)}) custom-call(bf16[3072,512]{1,0:T(8,128)(2,1)S(1)} %get-tuple-element.109.refs_0_, bf16[1024,512]{1,0:T(8,128)(2,1)S(1)} %get-tuple-element.97.refs_1_, bf16[1024,512]{1,0:T(8,128)(2,1)S(1)} %get-tuple-element.99.refs_2_, s32[24]{0:T(128)S(1)} %copy-done.13, ...), custom_call_target="tpu_custom_call" | custom-call | flops 2500000000 | bytes 6996064 | tf_op jit(solution)/shard_map/pallas_call | solution.py:39
  152.8 1.1 collective-permute-done.26.refs_12_
  153.9 0.9 shard_map.210
  154.8 1.9 %collective-permute-start.27 = (bf16[48,512]{1,0:T(8,128)(2,1)S(1)}, bf16[48,512]{1,0:T(8,128)(2,1)S(1)}, u32[]{:S(2)}, u32[]{:S(2)}) collective-permute-start(bf16[48,512]{1,0:T(8,128)(2,1)S(1)} %get-tuple-element.131), channel_id=1, source_target_pairs={{0,4},{4,0},{8,12},{12,8},{16,20},{20,16},{24,28},{28,24},{32,36},... | collective-permute-start | bytes 147464 | tf_op jit(solution)/shard_map/ppermute | solution.py:491
  156.8 1.9 %collective-permute-start.28 = (bf16[16,512]{1,0:T(8,128)(2,1)S(1)}, bf16[16,512]{1,0:T(8,128)(2,1)S(1)}, u32[]{:S(2)}, u32[]{:S(2)}) collective-permute-start(bf16[16,512]{1,0:T(8,128)(2,1)S(1)} %get-tuple-element.137), channel_id=1, source_target_pairs={{0,500},{4,16},{8,508},{12,24},{16,4},{20,32},{24,12},{28,40},{32,... | collective-permute-start | bytes 49160 | tf_op jit(solution)/shard_map/ppermute | solution.py:491
  158.7 6.9 %collective-permute-start.29 = (bf16[32,512]{1,0:T(8,128)(2,1)S(1)}, bf16[32,512]{1,0:T(8,128)(2,1)S(1)}, u32[]{:S(2)}, u32[]{:S(2)}) collective-permute-start(bf16[32,512]{1,0:T(8,128)(2,1)S(1)} %pad_maximum_fusion.4.refs_4_), channel_id=1, source_target_pairs={{0,504},{4,508},{8,0},{12,4},{16,8},{20,12},{24,16},{28,20},{32,24... | collective-permute-start | bytes 98312 | tf_op jit(solution)/shard_map/ppermute | solution.py:491
  165.7 1.9 %collective-permute-start.30 = (bf16[32,512]{1,0:T(8,128)(2,1)S(1)}, bf16[32,512]{1,0:T(8,128)(2,1)S(1)}, u32[]{:S(2)}, u32[]{:S(2)}) collective-permute-start(bf16[32,512]{1,0:T(8,128)(2,1)S(1)} %pad_maximum_fusion.5.refs_5_), channel_id=1, source_target_pairs={{0,8},{4,12},{8,16},{12,20},{16,24},{20,28},{24,32},{28,36},{32,40... | collective-permute-start | bytes 98312 | tf_op jit(solution)/shard_map/ppermute | solution.py:491
  167.6 3.6 %shard_map.212.refs_0_ = bf16[1024,512]{1,0:T(8,128)(2,1)S(1)} custom-call(bf16[256,512]{1,0:T(8,128)(2,1)S(1)} %get-tuple-element.134.refs_0_, bf16[2048,512]{1,0:T(8,128)(2,1)S(1)} %get-tuple-element.135.refs_1_, s32[1,2048]{1,0:T(1,128)S(1)} %copy-done.10, s32[1,2048]{1,0:T(1,128)S(1)} %copy-done.11, bf16[32,512]{1,0:T(8,128)(2,1)S(1)} %pad_maximum_fusion.4.refs_4_, ...), custom_call_target="tpu_custom_call" | custom-call | flops 4000000000 | bytes 3424256 | tf_op jit(solution)/shard_map/pallas_call | solution.py:39
  171.2 1.5 shard_map.211
  172.7 1.4 collective-permute-done.30.refs_8_
  174.2 2.7 %shard_map.213 = bf16[474,1024]{1,0:T(8,128)(2,1)} custom-call(bf16[1024,512]{1,0:T(8,128)(2,1)S(1)} %shard_map.212.refs_0_, bf16[2016,512]{1,0:T(8,128)(2,1)S(1)} %get-tuple-element.78.refs_3_.refs_5_.refs_6_.refs_1_, bf16[1024,512]{1,0:T(8,128)(2,1)S(1)} %get-tuple-element.136.refs_2_, bf16[1024,512]{1,0:T(8,128)(2,1)S(1)} %get-tuple-element.130.refs_13_.refs_3_, ...), custom_call_target="tpu_custom_call" | custom-call | flops 1500000000 | bytes 6336512 | tf_op jit(solution)/shard_map/pallas_call | solution.py:39
  (66 shorter events, 0.2 us)
Async XLA Ops:
  0.6 46.8 %copy-start.2 = (bf16[1,1024,474]{1,2,0:T(8,128)(2,1)S(1)}, bf16[1,1024,474]{1,2,0:T(8,128)(2,1)}, u32[]{:S(2)}) copy-start(bf16[1,1024,474]{1,2,0:T(8,128)(2,1)} %param.19) | copy-start | bytes 2912260
  5.3 19.3 %collective-permute-start.3 = (bf16[96,512]{1,0:T(8,128)(2,1)}, bf16[96,512]{1,0:T(8,128)(2,1)S(1)}, u32[]{:S(2)}, u32[]{:S(2)}) collective-permute-start(bf16[96,512]{1,0:T(8,128)(2,1)} %get-tuple-element.71), channel_id=1, source_target_pairs={{0,4},{4,0},{8,12},{12,8},{16,20},{20,16},{24,28},{28,24},{32,36},... | collective-permute-start | bytes 294920 | tf_op jit(solution)/shard_map/ppermute | solution.py:491
  14.1 33.3 %collective-permute-start.2 = (bf16[2016,128]{1,0:T(8,128)(2,1)}, bf16[2016,128]{1,0:T(8,128)(2,1)S(1)}, u32[]{:S(2)}, u32[]{:S(2)}) collective-permute-start(bf16[2016,128]{1,0:T(8,128)(2,1)} %get-tuple-element.70.refs_1_), channel_id=1, source_target_pairs={{0,3},{1,0},{2,1},{3,2},{4,7},{5,4},{6,5},{7,6},{8,11},{9,8},{10,9... | collective-permute-start | bytes 1548296 | tf_op jit(solution)/shard_map/ppermute | solution.py:543
  16.1 31.4 %collective-permute-start.1 = (bf16[2016,128]{1,0:T(8,128)(2,1)}, bf16[2016,128]{1,0:T(8,128)(2,1)S(1)}, u32[]{:S(2)}, u32[]{:S(2)}) collective-permute-start(bf16[2016,128]{1,0:T(8,128)(2,1)} %get-tuple-element.70.refs_1_), channel_id=1, source_target_pairs={{0,2},{1,3},{2,0},{3,1},{4,6},{5,7},{6,4},{7,5},{8,10},{9,11},{10,... | collective-permute-start | bytes 1548296 | tf_op jit(solution)/shard_map/ppermute | solution.py:543
  18.0 29.5 %collective-permute-start = (bf16[2016,128]{1,0:T(8,128)(2,1)}, bf16[2016,128]{1,0:T(8,128)(2,1)S(1)}, u32[]{:S(2)}, u32[]{:S(2)}) collective-permute-start(bf16[2016,128]{1,0:T(8,128)(2,1)} %get-tuple-element.70.refs_1_), channel_id=1, source_target_pairs={{0,1},{1,2},{2,3},{3,0},{4,5},{5,6},{6,7},{7,4},{8,9},{9,10},{10,1... | collective-permute-start | bytes 1548296 | tf_op jit(solution)/shard_map/ppermute | solution.py:543
  21.3 8.9 %collective-permute-start.4 = (bf16[32,512]{1,0:T(8,128)(2,1)}, bf16[32,512]{1,0:T(8,128)(2,1)S(1)}, u32[]{:S(2)}, u32[]{:S(2)}) collective-permute-start(bf16[32,512]{1,0:T(8,128)(2,1)} %get-tuple-element.72), channel_id=1, source_target_pairs={{0,500},{4,16},{8,508},{12,24},{16,4},{20,32},{24,12},{28,40},{32,... | collective-permute-start | bytes 98312 | tf_op jit(solution)/shard_map/ppermute | solution.py:491
  25.4 15.9 %collective-permute-start.5 = (bf16[64,512]{1,0:T(8,128)(2,1)S(1)}, bf16[64,512]{1,0:T(8,128)(2,1)S(1)}, u32[]{:S(2)}, u32[]{:S(2)}) collective-permute-start(bf16[64,512]{1,0:T(8,128)(2,1)S(1)} %pad_maximum_fusion), channel_id=1, source_target_pairs={{0,8},{4,12},{8,16},{12,20},{16,24},{20,28},{24,32},{28,36},{32,40... | collective-permute-start | bytes 196616 | tf_op jit(solution)/shard_map/ppermute | solution.py:491
  30.2 15.3 %collective-permute-start.6 = (bf16[64,512]{1,0:T(8,128)(2,1)S(1)}, bf16[64,512]{1,0:T(8,128)(2,1)S(1)}, u32[]{:S(2)}, u32[]{:S(2)}) collective-permute-start(bf16[64,512]{1,0:T(8,128)(2,1)S(1)} %pad_maximum_fusion.1), channel_id=1, source_target_pairs={{0,504},{4,508},{8,0},{12,4},{16,8},{20,12},{24,16},{28,20},{32,24... | collective-permute-start | bytes 196616 | tf_op jit(solution)/shard_map/ppermute | solution.py:491
  41.3 9.8 %copy-start = (s32[6,128,128]{2,1,0:T(8,128)S(1)}, s32[6,128,128]{2,1,0:T(8,128)}, u32[]{:S(2)}) copy-start(s32[6,128,128]{2,1,0:T(8,128)} %get-tuple-element.76.refs_4_.refs_2_.refs_8_.refs_3_.refs_6_) | copy-start | bytes 1179652
  41.3 9.8 %copy-start.5 = (bf16[256,512]{1,0:T(8,128)(2,1)S(1)}, bf16[256,512]{1,0:T(8,128)(2,1)}, u32[]{:S(2)}) copy-start(bf16[256,512]{1,0:T(8,128)(2,1)} %refs_1_.3) | copy-start | bytes 786436
  41.4 9.8 %copy-start.10 = (s32[1,2048]{1,0:T(1,128)S(1)}, s32[1,2048]{1,0:T(1,128)}, u32[]{:S(2)}) copy-start(s32[1,2048]{1,0:T(1,128)} %refs_2_.13) | copy-start | bytes 24580
  41.4 9.8 %copy-start.11 = (s32[1,2048]{1,0:T(1,128)S(1)}, s32[1,2048]{1,0:T(1,128)}, u32[]{:S(2)}) copy-start(s32[1,2048]{1,0:T(1,128)} %refs_3_.13) | copy-start | bytes 24580
  41.4 15.7 %collective-permute-start.8 = (bf16[2304,128]{1,0:T(8,128)(2,1)}, bf16[2304,128]{1,0:T(8,128)(2,1)S(1)}, u32[]{:S(2)}, u32[]{:S(2)}) collective-permute-start(bf16[2304,128]{1,0:T(8,128)(2,1)} %get-tuple-element.80.refs_0_), channel_id=1, source_target_pairs={{0,3},{1,0},{2,1},{3,2},{4,7},{5,4},{6,5},{7,6},{8,11},{9,8},{10,9... | collective-permute-start | bytes 1769480 | tf_op jit(solution)/shard_map/ppermute | solution.py:543
  45.5 16.4 %collective-permute-start.7 = (bf16[2304,128]{1,0:T(8,128)(2,1)}, bf16[2304,128]{1,0:T(8,128)(2,1)S(1)}, u32[]{:S(2)}, u32[]{:S(2)}) collective-permute-start(bf16[2304,128]{1,0:T(8,128)(2,1)} %get-tuple-element.80.refs_0_), channel_id=1, source_target_pairs={{0,1},{1,2},{2,3},{3,0},{4,5},{5,6},{6,7},{7,4},{8,9},{9,10},{10,1... | collective-permute-start | bytes 1769480 | tf_op jit(solution)/shard_map/ppermute | solution.py:543
  47.5 1.0 copy-start.12
  61.9 21.5 %copy-start.8 = (s32[1,2048]{1,0:T(1,128)S(1)}, s32[1,2048]{1,0:T(1,128)}, u32[]{:S(2)}) copy-start(s32[1,2048]{1,0:T(1,128)} %refs_2_.12) | copy-start | bytes 24580
  61.9 21.5 %copy-start.9 = (s32[1,2048]{1,0:T(1,128)S(1)}, s32[1,2048]{1,0:T(1,128)}, u32[]{:S(2)}) copy-start(s32[1,2048]{1,0:T(1,128)} %refs_3_.12) | copy-start | bytes 24580
  62.7 11.9 %collective-permute-start.9 = (bf16[24,512]{1,0:T(8,128)(2,1)S(1)}, bf16[24,512]{1,0:T(8,128)(2,1)S(1)}, u32[]{:S(2)}, u32[]{:S(2)}) collective-permute-start(bf16[24,512]{1,0:T(8,128)(2,1)S(1)} %get-tuple-element.83), channel_id=1, source_target_pairs={{0,4},{4,0},{8,12},{12,8},{16,20},{20,16},{24,28},{28,24},{32,36},... | collective-permute-start | bytes 73736 | tf_op jit(solution)/shard_map/ppermute | solution.py:491
  67.3 18.8 %collective-permute-start.11 = (bf16[1152,128]{1,0:T(8,128)(2,1)S(1)}, bf16[1152,128]{1,0:T(8,128)(2,1)S(1)}, u32[]{:S(2)}, u32[]{:S(2)}) collective-permute-start(bf16[1152,128]{1,0:T(8,128)(2,1)S(1)} %slice.61), channel_id=1, source_target_pairs={{0,3},{1,0},{2,1},{3,2},{4,7},{5,4},{6,5},{7,6},{8,11},{9,8},{10,9... | collective-permute-start | bytes 884744 | tf_op jit(solution)/shard_map/ppermute | solution.py:543
  69.3 16.9 %collective-permute-start.10 = (bf16[1152,128]{1,0:T(8,128)(2,1)S(1)}, bf16[1152,128]{1,0:T(8,128)(2,1)S(1)}, u32[]{:S(2)}, u32[]{:S(2)}) collective-permute-start(bf16[1152,128]{1,0:T(8,128)(2,1)S(1)} %slice.60), channel_id=1, source_target_pairs={{0,1},{1,2},{2,3},{3,0},{4,5},{5,6},{6,7},{7,4},{8,9},{9,10},{10,1... | collective-permute-start | bytes 884744 | tf_op jit(solution)/shard_map/ppermute | solution.py:543
  72.6 14.1 %collective-permute-start.12 = (bf16[8,512]{1,0:T(8,128)(2,1)S(1)}, bf16[8,512]{1,0:T(8,128)(2,1)S(1)}, u32[]{:S(2)}, u32[]{:S(2)}) collective-permute-start(bf16[8,512]{1,0:T(8,128)(2,1)S(1)} %get-tuple-element.88), channel_id=1, source_target_pairs={{0,500},{4,16},{8,508},{12,24},{16,4},{20,32},{24,12},{28,40},{32,... | collective-permute-start | bytes 24584 | tf_op jit(solution)/shard_map/ppermute | solution.py:491
  74.6 12.2 %collective-permute-start.13 = (bf16[16,512]{1,0:T(8,128)(2,1)S(1)}, bf16[16,512]{1,0:T(8,128)(2,1)S(1)}, u32[]{:S(2)}, u32[]{:S(2)}) collective-permute-start(bf16[16,512]{1,0:T(8,128)(2,1)S(1)} %pad_maximum_fusion.6.refs_4_.refs_5_), channel_id=1, source_target_pairs={{0,8},{4,12},{8,16},{12,20},{16,24},{20,28},{24,32},{28,36},{32,40... | collective-permute-start | bytes 49160 | tf_op jit(solution)/shard_map/ppermute | solution.py:491
  76.5 10.3 %collective-permute-start.14 = (bf16[16,512]{1,0:T(8,128)(2,1)S(1)}, bf16[16,512]{1,0:T(8,128)(2,1)S(1)}, u32[]{:S(2)}, u32[]{:S(2)}) collective-permute-start(bf16[16,512]{1,0:T(8,128)(2,1)S(1)} %pad_maximum_fusion.7.refs_5_.refs_6_), channel_id=1, source_target_pairs={{0,504},{4,508},{8,0},{12,4},{16,8},{20,12},{24,16},{28,20},{32,24... | collective-permute-start | bytes 49160 | tf_op jit(solution)/shard_map/ppermute | solution.py:491
  83.4 2.7 %copy-start.4 = (bf16[2304,128]{1,0:T(8,128)(2,1)S(1)}, bf16[2304,128]{1,0:T(8,128)(2,1)}, u32[]{:S(2)}) copy-start(bf16[2304,128]{1,0:T(8,128)(2,1)} %get-tuple-element.80.refs_0_) | copy-start | bytes 1769476
  86.1 0.7 copy-start.3
  87.9 6.5 %collective-permute-start.15 = (bf16[24,512]{1,0:T(8,128)(2,1)S(1)}, bf16[24,512]{1,0:T(8,128)(2,1)S(1)}, u32[]{:S(2)}, u32[]{:S(2)}) collective-permute-start(bf16[24,512]{1,0:T(8,128)(2,1)S(1)} %get-tuple-element.91), channel_id=1, source_target_pairs={{0,4},{4,0},{8,12},{12,8},{16,20},{20,16},{24,28},{28,24},{32,36},... | collective-permute-start | bytes 73736 | tf_op jit(solution)/shard_map/ppermute | solution.py:491
  92.5 13.9 %collective-permute-start.16 = (bf16[8,512]{1,0:T(8,128)(2,1)S(1)}, bf16[8,512]{1,0:T(8,128)(2,1)S(1)}, u32[]{:S(2)}, u32[]{:S(2)}) collective-permute-start(bf16[8,512]{1,0:T(8,128)(2,1)S(1)} %get-tuple-element.95), channel_id=1, source_target_pairs={{0,500},{4,16},{8,508},{12,24},{16,4},{20,32},{24,12},{28,40},{32,... | collective-permute-start | bytes 24584 | tf_op jit(solution)/shard_map/ppermute | solution.py:491
  94.4 11.9 %collective-permute-start.17 = (bf16[16,512]{1,0:T(8,128)(2,1)S(1)}, bf16[16,512]{1,0:T(8,128)(2,1)S(1)}, u32[]{:S(2)}, u32[]{:S(2)}) collective-permute-start(bf16[16,512]{1,0:T(8,128)(2,1)S(1)} %pad_maximum_fusion.8.refs_4_.refs_3_), channel_id=1, source_target_pairs={{0,8},{4,12},{8,16},{12,20},{16,24},{20,28},{24,32},{28,36},{32,40... | collective-permute-start | bytes 49160 | tf_op jit(solution)/shard_map/ppermute | solution.py:491
  96.4 10.0 %collective-permute-start.18 = (bf16[16,512]{1,0:T(8,128)(2,1)S(1)}, bf16[16,512]{1,0:T(8,128)(2,1)S(1)}, u32[]{:S(2)}, u32[]{:S(2)}) collective-permute-start(bf16[16,512]{1,0:T(8,128)(2,1)S(1)} %pad_maximum_fusion.9.refs_5_.refs_4_), channel_id=1, source_target_pairs={{0,504},{4,508},{8,0},{12,4},{16,8},{20,12},{24,16},{28,20},{32,24... | collective-permute-start | bytes 49160 | tf_op jit(solution)/shard_map/ppermute | solution.py:491
  103.1 2.7 %copy-start.1 = (bf16[1,1024,227]{1,2,0:T(8,128)(2,1)S(1)}, bf16[1,1024,227]{1,2,0:T(8,128)(2,1)}, u32[]{:S(2)}) copy-start(bf16[1,1024,227]{1,2,0:T(8,128)(2,1)} %param.28) | copy-start | bytes 1394692
  106.3 1.5 copy-start.6
  106.3 1.5 copy-start.7
  106.3 1.5 copy-start.13
  114.8 5.1 %collective-permute-start.19 = (bf16[48,512]{1,0:T(8,128)(2,1)S(1)}, bf16[48,512]{1,0:T(8,128)(2,1)S(1)}, u32[]{:S(2)}, u32[]{:S(2)}) collective-permute-start(bf16[48,512]{1,0:T(8,128)(2,1)S(1)} %get-tuple-element.106.refs_5_), channel_id=1, source_target_pairs={{0,4},{4,0},{8,12},{12,8},{16,20},{20,16},{24,28},{28,24},{32,36},... | collective-permute-start | bytes 147464 | tf_op jit(solution)/shard_map/ppermute | solution.py:491
  117.9 15.2 %collective-permute-start.20 = (bf16[16,512]{1,0:T(8,128)(2,1)S(1)}, bf16[16,512]{1,0:T(8,128)(2,1)S(1)}, u32[]{:S(2)}, u32[]{:S(2)}) collective-permute-start(bf16[16,512]{1,0:T(8,128)(2,1)S(1)} %get-tuple-element.110.refs_6_), channel_id=1, source_target_pairs={{0,500},{4,16},{8,508},{12,24},{16,4},{20,32},{24,12},{28,40},{32,... | collective-permute-start | bytes 49160 | tf_op jit(solution)/shard_map/ppermute | solution.py:491
  120.0 13.1 %collective-permute-start.21 = (bf16[32,512]{1,0:T(8,128)(2,1)S(1)}, bf16[32,512]{1,0:T(8,128)(2,1)S(1)}, u32[]{:S(2)}, u32[]{:S(2)}) collective-permute-start(bf16[32,512]{1,0:T(8,128)(2,1)S(1)} %pad_maximum_fusion.2.refs_4_.refs_9_), channel_id=1, source_target_pairs={{0,8},{4,12},{8,16},{12,20},{16,24},{20,28},{24,32},{28,36},{32,40... | collective-permute-start | bytes 98312 | tf_op jit(solution)/shard_map/ppermute | solution.py:491
  122.6 10.5 %collective-permute-start.22 = (bf16[32,512]{1,0:T(8,128)(2,1)S(1)}, bf16[32,512]{1,0:T(8,128)(2,1)S(1)}, u32[]{:S(2)}, u32[]{:S(2)}) collective-permute-start(bf16[32,512]{1,0:T(8,128)(2,1)S(1)} %pad_maximum_fusion.3.refs_5_.refs_10_), channel_id=1, source_target_pairs={{0,504},{4,508},{8,0},{12,4},{16,8},{20,12},{24,16},{28,20},{32,24... | collective-permute-start | bytes 98312 | tf_op jit(solution)/shard_map/ppermute | solution.py:491
  134.0 5.5 %collective-permute-start.23 = (bf16[24,512]{1,0:T(8,128)(2,1)S(1)}, bf16[24,512]{1,0:T(8,128)(2,1)S(1)}, u32[]{:S(2)}, u32[]{:S(2)}) collective-permute-start(bf16[24,512]{1,0:T(8,128)(2,1)S(1)} %get-tuple-element.118.refs_5_), channel_id=1, source_target_pairs={{0,4},{4,0},{8,12},{12,8},{16,20},{20,16},{24,28},{28,24},{32,36},... | collective-permute-start | bytes 73736 | tf_op jit(solution)/shard_map/ppermute | solution.py:491
  137.6 15.2 %collective-permute-start.24 = (bf16[8,512]{1,0:T(8,128)(2,1)S(1)}, bf16[8,512]{1,0:T(8,128)(2,1)S(1)}, u32[]{:S(2)}, u32[]{:S(2)}) collective-permute-start(bf16[8,512]{1,0:T(8,128)(2,1)S(1)} %get-tuple-element.124.refs_6_), channel_id=1, source_target_pairs={{0,500},{4,16},{8,508},{12,24},{16,4},{20,32},{24,12},{28,40},{32,... | collective-permute-start | bytes 24584 | tf_op jit(solution)/shard_map/ppermute | solution.py:491
  139.6 13.2 %collective-permute-start.25 = (bf16[16,512]{1,0:T(8,128)(2,1)S(1)}, bf16[16,512]{1,0:T(8,128)(2,1)S(1)}, u32[]{:S(2)}, u32[]{:S(2)}) collective-permute-start(bf16[16,512]{1,0:T(8,128)(2,1)S(1)} %pad_maximum_fusion.10.refs_12_.refs_9_), channel_id=1, source_target_pairs={{0,504},{4,508},{8,0},{12,4},{16,8},{20,12},{24,16},{28,20},{32,24... | collective-permute-start | bytes 49160 | tf_op jit(solution)/shard_map/ppermute | solution.py:491
  146.1 7.8 %collective-permute-start.26 = (bf16[16,512]{1,0:T(8,128)(2,1)S(1)}, bf16[16,512]{1,0:T(8,128)(2,1)S(1)}, u32[]{:S(2)}, u32[]{:S(2)}) collective-permute-start(bf16[16,512]{1,0:T(8,128)(2,1)S(1)} %pad_maximum_fusion.11.refs_13_.refs_10_), channel_id=1, source_target_pairs={{0,8},{4,12},{8,16},{12,20},{16,24},{20,28},{24,32},{28,36},{32,40... | collective-permute-start | bytes 49160 | tf_op jit(solution)/shard_map/ppermute | solution.py:491
  154.8 3.9 %collective-permute-start.27 = (bf16[48,512]{1,0:T(8,128)(2,1)S(1)}, bf16[48,512]{1,0:T(8,128)(2,1)S(1)}, u32[]{:S(2)}, u32[]{:S(2)}) collective-permute-start(bf16[48,512]{1,0:T(8,128)(2,1)S(1)} %get-tuple-element.131), channel_id=1, source_target_pairs={{0,4},{4,0},{8,12},{12,8},{16,20},{20,16},{24,28},{28,24},{32,36},... | collective-permute-start | bytes 147464 | tf_op jit(solution)/shard_map/ppermute | solution.py:491
  156.8 16.0 %collective-permute-start.28 = (bf16[16,512]{1,0:T(8,128)(2,1)S(1)}, bf16[16,512]{1,0:T(8,128)(2,1)S(1)}, u32[]{:S(2)}, u32[]{:S(2)}) collective-permute-start(bf16[16,512]{1,0:T(8,128)(2,1)S(1)} %get-tuple-element.137), channel_id=1, source_target_pairs={{0,500},{4,16},{8,508},{12,24},{16,4},{20,32},{24,12},{28,40},{32,... | collective-permute-start | bytes 49160 | tf_op jit(solution)/shard_map/ppermute | solution.py:491
  158.7 14.0 %collective-permute-start.29 = (bf16[32,512]{1,0:T(8,128)(2,1)S(1)}, bf16[32,512]{1,0:T(8,128)(2,1)S(1)}, u32[]{:S(2)}, u32[]{:S(2)}) collective-permute-start(bf16[32,512]{1,0:T(8,128)(2,1)S(1)} %pad_maximum_fusion.4.refs_4_), channel_id=1, source_target_pairs={{0,504},{4,508},{8,0},{12,4},{16,8},{20,12},{24,16},{28,20},{32,24... | collective-permute-start | bytes 98312 | tf_op jit(solution)/shard_map/ppermute | solution.py:491
  165.7 8.5 %collective-permute-start.30 = (bf16[32,512]{1,0:T(8,128)(2,1)S(1)}, bf16[32,512]{1,0:T(8,128)(2,1)S(1)}, u32[]{:S(2)}, u32[]{:S(2)}) collective-permute-start(bf16[32,512]{1,0:T(8,128)(2,1)S(1)} %pad_maximum_fusion.5.refs_5_), channel_id=1, source_target_pairs={{0,8},{4,12},{8,16},{12,20},{16,24},{20,28},{24,32},{28,36},{32,40... | collective-permute-start | bytes 98312 | tf_op jit(solution)/shard_map/ppermute | solution.py:491
